TPU v7x, 32 devices: a whole 2x2x4 slice. The times are simulated.
32 devices in a mesh: sn: 8 (over y, x, core), rhs: 4 (over z).
Axes of the slice: x: 2, y: 2, z: 4, core: 2. Of those that a mesh axis runs over, the one named last changes fastest.
Arguments:
- rhs_leaf: float32 [256, 256, 128], P('sn', 'rhs'), may hold values from -6 to 6
- rhs_top: float32 [8, 256, 128], P('sn', 'rhs'), may hold values from -6 to 6
- leaf_blocks: float32 [256, 3, 128, 128], P('sn', None, 'rhs'), may hold values from -0.078125 to 0.078125
- leaf_dinv: float32 [256, 128, 128], P('sn', 'rhs')
- leaf_struct: int32 [256, 3], P('sn'), may hold values from 1 to 39, as said below
- top_blocks: float32 [8, 8, 128, 128], P(None, 'sn', 'rhs'), may hold values from -0.1875 to 0.1875
- top_dinv: float32 [8, 128, 128], P('sn', 'rhs')
Outputs:
- leaf_solution: float32 [256, 256, 128], P('sn', 'rhs')
- top_solution: float32 [8, 256, 128], P('sn', 'rhs')
Inputs may be any that keep to these rules, and one draw needn't show every extreme that they name: `leaf_struct`: subtree d hangs below top supernode a = 4 * (d // 4). Row d * 32 + s names 3 distinct ancestors of leaf supernode s of subtree d: a value v < 32 is supernode v of the same subtree, with v > s; a value 32 + k is a top supernode k on a's path to the root, that is k = a or the factor holds top block (k, a). Column 0 is the elimination tree parent: s + 1, except for the subtree's last supernode, whose parent is 32 + a.
All inputs are finite; a program needn't handle non-finite values.
Results may differ from a plain program's by a relative error of at most 0.00018.
Values sent between devices are 32-bit elements; how exact they have to be, the bound alone decides.
No kernel may reach another device: no remote copies, remote signals or barrier semaphores. Data moves between devices by JAX's collectives and lax.ppermute only.
A program may use at most 64 MiB of HBM per device.

v0:
```python
import functools

import jax
import jax.numpy as jnp
import numpy as np
from jax import lax
from jax.experimental import pallas as pl
from jax.experimental.pallas import tpu as pltpu
from jax.sharding import Mesh
from jax.sharding import PartitionSpec as P

CHUNKS = 2
TURNS = 4
GROUP = 4
f32 = jnp.float32
bf16 = jnp.bfloat16
SMEM = pl.BlockSpec(memory_space=pltpu.SMEM)
VMEM = pl.BlockSpec(memory_space=pltpu.VMEM)


def params():
    return pltpu.CompilerParams(vmem_limit_bytes=28 * 2**20)


def split(value):
    high = value.astype(bf16)
    return high, (value - high.astype(f32)).astype(bf16)


def product(left, right, transposed):
    dims = (((1,), (1 if transposed else 0,)), ((), ()))

    def dot(a, b):
        return lax.dot_general(a, b, dims, preferred_element_type=f32)

    rows = left[0].shape[0]
    if rows % 16:
        return dot(left[0], right[0]) + (dot(left[1], right[0]) + dot(left[0], right[1]))
    both = dot(jnp.concatenate(left, axis=0), right[0])
    return both[:rows] + (both[rows:] + dot(left[0], right[1]))


def ancestors_of(tops):
    def level(t):
        return ((t + 1) & -(t + 1)).bit_length() - 1

    return [[t for t in range(j + 1, tops) if t + 1 - 2 ** level(t) <= j] for j in range(tops)]


def paths_of(subtrees, above):
    return [[4 * (d // 4)] + above[4 * (d // 4)] for d in range(subtrees)]


def padded(rows, width):
    return np.array([row + [row[0] if row else 0] * (width - len(row)) for row in rows], np.int32)


def forward_kernel(base, first, last, width, *refs):
    meta, kept, passed, rhs, rhs_top = refs[0], refs[1:5], refs[5:9], refs[9], refs[10]
    refs = refs[11:]
    if not first:
        acc_in, refs = refs[0], refs[1:]
    acc, high, low, scaled, refs = refs[0], refs[1], refs[2], refs[3], refs[4:]
    if last:
        payload, refs = refs[0], refs[1:]
    full, arrived = refs
    steps, columns, rows = scaled.shape[0], scaled.shape[1], kept[0].shape[2]
    leafs = steps * CHUNKS
    wide = full.shape[2]

    def copies(pieces, group):
        made = []
        for place, piece in enumerate(pieces):
            offset = pl.multiple_of(meta[3 * leafs + place] * rows, rows)
            start = group * GROUP + (base if piece.shape[0] > steps else 0)
            made.append(
                pltpu.make_async_copy(
                    piece.at[pl.ds(start, GROUP)],
                    full.at[pl.ds(group * GROUP, GROUP), :, pl.ds(offset, rows), :],
                    arrived.at[group, place],
                )
            )
        return made

    def start(pieces):
        for group in range(steps // GROUP):
            for copy in copies(pieces, group):
                copy.start()

    keeps = meta[3 * leafs + 4 + width]
    pl.when(keeps == 1)(lambda: start(kept))
    pl.when(keeps == 0)(lambda: start(passed))
    if first:
        acc[...] = jnp.zeros_like(acc)
    else:
        acc[...] = acc_in[...]
    for group in range(steps // GROUP):
        for copy in copies(kept, group):
            copy.wait()
        members = range(group * GROUP, (group + 1) * GROUP)
        for s in members:
            blocks = split(full[s, 0:3].reshape(3 * wide, wide))
            merged = split(product(blocks, split(full[s, 3]), False))
            high[s] = merged[0]
            low[s] = merged[1]
        for s in members:
            at = s * columns
            source = split(rhs[at : at + columns] - acc[base + s])
            outgoing = product(source, (high[s], low[s]), True)
            for r in range(3):
                target = meta[3 * (base + s) + r]
                acc[target] = acc[target] + outgoing[:, r * wide : (r + 1) * wide]
            inverse = split(full[s, 3])
            solved = split(product(source, inverse, True))
            scaled[s] = product(solved, inverse, False)
    if last:
        peers, part = payload.shape[0], payload.shape[2]
        groups = columns // part
        for i in range(width + 1):
            node = acc[leafs + meta[3 * leafs + 4 + i]] if i < width else rhs_top[...]
            for p in range(peers):
                at = (p % groups) * part
                payload[p, i] = node[at : at + part]


def backward_kernel(base, first, width, meta, high, low, scaled, state, out, z):
    steps, wide = scaled.shape[0], scaled.shape[2]
    leafs = steps * TURNS
    if first:
        part = state.shape[2]
        groups = scaled.shape[1] // part
        z[...] = jnp.zeros_like(z)
        for i in range(width):
            node = leafs + meta[3 * leafs + 4 + i]
            for p in range(groups):
                z[node, p * part : (p + 1) * part, :] = state[p, i]
    else:
        z[...] = state[...]
    for s in range(steps - 1, -1, -1):
        total = scaled[s]
        for r in (2, 1, 0):
            source = split(z[meta[3 * (base + s) + r]])
            at = slice(r * wide, (r + 1) * wide)
            total = total - product(source, (high[s, at], low[s, at]), False)
        z[base + s] = total
        out[s] = total


def top_prepare_kernel(top, high, low, inverse_high, inverse_low):
    count, wide = top.shape[1] - 1, top.shape[2]
    inverse = split(top[0, count])
    merged = product(split(top[0, :count].reshape(count * wide, wide)), inverse, False)
    high[0], low[0] = split(merged)
    inverse_high[0], inverse_low[0] = inverse


def top_kernel(above, paths, incoming, high, low, inverse_high, inverse_low, outgoing):
    tops, wide = len(above), high.shape[2]
    width = outgoing.shape[1] - 1
    sources = [incoming[t, width] for t in range(tops)]
    for d, path in enumerate(paths):
        for i, t in enumerate(path):
            sources[t] = sources[t] - incoming[d, i]
    scaled = []
    for j in range(tops):
        source = split(sources[j])
        count = len(above[j])
        if count:
            rows = slice(0, count * wide)
            updates = product(source, (high[j, rows], low[j, rows]), True)
            for i, t in enumerate(above[j]):
                sources[t] = sources[t] - updates[:, i * wide : (i + 1) * wide]
        inverse = (inverse_high[j], inverse_low[j])
        scaled.append(product(split(product(source, inverse, True)), inverse, False))
    solved = [None] * tops
    parts = [None] * tops
    for j in range(tops - 1, -1, -1):
        total = scaled[j]
        for i, t in enumerate(above[j]):
            rows = slice(i * wide, (i + 1) * wide)
            total = total - product(parts[t], (high[j, rows], low[j, rows]), False)
        solved[j] = total
        parts[j] = split(total)
    for p in range(outgoing.shape[0]):
        path = paths[p]
        for i in range(width):
            outgoing[p, i] = solved[path[i] if i < len(path) else path[0]]
        outgoing[p, width] = solved[p]


def local(rhs_leaf, rhs_top, leaf_blocks, leaf_dinv, leaf_struct, top_blocks, top_dinv):
    leafs, columns, wide = rhs_leaf.shape
    tops = top_blocks.shape[0]
    steps = leafs // CHUNKS
    above = ancestors_of(tops)
    most = max(len(row) for row in above)
    width = most + 1
    paths = paths_of(tops, above)
    groups = min(tops, columns // 8)
    part = columns // groups

    core, zh, zl = lax.axis_index("core"), lax.axis_index("zh"), lax.axis_index("zl")
    xy = lax.axis_index("xy")

    def swap(value):
        return lax.ppermute(value, ("core", "zh"), [(0, 0), (1, 2), (2, 1), (3, 3)])

    def to_keeper(value):
        return lax.ppermute(value, ("core", "zh"), [(1, 0), (2, 3)])

    def to_trader(value):
        return lax.ppermute(value, ("core", "zh"), [(0, 2), (3, 1)])

    def keepers(value):
        return lax.ppermute(value, ("core", "zh", "zl"), [(0, 1), (1, 0), (6, 7), (7, 6)])

    def other(value, *axes):
        last = 2 ** len(axes) - 1
        return lax.ppermute(value, axes, [(i, last - i) for i in range(last + 1)])

    def after(first, value):
        return lax.optimization_barrier((first, value))[1]

    chosen = jnp.take(top_blocks[:, 0], jnp.asarray(padded(above, most))[2 * xy + core], axis=0)
    top = jnp.concatenate([chosen, top_dinv], axis=0)
    top = lax.dynamic_update_slice(
        jnp.zeros((width, wide, wide), f32), top, (0, (2 * zh + zl) * top.shape[1], 0)
    )
    summed = lax.psum(top, ("zh", "zl"))
    names = jnp.zeros((8, wide), f32).at[:3, :leafs].set(leaf_struct.T.astype(f32))
    sides = jnp.concatenate([rhs_leaf.reshape(-1, wide), rhs_top.reshape(-1, wide), names], axis=0)
    def joined(at):
        return jnp.concatenate([leaf_blocks[at], leaf_dinv[at][:, None]], axis=1)

    own = joined(slice(None))
    parts = [joined(slice(k * steps, (k + 1) * steps)) for k in range(CHUNKS)]
    near = keepers(own)
    sides = swap(sides)
    far = [to_keeper(part) for part in parts]
    across = [keepers(after((sides, summed), far[0]))]
    early = [to_trader(value) for value in after(summed, (own, near, far[0]))]
    across += [keepers(after(early, value)) for value in far[1:]]
    top = lax.all_gather(after(far[-1], summed), ("xy", "core"), axis=0, tiled=False)

    names = sides[(leafs + 1) * columns :][:3, :leafs].T.astype(jnp.int32).reshape(-1)
    path = jnp.asarray(padded(paths, width))[2 * xy + zh]
    places = jnp.stack([2 * zh + zl, 2 * zh + 1 - zl, 2 - 2 * zh + zl, 3 - 2 * zh - zl])
    keeps = (core == zh).astype(jnp.int32)
    meta = jnp.concatenate([names, places.astype(jnp.int32), path, keeps[None]])

    vectors = jax.ShapeDtypeStruct((leafs + tops, columns, wide), f32)
    merged = jax.ShapeDtypeStruct((steps, 3 * wide, wide), bf16)
    chunk = jax.ShapeDtypeStruct((steps, columns, wide), f32)
    cost = pl.CostEstimate(flops=4 * 10**9, bytes_accessed=8 * 2**20, transcendentals=0)
    factors, state = [], None
    for k in range(CHUNKS):
        last = k == CHUNKS - 1
        shapes = [vectors, merged, merged, chunk]
        if k == 0:
            passed = (early[2], to_trader(across[k]))
        else:
            passed = (to_trader(far[k]), to_trader(after(state, across[k])))
        specs = [SMEM] + [pl.BlockSpec(memory_space=pl.ANY)] * 8 + [
            pl.BlockSpec((steps * columns, wide), functools.partial(lambda k, i: (k, 0), k)),
            pl.BlockSpec((columns, wide), lambda i: (leafs, 0)),
        ]
        if last:
            shapes.append(jax.ShapeDtypeStruct((tops, width + 1, part, wide), f32))
        before = () if k == 0 else (state,)
        results = pl.pallas_call(
            functools.partial(forward_kernel, k * steps, k == 0, last, width),
            grid=(1,),
            in_specs=specs + [VMEM] * (k > 0),
            out_specs=[VMEM] * len(shapes),
            out_shape=shapes,
            scratch_shapes=[
                pltpu.VMEM((steps, 4, wide, wide), f32),
                pltpu.SemaphoreType.DMA((steps // GROUP, 4)),
            ],
            compiler_params=params(),
            cost_estimate=cost,
            name="leaf_forward",
        )(meta, own, near, far[k], across[k], *early[:2], *passed, sides, sides, *before)
        state = results[0]
        factors.append(results[1:4])

    def whole(*shape):
        return pl.BlockSpec((1,) + shape, lambda t: (t,) + (0,) * len(shape))

    top_factor = pl.pallas_call(
        top_prepare_kernel,
        grid=(tops,),
        in_specs=[whole(*top.shape[1:])],
        out_specs=[whole(most * wide, wide)] * 2 + [whole(wide, wide)] * 2,
        out_shape=[jax.ShapeDtypeStruct((tops, most * wide, wide), bf16)] * 2
        + [jax.ShapeDtypeStruct((tops, wide, wide), bf16)] * 2,
        compiler_params=params(),
        name="top_prepare",
    )(after(results[4], top))

    incoming = lax.all_to_all(results[4], ("xy", "zh"), split_axis=0, concat_axis=0, tiled=True)
    outgoing = pl.pallas_call(
        functools.partial(top_kernel, above, paths),
        in_specs=[VMEM] * 5,
        out_specs=VMEM,
        out_shape=jax.ShapeDtypeStruct((tops, width + 1, part, wide), f32),
        compiler_params=params(),
        name="top_solve",
    )(incoming, *top_factor)
    state = lax.all_to_all(outgoing, ("xy", "zh"), split_axis=0, concat_axis=0, tiled=True)
    own_top = state[:groups, width].reshape(1, columns, wide)

    found = [None] * TURNS
    steps = leafs // TURNS
    share = TURNS // CHUNKS
    chunk = jax.ShapeDtypeStruct((steps, columns, wide), f32)
    for k in range(TURNS - 1, -1, -1):
        part_of = [
            pl.BlockSpec((steps,) + shape, functools.partial(lambda k, i: (k, 0, 0), k % share))
            for shape in ((3 * wide, wide), (3 * wide, wide), (columns, wide))
        ]
        found[k], state = pl.pallas_call(
            functools.partial(backward_kernel, k * steps, k == TURNS - 1, width),
            grid=(1,),
            in_specs=[SMEM] + part_of + [VMEM],
            out_specs=[VMEM] * 2,
            out_shape=[chunk, vectors],
            compiler_params=params(),
            cost_estimate=cost,
            name="leaf_backward",
        )(meta, *factors[k // share], state)
    late = swap(found[-1])
    middle = swap(jnp.concatenate(found[1:-1] + [own_top], axis=0))
    first = swap(after(late, found[0]))
    leaf_solution = jnp.concatenate([first, middle[:-1], late], axis=0)
    return (leaf_solution, middle[-1:])


def solution(mesh):
    subtrees, quarters = mesh.devices.shape
    fine = Mesh(
        mesh.devices.reshape(subtrees // 2, 2, 2, quarters // 2), ("xy", "core", "zh", "zl")
    )
    sn, rhs = ("xy", "core"), ("zh", "zl")
    return jax.shard_map(
        local,
        mesh=fine,
        in_specs=(
            P(sn, rhs, None),
            P(sn, rhs, None),
            P(sn, None, rhs, None),
            P(sn, rhs, None),
            P(sn, None),
            P(None, sn, rhs, None),
            P(sn, rhs, None),
        ),
        out_specs=(P(sn, rhs, None), P(sn, rhs, None)),
        check_vma=False,
    )
```

profile of v0, /device:TPU:1, one launch (start us, length us, event | category | flops | bytes accessed | tf_op | source)
XLA Modules:
  0.0 209.4 jit_solution(7710438141774334796)
XLA Ops:
  7.2 1.9 pad_maximum_fusion.refs_1_
  9.1 2.0 collective-permute-start.1
  11.1 0.7 slice_bitcast_fusion
  11.9 1.0 fusion.3
  12.9 1.1 pad_maximum_fusion.2
  14.0 7.2 %collective-permute-start.3 = (f32[16,4,32,128]{3,2,1,0:T(8,128)}, f32[16,4,32,128]{3,2,1,0:T(8,128)}, u32[]{:S(2)}, u32[]{:S(2)}) collective-permute-start(f32[16,4,32,128]{3,2,1,0:T(8,128)} %pad_maximum_fusion.2), channel_id=1, source_target_pairs={{2,0},{4,6},{3,1},{5,7},{10,8},{12,14},{11,9},{13,15},{18,16},{20,... | collective-permute-start | bytes 3145736 | tf_op jit(solution)/shard_map/ppermute | solution.py:209
  21.2 1.1 select_maximum_fusion
  22.3 3.1 %collective-permute-start = (f32[2120,128]{1,0:T(8,128)}, f32[2120,128]{1,0:T(8,128)S(1)}, u32[]{:S(2)}, u32[]{:S(2)}) collective-permute-start(f32[2120,128]{1,0:T(8,128)} %select_maximum_fusion), channel_id=1, source_target_pairs={{0,0},{2,4},{4,2},{6,6},{1,1},{3,5},{5,3},{7,7},{8,8},{10,12},{12,... | collective-permute-start | bytes 3256328 | tf_op jit(solution)/shard_map/ppermute | solution.py:206
  26.7 0.7 compare_and_fusion
  27.4 0.7 broadcast_in_dim.33
  28.9 42.0 %all-reduce.3.cloned.1.call-done = f32[4,128,128]{2,1,0:T(8,128)} async-done(((f32[4,128,128]{2,1,0:T(8,128)}), f32[4,128,128]{2,1,0:T(8,128)}) %all-reduce.3.cloned.1.call-update) | async-done | bytes 262160 | tf_op jit(solution)/shard_map/psum | solution.py:229
  70.9 1.3 collective-permute-start.4
  72.2 1.3 collective-permute-start.5
  73.5 1.3 pad_maximum_fusion.1
  74.8 5.9 %collective-permute-start.2 = (f32[16,4,32,128]{3,2,1,0:T(8,128)S(1)}, f32[16,4,32,128]{3,2,1,0:T(8,128)}, u32[]{:S(2)}, u32[]{:S(2)}) collective-permute-start(f32[16,4,32,128]{3,2,1,0:T(8,128)S(1)} %pad_maximum_fusion.1), channel_id=1, source_target_pairs={{2,0},{4,6},{3,1},{5,7},{10,8},{12,14},{11,9},{13,15},{18,16},{20,... | collective-permute-start | bytes 3145736 | tf_op jit(solution)/shard_map/ppermute | solution.py:209
  80.7 1.6 collective-permute-start.9
  82.3 1.3 collective-permute-start.6
  83.6 16.5 %collective-permute-done.2.refs_3_ = f32[16,4,32,128]{3,2,1,0:T(8,128)} collective-permute-done((f32[16,4,32,128]{3,2,1,0:T(8,128)S(1)}, f32[16,4,32,128]{3,2,1,0:T(8,128)}, u32[]{:S(2)}, u32[]{:S(2)}) %collective-permute-start.2) | collective-permute-done | bytes 1048608 | tf_op jit(solution)/shard_map/ppermute | solution.py:209
  100.1 1.3 collective-permute-start.10
  101.4 1.7 collective-permute-start.7
  103.7 1.3 collective-permute-start.8
  105.3 6.5 %collective-permute-done.10.refs_8_ = f32[16,4,32,128]{3,2,1,0:T(8,128)} collective-permute-done((f32[16,4,32,128]{3,2,1,0:T(8,128)}, f32[16,4,32,128]{3,2,1,0:T(8,128)}, u32[]{:S(2)}, u32[]{:S(2)}) %collective-permute-start.10) | collective-permute-done | bytes 1048608 | tf_op jit(solution)/shard_map/ppermute | solution.py:212
  111.9 8.3 %leaf_forward.2 = (f32[40,64,128]{2,1,0:T(8,128)S(1)}, bf16[16,384,128]{2,1,0:T(8,128)(2,1)S(1)}, bf16[16,384,128]{2,1,0:T(8,128)(2,1)S(1)}, f32[16,64,128]{2,1,0:T(8,128)S(1)}) custom-call(s32[105]{0:T(128)S(1)} %concatenate.27.refs_0_.meta, f32[32,4,32,128]{3,2,1,0:T(8,128)S(1)} %pad_maximum_fusion.refs_1_, ...), custom_call_target="tpu_custom_call" | custom-call | flops 4000000000 | bytes 8388608 | tf_op jit(solution)/shard_map/leaf_forward/pallas_call | solution.py:270
  120.2 1.1 copy-done.8
  121.3 1.1 copy-done.10
  122.5 1.3 collective-permute-start.11
  123.8 7.3 %collective-permute-done.11.refs_8_ = f32[16,4,32,128]{3,2,1,0:T(8,128)S(1)} collective-permute-done((f32[16,4,32,128]{3,2,1,0:T(8,128)}, f32[16,4,32,128]{3,2,1,0:T(8,128)S(1)}, u32[]{:S(2)}, u32[]{:S(2)}) %collective-permute-start.11) | collective-permute-done | bytes 1048608 | tf_op jit(solution)/shard_map/ppermute | solution.py:212
  131.1 9.1 %leaf_forward.3 = (f32[40,64,128]{2,1,0:T(8,128)}, bf16[16,384,128]{2,1,0:T(8,128)(2,1)S(1)}, bf16[16,384,128]{2,1,0:T(8,128)(2,1)S(1)}, f32[16,64,128]{2,1,0:T(8,128)S(1)}, f32[8,5,8,128]{3,2,1,0:T(8,128)}) custom-call(s32[105]{0:T(128)S(1)} %concatenate.27.refs_0_.meta, f32[32,4,32,128]{3,2,1,0:T(8,128)S(1)} %pad_maximum_fusion.refs_1_, ...), custom_call_target="tpu_custom_call" | custom-call | flops 4000000000 | bytes 8388608 | tf_op jit(solution)/shard_map/leaf_forward/pallas_call | solution.py:270
  140.3 1.2 copy-done.2
  141.4 1.2 copy-done.4
  142.6 0.8 copy-done.6
  143.4 3.4 %all-to-all-start = ((f32[8,5,8,128]{3,2,1,0:T(8,128)}), f32[8,5,8,128]{3,2,1,0:T(8,128)S(1)}, u32[]{:S(2)}, u32[]{:S(2)}) async-start(f32[8,5,8,128]{3,2,1,0:T(8,128)} %get-tuple-element.52), calls=%async_computation | async-start | bytes 327680 | tf_op jit(solution)/shard_map/all_to_all | solution.py:301
  146.9 1.6 copy-done.1
  148.5 1.9 top_prepare.1
  150.4 5.4 %all-to-all-done.incoming = f32[8,5,8,128]{3,2,1,0:T(8,128)S(1)} async-done(((f32[8,5,8,128]{3,2,1,0:T(8,128)}), f32[8,5,8,128]{3,2,1,0:T(8,128)S(1)}, u32[]{:S(2)}, u32[]{:S(2)}) %all-to-all-start) | async-done | bytes 163872 | tf_op jit(solution)/shard_map/all_to_all | solution.py:301
  155.8 2.7 %top_solve.1 = f32[8,5,8,128]{3,2,1,0:T(8,128)S(1)} custom-call(f32[8,5,8,128]{3,2,1,0:T(8,128)S(1)} %all-to-all-done.incoming, bf16[8,384,128]{2,1,0:T(8,128)(2,1)S(1)} %get-tuple-element.55.high, bf16[8,384,128]{2,1,0:T(8,128)(2,1)S(1)} %get-tuple-element.56.low, bf16[8,128,128]{2,1,0:T(8,128)(2,1)S(1)} %get-tuple-element.57.inverse_high, ...), custom_call_target="tpu_custom_call" | custom-call | tf_op jit(solution)/shard_map/top_solve/pallas_call | solution.py:302
  158.5 9.9 %all_to_all.10.state = f32[8,5,8,128]{3,2,1,0:T(8,128)S(1)} all-to-all(f32[8,5,8,128]{3,2,1,0:T(8,128)S(1)} %top_solve.1), channel_id=1, replica_groups=mesh['xy'=4,'core'=2,'zh'=2,'zl'=2] {'xy','zh'}, dimensions={0} | all-to-all | bytes 327680 | tf_op jit(solution)/shard_map/all_to_all | solution.py:310
  168.4 1.4 copy-done.5
  169.9 2.1 %leaf_backward.4 = (f32[8,64,128]{2,1,0:T(8,128)S(1)}, f32[40,64,128]{2,1,0:T(8,128)S(1)}) custom-call(s32[105]{0:T(128)S(1)} %concatenate.27.refs_0_.meta, bf16[16,384,128]{2,1,0:T(8,128)(2,1)S(1)} %copy-done.3, bf16[16,384,128]{2,1,0:T(8,128)(2,1)S(1)} %copy-done.5, f32[16,64,128]{2,1,0:T(8,128)S(1)} %copy-done.7, f32[8,5,8,128]{3,2,1,0:T(8,128)S(1)} %all_to_all.10.state), custom_call_target="tpu_custom_call" | custom-call | flops 4000000000 | bytes 8388608 | tf_op jit(solution)/shard_map/leaf_backward/pallas_call | solution.py:322
  172.0 2.1 %leaf_backward.5 = (f32[8,64,128]{2,1,0:T(8,128)S(1)}, f32[40,64,128]{2,1,0:T(8,128)S(1)}) custom-call(s32[105]{0:T(128)S(1)} %concatenate.27.refs_0_.meta, bf16[16,384,128]{2,1,0:T(8,128)(2,1)S(1)} %copy-done.3, bf16[16,384,128]{2,1,0:T(8,128)(2,1)S(1)} %copy-done.5, f32[16,64,128]{2,1,0:T(8,128)S(1)} %copy-done.7, f32[40,64,128]{2,1,0:T(8,128)S(1)} %get-tuple-element.63.state), custom_call_target="tpu_custom_call" | custom-call | flops 4000000000 | bytes 8388608 | tf_op jit(solution)/shard_map/leaf_backward/pallas_call | solution.py:322
  174.1 2.5 %collective-permute-start.12 = (f32[8,64,128]{2,1,0:T(8,128)S(1)}, f32[8,64,128]{2,1,0:T(8,128)S(1)}, u32[]{:S(2)}, u32[]{:S(2)}) collective-permute-start(f32[8,64,128]{2,1,0:T(8,128)S(1)} %get-tuple-element.59), channel_id=1, source_target_pairs={{0,0},{2,4},{4,2},{6,6},{1,1},{3,5},{5,3},{7,7},{8,8},{10,12},{12,... | collective-permute-start | bytes 786440 | tf_op jit(solution)/shard_map/ppermute | solution.py:206
  176.6 2.1 %leaf_backward.6 = (f32[8,64,128]{2,1,0:T(8,128)S(1)}, f32[40,64,128]{2,1,0:T(8,128)S(1)}) custom-call(s32[105]{0:T(128)S(1)} %concatenate.27.refs_0_.meta, bf16[16,384,128]{2,1,0:T(8,128)(2,1)S(1)} %copy-done.9, bf16[16,384,128]{2,1,0:T(8,128)(2,1)S(1)} %copy-done.11, f32[16,64,128]{2,1,0:T(8,128)S(1)} %copy-done.13, f32[40,64,128]{2,1,0:T(8,128)S(1)} %get-tuple-element.64.state), custom_call_target="tpu_custom_call" | custom-call | flops 4000000000 | bytes 8388608 | tf_op jit(solution)/shard_map/leaf_backward/pallas_call | solution.py:322
  178.8 4.0 %collective-permute-start.14 = (f32[17,64,128]{2,1,0:T(8,128)S(1)}, f32[17,64,128]{2,1,0:T(8,128)S(1)}, u32[]{:S(2)}, u32[]{:S(2)}) collective-permute-start(f32[17,64,128]{2,1,0:T(8,128)S(1)} %pad_maximum_fusion.4), channel_id=1, source_target_pairs={{0,0},{2,4},{4,2},{6,6},{1,1},{3,5},{5,3},{7,7},{8,8},{10,12},{12,... | collective-permute-start | bytes 1671176 | tf_op jit(solution)/shard_map/ppermute | solution.py:206
  182.8 3.3 %leaf_backward.7 = (f32[8,64,128]{2,1,0:T(8,128)S(1)}, f32[40,64,128]{2,1,0:T(8,128)}) custom-call(s32[105]{0:T(128)S(1)} %concatenate.27.refs_0_.meta, bf16[16,384,128]{2,1,0:T(8,128)(2,1)S(1)} %copy-done.9, bf16[16,384,128]{2,1,0:T(8,128)(2,1)S(1)} %copy-done.11, f32[16,64,128]{2,1,0:T(8,128)S(1)} %copy-done.13, f32[40,64,128]{2,1,0:T(8,128)S(1)} %get-tuple-element.65.state), custom_call_target="tpu_custom_call" | custom-call | flops 4000000000 | bytes 8388608 | tf_op jit(solution)/shard_map/leaf_backward/pallas_call | solution.py:322
  186.1 2.5 %collective-permute-start.13 = (f32[8,64,128]{2,1,0:T(8,128)S(1)}, f32[8,64,128]{2,1,0:T(8,128)S(1)}, u32[]{:S(2)}, u32[]{:S(2)}) collective-permute-start(f32[8,64,128]{2,1,0:T(8,128)S(1)} %get-tuple-element.67), channel_id=1, source_target_pairs={{0,0},{2,4},{4,2},{6,6},{1,1},{3,5},{5,3},{7,7},{8,8},{10,12},{12,... | collective-permute-start | bytes 786440 | tf_op jit(solution)/shard_map/ppermute | solution.py:206
  188.5 10.1 %collective-permute-done.14 = f32[17,64,128]{2,1,0:T(8,128)S(1)} collective-permute-done((f32[17,64,128]{2,1,0:T(8,128)S(1)}, f32[17,64,128]{2,1,0:T(8,128)S(1)}, u32[]{:S(2)}, u32[]{:S(2)}) %collective-permute-start.14) | collective-permute-done | bytes 557088 | tf_op jit(solution)/shard_map/ppermute | solution.py:206
  199.3 2.1 %collective-permute-done.13 = f32[8,64,128]{2,1,0:T(8,128)S(1)} collective-permute-done((f32[8,64,128]{2,1,0:T(8,128)S(1)}, f32[8,64,128]{2,1,0:T(8,128)S(1)}, u32[]{:S(2)}, u32[]{:S(2)}) %collective-permute-start.13) | collective-permute-done | bytes 262176 | tf_op jit(solution)/shard_map/ppermute | solution.py:206
  201.5 1.1 pad_maximum_fusion.3
  (63 shorter events, 3.9 us)
Async XLA Ops:
  7.2 18.9 %copy-start = (f32[8,1,32,128]{3,2,1,0:T(8,128)S(1)}, f32[8,1,32,128]{3,2,1,0:T(8,128)}, u32[]{:S(2)}) copy-start(f32[8,1,32,128]{3,2,1,0:T(8,128)} %param.16) | copy-start | bytes 393220
  7.2 63.7 %all-reduce.3.cloned.1.call-start = ((), (), s32[]{:S(2)}) async-start(), calls=%async_computation.2 | async-start | bytes 524288 | tf_op jit(solution)/shard_map/psum | solution.py:229
  7.2 3.9 %copy-start.15 = (f32[32,32,128]{2,1,0:T(8,128)S(1)}, f32[32,32,128]{2,1,0:T(8,128)}, u32[]{:S(2)}) copy-start(f32[32,32,128]{2,1,0:T(8,128)} %param.14) | copy-start | bytes 1572868
  7.2 4.7 %copy-start.14 = (f32[32,3,32,128]{3,2,1,0:T(8,128)S(1)}, f32[32,3,32,128]{3,2,1,0:T(8,128)}, u32[]{:S(2)}) copy-start(f32[32,3,32,128]{3,2,1,0:T(8,128)} %param.13) | copy-start | bytes 4718596
  9.1 61.7 %collective-permute-start.1 = (f32[32,4,32,128]{3,2,1,0:T(8,128)S(1)}, f32[32,4,32,128]{3,2,1,0:T(8,128)}, u32[]{:S(2)}, u32[]{:S(2)}) collective-permute-start(f32[32,4,32,128]{3,2,1,0:T(8,128)S(1)} %pad_maximum_fusion.refs_1_), channel_id=1, source_target_pairs={{0,1},{1,0},{6,7},{7,6},{8,9},{9,8},{14,15},{15,14},{16,17},{17,16... | collective-permute-start | bytes 6291464 | tf_op jit(solution)/shard_map/ppermute | solution.py:215
  12.9 8.3 %copy-start.19 = (s32[32,3]{0,1:T(4,128)S(1)}, s32[32,3]{0,1:T(4,128)}, u32[]{:S(2)}) copy-start(s32[32,3]{0,1:T(4,128)} %param.15) | copy-start | bytes 1156
  12.9 8.3 %copy-start.16 = (f32[32,64,128]{2,1,0:T(8,128)S(1)}, f32[32,64,128]{2,1,0:T(8,128)}, u32[]{:S(2)}) copy-start(f32[32,64,128]{2,1,0:T(8,128)} %param.11) | copy-start | bytes 3145732
  12.9 8.3 %copy-start.17 = (f32[1,64,128]{2,1,0:T(8,128)S(1)}, f32[1,64,128]{2,1,0:T(8,128)}, u32[]{:S(2)}) copy-start(f32[1,64,128]{2,1,0:T(8,128)} %param.12) | copy-start | bytes 98308
  14.0 56.9 %collective-permute-start.3 = (f32[16,4,32,128]{3,2,1,0:T(8,128)}, f32[16,4,32,128]{3,2,1,0:T(8,128)}, u32[]{:S(2)}, u32[]{:S(2)}) collective-permute-start(f32[16,4,32,128]{3,2,1,0:T(8,128)} %pad_maximum_fusion.2), channel_id=1, source_target_pairs={{2,0},{4,6},{3,1},{5,7},{10,8},{12,14},{11,9},{13,15},{18,16},{20,... | collective-permute-start | bytes 3145736 | tf_op jit(solution)/shard_map/ppermute | solution.py:209
  21.2 7.0 %copy-start.18 = (f32[1,32,128]{2,1,0:T(8,128)S(1)}, f32[1,32,128]{2,1,0:T(8,128)}, u32[]{:S(2)}) copy-start(f32[1,32,128]{2,1,0:T(8,128)} %param.17) | copy-start | bytes 49156
  22.3 58.4 %collective-permute-start = (f32[2120,128]{1,0:T(8,128)}, f32[2120,128]{1,0:T(8,128)S(1)}, u32[]{:S(2)}, u32[]{:S(2)}) collective-permute-start(f32[2120,128]{1,0:T(8,128)} %select_maximum_fusion), channel_id=1, source_target_pairs={{0,0},{2,4},{4,2},{6,6},{1,1},{3,5},{5,3},{7,7},{8,8},{10,12},{12,... | collective-permute-start | bytes 3256328 | tf_op jit(solution)/shard_map/ppermute | solution.py:206
  28.8 118.0 %all-gather.3.cloned.1.call-start = ((), (), s32[]{:S(2)}) async-start(), calls=%async_computation.3 | async-start | bytes 2359296 | tf_op jit(solution)/shard_map/all_gather | solution.py:243
  70.9 30.5 %collective-permute-start.4 = (f32[32,4,32,128]{3,2,1,0:T(8,128)S(1)}, f32[32,4,32,128]{3,2,1,0:T(8,128)}, u32[]{:S(2)}, u32[]{:S(2)}) collective-permute-start(f32[32,4,32,128]{3,2,1,0:T(8,128)S(1)} %pad_maximum_fusion.refs_1_), channel_id=1, source_target_pairs={{0,4},{6,2},{1,5},{7,3},{8,12},{14,10},{9,13},{15,11},{16,20},{22,... | collective-permute-start | bytes 6291464 | tf_op jit(solution)/shard_map/ppermute | solution.py:212
  72.2 29.2 %collective-permute-start.5 = (f32[32,4,32,128]{3,2,1,0:T(8,128)}, f32[32,4,32,128]{3,2,1,0:T(8,128)}, u32[]{:S(2)}, u32[]{:S(2)}) collective-permute-start(f32[32,4,32,128]{3,2,1,0:T(8,128)} %collective-permute-done.1.refs_2_), channel_id=1, source_target_pairs={{0,4},{6,2},{1,5},{7,3},{8,12},{14,10},{9,13},{15,11},{16,20},{22,... | collective-permute-start | bytes 6291464 | tf_op jit(solution)/shard_map/ppermute | solution.py:212
  74.8 25.3 %collective-permute-start.2 = (f32[16,4,32,128]{3,2,1,0:T(8,128)S(1)}, f32[16,4,32,128]{3,2,1,0:T(8,128)}, u32[]{:S(2)}, u32[]{:S(2)}) collective-permute-start(f32[16,4,32,128]{3,2,1,0:T(8,128)S(1)} %pad_maximum_fusion.1), channel_id=1, source_target_pairs={{2,0},{4,6},{3,1},{5,7},{10,8},{12,14},{11,9},{13,15},{18,16},{20,... | collective-permute-start | bytes 3145736 | tf_op jit(solution)/shard_map/ppermute | solution.py:209
  80.7 19.4 %collective-permute-start.9 = (f32[16,4,32,128]{3,2,1,0:T(8,128)}, f32[16,4,32,128]{3,2,1,0:T(8,128)}, u32[]{:S(2)}, u32[]{:S(2)}) collective-permute-start(f32[16,4,32,128]{3,2,1,0:T(8,128)} %collective-permute-done.3.refs_3_), channel_id=1, source_target_pairs={{0,1},{1,0},{6,7},{7,6},{8,9},{9,8},{14,15},{15,14},{16,17},{17,16... | collective-permute-start | bytes 3145736 | tf_op jit(solution)/shard_map/ppermute | solution.py:215
  82.3 19.1 %collective-permute-start.6 = (f32[16,4,32,128]{3,2,1,0:T(8,128)}, f32[16,4,32,128]{3,2,1,0:T(8,128)}, u32[]{:S(2)}, u32[]{:S(2)}) collective-permute-start(f32[16,4,32,128]{3,2,1,0:T(8,128)} %collective-permute-done.3.refs_3_), channel_id=1, source_target_pairs={{0,4},{6,2},{1,5},{7,3},{8,12},{14,10},{9,13},{15,11},{16,20},{22,... | collective-permute-start | bytes 3145736 | tf_op jit(solution)/shard_map/ppermute | solution.py:212
  100.1 11.8 %collective-permute-start.10 = (f32[16,4,32,128]{3,2,1,0:T(8,128)}, f32[16,4,32,128]{3,2,1,0:T(8,128)}, u32[]{:S(2)}, u32[]{:S(2)}) collective-permute-start(f32[16,4,32,128]{3,2,1,0:T(8,128)} %collective-permute-done.9.refs_4_), channel_id=1, source_target_pairs={{0,4},{6,2},{1,5},{7,3},{8,12},{14,10},{9,13},{15,11},{16,20},{22,... | collective-permute-start | bytes 3145736 | tf_op jit(solution)/shard_map/ppermute | solution.py:212
  101.4 21.1 %collective-permute-start.7 = (f32[16,4,32,128]{3,2,1,0:T(8,128)}, f32[16,4,32,128]{3,2,1,0:T(8,128)}, u32[]{:S(2)}, u32[]{:S(2)}) collective-permute-start(f32[16,4,32,128]{3,2,1,0:T(8,128)} %collective-permute-done.2.refs_3_), channel_id=1, source_target_pairs={{0,1},{1,0},{6,7},{7,6},{8,9},{9,8},{14,15},{15,14},{16,17},{17,16... | collective-permute-start | bytes 3145736 | tf_op jit(solution)/shard_map/ppermute | solution.py:215
  103.7 20.0 %collective-permute-start.8 = (f32[16,4,32,128]{3,2,1,0:T(8,128)}, f32[16,4,32,128]{3,2,1,0:T(8,128)}, u32[]{:S(2)}, u32[]{:S(2)}) collective-permute-start(f32[16,4,32,128]{3,2,1,0:T(8,128)} %collective-permute-done.2.refs_3_), channel_id=1, source_target_pairs={{0,4},{6,2},{1,5},{7,3},{8,12},{14,10},{9,13},{15,11},{16,20},{22,... | collective-permute-start | bytes 3145736 | tf_op jit(solution)/shard_map/ppermute | solution.py:212
  120.2 1.1 copy-start.8
  121.3 1.1 copy-start.10
  122.5 17.8 %copy-start.12 = (f32[16,64,128]{2,1,0:T(8,128)}, f32[16,64,128]{2,1,0:T(8,128)S(1)}, u32[]{:S(2)}) copy-start(f32[16,64,128]{2,1,0:T(8,128)S(1)} %get-tuple-element.62.scaled) | copy-start | bytes 1572868
  122.5 8.6 %collective-permute-start.11 = (f32[16,4,32,128]{3,2,1,0:T(8,128)}, f32[16,4,32,128]{3,2,1,0:T(8,128)S(1)}, u32[]{:S(2)}, u32[]{:S(2)}) collective-permute-start(f32[16,4,32,128]{3,2,1,0:T(8,128)} %collective-permute-done.7.refs_4_), channel_id=1, source_target_pairs={{0,4},{6,2},{1,5},{7,3},{8,12},{14,10},{9,13},{15,11},{16,20},{22,... | collective-permute-start | bytes 3145736 | tf_op jit(solution)/shard_map/ppermute | solution.py:212
  140.3 1.2 copy-start.2
  141.4 1.2 copy-start.4
  142.6 0.8 copy-start.6
  143.4 12.4 %all-to-all-start = ((f32[8,5,8,128]{3,2,1,0:T(8,128)}), f32[8,5,8,128]{3,2,1,0:T(8,128)S(1)}, u32[]{:S(2)}, u32[]{:S(2)}) async-start(f32[8,5,8,128]{3,2,1,0:T(8,128)} %get-tuple-element.52), calls=%async_computation | async-start | bytes 327680 | tf_op jit(solution)/shard_map/all_to_all | solution.py:301
  146.9 1.6 copy-start.1
  155.8 12.6 %copy-start.3 = (bf16[16,384,128]{2,1,0:T(8,128)(2,1)S(1)}, bf16[16,384,128]{2,1,0:T(8,128)(2,1)}, u32[]{:S(2)}) copy-start(bf16[16,384,128]{2,1,0:T(8,128)(2,1)} %copy-done.2) | copy-start | bytes 4718596
  155.8 12.6 %copy-start.7 = (f32[16,64,128]{2,1,0:T(8,128)S(1)}, f32[16,64,128]{2,1,0:T(8,128)}, u32[]{:S(2)}) copy-start(f32[16,64,128]{2,1,0:T(8,128)} %copy-done.6) | copy-start | bytes 1572868
  168.4 1.4 copy-start.5
  172.0 4.6 %copy-start.9 = (bf16[16,384,128]{2,1,0:T(8,128)(2,1)S(1)}, bf16[16,384,128]{2,1,0:T(8,128)(2,1)}, u32[]{:S(2)}) copy-start(bf16[16,384,128]{2,1,0:T(8,128)(2,1)} %copy-done.8) | copy-start | bytes 4718596
  172.0 4.6 %copy-start.11 = (bf16[16,384,128]{2,1,0:T(8,128)(2,1)S(1)}, bf16[16,384,128]{2,1,0:T(8,128)(2,1)}, u32[]{:S(2)}) copy-start(bf16[16,384,128]{2,1,0:T(8,128)(2,1)} %copy-done.10) | copy-start | bytes 4718596
  172.0 4.6 %copy-start.13 = (f32[16,64,128]{2,1,0:T(8,128)S(1)}, f32[16,64,128]{2,1,0:T(8,128)}, u32[]{:S(2)}) copy-start(f32[16,64,128]{2,1,0:T(8,128)} %copy-done.12) | copy-start | bytes 1572868
  174.1 12.0 %collective-permute-start.12 = (f32[8,64,128]{2,1,0:T(8,128)S(1)}, f32[8,64,128]{2,1,0:T(8,128)S(1)}, u32[]{:S(2)}, u32[]{:S(2)}) collective-permute-start(f32[8,64,128]{2,1,0:T(8,128)S(1)} %get-tuple-element.59), channel_id=1, source_target_pairs={{0,0},{2,4},{4,2},{6,6},{1,1},{3,5},{5,3},{7,7},{8,8},{10,12},{12,... | collective-permute-start | bytes 786440 | tf_op jit(solution)/shard_map/ppermute | solution.py:206
  178.8 19.8 %collective-permute-start.14 = (f32[17,64,128]{2,1,0:T(8,128)S(1)}, f32[17,64,128]{2,1,0:T(8,128)S(1)}, u32[]{:S(2)}, u32[]{:S(2)}) collective-permute-start(f32[17,64,128]{2,1,0:T(8,128)S(1)} %pad_maximum_fusion.4), channel_id=1, source_target_pairs={{0,0},{2,4},{4,2},{6,6},{1,1},{3,5},{5,3},{7,7},{8,8},{10,12},{12,... | collective-permute-start | bytes 1671176 | tf_op jit(solution)/shard_map/ppermute | solution.py:206
  186.1 15.4 %collective-permute-start.13 = (f32[8,64,128]{2,1,0:T(8,128)S(1)}, f32[8,64,128]{2,1,0:T(8,128)S(1)}, u32[]{:S(2)}, u32[]{:S(2)}) collective-permute-start(f32[8,64,128]{2,1,0:T(8,128)S(1)} %get-tuple-element.67), channel_id=1, source_target_pairs={{0,0},{2,4},{4,2},{6,6},{1,1},{3,5},{5,3},{7,7},{8,8},{10,12},{12,... | collective-permute-start | bytes 786440 | tf_op jit(solution)/shard_map/ppermute | solution.py:206
Sparse Core Ops, SparseCore 0:
  29.0 41.8 all-reduce.2
  100.2 32.3 all-gather.2
where the time goes:
time: 210 us; the launch traced here: 209 us
  waiting for transfers between devices  90.1 us (43%)
  starting transfers between devices  41.6 us (20%)
  Pallas kernels  31.6 us (15%)
  between operations  14.4 us (7%)
  local copies, waits for them, and re-layouts  13.2 us (6%)
  blocking collectives  9.91 us (5%)
  other arithmetic  8.58 us (4%)
    psum x1, waiting for transfers between devices, local(): summed = lax.psum(top, ('zh', 'zl'))  42 us
    pallas_call x2, Pallas kernels, local(): pl.pallas_call(functools.partial(forward_kernel, k * steps, k == 0, last,...  17.4 us
    ppermute x2, waiting for transfers between devices, to_keeper(): return lax.ppermute(value, ('core', 'zh'), [(1, 0), (2, 3)])  16.5 us
    ppermute x6, waiting for transfers between devices, to_trader(): return lax.ppermute(value, ('core', 'zh'), [(0, 2), (3, 1)])  13.9 us
    ppermute x2, starting transfers between devices, to_keeper(): return lax.ppermute(value, ('core', 'zh'), [(1, 0), (2, 3)])  13.1 us
    ppermute x4, waiting for transfers between devices, swap(): return lax.ppermute(value, ('core', 'zh'), [(0, 0), (1, 2), (2, 1), (3, 3)])  12.3 us
    ppermute x4, starting transfers between devices, swap(): return lax.ppermute(value, ('core', 'zh'), [(0, 0), (1, 2), (2, 1), (3, 3)])  12 us
    all_to_all x1, blocking collectives, local(): lax.all_to_all(outgoing, ('xy', 'zh'), split_axis=0, concat_axis=0, tiled...  9.91 us
  transfers between devices with their start and end apart: 18, of which 7 were waited for; matrix products, arithmetic and copies ran while one was open for 5% of the time, Pallas kernels for 12%

commit v1 on v0

--- a/solution.py
+++ b/solution.py
@@ -9,7 +9,7 @@
 from jax.sharding import Mesh
 from jax.sharding import PartitionSpec as P
 
-CHUNKS = 2
+CHUNKS = (3, 1)
 TURNS = 4
 GROUP = 4
 f32 = jnp.float32
@@ -55,7 +55,7 @@
     return np.array([row + [row[0] if row else 0] * (width - len(row)) for row in rows], np.int32)
 
 
-def forward_kernel(base, first, last, width, *refs):
+def forward_kernel(base, leafs, first, last, width, *refs):
     meta, kept, passed, rhs, rhs_top = refs[0], refs[1:5], refs[5:9], refs[9], refs[10]
     refs = refs[11:]
     if not first:
@@ -65,7 +65,6 @@
         payload, refs = refs[0], refs[1:]
     full, arrived = refs
     steps, columns, rows = scaled.shape[0], scaled.shape[1], kept[0].shape[2]
-    leafs = steps * CHUNKS
     wide = full.shape[2]
 
     def copies(pieces, group):
@@ -146,10 +145,13 @@
         out[s] = total
 
 
-def top_prepare_kernel(top, high, low, inverse_high, inverse_low):
-    count, wide = top.shape[1] - 1, top.shape[2]
-    inverse = split(top[0, count])
-    merged = product(split(top[0, :count].reshape(count * wide, wide)), inverse, False)
+def top_prepare_kernel(places, top, high, low, inverse_high, inverse_low, full):
+    blocks, rows, wide = top.shape[2], top.shape[3], top.shape[4]
+    for place in range(top.shape[1]):
+        offset = pl.multiple_of(places[place] * rows, rows)
+        full[:, pl.ds(offset, rows), :] = top[0, place]
+    inverse = split(full[blocks - 1])
+    merged = product(split(full[: blocks - 1].reshape((blocks - 1) * wide, wide)), inverse, False)
     high[0], low[0] = split(merged)
     inverse_high[0], inverse_low[0] = inverse
 
@@ -191,7 +193,8 @@
 def local(rhs_leaf, rhs_top, leaf_blocks, leaf_dinv, leaf_struct, top_blocks, top_dinv):
     leafs, columns, wide = rhs_leaf.shape
     tops = top_blocks.shape[0]
-    steps = leafs // CHUNKS
+    turn = leafs // TURNS
+    starts = [turn * sum(CHUNKS[:k]) for k in range(len(CHUNKS) + 1)]
     above = ancestors_of(tops)
     most = max(len(row) for row in above)
     width = most + 1
@@ -223,24 +226,25 @@
 
     chosen = jnp.take(top_blocks[:, 0], jnp.asarray(padded(above, most))[2 * xy + core], axis=0)
     top = jnp.concatenate([chosen, top_dinv], axis=0)
-    top = lax.dynamic_update_slice(
-        jnp.zeros((width, wide, wide), f32), top, (0, (2 * zh + zl) * top.shape[1], 0)
-    )
-    summed = lax.psum(top, ("zh", "zl"))
+    top = jnp.stack([top, other(top, "zh")])
+    top = jnp.concatenate([top, other(top, "zl")])
+
     names = jnp.zeros((8, wide), f32).at[:3, :leafs].set(leaf_struct.T.astype(f32))
     sides = jnp.concatenate([rhs_leaf.reshape(-1, wide), rhs_top.reshape(-1, wide), names], axis=0)
     def joined(at):
         return jnp.concatenate([leaf_blocks[at], leaf_dinv[at][:, None]], axis=1)
 
     own = joined(slice(None))
-    parts = [joined(slice(k * steps, (k + 1) * steps)) for k in range(CHUNKS)]
+    parts = [joined(slice(at, end)) for at, end in zip(starts, starts[1:])]
+    own, parts, sides = after(top, (own, parts, sides))
+
     near = keepers(own)
     sides = swap(sides)
     far = [to_keeper(part) for part in parts]
-    across = [keepers(after((sides, summed), far[0]))]
-    early = [to_trader(value) for value in after(summed, (own, near, far[0]))]
+    across = [keepers(after(sides, far[0]))]
+    early = [to_trader(value) for value in (own, near, far[0])]
     across += [keepers(after(early, value)) for value in far[1:]]
-    top = lax.all_gather(after(far[-1], summed), ("xy", "core"), axis=0, tiled=False)
+    top = lax.all_gather(after(far[-1], top), ("xy", "core"), axis=0, tiled=False)
 
     names = sides[(leafs + 1) * columns :][:3, :leafs].T.astype(jnp.int32).reshape(-1)
     path = jnp.asarray(padded(paths, width))[2 * xy + zh]
@@ -249,26 +253,27 @@
     meta = jnp.concatenate([names, places.astype(jnp.int32), path, keeps[None]])
 
     vectors = jax.ShapeDtypeStruct((leafs + tops, columns, wide), f32)
-    merged = jax.ShapeDtypeStruct((steps, 3 * wide, wide), bf16)
-    chunk = jax.ShapeDtypeStruct((steps, columns, wide), f32)
     cost = pl.CostEstimate(flops=4 * 10**9, bytes_accessed=8 * 2**20, transcendentals=0)
     factors, state = [], None
-    for k in range(CHUNKS):
-        last = k == CHUNKS - 1
+    for k, base in enumerate(starts[:-1]):
+        last = k == len(CHUNKS) - 1
+        steps = starts[k + 1] - base
+        merged = jax.ShapeDtypeStruct((steps, 3 * wide, wide), bf16)
+        chunk = jax.ShapeDtypeStruct((steps, columns, wide), f32)
         shapes = [vectors, merged, merged, chunk]
         if k == 0:
-            passed = (early[2], to_trader(across[k]))
+            passed = (early[2], to_trader(after(far[-1], across[k])))
         else:
             passed = (to_trader(far[k]), to_trader(after(state, across[k])))
         specs = [SMEM] + [pl.BlockSpec(memory_space=pl.ANY)] * 8 + [
-            pl.BlockSpec((steps * columns, wide), functools.partial(lambda k, i: (k, 0), k)),
+            pl.BlockSpec((steps * columns, wide), functools.partial(lambda k, i: (k, 0), base // steps)),
             pl.BlockSpec((columns, wide), lambda i: (leafs, 0)),
         ]
         if last:
             shapes.append(jax.ShapeDtypeStruct((tops, width + 1, part, wide), f32))
         before = () if k == 0 else (state,)
         results = pl.pallas_call(
-            functools.partial(forward_kernel, k * steps, k == 0, last, width),
+            functools.partial(forward_kernel, base, leafs, k == 0, last, width),
             grid=(1,),
             in_specs=specs + [VMEM] * (k > 0),
             out_specs=[VMEM] * len(shapes),
@@ -287,16 +292,18 @@
     def whole(*shape):
         return pl.BlockSpec((1,) + shape, lambda t: (t,) + (0,) * len(shape))
 
+    top_places = jnp.stack([2 * zh + zl, 2 - 2 * zh + zl, 2 * zh + 1 - zl, 3 - 2 * zh - zl])
     top_factor = pl.pallas_call(
         top_prepare_kernel,
         grid=(tops,),
-        in_specs=[whole(*top.shape[1:])],
+        in_specs=[SMEM, whole(*top.shape[1:])],
         out_specs=[whole(most * wide, wide)] * 2 + [whole(wide, wide)] * 2,
         out_shape=[jax.ShapeDtypeStruct((tops, most * wide, wide), bf16)] * 2
         + [jax.ShapeDtypeStruct((tops, wide, wide), bf16)] * 2,
+        scratch_shapes=[pltpu.VMEM((width, wide, wide), f32)],
         compiler_params=params(),
         name="top_prepare",
-    )(after(results[4], top))
+    )(top_places.astype(jnp.int32), after(results[4], top))
 
     incoming = lax.all_to_all(results[4], ("xy", "zh"), split_axis=0, concat_axis=0, tiled=True)
     outgoing = pl.pallas_call(
@@ -311,16 +318,17 @@
     own_top = state[:groups, width].reshape(1, columns, wide)
 
     found = [None] * TURNS
-    steps = leafs // TURNS
-    share = TURNS // CHUNKS
-    chunk = jax.ShapeDtypeStruct((steps, columns, wide), f32)
+    chunk = jax.ShapeDtypeStruct((turn, columns, wide), f32)
     for k in range(TURNS - 1, -1, -1):
+        held = max(i for i, at in enumerate(starts[:-1]) if at <= k * turn)
         part_of = [
-            pl.BlockSpec((steps,) + shape, functools.partial(lambda k, i: (k, 0, 0), k % share))
+            pl.BlockSpec(
+                (turn,) + shape, functools.partial(lambda at, i: (at, 0, 0), k - starts[held] // turn)
+            )
             for shape in ((3 * wide, wide), (3 * wide, wide), (columns, wide))
         ]
         found[k], state = pl.pallas_call(
-            functools.partial(backward_kernel, k * steps, k == TURNS - 1, width),
+            functools.partial(backward_kernel, k * turn, k == TURNS - 1, width),
             grid=(1,),
             in_specs=[SMEM] + part_of + [VMEM],
             out_specs=[VMEM] * 2,
@@ -328,7 +336,7 @@
             compiler_params=params(),
             cost_estimate=cost,
             name="leaf_backward",
-        )(meta, *factors[k // share], state)
+        )(meta, *factors[held], state)
     late = swap(found[-1])
     middle = swap(jnp.concatenate(found[1:-1] + [own_top], axis=0))
     first = swap(after(late, found[0]))

time: 210 us -> 206 us (0.981)
  local copies, waits for them, and re-layouts: 13.2 us -> 8.64 us
    ppermute x4, waiting for transfers between devices: 12.3 us -> 67 us  [swap(): return lax.ppermute(value, ('core', 'zh'), [(0, 0), (1, 2), (2, 1), (3, 3)])]
    psum x1 -> x0, waiting for transfers between devices: 42 us -> none  [local(): summed = lax.psum(top, ('zh', 'zl'))]
    ppermute x2, waiting for transfers between devices: 16.5 us -> 7.51 us  [to_keeper(): return lax.ppermute(value, ('core', 'zh'), [(1, 0), (2, 3)])]
    ppermute x2, starting transfers between devices: 13.1 us -> 6.87 us  [to_keeper(): return lax.ppermute(value, ('core', 'zh'), [(1, 0), (2, 3)])]
    ppermute x0 -> x2, starting transfers between devices: none -> 4.57 us  [other(): return lax.ppermute(value, axes, [(i, last - i) for i in range(last + 1)])]
    ppermute x6, waiting for transfers between devices: 13.9 us -> 9.37 us  [to_trader(): return lax.ppermute(value, ('core', 'zh'), [(0, 2), (3, 1)])]
    unnamed x40 -> x34, local copies, waits for them, and re-layouts: 8.51 us -> 4.5 us
  transfers between devices with their start and end apart: 18 -> 19, of which waited for: 7 -> 10; matrix products, arithmetic and copies ran while one was open for 5% -> 4% of each run, Pallas kernels for 12% -> 11%
where the time goes in v1:
time: 206 us; the launch traced here: 205 us
  waiting for transfers between devices  88.5 us (43%)
  starting transfers between devices  42.5 us (21%)
  Pallas kernels  32.4 us (16%)
  between operations  14.4 us (7%)
  blocking collectives  9.75 us (5%)
  other arithmetic  9.06 us (4%)
  local copies, waits for them, and re-layouts  8.64 us (4%)
    ppermute x4, waiting for transfers between devices, swap(): return lax.ppermute(value, ('core', 'zh'), [(0, 0), (1, 2), (2, 1), (3, 3)])  67 us
    pallas_call x2, Pallas kernels, local(): pl.pallas_call(functools.partial(forward_kernel, base, leafs, k == 0, las...  17.3 us
    ppermute x4, starting transfers between devices, swap(): return lax.ppermute(value, ('core', 'zh'), [(0, 0), (1, 2), (2, 1), (3, 3)])  13.2 us
    all_to_all x1, blocking collectives, local(): lax.all_to_all(outgoing, ('xy', 'zh'), split_axis=0, concat_axis=0, tiled...  9.75 us
    pallas_call x4, Pallas kernels, local(): pl.pallas_call(functools.partial(backward_kernel, k * turn, k == TURNS -...  9.64 us
    ppermute x6, waiting for transfers between devices, to_trader(): return lax.ppermute(value, ('core', 'zh'), [(0, 2), (3, 1)])  9.37 us
    ppermute x6, starting transfers between devices, to_trader(): return lax.ppermute(value, ('core', 'zh'), [(0, 2), (3, 1)])  7.73 us
    ppermute x2, waiting for transfers between devices, to_keeper(): return lax.ppermute(value, ('core', 'zh'), [(1, 0), (2, 3)])  7.51 us
  transfers between devices with their start and end apart: 19, of which 10 were waited for; matrix products, arithmetic and copies ran while one was open for 4% of the time, Pallas kernels for 11%

profile of v1, /device:TPU:1, one launch (start us, length us, event | category | flops | bytes accessed | tf_op | source)
XLA Modules:
  0.0 205.3 jit_solution(11541102833308427372)
XLA Ops:
  7.2 0.8 fusion.1
  9.4 0.7 fusion.2
  10.1 3.2 %collective-permute-start = (f32[4,32,128]{2,1,0:T(8,128)S(1)}, f32[4,32,128]{2,1,0:T(8,128)S(1)}, u32[]{:S(2)}, u32[]{:S(2)}) collective-permute-start(f32[4,32,128]{2,1,0:T(8,128)S(1)} %get-tuple-element.75), channel_id=1, source_target_pairs={{0,2},{2,0},{1,3},{3,1},{4,6},{6,4},{5,7},{7,5},{8,10},{10,8},{9,1... | collective-permute-start | bytes 196616 | tf_op jit(solution)/shard_map/ppermute | solution.py:222
  13.3 1.0 slice_bitcast_fusion
  14.4 0.9 slice_bitcast_fusion.1
  16.0 1.8 select_maximum_fusion
  18.1 1.4 collective-permute-start.1
  19.4 1.3 pad_maximum_fusion.1
  20.7 0.8 pad_maximum_fusion.4
  21.9 0.7 pad_maximum_fusion.5
  22.7 4.7 %collective-permute-start.7 = (f32[24,4,32,128]{3,2,1,0:T(8,128)}, f32[24,4,32,128]{3,2,1,0:T(8,128)}, u32[]{:S(2)}, u32[]{:S(2)}) collective-permute-start(f32[24,4,32,128]{3,2,1,0:T(8,128)} %pad_maximum_fusion.1), channel_id=1, source_target_pairs={{2,0},{4,6},{3,1},{5,7},{10,8},{12,14},{11,9},{13,15},{18,16},{20,... | collective-permute-start | bytes 4718600 | tf_op jit(solution)/shard_map/ppermute | solution.py:212
  27.4 2.0 collective-permute-start.3
  29.5 4.9 %collective-permute-start.2 = (f32[2120,128]{1,0:T(8,128)}, f32[2120,128]{1,0:T(8,128)S(1)}, u32[]{:S(2)}, u32[]{:S(2)}) collective-permute-start(f32[2120,128]{1,0:T(8,128)} %select_maximum_fusion), channel_id=1, source_target_pairs={{0,0},{2,4},{4,2},{6,6},{1,1},{3,5},{5,3},{7,7},{8,8},{10,12},{12,... | collective-permute-start | bytes 3256328 | tf_op jit(solution)/shard_map/ppermute | solution.py:209
  34.3 52.2 %collective-permute-done.2.refs_9_.refs_10_ = f32[2120,128]{1,0:T(8,128)S(1)} collective-permute-done((f32[2120,128]{1,0:T(8,128)}, f32[2120,128]{1,0:T(8,128)S(1)}, u32[]{:S(2)}, u32[]{:S(2)}) %collective-permute-start.2) | collective-permute-done | bytes 1085472 | tf_op jit(solution)/shard_map/ppermute | solution.py:209
  86.5 1.8 collective-permute-start.11
  88.3 2.1 %collective-permute-start.4 = (f32[8,4,32,128]{3,2,1,0:T(8,128)}, f32[8,4,32,128]{3,2,1,0:T(8,128)}, u32[]{:S(2)}, u32[]{:S(2)}) collective-permute-start(f32[8,4,32,128]{3,2,1,0:T(8,128)} %pad_maximum_fusion.4), channel_id=1, source_target_pairs={{2,0},{4,6},{3,1},{5,7},{10,8},{12,14},{11,9},{13,15},{18,16},{20,... | collective-permute-start | bytes 1572872 | tf_op jit(solution)/shard_map/ppermute | solution.py:212
  90.4 1.3 collective-permute-start.5
  91.7 1.3 collective-permute-start.6
  93.0 7.5 %collective-permute-done.4.refs_3_ = f32[8,4,32,128]{3,2,1,0:T(8,128)} collective-permute-done((f32[8,4,32,128]{3,2,1,0:T(8,128)}, f32[8,4,32,128]{3,2,1,0:T(8,128)}, u32[]{:S(2)}, u32[]{:S(2)}) %collective-permute-start.4) | collective-permute-done | bytes 524320 | tf_op jit(solution)/shard_map/ppermute | solution.py:212
  100.6 1.3 collective-permute-start.8
  101.9 1.3 collective-permute-start.12
  103.9 1.3 collective-permute-start.10
  105.2 1.0 collective-permute-done.8.refs_7_
  106.2 1.5 collective-permute-start.9
  108.0 1.4 collective-permute-done.12.refs_8_
  109.4 11.5 %leaf_forward.2 = (f32[40,64,128]{2,1,0:T(8,128)S(1)}, bf16[24,384,128]{2,1,0:T(8,128)(2,1)S(1)}, bf16[24,384,128]{2,1,0:T(8,128)(2,1)S(1)}, f32[24,64,128]{2,1,0:T(8,128)S(1)}) custom-call(s32[105]{0:T(128)S(1)} %concatenate.36.refs_0_.meta, f32[32,4,32,128]{3,2,1,0:T(8,128)S(1)} %pad_maximum_fusion.refs_1_, ...), custom_call_target="tpu_custom_call" | custom-call | flops 4000000000 | bytes 8388608 | tf_op jit(solution)/shard_map/leaf_forward/pallas_call | solution.py:275
  120.9 1.3 collective-permute-start.13
  122.2 7.0 %collective-permute-done.13.refs_8_ = f32[8,4,32,128]{3,2,1,0:T(8,128)S(1)} collective-permute-done((f32[8,4,32,128]{3,2,1,0:T(8,128)}, f32[8,4,32,128]{3,2,1,0:T(8,128)S(1)}, u32[]{:S(2)}, u32[]{:S(2)}) %collective-permute-start.13) | collective-permute-done | bytes 524320 | tf_op jit(solution)/shard_map/ppermute | solution.py:215
  129.2 5.8 %leaf_forward.3 = (f32[40,64,128]{2,1,0:T(8,128)}, bf16[8,384,128]{2,1,0:T(8,128)(2,1)S(1)}, bf16[8,384,128]{2,1,0:T(8,128)(2,1)S(1)}, f32[8,64,128]{2,1,0:T(8,128)S(1)}, f32[8,5,8,128]{3,2,1,0:T(8,128)}) custom-call(s32[105]{0:T(128)S(1)} %concatenate.36.refs_0_.meta, f32[32,4,32,128]{3,2,1,0:T(8,128)S(1)} %pad_maximum_fusion.refs_1_, ...), custom_call_target="tpu_custom_call" | custom-call | flops 4000000000 | bytes 8388608 | tf_op jit(solution)/shard_map/leaf_forward/pallas_call | solution.py:275
  135.1 0.9 copy-done.8
  135.9 0.9 copy-done.10
  137.5 4.7 %all-to-all-start = ((f32[8,5,8,128]{3,2,1,0:T(8,128)}), f32[8,5,8,128]{3,2,1,0:T(8,128)S(1)}, u32[]{:S(2)}, u32[]{:S(2)}) async-start(f32[8,5,8,128]{3,2,1,0:T(8,128)} %get-tuple-element.56), calls=%async_computation | async-start | bytes 327680 | tf_op jit(solution)/shard_map/all_to_all | solution.py:308
  142.4 1.6 copy-done.1
  143.9 2.7 %top_prepare.1 = (bf16[8,384,128]{2,1,0:T(8,128)(2,1)S(1)}, bf16[8,384,128]{2,1,0:T(8,128)(2,1)S(1)}, bf16[8,128,128]{2,1,0:T(8,128)(2,1)S(1)}, bf16[8,128,128]{2,1,0:T(8,128)(2,1)S(1)}) custom-call(s32[4]{0:T(128)S(1)} %pad_add_fusion.places, f32[8,4,4,32,128]{4,3,2,1,0:T(8,128)S(1)} %bitcast.32), custom_call_target="tpu_custom_call" | custom-call | tf_op jit(solution)/shard_map/top_prepare/pallas_call | solution.py:296
  146.7 4.3 %all-to-all-done.incoming = f32[8,5,8,128]{3,2,1,0:T(8,128)S(1)} async-done(((f32[8,5,8,128]{3,2,1,0:T(8,128)}), f32[8,5,8,128]{3,2,1,0:T(8,128)S(1)}, u32[]{:S(2)}, u32[]{:S(2)}) %all-to-all-start) | async-done | bytes 163872 | tf_op jit(solution)/shard_map/all_to_all | solution.py:308
  150.9 2.7 %top_solve.1 = f32[8,5,8,128]{3,2,1,0:T(8,128)S(1)} custom-call(f32[8,5,8,128]{3,2,1,0:T(8,128)S(1)} %all-to-all-done.incoming, bf16[8,384,128]{2,1,0:T(8,128)(2,1)S(1)} %get-tuple-element.59.high, bf16[8,384,128]{2,1,0:T(8,128)(2,1)S(1)} %get-tuple-element.60.low, bf16[8,128,128]{2,1,0:T(8,128)(2,1)S(1)} %get-tuple-element.61.inverse_high, ...), custom_call_target="tpu_custom_call" | custom-call | tf_op jit(solution)/shard_map/top_solve/pallas_call | solution.py:309
  153.6 9.7 %all_to_all.10.state = f32[8,5,8,128]{3,2,1,0:T(8,128)S(1)} all-to-all(f32[8,5,8,128]{3,2,1,0:T(8,128)S(1)} %top_solve.1), channel_id=1, replica_groups=mesh['xy'=4,'core'=2,'zh'=2,'zl'=2] {'xy','zh'}, dimensions={0} | all-to-all | bytes 327680 | tf_op jit(solution)/shard_map/all_to_all | solution.py:317
  163.4 2.1 %leaf_backward.4 = (f32[8,64,128]{2,1,0:T(8,128)S(1)}, f32[40,64,128]{2,1,0:T(8,128)S(1)}) custom-call(s32[105]{0:T(128)S(1)} %concatenate.36.refs_0_.meta, bf16[8,384,128]{2,1,0:T(8,128)(2,1)S(1)} %copy-done.9, bf16[8,384,128]{2,1,0:T(8,128)(2,1)S(1)} %copy-done.11, f32[8,64,128]{2,1,0:T(8,128)S(1)} %copy-done.13, f32[8,5,8,128]{3,2,1,0:T(8,128)S(1)} %all_to_all.10.state), custom_call_target="tpu_custom_call" | custom-call | flops 4000000000 | bytes 8388608 | tf_op jit(solution)/shard_map/leaf_backward/pallas_call | solution.py:330
  165.9 2.1 %leaf_backward.5 = (f32[8,64,128]{2,1,0:T(8,128)S(1)}, f32[40,64,128]{2,1,0:T(8,128)S(1)}) custom-call(s32[105]{0:T(128)S(1)} %concatenate.36.refs_0_.meta, bf16[24,384,128]{2,1,0:T(8,128)(2,1)S(1)} %copy-done.3, bf16[24,384,128]{2,1,0:T(8,128)(2,1)S(1)} %copy-done.5, f32[24,64,128]{2,1,0:T(8,128)S(1)} %copy-done.7, f32[40,64,128]{2,1,0:T(8,128)S(1)} %get-tuple-element.67.state), custom_call_target="tpu_custom_call" | custom-call | flops 4000000000 | bytes 8388608 | tf_op jit(solution)/shard_map/leaf_backward/pallas_call | solution.py:330
  168.1 2.1 %leaf_backward.6 = (f32[8,64,128]{2,1,0:T(8,128)S(1)}, f32[40,64,128]{2,1,0:T(8,128)S(1)}) custom-call(s32[105]{0:T(128)S(1)} %concatenate.36.refs_0_.meta, bf16[24,384,128]{2,1,0:T(8,128)(2,1)S(1)} %copy-done.3, bf16[24,384,128]{2,1,0:T(8,128)(2,1)S(1)} %copy-done.5, f32[24,64,128]{2,1,0:T(8,128)S(1)} %copy-done.7, f32[40,64,128]{2,1,0:T(8,128)S(1)} %get-tuple-element.68.state), custom_call_target="tpu_custom_call" | custom-call | flops 4000000000 | bytes 8388608 | tf_op jit(solution)/shard_map/leaf_backward/pallas_call | solution.py:330
  170.2 2.7 %collective-permute-start.14 = (f32[8,64,128]{2,1,0:T(8,128)S(1)}, f32[8,64,128]{2,1,0:T(8,128)S(1)}, u32[]{:S(2)}, u32[]{:S(2)}) collective-permute-start(f32[8,64,128]{2,1,0:T(8,128)S(1)} %get-tuple-element.63), channel_id=1, source_target_pairs={{0,0},{2,4},{4,2},{6,6},{1,1},{3,5},{5,3},{7,7},{8,8},{10,12},{12,... | collective-permute-start | bytes 786440 | tf_op jit(solution)/shard_map/ppermute | solution.py:209
  172.9 3.8 %collective-permute-start.16 = (f32[17,64,128]{2,1,0:T(8,128)S(1)}, f32[17,64,128]{2,1,0:T(8,128)S(1)}, u32[]{:S(2)}, u32[]{:S(2)}) collective-permute-start(f32[17,64,128]{2,1,0:T(8,128)S(1)} %pad_maximum_fusion.3), channel_id=1, source_target_pairs={{0,0},{2,4},{4,2},{6,6},{1,1},{3,5},{5,3},{7,7},{8,8},{10,12},{12,... | collective-permute-start | bytes 1671176 | tf_op jit(solution)/shard_map/ppermute | solution.py:209
  176.7 3.2 %leaf_backward.7 = (f32[8,64,128]{2,1,0:T(8,128)S(1)}, f32[40,64,128]{2,1,0:T(8,128)}) custom-call(s32[105]{0:T(128)S(1)} %concatenate.36.refs_0_.meta, bf16[24,384,128]{2,1,0:T(8,128)(2,1)S(1)} %copy-done.3, bf16[24,384,128]{2,1,0:T(8,128)(2,1)S(1)} %copy-done.5, f32[24,64,128]{2,1,0:T(8,128)S(1)} %copy-done.7, f32[40,64,128]{2,1,0:T(8,128)S(1)} %get-tuple-element.69.state), custom_call_target="tpu_custom_call" | custom-call | flops 4000000000 | bytes 8388608 | tf_op jit(solution)/shard_map/leaf_backward/pallas_call | solution.py:330
  180.0 5.8 %collective-permute-done.14 = f32[8,64,128]{2,1,0:T(8,128)S(1)} collective-permute-done((f32[8,64,128]{2,1,0:T(8,128)S(1)}, f32[8,64,128]{2,1,0:T(8,128)S(1)}, u32[]{:S(2)}, u32[]{:S(2)}) %collective-permute-start.14) | collective-permute-done | bytes 262176 | tf_op jit(solution)/shard_map/ppermute | solution.py:209
  185.8 1.9 collective-permute-start.15
  187.7 6.9 %collective-permute-done.16 = f32[17,64,128]{2,1,0:T(8,128)S(1)} collective-permute-done((f32[17,64,128]{2,1,0:T(8,128)S(1)}, f32[17,64,128]{2,1,0:T(8,128)S(1)}, u32[]{:S(2)}, u32[]{:S(2)}) %collective-permute-start.16) | collective-permute-done | bytes 557088 | tf_op jit(solution)/shard_map/ppermute | solution.py:209
  195.2 2.2 %collective-permute-done.15 = f32[8,64,128]{2,1,0:T(8,128)S(1)} collective-permute-done((f32[8,64,128]{2,1,0:T(8,128)S(1)}, f32[8,64,128]{2,1,0:T(8,128)S(1)}, u32[]{:S(2)}, u32[]{:S(2)}) %collective-permute-start.15) | collective-permute-done | bytes 262176 | tf_op jit(solution)/shard_map/ppermute | solution.py:209
  197.4 1.1 pad_maximum_fusion.2
  (64 shorter events, 5.6 us)
Async XLA Ops:
  7.2 1.6 copy-start
  7.2 8.8 %copy-start.16 = (f32[32,64,128]{2,1,0:T(8,128)S(1)}, f32[32,64,128]{2,1,0:T(8,128)}, u32[]{:S(2)}) copy-start(f32[32,64,128]{2,1,0:T(8,128)} %param.11) | copy-start | bytes 3145732
  7.2 135.2 %all-gather.3.cloned.1.call-start = ((), (), s32[]{:S(2)}) async-start(), calls=%async_computation.2 | async-start | bytes 2359296 | tf_op jit(solution)/shard_map/all_gather | solution.py:247
  10.1 7.7 %copy-start.14 = (f32[32,3,32,128]{3,2,1,0:T(8,128)S(1)}, f32[32,3,32,128]{3,2,1,0:T(8,128)}, u32[]{:S(2)}) copy-start(f32[32,3,32,128]{3,2,1,0:T(8,128)} %param.13) | copy-start | bytes 4718596
  10.1 7.7 %copy-start.15 = (f32[32,32,128]{2,1,0:T(8,128)S(1)}, f32[32,32,128]{2,1,0:T(8,128)}, u32[]{:S(2)}) copy-start(f32[32,32,128]{2,1,0:T(8,128)} %param.14) | copy-start | bytes 1572868
  10.1 7.9 %collective-permute-start = (f32[4,32,128]{2,1,0:T(8,128)S(1)}, f32[4,32,128]{2,1,0:T(8,128)S(1)}, u32[]{:S(2)}, u32[]{:S(2)}) collective-permute-start(f32[4,32,128]{2,1,0:T(8,128)S(1)} %get-tuple-element.75), channel_id=1, source_target_pairs={{0,2},{2,0},{1,3},{3,1},{4,6},{6,4},{5,7},{7,5},{8,10},{10,8},{9,1... | collective-permute-start | bytes 196616 | tf_op jit(solution)/shard_map/ppermute | solution.py:222
  18.0 1.4 slice-start
  18.0 2.7 %slice-start.1 = ((f32[32,3,32,128]{3,2,1,0:T(8,128)}), f32[8,3,32,128]{3,2,1,0:T(8,128)S(1)}, s32[]{:S(2)}) async-start(f32[32,3,32,128]{3,2,1,0:T(8,128)} %param.13), calls=%async_computation.4 | async-start | bytes 786432 | tf_op jit(solution)/shard_map/slice | solution.py:235
  18.1 3.9 %collective-permute-start.1 = (f32[2,4,32,128]{3,2,1,0:T(8,128)S(1)}, f32[2,4,32,128]{3,2,1,0:T(8,128)S(1)}, u32[]{:S(2)}, u32[]{:S(2)}) collective-permute-start(f32[2,4,32,128]{3,2,1,0:T(8,128)S(1)} %pad_maximum_fusion.6), channel_id=1, source_target_pairs={{0,1},{1,0},{2,3},{3,2},{4,5},{5,4},{6,7},{7,6},{8,9},{9,8},{10,11... | collective-permute-start | bytes 393224 | tf_op jit(solution)/shard_map/ppermute | solution.py:222
  22.7 63.9 %collective-permute-start.7 = (f32[24,4,32,128]{3,2,1,0:T(8,128)}, f32[24,4,32,128]{3,2,1,0:T(8,128)}, u32[]{:S(2)}, u32[]{:S(2)}) collective-permute-start(f32[24,4,32,128]{3,2,1,0:T(8,128)} %pad_maximum_fusion.1), channel_id=1, source_target_pairs={{2,0},{4,6},{3,1},{5,7},{10,8},{12,14},{11,9},{13,15},{18,16},{20,... | collective-permute-start | bytes 4718600 | tf_op jit(solution)/shard_map/ppermute | solution.py:212
  27.4 64.3 %collective-permute-start.3 = (f32[32,4,32,128]{3,2,1,0:T(8,128)S(1)}, f32[32,4,32,128]{3,2,1,0:T(8,128)}, u32[]{:S(2)}, u32[]{:S(2)}) collective-permute-start(f32[32,4,32,128]{3,2,1,0:T(8,128)S(1)} %pad_maximum_fusion.refs_1_), channel_id=1, source_target_pairs={{0,1},{1,0},{6,7},{7,6},{8,9},{9,8},{14,15},{15,14},{16,17},{17,16... | collective-permute-start | bytes 6291464 | tf_op jit(solution)/shard_map/ppermute | solution.py:218
  29.5 57.1 %collective-permute-start.2 = (f32[2120,128]{1,0:T(8,128)}, f32[2120,128]{1,0:T(8,128)S(1)}, u32[]{:S(2)}, u32[]{:S(2)}) collective-permute-start(f32[2120,128]{1,0:T(8,128)} %select_maximum_fusion), channel_id=1, source_target_pairs={{0,0},{2,4},{4,2},{6,6},{1,1},{3,5},{5,3},{7,7},{8,8},{10,12},{12,... | collective-permute-start | bytes 3256328 | tf_op jit(solution)/shard_map/ppermute | solution.py:209
  86.5 15.4 %collective-permute-start.11 = (f32[24,4,32,128]{3,2,1,0:T(8,128)}, f32[24,4,32,128]{3,2,1,0:T(8,128)}, u32[]{:S(2)}, u32[]{:S(2)}) collective-permute-start(f32[24,4,32,128]{3,2,1,0:T(8,128)} %collective-permute-done.7.refs_3_), channel_id=1, source_target_pairs={{0,1},{1,0},{6,7},{7,6},{8,9},{9,8},{14,15},{15,14},{16,17},{17,16... | collective-permute-start | bytes 4718600 | tf_op jit(solution)/shard_map/ppermute | solution.py:218
  88.3 12.2 %collective-permute-start.4 = (f32[8,4,32,128]{3,2,1,0:T(8,128)}, f32[8,4,32,128]{3,2,1,0:T(8,128)}, u32[]{:S(2)}, u32[]{:S(2)}) collective-permute-start(f32[8,4,32,128]{3,2,1,0:T(8,128)} %pad_maximum_fusion.4), channel_id=1, source_target_pairs={{2,0},{4,6},{3,1},{5,7},{10,8},{12,14},{11,9},{13,15},{18,16},{20,... | collective-permute-start | bytes 1572872 | tf_op jit(solution)/shard_map/ppermute | solution.py:212
  90.4 14.8 %collective-permute-start.5 = (f32[32,4,32,128]{3,2,1,0:T(8,128)S(1)}, f32[32,4,32,128]{3,2,1,0:T(8,128)}, u32[]{:S(2)}, u32[]{:S(2)}) collective-permute-start(f32[32,4,32,128]{3,2,1,0:T(8,128)S(1)} %pad_maximum_fusion.refs_1_), channel_id=1, source_target_pairs={{0,4},{6,2},{1,5},{7,3},{8,12},{14,10},{9,13},{15,11},{16,20},{22,... | collective-permute-start | bytes 6291464 | tf_op jit(solution)/shard_map/ppermute | solution.py:215
  91.7 14.5 %collective-permute-start.6 = (f32[32,4,32,128]{3,2,1,0:T(8,128)}, f32[32,4,32,128]{3,2,1,0:T(8,128)}, u32[]{:S(2)}, u32[]{:S(2)}) collective-permute-start(f32[32,4,32,128]{3,2,1,0:T(8,128)} %collective-permute-done.3.refs_2_), channel_id=1, source_target_pairs={{0,4},{6,2},{1,5},{7,3},{8,12},{14,10},{9,13},{15,11},{16,20},{22,... | collective-permute-start | bytes 6291464 | tf_op jit(solution)/shard_map/ppermute | solution.py:215
  100.6 5.6 %collective-permute-start.8 = (f32[24,4,32,128]{3,2,1,0:T(8,128)}, f32[24,4,32,128]{3,2,1,0:T(8,128)}, u32[]{:S(2)}, u32[]{:S(2)}) collective-permute-start(f32[24,4,32,128]{3,2,1,0:T(8,128)} %collective-permute-done.7.refs_3_), channel_id=1, source_target_pairs={{0,4},{6,2},{1,5},{7,3},{8,12},{14,10},{9,13},{15,11},{16,20},{22,... | collective-permute-start | bytes 4718600 | tf_op jit(solution)/shard_map/ppermute | solution.py:215
  101.9 7.5 %collective-permute-start.12 = (f32[24,4,32,128]{3,2,1,0:T(8,128)}, f32[24,4,32,128]{3,2,1,0:T(8,128)}, u32[]{:S(2)}, u32[]{:S(2)}) collective-permute-start(f32[24,4,32,128]{3,2,1,0:T(8,128)} %collective-permute-done.11.refs_4_), channel_id=1, source_target_pairs={{0,4},{6,2},{1,5},{7,3},{8,12},{14,10},{9,13},{15,11},{16,20},{22,... | collective-permute-start | bytes 4718600 | tf_op jit(solution)/shard_map/ppermute | solution.py:215
  103.9 18.3 %collective-permute-start.10 = (f32[8,4,32,128]{3,2,1,0:T(8,128)}, f32[8,4,32,128]{3,2,1,0:T(8,128)}, u32[]{:S(2)}, u32[]{:S(2)}) collective-permute-start(f32[8,4,32,128]{3,2,1,0:T(8,128)} %collective-permute-done.4.refs_3_), channel_id=1, source_target_pairs={{0,4},{6,2},{1,5},{7,3},{8,12},{14,10},{9,13},{15,11},{16,20},{22,... | collective-permute-start | bytes 1572872 | tf_op jit(solution)/shard_map/ppermute | solution.py:215
  106.2 14.7 %collective-permute-start.9 = (f32[8,4,32,128]{3,2,1,0:T(8,128)}, f32[8,4,32,128]{3,2,1,0:T(8,128)}, u32[]{:S(2)}, u32[]{:S(2)}) collective-permute-start(f32[8,4,32,128]{3,2,1,0:T(8,128)} %collective-permute-done.4.refs_3_), channel_id=1, source_target_pairs={{0,1},{1,0},{6,7},{7,6},{8,9},{9,8},{14,15},{15,14},{16,17},{17,16... | collective-permute-start | bytes 1572872 | tf_op jit(solution)/shard_map/ppermute | solution.py:218
  120.9 14.2 %copy-start.2 = (bf16[24,384,128]{2,1,0:T(8,128)(2,1)}, bf16[24,384,128]{2,1,0:T(8,128)(2,1)S(1)}, u32[]{:S(2)}) copy-start(bf16[24,384,128]{2,1,0:T(8,128)(2,1)S(1)} %get-tuple-element.64.high) | copy-start | bytes 7077892
  120.9 14.2 %copy-start.4 = (bf16[24,384,128]{2,1,0:T(8,128)(2,1)}, bf16[24,384,128]{2,1,0:T(8,128)(2,1)S(1)}, u32[]{:S(2)}) copy-start(bf16[24,384,128]{2,1,0:T(8,128)(2,1)S(1)} %get-tuple-element.65.low) | copy-start | bytes 7077892
  120.9 14.2 %copy-start.6 = (f32[24,64,128]{2,1,0:T(8,128)}, f32[24,64,128]{2,1,0:T(8,128)S(1)}, u32[]{:S(2)}) copy-start(f32[24,64,128]{2,1,0:T(8,128)S(1)} %get-tuple-element.66.scaled) | copy-start | bytes 2359300
  120.9 8.3 %collective-permute-start.13 = (f32[8,4,32,128]{3,2,1,0:T(8,128)}, f32[8,4,32,128]{3,2,1,0:T(8,128)S(1)}, u32[]{:S(2)}, u32[]{:S(2)}) collective-permute-start(f32[8,4,32,128]{3,2,1,0:T(8,128)} %collective-permute-done.9.refs_4_), channel_id=1, source_target_pairs={{0,4},{6,2},{1,5},{7,3},{8,12},{14,10},{9,13},{15,11},{16,20},{22,... | collective-permute-start | bytes 1572872 | tf_op jit(solution)/shard_map/ppermute | solution.py:215
  135.0 0.9 copy-start.8
  135.9 0.9 copy-start.10
  136.8 0.7 copy-start.12
  137.5 13.4 %all-to-all-start = ((f32[8,5,8,128]{3,2,1,0:T(8,128)}), f32[8,5,8,128]{3,2,1,0:T(8,128)S(1)}, u32[]{:S(2)}, u32[]{:S(2)}) async-start(f32[8,5,8,128]{3,2,1,0:T(8,128)} %get-tuple-element.56), calls=%async_computation | async-start | bytes 327680 | tf_op jit(solution)/shard_map/all_to_all | solution.py:308
  142.4 1.6 copy-start.1
  150.9 12.5 %copy-start.9 = (bf16[8,384,128]{2,1,0:T(8,128)(2,1)S(1)}, bf16[8,384,128]{2,1,0:T(8,128)(2,1)}, u32[]{:S(2)}) copy-start(bf16[8,384,128]{2,1,0:T(8,128)(2,1)} %copy-done.8) | copy-start | bytes 2359300
  150.9 12.5 %copy-start.11 = (bf16[8,384,128]{2,1,0:T(8,128)(2,1)S(1)}, bf16[8,384,128]{2,1,0:T(8,128)(2,1)}, u32[]{:S(2)}) copy-start(bf16[8,384,128]{2,1,0:T(8,128)(2,1)} %copy-done.10) | copy-start | bytes 2359300
  150.9 12.5 %copy-start.13 = (f32[8,64,128]{2,1,0:T(8,128)S(1)}, f32[8,64,128]{2,1,0:T(8,128)}, u32[]{:S(2)}) copy-start(f32[8,64,128]{2,1,0:T(8,128)} %copy-done.12) | copy-start | bytes 786436
  163.4 2.2 %copy-start.3 = (bf16[24,384,128]{2,1,0:T(8,128)(2,1)S(1)}, bf16[24,384,128]{2,1,0:T(8,128)(2,1)}, u32[]{:S(2)}) copy-start(bf16[24,384,128]{2,1,0:T(8,128)(2,1)} %copy-done.2) | copy-start | bytes 7077892
  163.4 2.4 %copy-start.5 = (bf16[24,384,128]{2,1,0:T(8,128)(2,1)S(1)}, bf16[24,384,128]{2,1,0:T(8,128)(2,1)}, u32[]{:S(2)}) copy-start(bf16[24,384,128]{2,1,0:T(8,128)(2,1)} %copy-done.4) | copy-start | bytes 7077892
  163.4 2.5 %copy-start.7 = (f32[24,64,128]{2,1,0:T(8,128)S(1)}, f32[24,64,128]{2,1,0:T(8,128)}, u32[]{:S(2)}) copy-start(f32[24,64,128]{2,1,0:T(8,128)} %copy-done.6) | copy-start | bytes 2359300
  170.2 15.6 %collective-permute-start.14 = (f32[8,64,128]{2,1,0:T(8,128)S(1)}, f32[8,64,128]{2,1,0:T(8,128)S(1)}, u32[]{:S(2)}, u32[]{:S(2)}) collective-permute-start(f32[8,64,128]{2,1,0:T(8,128)S(1)} %get-tuple-element.63), channel_id=1, source_target_pairs={{0,0},{2,4},{4,2},{6,6},{1,1},{3,5},{5,3},{7,7},{8,8},{10,12},{12,... | collective-permute-start | bytes 786440 | tf_op jit(solution)/shard_map/ppermute | solution.py:209
  172.9 21.6 %collective-permute-start.16 = (f32[17,64,128]{2,1,0:T(8,128)S(1)}, f32[17,64,128]{2,1,0:T(8,128)S(1)}, u32[]{:S(2)}, u32[]{:S(2)}) collective-permute-start(f32[17,64,128]{2,1,0:T(8,128)S(1)} %pad_maximum_fusion.3), channel_id=1, source_target_pairs={{0,0},{2,4},{4,2},{6,6},{1,1},{3,5},{5,3},{7,7},{8,8},{10,12},{12,... | collective-permute-start | bytes 1671176 | tf_op jit(solution)/shard_map/ppermute | solution.py:209
  185.8 11.6 %collective-permute-start.15 = (f32[8,64,128]{2,1,0:T(8,128)S(1)}, f32[8,64,128]{2,1,0:T(8,128)S(1)}, u32[]{:S(2)}, u32[]{:S(2)}) collective-permute-start(f32[8,64,128]{2,1,0:T(8,128)S(1)} %get-tuple-element.71), channel_id=1, source_target_pairs={{0,0},{2,4},{4,2},{6,6},{1,1},{3,5},{5,3},{7,7},{8,8},{10,12},{12,... | collective-permute-start | bytes 786440 | tf_op jit(solution)/shard_map/ppermute | solution.py:209
Sparse Core Ops, SparseCore 0:
  100.7 31.2 all-gather.2

commit v2 on v1

--- a/solution.py
+++ b/solution.py
@@ -241,10 +241,10 @@
     near = keepers(own)
     sides = swap(sides)
     far = [to_keeper(part) for part in parts]
-    across = [keepers(after(sides, far[0]))]
+    across = [keepers(far[0])]
     early = [to_trader(value) for value in (own, near, far[0])]
-    across += [keepers(after(early, value)) for value in far[1:]]
-    top = lax.all_gather(after(far[-1], top), ("xy", "core"), axis=0, tiled=False)
+    across += [keepers(after(early[:2], value)) for value in far[1:]]
+    top = lax.all_gather(after((far[-1], sides), top), ("xy", "core"), axis=0, tiled=False)
 
     names = sides[(leafs + 1) * columns :][:3, :leafs].T.astype(jnp.int32).reshape(-1)
     path = jnp.asarray(padded(paths, width))[2 * xy + zh]
@@ -253,7 +253,7 @@
     meta = jnp.concatenate([names, places.astype(jnp.int32), path, keeps[None]])
 
     vectors = jax.ShapeDtypeStruct((leafs + tops, columns, wide), f32)
-    cost = pl.CostEstimate(flops=4 * 10**9, bytes_accessed=8 * 2**20, transcendentals=0)
+    cost = pl.CostEstimate(flops=2**20, bytes_accessed=2**10, transcendentals=0)
     factors, state = [], None
     for k, base in enumerate(starts[:-1]):
         last = k == len(CHUNKS) - 1
@@ -337,11 +337,11 @@
             cost_estimate=cost,
             name="leaf_backward",
         )(meta, *factors[held], state)
-    late = swap(found[-1])
-    middle = swap(jnp.concatenate(found[1:-1] + [own_top], axis=0))
-    first = swap(after(late, found[0]))
-    leaf_solution = jnp.concatenate([first, middle[:-1], late], axis=0)
-    return (leaf_solution, middle[-1:])
+    half = TURNS // 2
+    late = swap(jnp.concatenate(found[half:] + [own_top], axis=0))
+    first = swap(jnp.concatenate(found[:half], axis=0))
+    leaf_solution = jnp.concatenate([first, late[:-1]], axis=0)
+    return (leaf_solution, late[-1:])
 
 
 def solution(mesh):

time: 206 us -> 228 us (1.11)
  local copies, waits for them, and re-layouts: 8.64 us -> 27.7 us
  starting transfers between devices: 42.5 us -> 39 us
  waiting for transfers between devices: 88.5 us -> 91.8 us
  blocking collectives: 9.75 us -> 12.3 us
    ppermute x4 -> x3, waiting for transfers between devices: 67 us -> 20.2 us  [swap(): return lax.ppermute(value, ('core', 'zh'), [(0, 0), (1, 2), (2, 1), (3, 3)])]
    ppermute x2, waiting for transfers between devices: 7.51 us -> 53.6 us  [to_keeper(): return lax.ppermute(value, ('core', 'zh'), [(1, 0), (2, 3)])]
    unnamed x34 -> x66, local copies, waits for them, and re-layouts: 4.5 us -> 23 us
    ppermute x6, waiting for transfers between devices: 9.37 us -> 17 us  [to_trader(): return lax.ppermute(value, ('core', 'zh'), [(0, 2), (3, 1)])]
    all_to_all x1, waiting for transfers between devices: 4.26 us -> 0.99 us  [local(): lax.all_to_all(results[4], ('xy', 'zh'), split_axis=0, concat_axis=0, til...]
    all_to_all x1, blocking collectives: 9.75 us -> 12.3 us  [local(): lax.all_to_all(outgoing, ('xy', 'zh'), split_axis=0, concat_axis=0, tiled...]
    ppermute x4 -> x3, starting transfers between devices: 13.2 us -> 11.4 us  [swap(): return lax.ppermute(value, ('core', 'zh'), [(0, 0), (1, 2), (2, 1), (3, 3)])]
  transfers between devices with their start and end apart: 19 -> 18, of which waited for: 10 -> 8; matrix products, arithmetic and copies ran while one was open for 4% -> 4% of each run, Pallas kernels for 11% -> 9%
where the time goes in v2:
time: 228 us; the launch traced here: 227 us
  waiting for transfers between devices  91.8 us (40%)
  starting transfers between devices  39 us (17%)
  Pallas kernels  32.4 us (14%)
  local copies, waits for them, and re-layouts  27.7 us (12%)
  between operations  14.4 us (6%)
  blocking collectives  12.3 us (5%)
  other arithmetic  9.1 us (4%)
    ppermute x2, waiting for transfers between devices, to_keeper(): return lax.ppermute(value, ('core', 'zh'), [(1, 0), (2, 3)])  53.6 us
    unnamed x66, local copies, waits for them, and re-layouts  23 us
    ppermute x3, waiting for transfers between devices, swap(): return lax.ppermute(value, ('core', 'zh'), [(0, 0), (1, 2), (2, 1), (3, 3)])  20.2 us
    pallas_call x2, Pallas kernels, local(): pl.pallas_call(functools.partial(forward_kernel, base, leafs, k == 0, las...  17.4 us
    ppermute x6, waiting for transfers between devices, to_trader(): return lax.ppermute(value, ('core', 'zh'), [(0, 2), (3, 1)])  17 us
    all_to_all x1, blocking collectives, local(): lax.all_to_all(outgoing, ('xy', 'zh'), split_axis=0, concat_axis=0, tiled...  12.3 us
    ppermute x3, starting transfers between devices, swap(): return lax.ppermute(value, ('core', 'zh'), [(0, 0), (1, 2), (2, 1), (3, 3)])  11.4 us
    pallas_call x4, Pallas kernels, local(): pl.pallas_call(functools.partial(backward_kernel, k * turn, k == TURNS -...  9.58 us
  transfers between devices with their start and end apart: 18, of which 8 were waited for; matrix products, arithmetic and copies ran while one was open for 4% of the time, Pallas kernels for 9%

profile of v2, /device:TPU:1, one launch (start us, length us, event | category | flops | bytes accessed | tf_op | source)
XLA Modules:
  0.0 226.8 jit_solution(7869768167499146306)
XLA Ops:
  10.1 3.2 %collective-permute-start = (f32[4,32,128]{2,1,0:T(8,128)S(1)}, f32[4,32,128]{2,1,0:T(8,128)S(1)}, u32[]{:S(2)}, u32[]{:S(2)}) collective-permute-start(f32[4,32,128]{2,1,0:T(8,128)S(1)} %get-tuple-element.71), channel_id=1, source_target_pairs={{0,2},{2,0},{1,3},{3,1},{4,6},{6,4},{5,7},{7,5},{8,10},{10,8},{9,1... | collective-permute-start | bytes 196616 | tf_op jit(solution)/shard_map/ppermute | solution.py:222
  13.3 1.0 slice_bitcast_fusion
  16.0 1.9 select_maximum_fusion
  18.1 1.4 collective-permute-start.1
  20.1 1.3 pad_maximum_fusion.1
  22.9 4.5 %collective-permute-start.4 = (f32[24,4,32,128]{3,2,1,0:T(8,128)}, f32[24,4,32,128]{3,2,1,0:T(8,128)}, u32[]{:S(2)}, u32[]{:S(2)}) collective-permute-start(f32[24,4,32,128]{3,2,1,0:T(8,128)} %pad_maximum_fusion.1), channel_id=1, source_target_pairs={{2,0},{4,6},{3,1},{5,7},{10,8},{12,14},{11,9},{13,15},{18,16},{20,... | collective-permute-start | bytes 4718600 | tf_op jit(solution)/shard_map/ppermute | solution.py:212
  27.5 2.0 collective-permute-start.3
  29.5 4.9 %collective-permute-start.2 = (f32[2120,128]{1,0:T(8,128)}, f32[2120,128]{1,0:T(8,128)S(1)}, u32[]{:S(2)}, u32[]{:S(2)}) collective-permute-start(f32[2120,128]{1,0:T(8,128)} %select_maximum_fusion), channel_id=1, source_target_pairs={{0,0},{2,4},{4,2},{6,6},{1,1},{3,5},{5,3},{7,7},{8,8},{10,12},{12,... | collective-permute-start | bytes 3256328 | tf_op jit(solution)/shard_map/ppermute | solution.py:209
  34.4 2.1 collective-permute-start.9
  36.5 20.9 %collective-permute-done.4.refs_3_ = f32[24,4,32,128]{3,2,1,0:T(8,128)} collective-permute-done((f32[24,4,32,128]{3,2,1,0:T(8,128)}, f32[24,4,32,128]{3,2,1,0:T(8,128)}, u32[]{:S(2)}, u32[]{:S(2)}) %collective-permute-start.4) | collective-permute-done | bytes 1572896 | tf_op jit(solution)/shard_map/ppermute | solution.py:212
  57.4 1.8 collective-permute-start.5
  59.2 32.7 %collective-permute-done.9.refs_3_ = f32[8,4,32,128]{3,2,1,0:T(8,128)} collective-permute-done((f32[8,4,32,128]{3,2,1,0:T(8,128)}, f32[8,4,32,128]{3,2,1,0:T(8,128)}, u32[]{:S(2)}, u32[]{:S(2)}) %collective-permute-start.9) | collective-permute-done | bytes 524320 | tf_op jit(solution)/shard_map/ppermute | solution.py:212
  92.0 1.3 collective-permute-start.6
  93.3 1.3 collective-permute-start.7
  94.6 1.3 collective-permute-start.8
  95.9 1.3 collective-permute-start.10
  97.2 6.4 %collective-permute-done.6.refs_5_ = f32[32,4,32,128]{3,2,1,0:T(8,128)S(1)} collective-permute-done((f32[32,4,32,128]{3,2,1,0:T(8,128)S(1)}, f32[32,4,32,128]{3,2,1,0:T(8,128)S(1)}, u32[]{:S(2)}, u32[]{:S(2)}) %collective-permute-start.6) | collective-permute-done | bytes 2097184 | tf_op jit(solution)/shard_map/ppermute | solution.py:215
  103.6 1.4 copy-done.8
  104.9 4.8 %collective-permute-done.7.refs_6_ = f32[32,4,32,128]{3,2,1,0:T(8,128)S(1)} collective-permute-done((f32[32,4,32,128]{3,2,1,0:T(8,128)}, f32[32,4,32,128]{3,2,1,0:T(8,128)S(1)}, u32[]{:S(2)}, u32[]{:S(2)}) %collective-permute-start.7) | collective-permute-done | bytes 2097184 | tf_op jit(solution)/shard_map/ppermute | solution.py:215
  109.8 1.3 copy-done.11
  111.1 1.5 collective-permute-start.11
  113.2 1.3 collective-permute-start.12
  114.5 1.0 copy-done.5
  115.8 1.6 copy-done.4
  117.4 1.2 copy-done.6
  118.7 1.6 copy-done.9
  120.3 1.6 copy-done.12
  121.9 11.6 %leaf_forward.2 = (f32[40,64,128]{2,1,0:T(8,128)S(1)}, bf16[24,384,128]{2,1,0:T(8,128)(2,1)S(1)}, bf16[24,384,128]{2,1,0:T(8,128)(2,1)S(1)}, f32[24,64,128]{2,1,0:T(8,128)S(1)}) custom-call(s32[105]{0:T(128)S(1)} %concatenate.39.refs_0_.meta, f32[32,4,32,128]{3,2,1,0:T(8,128)S(1)} %copy-done.4, f32[32,4,32,128]{3,2,1,0:T(8,128)} %collective-permute-done.3.refs_2_, ...), custom_call_target="tpu_custom_call" | custom-call | flops 1048576 | bytes 1024 | tf_op jit(solution)/shard_map/leaf_forward/pallas_call | solution.py:275
  133.5 1.3 collective-permute-start.13
  134.8 5.8 %collective-permute-done.13.refs_8_ = f32[8,4,32,128]{3,2,1,0:T(8,128)S(1)} collective-permute-done((f32[8,4,32,128]{3,2,1,0:T(8,128)}, f32[8,4,32,128]{3,2,1,0:T(8,128)S(1)}, u32[]{:S(2)}, u32[]{:S(2)}) %collective-permute-start.13) | collective-permute-done | bytes 524320 | tf_op jit(solution)/shard_map/ppermute | solution.py:215
  140.6 5.8 %leaf_forward.3 = (f32[40,64,128]{2,1,0:T(8,128)}, bf16[8,384,128]{2,1,0:T(8,128)(2,1)S(1)}, bf16[8,384,128]{2,1,0:T(8,128)(2,1)S(1)}, f32[8,64,128]{2,1,0:T(8,128)S(1)}, f32[8,5,8,128]{3,2,1,0:T(8,128)S(1)}) custom-call(s32[105]{0:T(128)S(1)} %concatenate.39.refs_0_.meta, f32[32,4,32,128]{3,2,1,0:T(8,128)S(1)} %copy-done.4, ...), custom_call_target="tpu_custom_call" | custom-call | flops 1048576 | bytes 1024 | tf_op jit(solution)/shard_map/leaf_forward/pallas_call | solution.py:275
  149.6 3.4 %all-to-all-start = ((f32[8,5,8,128]{3,2,1,0:T(8,128)}), f32[8,5,8,128]{3,2,1,0:T(8,128)S(1)}, u32[]{:S(2)}, u32[]{:S(2)}) async-start(f32[8,5,8,128]{3,2,1,0:T(8,128)} %copy-done.29), calls=%async_computation | async-start | bytes 327680 | tf_op jit(solution)/shard_map/all_to_all | solution.py:308
  153.1 1.6 copy-done.14
  154.7 2.7 %top_prepare.1 = (bf16[8,384,128]{2,1,0:T(8,128)(2,1)S(1)}, bf16[8,384,128]{2,1,0:T(8,128)(2,1)S(1)}, bf16[8,128,128]{2,1,0:T(8,128)(2,1)S(1)}, bf16[8,128,128]{2,1,0:T(8,128)(2,1)S(1)}) custom-call(s32[4]{0:T(128)S(1)} %pad_add_fusion.places, f32[8,4,4,32,128]{4,3,2,1,0:T(8,128)S(1)} %bitcast.32), custom_call_target="tpu_custom_call" | custom-call | tf_op jit(solution)/shard_map/top_prepare/pallas_call | solution.py:296
  160.6 1.0 all-to-all-done.incoming
  161.6 1.3 copy-done.20
  162.8 1.1 copy-done.22
  165.9 2.7 %top_solve.1 = f32[8,5,8,128]{3,2,1,0:T(8,128)S(1)} custom-call(f32[8,5,8,128]{3,2,1,0:T(8,128)S(1)} %all-to-all-done.incoming, bf16[8,384,128]{2,1,0:T(8,128)(2,1)S(1)} %copy-done.20, bf16[8,384,128]{2,1,0:T(8,128)(2,1)S(1)} %copy-done.22, bf16[8,128,128]{2,1,0:T(8,128)(2,1)S(1)} %copy-done.26, bf16[8,128,128]{2,1,0:T(8,128)(2,1)S(1)} %copy-done.28), custom_call_target="tpu_custom_call" | custom-call | tf_op jit(solution)/shard_map/top_solve/pallas_call | solution.py:309
  168.6 12.3 %all_to_all.10.state = f32[8,5,8,128]{3,2,1,0:T(8,128)S(1)} all-to-all(f32[8,5,8,128]{3,2,1,0:T(8,128)S(1)} %top_solve.1), channel_id=1, replica_groups=mesh['xy'=4,'core'=2,'zh'=2,'zl'=2] {'xy','zh'}, dimensions={0} | all-to-all | bytes 327680 | tf_op jit(solution)/shard_map/all_to_all | solution.py:317
  181.9 2.1 leaf_backward.4
  184.0 2.1 leaf_backward.5
  186.1 2.1 leaf_backward.6
  188.2 3.2 %leaf_backward.7 = (f32[8,64,128]{2,1,0:T(8,128)S(1)}, f32[40,64,128]{2,1,0:T(8,128)}) custom-call(s32[105]{0:T(128)S(1)} %concatenate.39.refs_0_.meta, bf16[24,384,128]{2,1,0:T(8,128)(2,1)S(1)} %get-tuple-element.47.high, bf16[24,384,128]{2,1,0:T(8,128)(2,1)S(1)} %copy-done.2, f32[24,64,128]{2,1,0:T(8,128)S(1)} %get-tuple-element.49.scaled, ...), custom_call_target="tpu_custom_call" | custom-call | flops 1048576 | bytes 1024 | tf_op jit(solution)/shard_map/leaf_backward/pallas_call | solution.py:330
  191.5 2.4 %collective-permute-start.15 = (f32[17,64,128]{2,1,0:T(8,128)S(1)}, f32[17,64,128]{2,1,0:T(8,128)S(1)}, u32[]{:S(2)}, u32[]{:S(2)}) collective-permute-start(f32[17,64,128]{2,1,0:T(8,128)S(1)} %pad_maximum_fusion.3), channel_id=1, source_target_pairs={{0,0},{2,4},{4,2},{6,6},{1,1},{3,5},{5,3},{7,7},{8,8},{10,12},{12,... | collective-permute-start | bytes 1671176 | tf_op jit(solution)/shard_map/ppermute | solution.py:209
  194.0 4.0 %collective-permute-start.14 = (f32[16,64,128]{2,1,0:T(8,128)S(1)}, f32[16,64,128]{2,1,0:T(8,128)S(1)}, u32[]{:S(2)}, u32[]{:S(2)}) collective-permute-start(f32[16,64,128]{2,1,0:T(8,128)S(1)} %pad_maximum_fusion.5), channel_id=1, source_target_pairs={{0,0},{2,4},{4,2},{6,6},{1,1},{3,5},{5,3},{7,7},{8,8},{10,12},{12,... | collective-permute-start | bytes 1572872 | tf_op jit(solution)/shard_map/ppermute | solution.py:209
  198.1 15.2 %collective-permute-done.15 = f32[17,64,128]{2,1,0:T(8,128)S(1)} collective-permute-done((f32[17,64,128]{2,1,0:T(8,128)S(1)}, f32[17,64,128]{2,1,0:T(8,128)S(1)}, u32[]{:S(2)}, u32[]{:S(2)}) %collective-permute-start.15) | collective-permute-done | bytes 557088 | tf_op jit(solution)/shard_map/ppermute | solution.py:209
  213.9 5.0 %collective-permute-done.14 = f32[16,64,128]{2,1,0:T(8,128)S(1)} collective-permute-done((f32[16,64,128]{2,1,0:T(8,128)S(1)}, f32[16,64,128]{2,1,0:T(8,128)S(1)}, u32[]{:S(2)}, u32[]{:S(2)}) %collective-permute-start.14) | collective-permute-done | bytes 524320 | tf_op jit(solution)/shard_map/ppermute | solution.py:209
  218.9 1.0 pad_maximum_fusion.2
  (95 shorter events, 18.0 us)
Async XLA Ops:
  7.2 1.6 copy-start
  7.2 8.8 %copy-start.32 = (f32[32,64,128]{2,1,0:T(8,128)S(1)}, f32[32,64,128]{2,1,0:T(8,128)}, u32[]{:S(2)}) copy-start(f32[32,64,128]{2,1,0:T(8,128)} %param.11) | copy-start | bytes 3145732
  7.2 145.9 %all-gather.3.cloned.1.call-start = ((), (), s32[]{:S(2)}) async-start(), calls=%async_computation.2 | async-start | bytes 2359296 | tf_op jit(solution)/shard_map/all_gather | solution.py:247
  10.1 7.7 %copy-start.30 = (f32[32,3,32,128]{3,2,1,0:T(8,128)S(1)}, f32[32,3,32,128]{3,2,1,0:T(8,128)}, u32[]{:S(2)}) copy-start(f32[32,3,32,128]{3,2,1,0:T(8,128)} %param.13) | copy-start | bytes 4718596
  10.1 7.7 %copy-start.31 = (f32[32,32,128]{2,1,0:T(8,128)S(1)}, f32[32,32,128]{2,1,0:T(8,128)}, u32[]{:S(2)}) copy-start(f32[32,32,128]{2,1,0:T(8,128)} %param.14) | copy-start | bytes 1572868
  10.1 7.9 %collective-permute-start = (f32[4,32,128]{2,1,0:T(8,128)S(1)}, f32[4,32,128]{2,1,0:T(8,128)S(1)}, u32[]{:S(2)}, u32[]{:S(2)}) collective-permute-start(f32[4,32,128]{2,1,0:T(8,128)S(1)} %get-tuple-element.71), channel_id=1, source_target_pairs={{0,2},{2,0},{1,3},{3,1},{4,6},{6,4},{5,7},{7,5},{8,10},{10,8},{9,1... | collective-permute-start | bytes 196616 | tf_op jit(solution)/shard_map/ppermute | solution.py:222
  18.0 73.9 %copy-start.3 = (f32[32,4,32,128]{3,2,1,0:T(8,128)}, f32[32,4,32,128]{3,2,1,0:T(8,128)S(1)}, u32[]{:S(2)}) copy-start(f32[32,4,32,128]{3,2,1,0:T(8,128)S(1)} %pad_maximum_fusion.refs_1_) | copy-start | bytes 6291460
  18.0 2.0 slice-start
  18.1 3.3 %slice-start.1 = ((f32[32,3,32,128]{3,2,1,0:T(8,128)}), f32[8,3,32,128]{3,2,1,0:T(8,128)S(1)}, s32[]{:S(2)}) async-start(f32[32,3,32,128]{3,2,1,0:T(8,128)} %param.13), calls=%async_computation.4 | async-start | bytes 786432 | tf_op jit(solution)/shard_map/slice | solution.py:235
  18.1 4.1 %collective-permute-start.1 = (f32[2,4,32,128]{3,2,1,0:T(8,128)S(1)}, f32[2,4,32,128]{3,2,1,0:T(8,128)S(1)}, u32[]{:S(2)}, u32[]{:S(2)}) collective-permute-start(f32[2,4,32,128]{3,2,1,0:T(8,128)S(1)} %pad_maximum_fusion.7), channel_id=1, source_target_pairs={{0,1},{1,0},{2,3},{3,2},{4,5},{5,4},{6,7},{7,6},{8,9},{9,8},{10,11... | collective-permute-start | bytes 393224 | tf_op jit(solution)/shard_map/ppermute | solution.py:222
  22.9 34.5 %collective-permute-start.4 = (f32[24,4,32,128]{3,2,1,0:T(8,128)}, f32[24,4,32,128]{3,2,1,0:T(8,128)}, u32[]{:S(2)}, u32[]{:S(2)}) collective-permute-start(f32[24,4,32,128]{3,2,1,0:T(8,128)} %pad_maximum_fusion.1), channel_id=1, source_target_pairs={{2,0},{4,6},{3,1},{5,7},{10,8},{12,14},{11,9},{13,15},{18,16},{20,... | collective-permute-start | bytes 4718600 | tf_op jit(solution)/shard_map/ppermute | solution.py:212
  27.5 65.8 %collective-permute-start.3 = (f32[32,4,32,128]{3,2,1,0:T(8,128)S(1)}, f32[32,4,32,128]{3,2,1,0:T(8,128)}, u32[]{:S(2)}, u32[]{:S(2)}) collective-permute-start(f32[32,4,32,128]{3,2,1,0:T(8,128)S(1)} %pad_maximum_fusion.refs_1_), channel_id=1, source_target_pairs={{0,1},{1,0},{6,7},{7,6},{8,9},{9,8},{14,15},{15,14},{16,17},{17,16... | collective-permute-start | bytes 6291464 | tf_op jit(solution)/shard_map/ppermute | solution.py:218
  29.5 62.4 %collective-permute-start.2 = (f32[2120,128]{1,0:T(8,128)}, f32[2120,128]{1,0:T(8,128)S(1)}, u32[]{:S(2)}, u32[]{:S(2)}) collective-permute-start(f32[2120,128]{1,0:T(8,128)} %select_maximum_fusion), channel_id=1, source_target_pairs={{0,0},{2,4},{4,2},{6,6},{1,1},{3,5},{5,3},{7,7},{8,8},{10,12},{12,... | collective-permute-start | bytes 3256328 | tf_op jit(solution)/shard_map/ppermute | solution.py:209
  34.4 57.5 %collective-permute-start.9 = (f32[8,4,32,128]{3,2,1,0:T(8,128)}, f32[8,4,32,128]{3,2,1,0:T(8,128)}, u32[]{:S(2)}, u32[]{:S(2)}) collective-permute-start(f32[8,4,32,128]{3,2,1,0:T(8,128)} %pad_maximum_fusion.4), channel_id=1, source_target_pairs={{2,0},{4,6},{3,1},{5,7},{10,8},{12,14},{11,9},{13,15},{18,16},{20,... | collective-permute-start | bytes 1572872 | tf_op jit(solution)/shard_map/ppermute | solution.py:212
  57.4 38.4 %collective-permute-start.5 = (f32[24,4,32,128]{3,2,1,0:T(8,128)}, f32[24,4,32,128]{3,2,1,0:T(8,128)}, u32[]{:S(2)}, u32[]{:S(2)}) collective-permute-start(f32[24,4,32,128]{3,2,1,0:T(8,128)} %collective-permute-done.4.refs_3_), channel_id=1, source_target_pairs={{0,1},{1,0},{6,7},{7,6},{8,9},{9,8},{14,15},{15,14},{16,17},{17,16... | collective-permute-start | bytes 4718600 | tf_op jit(solution)/shard_map/ppermute | solution.py:218
  92.0 11.6 %collective-permute-start.6 = (f32[32,4,32,128]{3,2,1,0:T(8,128)S(1)}, f32[32,4,32,128]{3,2,1,0:T(8,128)S(1)}, u32[]{:S(2)}, u32[]{:S(2)}) collective-permute-start(f32[32,4,32,128]{3,2,1,0:T(8,128)S(1)} %pad_maximum_fusion.refs_1_), channel_id=1, source_target_pairs={{0,4},{6,2},{1,5},{7,3},{8,12},{14,10},{9,13},{15,11},{16,20},{22,... | collective-permute-start | bytes 6291464 | tf_op jit(solution)/shard_map/ppermute | solution.py:215
  93.3 16.5 %collective-permute-start.7 = (f32[32,4,32,128]{3,2,1,0:T(8,128)}, f32[32,4,32,128]{3,2,1,0:T(8,128)S(1)}, u32[]{:S(2)}, u32[]{:S(2)}) collective-permute-start(f32[32,4,32,128]{3,2,1,0:T(8,128)} %collective-permute-done.3.refs_2_), channel_id=1, source_target_pairs={{0,4},{6,2},{1,5},{7,3},{8,12},{14,10},{9,13},{15,11},{16,20},{22,... | collective-permute-start | bytes 6291464 | tf_op jit(solution)/shard_map/ppermute | solution.py:215
  94.6 21.2 %collective-permute-start.8 = (f32[24,4,32,128]{3,2,1,0:T(8,128)}, f32[24,4,32,128]{3,2,1,0:T(8,128)}, u32[]{:S(2)}, u32[]{:S(2)}) collective-permute-start(f32[24,4,32,128]{3,2,1,0:T(8,128)} %collective-permute-done.4.refs_3_), channel_id=1, source_target_pairs={{0,4},{6,2},{1,5},{7,3},{8,12},{14,10},{9,13},{15,11},{16,20},{22,... | collective-permute-start | bytes 4718600 | tf_op jit(solution)/shard_map/ppermute | solution.py:215
  95.9 19.9 %collective-permute-start.10 = (f32[24,4,32,128]{3,2,1,0:T(8,128)}, f32[24,4,32,128]{3,2,1,0:T(8,128)}, u32[]{:S(2)}, u32[]{:S(2)}) collective-permute-start(f32[24,4,32,128]{3,2,1,0:T(8,128)} %collective-permute-done.5.refs_4_), channel_id=1, source_target_pairs={{0,4},{6,2},{1,5},{7,3},{8,12},{14,10},{9,13},{15,11},{16,20},{22,... | collective-permute-start | bytes 4718600 | tf_op jit(solution)/shard_map/ppermute | solution.py:215
  103.6 1.4 copy-start.8
  109.8 1.3 copy-start.11
  111.1 22.4 %collective-permute-start.11 = (f32[8,4,32,128]{3,2,1,0:T(8,128)}, f32[8,4,32,128]{3,2,1,0:T(8,128)}, u32[]{:S(2)}, u32[]{:S(2)}) collective-permute-start(f32[8,4,32,128]{3,2,1,0:T(8,128)} %collective-permute-done.9.refs_3_), channel_id=1, source_target_pairs={{0,1},{1,0},{6,7},{7,6},{8,9},{9,8},{14,15},{15,14},{16,17},{17,16... | collective-permute-start | bytes 1572872 | tf_op jit(solution)/shard_map/ppermute | solution.py:218
  113.2 21.6 %collective-permute-start.12 = (f32[8,4,32,128]{3,2,1,0:T(8,128)}, f32[8,4,32,128]{3,2,1,0:T(8,128)}, u32[]{:S(2)}, u32[]{:S(2)}) collective-permute-start(f32[8,4,32,128]{3,2,1,0:T(8,128)} %collective-permute-done.9.refs_3_), channel_id=1, source_target_pairs={{0,4},{6,2},{1,5},{7,3},{8,12},{14,10},{9,13},{15,11},{16,20},{22,... | collective-permute-start | bytes 1572872 | tf_op jit(solution)/shard_map/ppermute | solution.py:215
  114.5 1.0 copy-start.5
  115.8 1.6 copy-start.4
  117.4 1.2 copy-start.6
  118.7 1.6 copy-start.9
  120.3 1.6 copy-start.12
  121.8 18.8 %copy-start.7 = (f32[2120,128]{1,0:T(8,128)S(1)}, f32[2120,128]{1,0:T(8,128)}, u32[]{:S(2)}) copy-start(f32[2120,128]{1,0:T(8,128)} %copy-done.5) | copy-start | bytes 3256324
  121.9 18.8 %copy-start.10 = (f32[32,4,32,128]{3,2,1,0:T(8,128)S(1)}, f32[32,4,32,128]{3,2,1,0:T(8,128)}, u32[]{:S(2)}) copy-start(f32[32,4,32,128]{3,2,1,0:T(8,128)} %copy-done.8) | copy-start | bytes 6291460
  121.9 18.8 %copy-start.13 = (f32[32,4,32,128]{3,2,1,0:T(8,128)S(1)}, f32[32,4,32,128]{3,2,1,0:T(8,128)}, u32[]{:S(2)}) copy-start(f32[32,4,32,128]{3,2,1,0:T(8,128)} %copy-done.11) | copy-start | bytes 6291460
  133.5 12.9 %copy-start.1 = (bf16[24,384,128]{2,1,0:T(8,128)(2,1)}, bf16[24,384,128]{2,1,0:T(8,128)(2,1)S(1)}, u32[]{:S(2)}) copy-start(bf16[24,384,128]{2,1,0:T(8,128)(2,1)S(1)} %get-tuple-element.48.low) | copy-start | bytes 7077892
  133.5 7.1 %collective-permute-start.13 = (f32[8,4,32,128]{3,2,1,0:T(8,128)}, f32[8,4,32,128]{3,2,1,0:T(8,128)S(1)}, u32[]{:S(2)}, u32[]{:S(2)}) collective-permute-start(f32[8,4,32,128]{3,2,1,0:T(8,128)} %collective-permute-done.11.refs_4_), channel_id=1, source_target_pairs={{0,4},{6,2},{1,5},{7,3},{8,12},{14,10},{9,13},{15,11},{16,20},{22,... | collective-permute-start | bytes 1572872 | tf_op jit(solution)/shard_map/ppermute | solution.py:215
  146.4 0.9 copy-start.15
  149.6 12.0 %all-to-all-start = ((f32[8,5,8,128]{3,2,1,0:T(8,128)}), f32[8,5,8,128]{3,2,1,0:T(8,128)S(1)}, u32[]{:S(2)}, u32[]{:S(2)}) async-start(f32[8,5,8,128]{3,2,1,0:T(8,128)} %copy-done.29), calls=%async_computation | async-start | bytes 327680 | tf_op jit(solution)/shard_map/all_to_all | solution.py:308
  153.1 1.6 copy-start.14
  157.4 0.9 copy-start.19
  158.3 0.9 copy-start.21
  161.6 19.4 %copy-start.16 = (bf16[8,384,128]{2,1,0:T(8,128)(2,1)S(1)}, bf16[8,384,128]{2,1,0:T(8,128)(2,1)}, u32[]{:S(2)}) copy-start(bf16[8,384,128]{2,1,0:T(8,128)(2,1)} %copy-done.15) | copy-start | bytes 2359300
  161.6 19.4 %copy-start.18 = (bf16[8,384,128]{2,1,0:T(8,128)(2,1)S(1)}, bf16[8,384,128]{2,1,0:T(8,128)(2,1)}, u32[]{:S(2)}) copy-start(bf16[8,384,128]{2,1,0:T(8,128)(2,1)} %copy-done.17) | copy-start | bytes 2359300
  161.6 1.3 copy-start.20
  162.8 1.1 copy-start.22
  164.0 0.9 copy-start.26
  164.9 0.9 copy-start.28
  165.9 18.1 %copy-start.2 = (bf16[24,384,128]{2,1,0:T(8,128)(2,1)S(1)}, bf16[24,384,128]{2,1,0:T(8,128)(2,1)}, u32[]{:S(2)}) copy-start(bf16[24,384,128]{2,1,0:T(8,128)(2,1)} %copy-done.1) | copy-start | bytes 7077892
  180.9 1.0 copy-start.24
  191.5 21.7 %collective-permute-start.15 = (f32[17,64,128]{2,1,0:T(8,128)S(1)}, f32[17,64,128]{2,1,0:T(8,128)S(1)}, u32[]{:S(2)}, u32[]{:S(2)}) collective-permute-start(f32[17,64,128]{2,1,0:T(8,128)S(1)} %pad_maximum_fusion.3), channel_id=1, source_target_pairs={{0,0},{2,4},{4,2},{6,6},{1,1},{3,5},{5,3},{7,7},{8,8},{10,12},{12,... | collective-permute-start | bytes 1671176 | tf_op jit(solution)/shard_map/ppermute | solution.py:209
  194.0 24.9 %collective-permute-start.14 = (f32[16,64,128]{2,1,0:T(8,128)S(1)}, f32[16,64,128]{2,1,0:T(8,128)S(1)}, u32[]{:S(2)}, u32[]{:S(2)}) collective-permute-start(f32[16,64,128]{2,1,0:T(8,128)S(1)} %pad_maximum_fusion.5), channel_id=1, source_target_pairs={{0,0},{2,4},{4,2},{6,6},{1,1},{3,5},{5,3},{7,7},{8,8},{10,12},{12,... | collective-permute-start | bytes 1572872 | tf_op jit(solution)/shard_map/ppermute | solution.py:209
  (5 other events, 3.7 us)
Sparse Core Ops, SparseCore 0:
  92.1 34.6 all-gather.2

commit v3 on v2

--- a/solution.py
+++ b/solution.py
@@ -241,9 +241,8 @@
     near = keepers(own)
     sides = swap(sides)
     far = [to_keeper(part) for part in parts]
-    across = [keepers(far[0])]
     early = [to_trader(value) for value in (own, near, far[0])]
-    across += [keepers(after(early[:2], value)) for value in far[1:]]
+    across = [keepers(after(early, far[0]))] + [keepers(value) for value in far[1:]]
     top = lax.all_gather(after((far[-1], sides), top), ("xy", "core"), axis=0, tiled=False)
 
     names = sides[(leafs + 1) * columns :][:3, :leafs].T.astype(jnp.int32).reshape(-1)
@@ -253,7 +252,7 @@
     meta = jnp.concatenate([names, places.astype(jnp.int32), path, keeps[None]])
 
     vectors = jax.ShapeDtypeStruct((leafs + tops, columns, wide), f32)
-    cost = pl.CostEstimate(flops=2**20, bytes_accessed=2**10, transcendentals=0)
+    cost = pl.CostEstimate(flops=2**20, bytes_accessed=8 * 2**20, transcendentals=0)
     factors, state = [], None
     for k, base in enumerate(starts[:-1]):
         last = k == len(CHUNKS) - 1
@@ -262,7 +261,7 @@
         chunk = jax.ShapeDtypeStruct((steps, columns, wide), f32)
         shapes = [vectors, merged, merged, chunk]
         if k == 0:
-            passed = (early[2], to_trader(after(far[-1], across[k])))
+            passed = (early[2], to_trader(across[k]))
         else:
             passed = (to_trader(far[k]), to_trader(after(state, across[k])))
         specs = [SMEM] + [pl.BlockSpec(memory_space=pl.ANY)] * 8 + [
@@ -319,6 +318,7 @@
 
     found = [None] * TURNS
     chunk = jax.ShapeDtypeStruct((turn, columns, wide), f32)
+    cost = pl.CostEstimate(flops=4 * 10**9, bytes_accessed=8 * 2**20, transcendentals=0)
     for k in range(TURNS - 1, -1, -1):
         held = max(i for i, at in enumerate(starts[:-1]) if at <= k * turn)
         part_of = [

time: 228 us -> 229 us (level)
  starting transfers between devices: 39 us -> 46 us
  local copies, waits for them, and re-layouts: 27.7 us -> 22.4 us
  blocking collectives: 12.3 us -> 9.66 us
  waiting for transfers between devices: 91.8 us -> 94.3 us
    ppermute x2, waiting for transfers between devices: 53.6 us -> 39.5 us  [to_keeper(): return lax.ppermute(value, ('core', 'zh'), [(1, 0), (2, 3)])]
    ppermute x3, waiting for transfers between devices: 20.2 us -> 30.5 us  [swap(): return lax.ppermute(value, ('core', 'zh'), [(0, 0), (1, 2), (2, 1), (3, 3)])]
    ppermute x2, starting transfers between devices: 6.62 us -> 12.7 us  [to_keeper(): return lax.ppermute(value, ('core', 'zh'), [(1, 0), (2, 3)])]
    ppermute x6, waiting for transfers between devices: 17 us -> 22.2 us  [to_trader(): return lax.ppermute(value, ('core', 'zh'), [(0, 2), (3, 1)])]
    unnamed x66 -> x50, local copies, waits for them, and re-layouts: 23 us -> 18.3 us
    all_to_all x1, blocking collectives: 12.3 us -> 9.66 us  [local(): lax.all_to_all(outgoing, ('xy', 'zh'), split_axis=0, concat_axis=0, tiled...]
  transfers between devices with their start and end apart: 18 -> 18, of which waited for: 8 -> 9; matrix products, arithmetic and copies ran while one was open for 4% -> 4% of each run, Pallas kernels for 9% -> 9%
where the time goes in v3:
time: 229 us; the launch traced here: 228 us
  waiting for transfers between devices  94.3 us (41%)
  starting transfers between devices  46 us (20%)
  Pallas kernels  32 us (14%)
  local copies, waits for them, and re-layouts  22.4 us (10%)
  between operations  14.4 us (6%)
  blocking collectives  9.66 us (4%)
  other arithmetic  9.18 us (4%)
    ppermute x2, waiting for transfers between devices, to_keeper(): return lax.ppermute(value, ('core', 'zh'), [(1, 0), (2, 3)])  39.5 us
    ppermute x3, waiting for transfers between devices, swap(): return lax.ppermute(value, ('core', 'zh'), [(0, 0), (1, 2), (2, 1), (3, 3)])  30.5 us
    ppermute x6, waiting for transfers between devices, to_trader(): return lax.ppermute(value, ('core', 'zh'), [(0, 2), (3, 1)])  22.2 us
    unnamed x50, local copies, waits for them, and re-layouts  18.3 us
    pallas_call x2, Pallas kernels, local(): pl.pallas_call(functools.partial(forward_kernel, base, leafs, k == 0, las...  17 us
    ppermute x3, starting transfers between devices, swap(): return lax.ppermute(value, ('core', 'zh'), [(0, 0), (1, 2), (2, 1), (3, 3)])  13.2 us
    ppermute x2, starting transfers between devices, to_keeper(): return lax.ppermute(value, ('core', 'zh'), [(1, 0), (2, 3)])  12.7 us
    all_to_all x1, blocking collectives, local(): lax.all_to_all(outgoing, ('xy', 'zh'), split_axis=0, concat_axis=0, tiled...  9.66 us
  transfers between devices with their start and end apart: 18, of which 9 were waited for; matrix products, arithmetic and copies ran while one was open for 4% of the time, Pallas kernels for 9%

profile of v3, /device:TPU:1, one launch (start us, length us, event | category | flops | bytes accessed | tf_op | source)
XLA Modules:
  0.0 227.9 jit_solution(9262174672702549707)
XLA Ops:
  10.1 3.2 %collective-permute-start = (f32[4,32,128]{2,1,0:T(8,128)S(1)}, f32[4,32,128]{2,1,0:T(8,128)S(1)}, u32[]{:S(2)}, u32[]{:S(2)}) collective-permute-start(f32[4,32,128]{2,1,0:T(8,128)S(1)} %get-tuple-element.69), channel_id=1, source_target_pairs={{0,2},{2,0},{1,3},{3,1},{4,6},{6,4},{5,7},{7,5},{8,10},{10,8},{9,1... | collective-permute-start | bytes 196616 | tf_op jit(solution)/shard_map/ppermute | solution.py:222
  13.3 1.0 slice_bitcast_fusion
  14.4 0.9 slice_bitcast_fusion.1
  16.0 1.8 select_maximum_fusion
  18.1 1.4 collective-permute-start.1
  19.4 1.4 pad_maximum_fusion.1
  23.4 7.0 %collective-permute-start.4 = (f32[24,4,32,128]{3,2,1,0:T(8,128)}, f32[24,4,32,128]{3,2,1,0:T(8,128)}, u32[]{:S(2)}, u32[]{:S(2)}) collective-permute-start(f32[24,4,32,128]{3,2,1,0:T(8,128)} %pad_maximum_fusion.1), channel_id=1, source_target_pairs={{2,0},{4,6},{3,1},{5,7},{10,8},{12,14},{11,9},{13,15},{18,16},{20,... | collective-permute-start | bytes 4718600 | tf_op jit(solution)/shard_map/ppermute | solution.py:212
  30.4 1.3 collective-permute-start.5
  31.7 1.3 collective-permute-start.6
  33.0 1.4 copy-done.1
  34.4 29.4 %collective-permute-done.4.refs_3_ = f32[24,4,32,128]{3,2,1,0:T(8,128)} collective-permute-done((f32[24,4,32,128]{3,2,1,0:T(8,128)}, f32[24,4,32,128]{3,2,1,0:T(8,128)}, u32[]{:S(2)}, u32[]{:S(2)}) %collective-permute-start.4) | collective-permute-done | bytes 1572896 | tf_op jit(solution)/shard_map/ppermute | solution.py:212
  63.8 1.3 collective-permute-start.7
  65.1 5.7 %collective-permute-start.2 = (f32[2120,128]{1,0:T(8,128)}, f32[2120,128]{1,0:T(8,128)S(1)}, u32[]{:S(2)}, u32[]{:S(2)}) collective-permute-start(f32[2120,128]{1,0:T(8,128)} %select_maximum_fusion), channel_id=1, source_target_pairs={{0,0},{2,4},{4,2},{6,6},{1,1},{3,5},{5,3},{7,7},{8,8},{10,12},{12,... | collective-permute-start | bytes 3256328 | tf_op jit(solution)/shard_map/ppermute | solution.py:209
  70.8 5.7 %collective-permute-start.10 = (f32[8,4,32,128]{3,2,1,0:T(8,128)}, f32[8,4,32,128]{3,2,1,0:T(8,128)}, u32[]{:S(2)}, u32[]{:S(2)}) collective-permute-start(f32[8,4,32,128]{3,2,1,0:T(8,128)} %pad_maximum_fusion.4), channel_id=1, source_target_pairs={{2,0},{4,6},{3,1},{5,7},{10,8},{12,14},{11,9},{13,15},{18,16},{20,... | collective-permute-start | bytes 1572872 | tf_op jit(solution)/shard_map/ppermute | solution.py:212
  76.6 1.4 copy-done.3
  78.0 1.1 copy-done.8
  79.2 1.3 copy-done.5
  80.5 1.9 collective-permute-start.8
  82.4 10.1 %collective-permute-done.10.refs_3_ = f32[8,4,32,128]{3,2,1,0:T(8,128)} collective-permute-done((f32[8,4,32,128]{3,2,1,0:T(8,128)}, f32[8,4,32,128]{3,2,1,0:T(8,128)}, u32[]{:S(2)}, u32[]{:S(2)}) %collective-permute-start.10) | collective-permute-done | bytes 524320 | tf_op jit(solution)/shard_map/ppermute | solution.py:212
  92.5 8.7 %collective-permute-done.2.refs_9_.refs_10_ = f32[2120,128]{1,0:T(8,128)S(1)} collective-permute-done((f32[2120,128]{1,0:T(8,128)}, f32[2120,128]{1,0:T(8,128)S(1)}, u32[]{:S(2)}, u32[]{:S(2)}) %collective-permute-start.2) | collective-permute-done | bytes 1085472 | tf_op jit(solution)/shard_map/ppermute | solution.py:209
  101.3 1.3 collective-permute-start.9
  102.6 1.5 collective-permute-start.11
  104.7 1.3 collective-permute-start.12
  106.3 17.6 %collective-permute-done.9.refs_8_ = f32[24,4,32,128]{3,2,1,0:T(8,128)} collective-permute-done((f32[24,4,32,128]{3,2,1,0:T(8,128)}, f32[24,4,32,128]{3,2,1,0:T(8,128)}, u32[]{:S(2)}, u32[]{:S(2)}) %collective-permute-start.9) | collective-permute-done | bytes 1572896 | tf_op jit(solution)/shard_map/ppermute | solution.py:215
  123.9 1.6 copy-done.2
  125.5 1.6 copy-done.4
  127.1 1.6 copy-done.6
  128.7 1.4 copy-done.9
  130.2 11.3 %leaf_forward.2 = (f32[40,64,128]{2,1,0:T(8,128)S(1)}, bf16[24,384,128]{2,1,0:T(8,128)(2,1)S(1)}, bf16[24,384,128]{2,1,0:T(8,128)(2,1)S(1)}, f32[24,64,128]{2,1,0:T(8,128)S(1)}) custom-call(s32[105]{0:T(128)S(1)} %concatenate.39.refs_0_.meta, f32[32,4,32,128]{3,2,1,0:T(8,128)S(1)} %pad_maximum_fusion.refs_1_, f32[32,4,32,128]{3,2,1,0:T(8,128)S(1)} %copy-done.2, ...), custom_call_target="tpu_custom_call" | custom-call | flops 1048576 | bytes 8388608 | tf_op jit(solution)/shard_map/leaf_forward/pallas_call | solution.py:274
  141.4 1.5 copy-done.10
  143.8 1.3 collective-permute-start.13
  145.1 4.5 %collective-permute-done.13.refs_8_ = f32[8,4,32,128]{3,2,1,0:T(8,128)S(1)} collective-permute-done((f32[8,4,32,128]{3,2,1,0:T(8,128)}, f32[8,4,32,128]{3,2,1,0:T(8,128)S(1)}, u32[]{:S(2)}, u32[]{:S(2)}) %collective-permute-start.13) | collective-permute-done | bytes 524320 | tf_op jit(solution)/shard_map/ppermute | solution.py:215
  149.6 5.7 %leaf_forward.3 = (f32[40,64,128]{2,1,0:T(8,128)}, bf16[8,384,128]{2,1,0:T(8,128)(2,1)S(1)}, bf16[8,384,128]{2,1,0:T(8,128)(2,1)S(1)}, f32[8,64,128]{2,1,0:T(8,128)S(1)}, f32[8,5,8,128]{3,2,1,0:T(8,128)}) custom-call(s32[105]{0:T(128)S(1)} %concatenate.39.refs_0_.meta, f32[32,4,32,128]{3,2,1,0:T(8,128)S(1)} %pad_maximum_fusion.refs_1_, ...), custom_call_target="tpu_custom_call" | custom-call | flops 1048576 | bytes 8388608 | tf_op jit(solution)/shard_map/leaf_forward/pallas_call | solution.py:274
  157.8 3.6 %all-to-all-start = ((f32[8,5,8,128]{3,2,1,0:T(8,128)}), f32[8,5,8,128]{3,2,1,0:T(8,128)S(1)}, u32[]{:S(2)}, u32[]{:S(2)}) async-start(f32[8,5,8,128]{3,2,1,0:T(8,128)} %get-tuple-element.54), calls=%async_computation | async-start | bytes 327680 | tf_op jit(solution)/shard_map/all_to_all | solution.py:307
  161.5 1.6 copy-done.7
  163.1 2.7 %top_prepare.1 = (bf16[8,384,128]{2,1,0:T(8,128)(2,1)S(1)}, bf16[8,384,128]{2,1,0:T(8,128)(2,1)S(1)}, bf16[8,128,128]{2,1,0:T(8,128)(2,1)S(1)}, bf16[8,128,128]{2,1,0:T(8,128)(2,1)S(1)}) custom-call(s32[4]{0:T(128)S(1)} %pad_add_fusion.places, f32[8,4,4,32,128]{4,3,2,1,0:T(8,128)S(1)} %bitcast.32), custom_call_target="tpu_custom_call" | custom-call | tf_op jit(solution)/shard_map/top_prepare/pallas_call | solution.py:295
  165.8 1.8 all-to-all-done.incoming
  167.6 2.7 %top_solve.1 = f32[8,5,8,128]{3,2,1,0:T(8,128)S(1)} custom-call(f32[8,5,8,128]{3,2,1,0:T(8,128)S(1)} %all-to-all-done.incoming, bf16[8,384,128]{2,1,0:T(8,128)(2,1)S(1)} %get-tuple-element.57.high, bf16[8,384,128]{2,1,0:T(8,128)(2,1)S(1)} %get-tuple-element.58.low, bf16[8,128,128]{2,1,0:T(8,128)(2,1)S(1)} %get-tuple-element.59.inverse_high, ...), custom_call_target="tpu_custom_call" | custom-call | tf_op jit(solution)/shard_map/top_solve/pallas_call | solution.py:308
  170.3 9.7 %all_to_all.10.state = f32[8,5,8,128]{3,2,1,0:T(8,128)S(1)} all-to-all(f32[8,5,8,128]{3,2,1,0:T(8,128)S(1)} %top_solve.1), channel_id=1, replica_groups=mesh['xy'=4,'core'=2,'zh'=2,'zl'=2] {'xy','zh'}, dimensions={0} | all-to-all | bytes 327680 | tf_op jit(solution)/shard_map/all_to_all | solution.py:316
  180.0 2.1 leaf_backward.4
  182.5 2.1 leaf_backward.5
  184.6 2.1 leaf_backward.6
  186.7 3.3 %leaf_backward.7 = (f32[8,64,128]{2,1,0:T(8,128)S(1)}, f32[40,64,128]{2,1,0:T(8,128)}) custom-call(s32[105]{0:T(128)S(1)} %concatenate.39.refs_0_.meta, bf16[24,384,128]{2,1,0:T(8,128)(2,1)S(1)} %copy-done.11, bf16[24,384,128]{2,1,0:T(8,128)(2,1)S(1)} %copy-done.13, f32[24,64,128]{2,1,0:T(8,128)S(1)} %copy-done.15, f32[40,64,128]{2,1,0:T(8,128)S(1)} %get-tuple-element.63.state), custom_call_target="tpu_custom_call" | custom-call | flops 4000000000 | bytes 8388608 | tf_op jit(solution)/shard_map/leaf_backward/pallas_call | solution.py:330
  190.1 5.6 %collective-permute-start.15 = (f32[17,64,128]{2,1,0:T(8,128)S(1)}, f32[17,64,128]{2,1,0:T(8,128)S(1)}, u32[]{:S(2)}, u32[]{:S(2)}) collective-permute-start(f32[17,64,128]{2,1,0:T(8,128)S(1)} %pad_maximum_fusion.3), channel_id=1, source_target_pairs={{0,0},{2,4},{4,2},{6,6},{1,1},{3,5},{5,3},{7,7},{8,8},{10,12},{12,... | collective-permute-start | bytes 1671176 | tf_op jit(solution)/shard_map/ppermute | solution.py:209
  195.7 1.9 collective-permute-start.14
  197.6 16.8 %collective-permute-done.15 = f32[17,64,128]{2,1,0:T(8,128)S(1)} collective-permute-done((f32[17,64,128]{2,1,0:T(8,128)S(1)}, f32[17,64,128]{2,1,0:T(8,128)S(1)}, u32[]{:S(2)}, u32[]{:S(2)}) %collective-permute-start.15) | collective-permute-done | bytes 557088 | tf_op jit(solution)/shard_map/ppermute | solution.py:209
  215.1 5.0 %collective-permute-done.14 = f32[16,64,128]{2,1,0:T(8,128)S(1)} collective-permute-done((f32[16,64,128]{2,1,0:T(8,128)S(1)}, f32[16,64,128]{2,1,0:T(8,128)S(1)}, u32[]{:S(2)}, u32[]{:S(2)}) %collective-permute-start.14) | collective-permute-done | bytes 524320 | tf_op jit(solution)/shard_map/ppermute | solution.py:209
  220.0 1.0 pad_maximum_fusion.2
  (79 shorter events, 12.0 us)
Async XLA Ops:
  7.2 1.6 copy-start
  7.2 8.8 %copy-start.24 = (f32[32,64,128]{2,1,0:T(8,128)S(1)}, f32[32,64,128]{2,1,0:T(8,128)}, u32[]{:S(2)}) copy-start(f32[32,64,128]{2,1,0:T(8,128)} %param.11) | copy-start | bytes 3145732
  7.2 154.3 %all-gather.3.cloned.1.call-start = ((), (), s32[]{:S(2)}) async-start(), calls=%async_computation.2 | async-start | bytes 2359296 | tf_op jit(solution)/shard_map/all_gather | solution.py:246
  10.1 7.7 %copy-start.22 = (f32[32,3,32,128]{3,2,1,0:T(8,128)S(1)}, f32[32,3,32,128]{3,2,1,0:T(8,128)}, u32[]{:S(2)}) copy-start(f32[32,3,32,128]{3,2,1,0:T(8,128)} %param.13) | copy-start | bytes 4718596
  10.1 7.7 %copy-start.23 = (f32[32,32,128]{2,1,0:T(8,128)S(1)}, f32[32,32,128]{2,1,0:T(8,128)}, u32[]{:S(2)}) copy-start(f32[32,32,128]{2,1,0:T(8,128)} %param.14) | copy-start | bytes 1572868
  10.1 7.9 %collective-permute-start = (f32[4,32,128]{2,1,0:T(8,128)S(1)}, f32[4,32,128]{2,1,0:T(8,128)S(1)}, u32[]{:S(2)}, u32[]{:S(2)}) collective-permute-start(f32[4,32,128]{2,1,0:T(8,128)S(1)} %get-tuple-element.69), channel_id=1, source_target_pairs={{0,2},{2,0},{1,3},{3,1},{4,6},{6,4},{5,7},{7,5},{8,10},{10,8},{9,1... | collective-permute-start | bytes 196616 | tf_op jit(solution)/shard_map/ppermute | solution.py:222
  18.0 1.4 slice-start
  18.1 2.8 %slice-start.1 = ((f32[32,3,32,128]{3,2,1,0:T(8,128)}), f32[8,3,32,128]{3,2,1,0:T(8,128)S(1)}, s32[]{:S(2)}) async-start(f32[32,3,32,128]{3,2,1,0:T(8,128)} %param.13), calls=%async_computation.4 | async-start | bytes 786432 | tf_op jit(solution)/shard_map/slice | solution.py:235
  18.1 3.9 %collective-permute-start.1 = (f32[2,4,32,128]{3,2,1,0:T(8,128)S(1)}, f32[2,4,32,128]{3,2,1,0:T(8,128)S(1)}, u32[]{:S(2)}, u32[]{:S(2)}) collective-permute-start(f32[2,4,32,128]{3,2,1,0:T(8,128)S(1)} %pad_maximum_fusion.7), channel_id=1, source_target_pairs={{0,1},{1,0},{2,3},{3,2},{4,5},{5,4},{6,7},{7,6},{8,9},{9,8},{10,11... | collective-permute-start | bytes 393224 | tf_op jit(solution)/shard_map/ppermute | solution.py:222
  22.7 9.1 %collective-permute-start.3 = (f32[32,4,32,128]{3,2,1,0:T(8,128)S(1)}, f32[32,4,32,128]{3,2,1,0:T(8,128)S(1)}, u32[]{:S(2)}, u32[]{:S(2)}) collective-permute-start(f32[32,4,32,128]{3,2,1,0:T(8,128)S(1)} %pad_maximum_fusion.refs_1_), channel_id=1, source_target_pairs={{0,1},{1,0},{6,7},{7,6},{8,9},{9,8},{14,15},{15,14},{16,17},{17,16... | collective-permute-start | bytes 6291464 | tf_op jit(solution)/shard_map/ppermute | solution.py:218
  23.4 40.3 %collective-permute-start.4 = (f32[24,4,32,128]{3,2,1,0:T(8,128)}, f32[24,4,32,128]{3,2,1,0:T(8,128)}, u32[]{:S(2)}, u32[]{:S(2)}) collective-permute-start(f32[24,4,32,128]{3,2,1,0:T(8,128)} %pad_maximum_fusion.1), channel_id=1, source_target_pairs={{2,0},{4,6},{3,1},{5,7},{10,8},{12,14},{11,9},{13,15},{18,16},{20,... | collective-permute-start | bytes 4718600 | tf_op jit(solution)/shard_map/ppermute | solution.py:212
  30.4 46.1 %collective-permute-start.5 = (f32[32,4,32,128]{3,2,1,0:T(8,128)S(1)}, f32[32,4,32,128]{3,2,1,0:T(8,128)S(1)}, u32[]{:S(2)}, u32[]{:S(2)}) collective-permute-start(f32[32,4,32,128]{3,2,1,0:T(8,128)S(1)} %pad_maximum_fusion.refs_1_), channel_id=1, source_target_pairs={{0,4},{6,2},{1,5},{7,3},{8,12},{14,10},{9,13},{15,11},{16,20},{22,... | collective-permute-start | bytes 6291464 | tf_op jit(solution)/shard_map/ppermute | solution.py:215
  31.7 47.4 %collective-permute-start.6 = (f32[32,4,32,128]{3,2,1,0:T(8,128)S(1)}, f32[32,4,32,128]{3,2,1,0:T(8,128)S(1)}, u32[]{:S(2)}, u32[]{:S(2)}) collective-permute-start(f32[32,4,32,128]{3,2,1,0:T(8,128)S(1)} %collective-permute-done.3.refs_2_), channel_id=1, source_target_pairs={{0,4},{6,2},{1,5},{7,3},{8,12},{14,10},{9,13},{15,11},{16,20},{22,... | collective-permute-start | bytes 6291464 | tf_op jit(solution)/shard_map/ppermute | solution.py:215
  33.0 1.4 copy-start.1
  63.8 14.2 %collective-permute-start.7 = (f32[24,4,32,128]{3,2,1,0:T(8,128)}, f32[24,4,32,128]{3,2,1,0:T(8,128)S(1)}, u32[]{:S(2)}, u32[]{:S(2)}) collective-permute-start(f32[24,4,32,128]{3,2,1,0:T(8,128)} %collective-permute-done.4.refs_3_), channel_id=1, source_target_pairs={{0,4},{6,2},{1,5},{7,3},{8,12},{14,10},{9,13},{15,11},{16,20},{22,... | collective-permute-start | bytes 4718600 | tf_op jit(solution)/shard_map/ppermute | solution.py:215
  65.1 36.1 %collective-permute-start.2 = (f32[2120,128]{1,0:T(8,128)}, f32[2120,128]{1,0:T(8,128)S(1)}, u32[]{:S(2)}, u32[]{:S(2)}) collective-permute-start(f32[2120,128]{1,0:T(8,128)} %select_maximum_fusion), channel_id=1, source_target_pairs={{0,0},{2,4},{4,2},{6,6},{1,1},{3,5},{5,3},{7,7},{8,8},{10,12},{12,... | collective-permute-start | bytes 3256328 | tf_op jit(solution)/shard_map/ppermute | solution.py:209
  70.8 21.7 %collective-permute-start.10 = (f32[8,4,32,128]{3,2,1,0:T(8,128)}, f32[8,4,32,128]{3,2,1,0:T(8,128)}, u32[]{:S(2)}, u32[]{:S(2)}) collective-permute-start(f32[8,4,32,128]{3,2,1,0:T(8,128)} %pad_maximum_fusion.4), channel_id=1, source_target_pairs={{2,0},{4,6},{3,1},{5,7},{10,8},{12,14},{11,9},{13,15},{18,16},{20,... | collective-permute-start | bytes 1572872 | tf_op jit(solution)/shard_map/ppermute | solution.py:212
  76.6 1.4 copy-start.3
  78.0 1.1 copy-start.8
  79.2 1.3 copy-start.5
  80.5 20.8 %collective-permute-start.8 = (f32[24,4,32,128]{3,2,1,0:T(8,128)}, f32[24,4,32,128]{3,2,1,0:T(8,128)}, u32[]{:S(2)}, u32[]{:S(2)}) collective-permute-start(f32[24,4,32,128]{3,2,1,0:T(8,128)} %collective-permute-done.4.refs_3_), channel_id=1, source_target_pairs={{0,1},{1,0},{6,7},{7,6},{8,9},{9,8},{14,15},{15,14},{16,17},{17,16... | collective-permute-start | bytes 4718600 | tf_op jit(solution)/shard_map/ppermute | solution.py:218
  101.3 22.7 %collective-permute-start.9 = (f32[24,4,32,128]{3,2,1,0:T(8,128)}, f32[24,4,32,128]{3,2,1,0:T(8,128)}, u32[]{:S(2)}, u32[]{:S(2)}) collective-permute-start(f32[24,4,32,128]{3,2,1,0:T(8,128)} %collective-permute-done.8.refs_4_), channel_id=1, source_target_pairs={{0,4},{6,2},{1,5},{7,3},{8,12},{14,10},{9,13},{15,11},{16,20},{22,... | collective-permute-start | bytes 4718600 | tf_op jit(solution)/shard_map/ppermute | solution.py:215
  102.6 41.2 %collective-permute-start.11 = (f32[8,4,32,128]{3,2,1,0:T(8,128)}, f32[8,4,32,128]{3,2,1,0:T(8,128)}, u32[]{:S(2)}, u32[]{:S(2)}) collective-permute-start(f32[8,4,32,128]{3,2,1,0:T(8,128)} %collective-permute-done.10.refs_3_), channel_id=1, source_target_pairs={{0,1},{1,0},{6,7},{7,6},{8,9},{9,8},{14,15},{15,14},{16,17},{17,16... | collective-permute-start | bytes 1572872 | tf_op jit(solution)/shard_map/ppermute | solution.py:218
  104.7 40.3 %collective-permute-start.12 = (f32[8,4,32,128]{3,2,1,0:T(8,128)}, f32[8,4,32,128]{3,2,1,0:T(8,128)}, u32[]{:S(2)}, u32[]{:S(2)}) collective-permute-start(f32[8,4,32,128]{3,2,1,0:T(8,128)} %collective-permute-done.10.refs_3_), channel_id=1, source_target_pairs={{0,4},{6,2},{1,5},{7,3},{8,12},{14,10},{9,13},{15,11},{16,20},{22,... | collective-permute-start | bytes 1572872 | tf_op jit(solution)/shard_map/ppermute | solution.py:215
  123.9 1.6 copy-start.2
  125.5 1.6 copy-start.4
  127.1 1.6 copy-start.6
  128.7 1.4 copy-start.9
  141.4 1.5 copy-start.10
  142.9 0.9 copy-start.14
  143.8 11.6 %copy-start.12 = (bf16[24,384,128]{2,1,0:T(8,128)(2,1)}, bf16[24,384,128]{2,1,0:T(8,128)(2,1)S(1)}, u32[]{:S(2)}) copy-start(bf16[24,384,128]{2,1,0:T(8,128)(2,1)S(1)} %get-tuple-element.46.low) | copy-start | bytes 7077892
  143.8 5.8 %collective-permute-start.13 = (f32[8,4,32,128]{3,2,1,0:T(8,128)}, f32[8,4,32,128]{3,2,1,0:T(8,128)S(1)}, u32[]{:S(2)}, u32[]{:S(2)}) collective-permute-start(f32[8,4,32,128]{3,2,1,0:T(8,128)} %collective-permute-done.11.refs_4_), channel_id=1, source_target_pairs={{0,4},{6,2},{1,5},{7,3},{8,12},{14,10},{9,13},{15,11},{16,20},{22,... | collective-permute-start | bytes 1572872 | tf_op jit(solution)/shard_map/ppermute | solution.py:215
  155.3 0.9 copy-start.16
  156.2 0.9 copy-start.18
  157.1 0.7 copy-start.20
  157.8 9.7 %all-to-all-start = ((f32[8,5,8,128]{3,2,1,0:T(8,128)}), f32[8,5,8,128]{3,2,1,0:T(8,128)S(1)}, u32[]{:S(2)}, u32[]{:S(2)}) async-start(f32[8,5,8,128]{3,2,1,0:T(8,128)} %get-tuple-element.54), calls=%async_computation | async-start | bytes 327680 | tf_op jit(solution)/shard_map/all_to_all | solution.py:307
  161.5 1.6 copy-start.7
  167.6 12.4 %copy-start.17 = (bf16[8,384,128]{2,1,0:T(8,128)(2,1)S(1)}, bf16[8,384,128]{2,1,0:T(8,128)(2,1)}, u32[]{:S(2)}) copy-start(bf16[8,384,128]{2,1,0:T(8,128)(2,1)} %copy-done.16) | copy-start | bytes 2359300
  167.6 12.4 %copy-start.19 = (bf16[8,384,128]{2,1,0:T(8,128)(2,1)S(1)}, bf16[8,384,128]{2,1,0:T(8,128)(2,1)}, u32[]{:S(2)}) copy-start(bf16[8,384,128]{2,1,0:T(8,128)(2,1)} %copy-done.18) | copy-start | bytes 2359300
  167.6 12.4 %copy-start.21 = (f32[8,64,128]{2,1,0:T(8,128)S(1)}, f32[8,64,128]{2,1,0:T(8,128)}, u32[]{:S(2)}) copy-start(f32[8,64,128]{2,1,0:T(8,128)} %copy-done.20) | copy-start | bytes 786436
  179.9 2.2 copy-start.11
  180.0 2.4 %copy-start.13 = (bf16[24,384,128]{2,1,0:T(8,128)(2,1)S(1)}, bf16[24,384,128]{2,1,0:T(8,128)(2,1)}, u32[]{:S(2)}) copy-start(bf16[24,384,128]{2,1,0:T(8,128)(2,1)} %copy-done.12) | copy-start | bytes 7077892
  180.0 2.5 %copy-start.15 = (f32[24,64,128]{2,1,0:T(8,128)S(1)}, f32[24,64,128]{2,1,0:T(8,128)}, u32[]{:S(2)}) copy-start(f32[24,64,128]{2,1,0:T(8,128)} %copy-done.14) | copy-start | bytes 2359300
  190.1 24.4 %collective-permute-start.15 = (f32[17,64,128]{2,1,0:T(8,128)S(1)}, f32[17,64,128]{2,1,0:T(8,128)S(1)}, u32[]{:S(2)}, u32[]{:S(2)}) collective-permute-start(f32[17,64,128]{2,1,0:T(8,128)S(1)} %pad_maximum_fusion.3), channel_id=1, source_target_pairs={{0,0},{2,4},{4,2},{6,6},{1,1},{3,5},{5,3},{7,7},{8,8},{10,12},{12,... | collective-permute-start | bytes 1671176 | tf_op jit(solution)/shard_map/ppermute | solution.py:209
  195.7 24.4 %collective-permute-start.14 = (f32[16,64,128]{2,1,0:T(8,128)S(1)}, f32[16,64,128]{2,1,0:T(8,128)S(1)}, u32[]{:S(2)}, u32[]{:S(2)}) collective-permute-start(f32[16,64,128]{2,1,0:T(8,128)S(1)} %pad_maximum_fusion.5), channel_id=1, source_target_pairs={{0,0},{2,4},{4,2},{6,6},{1,1},{3,5},{5,3},{7,7},{8,8},{10,12},{12,... | collective-permute-start | bytes 1572872 | tf_op jit(solution)/shard_map/ppermute | solution.py:209
Sparse Core Ops, SparseCore 0:
  101.4 33.5 all-gather.2

commit v4 on v1

--- a/solution.py
+++ b/solution.py
@@ -241,10 +241,10 @@
     near = keepers(own)
     sides = swap(sides)
     far = [to_keeper(part) for part in parts]
-    across = [keepers(after(sides, far[0]))]
+    across = [keepers(far[0])]
     early = [to_trader(value) for value in (own, near, far[0])]
     across += [keepers(after(early, value)) for value in far[1:]]
-    top = lax.all_gather(after(far[-1], top), ("xy", "core"), axis=0, tiled=False)
+    top = lax.all_gather(after((far[-1], sides), top), ("xy", "core"), axis=0, tiled=False)
 
     names = sides[(leafs + 1) * columns :][:3, :leafs].T.astype(jnp.int32).reshape(-1)
     path = jnp.asarray(padded(paths, width))[2 * xy + zh]

time: 206 us -> 203 us (0.985)
  waiting for transfers between devices: 88.5 us -> 74.2 us
  starting transfers between devices: 42.5 us -> 53.3 us
    ppermute x4, waiting for transfers between devices: 67 us -> 16.6 us  [swap(): return lax.ppermute(value, ('core', 'zh'), [(0, 0), (1, 2), (2, 1), (3, 3)])]
    ppermute x2, waiting for transfers between devices: 7.51 us -> 40 us  [to_keeper(): return lax.ppermute(value, ('core', 'zh'), [(1, 0), (2, 3)])]
    ppermute x2, starting transfers between devices: 6.87 us -> 18 us  [to_keeper(): return lax.ppermute(value, ('core', 'zh'), [(1, 0), (2, 3)])]
    ppermute x6, waiting for transfers between devices: 9.37 us -> 15.4 us  [to_trader(): return lax.ppermute(value, ('core', 'zh'), [(0, 2), (3, 1)])]
    all_to_all x1, waiting for transfers between devices: 4.26 us -> 1.82 us  [local(): lax.all_to_all(results[4], ('xy', 'zh'), split_axis=0, concat_axis=0, til...]
  transfers between devices with their start and end apart: 19 -> 19, of which waited for: 10 -> 10; matrix products, arithmetic and copies ran while one was open for 4% -> 4% of each run, Pallas kernels for 11% -> 12%
where the time goes in v4:
time: 203 us; the launch traced here: 202 us
  waiting for transfers between devices  74.2 us (37%)
  starting transfers between devices  53.3 us (26%)
  Pallas kernels  32.3 us (16%)
  between operations  14.4 us (7%)
  blocking collectives  9.66 us (5%)
  other arithmetic  9.06 us (4%)
  local copies, waits for them, and re-layouts  8.64 us (4%)
    ppermute x2, waiting for transfers between devices, to_keeper(): return lax.ppermute(value, ('core', 'zh'), [(1, 0), (2, 3)])  40 us
    ppermute x2, starting transfers between devices, to_keeper(): return lax.ppermute(value, ('core', 'zh'), [(1, 0), (2, 3)])  18 us
    pallas_call x2, Pallas kernels, local(): pl.pallas_call(functools.partial(forward_kernel, base, leafs, k == 0, las...  17.3 us
    ppermute x4, waiting for transfers between devices, swap(): return lax.ppermute(value, ('core', 'zh'), [(0, 0), (1, 2), (2, 1), (3, 3)])  16.6 us
    ppermute x6, waiting for transfers between devices, to_trader(): return lax.ppermute(value, ('core', 'zh'), [(0, 2), (3, 1)])  15.4 us
    ppermute x4, starting transfers between devices, swap(): return lax.ppermute(value, ('core', 'zh'), [(0, 0), (1, 2), (2, 1), (3, 3)])  14.2 us
    all_to_all x1, blocking collectives, local(): lax.all_to_all(outgoing, ('xy', 'zh'), split_axis=0, concat_axis=0, tiled...  9.66 us
    pallas_call x4, Pallas kernels, local(): pl.pallas_call(functools.partial(backward_kernel, k * turn, k == TURNS -...  9.64 us
  transfers between devices with their start and end apart: 19, of which 10 were waited for; matrix products, arithmetic and copies ran while one was open for 4% of the time, Pallas kernels for 12%

profile of v4, /device:TPU:1, one launch (start us, length us, event | category | flops | bytes accessed | tf_op | source)
XLA Modules:
  0.0 201.7 jit_solution(15491503118085513694)
XLA Ops:
  7.2 0.8 fusion.1
  9.4 0.7 fusion.2
  10.1 3.2 %collective-permute-start = (f32[4,32,128]{2,1,0:T(8,128)S(1)}, f32[4,32,128]{2,1,0:T(8,128)S(1)}, u32[]{:S(2)}, u32[]{:S(2)}) collective-permute-start(f32[4,32,128]{2,1,0:T(8,128)S(1)} %get-tuple-element.73), channel_id=1, source_target_pairs={{0,2},{2,0},{1,3},{3,1},{4,6},{6,4},{5,7},{7,5},{8,10},{10,8},{9,1... | collective-permute-start | bytes 196616 | tf_op jit(solution)/shard_map/ppermute | solution.py:222
  13.3 1.0 slice_bitcast_fusion
  14.4 0.9 slice_bitcast_fusion.1
  16.0 1.8 select_maximum_fusion
  18.1 1.4 collective-permute-start.1
  19.4 1.3 pad_maximum_fusion.1
  20.7 0.8 pad_maximum_fusion.4
  21.9 0.7 pad_maximum_fusion.5
  22.7 4.7 %collective-permute-start.7 = (f32[24,4,32,128]{3,2,1,0:T(8,128)}, f32[24,4,32,128]{3,2,1,0:T(8,128)}, u32[]{:S(2)}, u32[]{:S(2)}) collective-permute-start(f32[24,4,32,128]{3,2,1,0:T(8,128)} %pad_maximum_fusion.1), channel_id=1, source_target_pairs={{2,0},{4,6},{3,1},{5,7},{10,8},{12,14},{11,9},{13,15},{18,16},{20,... | collective-permute-start | bytes 4718600 | tf_op jit(solution)/shard_map/ppermute | solution.py:212
  27.4 2.0 %collective-permute-start.3 = (f32[32,4,32,128]{3,2,1,0:T(8,128)S(1)}, f32[32,4,32,128]{3,2,1,0:T(8,128)}, u32[]{:S(2)}, u32[]{:S(2)}) collective-permute-start(f32[32,4,32,128]{3,2,1,0:T(8,128)S(1)} %pad_maximum_fusion.refs_1_), channel_id=1, source_target_pairs={{0,1},{1,0},{6,7},{7,6},{8,9},{9,8},{14,15},{15,14},{16,17},{17,16... | collective-permute-start | bytes 6291464 | tf_op jit(solution)/shard_map/ppermute | solution.py:218
  29.5 4.9 %collective-permute-start.2 = (f32[2120,128]{1,0:T(8,128)}, f32[2120,128]{1,0:T(8,128)S(1)}, u32[]{:S(2)}, u32[]{:S(2)}) collective-permute-start(f32[2120,128]{1,0:T(8,128)} %select_maximum_fusion), channel_id=1, source_target_pairs={{0,0},{2,4},{4,2},{6,6},{1,1},{3,5},{5,3},{7,7},{8,8},{10,12},{12,... | collective-permute-start | bytes 3256328 | tf_op jit(solution)/shard_map/ppermute | solution.py:209
  34.3 23.2 %collective-permute-done.7.refs_3_ = f32[24,4,32,128]{3,2,1,0:T(8,128)} collective-permute-done((f32[24,4,32,128]{3,2,1,0:T(8,128)}, f32[24,4,32,128]{3,2,1,0:T(8,128)}, u32[]{:S(2)}, u32[]{:S(2)}) %collective-permute-start.7) | collective-permute-done | bytes 1572896 | tf_op jit(solution)/shard_map/ppermute | solution.py:212
  57.5 1.8 collective-permute-start.11
  59.3 13.3 %collective-permute-start.4 = (f32[8,4,32,128]{3,2,1,0:T(8,128)}, f32[8,4,32,128]{3,2,1,0:T(8,128)}, u32[]{:S(2)}, u32[]{:S(2)}) collective-permute-start(f32[8,4,32,128]{3,2,1,0:T(8,128)} %pad_maximum_fusion.4), channel_id=1, source_target_pairs={{2,0},{4,6},{3,1},{5,7},{10,8},{12,14},{11,9},{13,15},{18,16},{20,... | collective-permute-start | bytes 1572872 | tf_op jit(solution)/shard_map/ppermute | solution.py:212
  72.6 1.3 collective-permute-start.5
  73.9 1.3 collective-permute-start.6
  75.2 16.8 %collective-permute-done.4.refs_3_ = f32[8,4,32,128]{3,2,1,0:T(8,128)} collective-permute-done((f32[8,4,32,128]{3,2,1,0:T(8,128)}, f32[8,4,32,128]{3,2,1,0:T(8,128)}, u32[]{:S(2)}, u32[]{:S(2)}) %collective-permute-start.4) | collective-permute-done | bytes 524320 | tf_op jit(solution)/shard_map/ppermute | solution.py:212
  92.0 1.3 collective-permute-start.8
  93.3 1.3 collective-permute-start.12
  95.3 1.3 collective-permute-start.10
  96.6 6.5 %collective-permute-done.8.refs_7_ = f32[24,4,32,128]{3,2,1,0:T(8,128)} collective-permute-done((f32[24,4,32,128]{3,2,1,0:T(8,128)}, f32[24,4,32,128]{3,2,1,0:T(8,128)}, u32[]{:S(2)}, u32[]{:S(2)}) %collective-permute-start.8) | collective-permute-done | bytes 1572896 | tf_op jit(solution)/shard_map/ppermute | solution.py:215
  103.1 1.5 collective-permute-start.9
  104.9 4.5 %collective-permute-done.12.refs_8_ = f32[24,4,32,128]{3,2,1,0:T(8,128)} collective-permute-done((f32[24,4,32,128]{3,2,1,0:T(8,128)}, f32[24,4,32,128]{3,2,1,0:T(8,128)}, u32[]{:S(2)}, u32[]{:S(2)}) %collective-permute-start.12) | collective-permute-done | bytes 1572896 | tf_op jit(solution)/shard_map/ppermute | solution.py:215
  109.4 11.5 %leaf_forward.2 = (f32[40,64,128]{2,1,0:T(8,128)S(1)}, bf16[24,384,128]{2,1,0:T(8,128)(2,1)S(1)}, bf16[24,384,128]{2,1,0:T(8,128)(2,1)S(1)}, f32[24,64,128]{2,1,0:T(8,128)S(1)}) custom-call(s32[105]{0:T(128)S(1)} %concatenate.36.refs_0_.meta, f32[32,4,32,128]{3,2,1,0:T(8,128)S(1)} %pad_maximum_fusion.refs_1_, ...), custom_call_target="tpu_custom_call" | custom-call | flops 4000000000 | bytes 8388608 | tf_op jit(solution)/shard_map/leaf_forward/pallas_call | solution.py:275
  120.9 1.3 collective-permute-start.13
  122.2 4.5 %collective-permute-done.13.refs_8_ = f32[8,4,32,128]{3,2,1,0:T(8,128)S(1)} collective-permute-done((f32[8,4,32,128]{3,2,1,0:T(8,128)}, f32[8,4,32,128]{3,2,1,0:T(8,128)S(1)}, u32[]{:S(2)}, u32[]{:S(2)}) %collective-permute-start.13) | collective-permute-done | bytes 524320 | tf_op jit(solution)/shard_map/ppermute | solution.py:215
  126.6 5.8 %leaf_forward.3 = (f32[40,64,128]{2,1,0:T(8,128)}, bf16[8,384,128]{2,1,0:T(8,128)(2,1)S(1)}, bf16[8,384,128]{2,1,0:T(8,128)(2,1)S(1)}, f32[8,64,128]{2,1,0:T(8,128)S(1)}, f32[8,5,8,128]{3,2,1,0:T(8,128)}) custom-call(s32[105]{0:T(128)S(1)} %concatenate.36.refs_0_.meta, f32[32,4,32,128]{3,2,1,0:T(8,128)S(1)} %pad_maximum_fusion.refs_1_, ...), custom_call_target="tpu_custom_call" | custom-call | flops 4000000000 | bytes 8388608 | tf_op jit(solution)/shard_map/leaf_forward/pallas_call | solution.py:275
  132.5 0.9 copy-done.8
  133.4 0.9 copy-done.10
  135.0 3.4 %all-to-all-start = ((f32[8,5,8,128]{3,2,1,0:T(8,128)}), f32[8,5,8,128]{3,2,1,0:T(8,128)S(1)}, u32[]{:S(2)}, u32[]{:S(2)}) async-start(f32[8,5,8,128]{3,2,1,0:T(8,128)} %get-tuple-element.54), calls=%async_computation | async-start | bytes 327680 | tf_op jit(solution)/shard_map/all_to_all | solution.py:308
  138.5 1.6 copy-done.1
  140.1 2.7 %top_prepare.1 = (bf16[8,384,128]{2,1,0:T(8,128)(2,1)S(1)}, bf16[8,384,128]{2,1,0:T(8,128)(2,1)S(1)}, bf16[8,128,128]{2,1,0:T(8,128)(2,1)S(1)}, bf16[8,128,128]{2,1,0:T(8,128)(2,1)S(1)}) custom-call(s32[4]{0:T(128)S(1)} %pad_add_fusion.places, f32[8,4,4,32,128]{4,3,2,1,0:T(8,128)S(1)} %bitcast.32), custom_call_target="tpu_custom_call" | custom-call | tf_op jit(solution)/shard_map/top_prepare/pallas_call | solution.py:296
  142.8 1.8 all-to-all-done.incoming
  144.6 2.7 %top_solve.1 = f32[8,5,8,128]{3,2,1,0:T(8,128)S(1)} custom-call(f32[8,5,8,128]{3,2,1,0:T(8,128)S(1)} %all-to-all-done.incoming, bf16[8,384,128]{2,1,0:T(8,128)(2,1)S(1)} %get-tuple-element.57.high, bf16[8,384,128]{2,1,0:T(8,128)(2,1)S(1)} %get-tuple-element.58.low, bf16[8,128,128]{2,1,0:T(8,128)(2,1)S(1)} %get-tuple-element.59.inverse_high, ...), custom_call_target="tpu_custom_call" | custom-call | tf_op jit(solution)/shard_map/top_solve/pallas_call | solution.py:309
  147.4 9.7 %all_to_all.10.state = f32[8,5,8,128]{3,2,1,0:T(8,128)S(1)} all-to-all(f32[8,5,8,128]{3,2,1,0:T(8,128)S(1)} %top_solve.1), channel_id=1, replica_groups=mesh['xy'=4,'core'=2,'zh'=2,'zl'=2] {'xy','zh'}, dimensions={0} | all-to-all | bytes 327680 | tf_op jit(solution)/shard_map/all_to_all | solution.py:317
  157.1 2.1 %leaf_backward.4 = (f32[8,64,128]{2,1,0:T(8,128)S(1)}, f32[40,64,128]{2,1,0:T(8,128)S(1)}) custom-call(s32[105]{0:T(128)S(1)} %concatenate.36.refs_0_.meta, bf16[8,384,128]{2,1,0:T(8,128)(2,1)S(1)} %copy-done.9, bf16[8,384,128]{2,1,0:T(8,128)(2,1)S(1)} %copy-done.11, f32[8,64,128]{2,1,0:T(8,128)S(1)} %copy-done.13, f32[8,5,8,128]{3,2,1,0:T(8,128)S(1)} %all_to_all.10.state), custom_call_target="tpu_custom_call" | custom-call | flops 4000000000 | bytes 8388608 | tf_op jit(solution)/shard_map/leaf_backward/pallas_call | solution.py:330
  159.6 2.1 %leaf_backward.5 = (f32[8,64,128]{2,1,0:T(8,128)S(1)}, f32[40,64,128]{2,1,0:T(8,128)S(1)}) custom-call(s32[105]{0:T(128)S(1)} %concatenate.36.refs_0_.meta, bf16[24,384,128]{2,1,0:T(8,128)(2,1)S(1)} %copy-done.3, bf16[24,384,128]{2,1,0:T(8,128)(2,1)S(1)} %copy-done.5, f32[24,64,128]{2,1,0:T(8,128)S(1)} %copy-done.7, f32[40,64,128]{2,1,0:T(8,128)S(1)} %get-tuple-element.65.state), custom_call_target="tpu_custom_call" | custom-call | flops 4000000000 | bytes 8388608 | tf_op jit(solution)/shard_map/leaf_backward/pallas_call | solution.py:330
  161.7 2.1 %leaf_backward.6 = (f32[8,64,128]{2,1,0:T(8,128)S(1)}, f32[40,64,128]{2,1,0:T(8,128)S(1)}) custom-call(s32[105]{0:T(128)S(1)} %concatenate.36.refs_0_.meta, bf16[24,384,128]{2,1,0:T(8,128)(2,1)S(1)} %copy-done.3, bf16[24,384,128]{2,1,0:T(8,128)(2,1)S(1)} %copy-done.5, f32[24,64,128]{2,1,0:T(8,128)S(1)} %copy-done.7, f32[40,64,128]{2,1,0:T(8,128)S(1)} %get-tuple-element.66.state), custom_call_target="tpu_custom_call" | custom-call | flops 4000000000 | bytes 8388608 | tf_op jit(solution)/shard_map/leaf_backward/pallas_call | solution.py:330
  163.8 5.5 %collective-permute-start.14 = (f32[8,64,128]{2,1,0:T(8,128)S(1)}, f32[8,64,128]{2,1,0:T(8,128)S(1)}, u32[]{:S(2)}, u32[]{:S(2)}) collective-permute-start(f32[8,64,128]{2,1,0:T(8,128)S(1)} %get-tuple-element.61), channel_id=1, source_target_pairs={{0,0},{2,4},{4,2},{6,6},{1,1},{3,5},{5,3},{7,7},{8,8},{10,12},{12,... | collective-permute-start | bytes 786440 | tf_op jit(solution)/shard_map/ppermute | solution.py:209
  169.4 1.9 collective-permute-start.16
  171.4 3.2 %leaf_backward.7 = (f32[8,64,128]{2,1,0:T(8,128)S(1)}, f32[40,64,128]{2,1,0:T(8,128)}) custom-call(s32[105]{0:T(128)S(1)} %concatenate.36.refs_0_.meta, bf16[24,384,128]{2,1,0:T(8,128)(2,1)S(1)} %copy-done.3, bf16[24,384,128]{2,1,0:T(8,128)(2,1)S(1)} %copy-done.5, f32[24,64,128]{2,1,0:T(8,128)S(1)} %copy-done.7, f32[40,64,128]{2,1,0:T(8,128)S(1)} %get-tuple-element.67.state), custom_call_target="tpu_custom_call" | custom-call | flops 4000000000 | bytes 8388608 | tf_op jit(solution)/shard_map/leaf_backward/pallas_call | solution.py:330
  174.6 7.6 %collective-permute-done.14 = f32[8,64,128]{2,1,0:T(8,128)S(1)} collective-permute-done((f32[8,64,128]{2,1,0:T(8,128)S(1)}, f32[8,64,128]{2,1,0:T(8,128)S(1)}, u32[]{:S(2)}, u32[]{:S(2)}) %collective-permute-start.14) | collective-permute-done | bytes 262176 | tf_op jit(solution)/shard_map/ppermute | solution.py:209
  182.2 1.9 collective-permute-start.15
  184.1 4.1 %collective-permute-done.16 = f32[17,64,128]{2,1,0:T(8,128)S(1)} collective-permute-done((f32[17,64,128]{2,1,0:T(8,128)S(1)}, f32[17,64,128]{2,1,0:T(8,128)S(1)}, u32[]{:S(2)}, u32[]{:S(2)}) %collective-permute-start.16) | collective-permute-done | bytes 557088 | tf_op jit(solution)/shard_map/ppermute | solution.py:209
  188.8 4.9 %collective-permute-done.15 = f32[8,64,128]{2,1,0:T(8,128)S(1)} collective-permute-done((f32[8,64,128]{2,1,0:T(8,128)S(1)}, f32[8,64,128]{2,1,0:T(8,128)S(1)}, u32[]{:S(2)}, u32[]{:S(2)}) %collective-permute-start.15) | collective-permute-done | bytes 262176 | tf_op jit(solution)/shard_map/ppermute | solution.py:209
  193.8 1.1 pad_maximum_fusion.2
  (64 shorter events, 5.6 us)
Async XLA Ops:
  7.2 1.6 copy-start
  7.2 8.8 %copy-start.16 = (f32[32,64,128]{2,1,0:T(8,128)S(1)}, f32[32,64,128]{2,1,0:T(8,128)}, u32[]{:S(2)}) copy-start(f32[32,64,128]{2,1,0:T(8,128)} %param.11) | copy-start | bytes 3145732
  7.2 131.3 %all-gather.3.cloned.1.call-start = ((), (), s32[]{:S(2)}) async-start(), calls=%async_computation.2 | async-start | bytes 2359296 | tf_op jit(solution)/shard_map/all_gather | solution.py:247
  10.1 7.7 %copy-start.14 = (f32[32,3,32,128]{3,2,1,0:T(8,128)S(1)}, f32[32,3,32,128]{3,2,1,0:T(8,128)}, u32[]{:S(2)}) copy-start(f32[32,3,32,128]{3,2,1,0:T(8,128)} %param.13) | copy-start | bytes 4718596
  10.1 7.7 %copy-start.15 = (f32[32,32,128]{2,1,0:T(8,128)S(1)}, f32[32,32,128]{2,1,0:T(8,128)}, u32[]{:S(2)}) copy-start(f32[32,32,128]{2,1,0:T(8,128)} %param.14) | copy-start | bytes 1572868
  10.1 7.9 %collective-permute-start = (f32[4,32,128]{2,1,0:T(8,128)S(1)}, f32[4,32,128]{2,1,0:T(8,128)S(1)}, u32[]{:S(2)}, u32[]{:S(2)}) collective-permute-start(f32[4,32,128]{2,1,0:T(8,128)S(1)} %get-tuple-element.73), channel_id=1, source_target_pairs={{0,2},{2,0},{1,3},{3,1},{4,6},{6,4},{5,7},{7,5},{8,10},{10,8},{9,1... | collective-permute-start | bytes 196616 | tf_op jit(solution)/shard_map/ppermute | solution.py:222
  18.0 1.4 slice-start
  18.0 2.7 %slice-start.1 = ((f32[32,3,32,128]{3,2,1,0:T(8,128)}), f32[8,3,32,128]{3,2,1,0:T(8,128)S(1)}, s32[]{:S(2)}) async-start(f32[32,3,32,128]{3,2,1,0:T(8,128)} %param.13), calls=%async_computation.4 | async-start | bytes 786432 | tf_op jit(solution)/shard_map/slice | solution.py:235
  18.1 3.9 %collective-permute-start.1 = (f32[2,4,32,128]{3,2,1,0:T(8,128)S(1)}, f32[2,4,32,128]{3,2,1,0:T(8,128)S(1)}, u32[]{:S(2)}, u32[]{:S(2)}) collective-permute-start(f32[2,4,32,128]{3,2,1,0:T(8,128)S(1)} %pad_maximum_fusion.6), channel_id=1, source_target_pairs={{0,1},{1,0},{2,3},{3,2},{4,5},{5,4},{6,7},{7,6},{8,9},{9,8},{10,11... | collective-permute-start | bytes 393224 | tf_op jit(solution)/shard_map/ppermute | solution.py:222
  22.7 34.8 %collective-permute-start.7 = (f32[24,4,32,128]{3,2,1,0:T(8,128)}, f32[24,4,32,128]{3,2,1,0:T(8,128)}, u32[]{:S(2)}, u32[]{:S(2)}) collective-permute-start(f32[24,4,32,128]{3,2,1,0:T(8,128)} %pad_maximum_fusion.1), channel_id=1, source_target_pairs={{2,0},{4,6},{3,1},{5,7},{10,8},{12,14},{11,9},{13,15},{18,16},{20,... | collective-permute-start | bytes 4718600 | tf_op jit(solution)/shard_map/ppermute | solution.py:212
  27.4 46.4 %collective-permute-start.3 = (f32[32,4,32,128]{3,2,1,0:T(8,128)S(1)}, f32[32,4,32,128]{3,2,1,0:T(8,128)}, u32[]{:S(2)}, u32[]{:S(2)}) collective-permute-start(f32[32,4,32,128]{3,2,1,0:T(8,128)S(1)} %pad_maximum_fusion.refs_1_), channel_id=1, source_target_pairs={{0,1},{1,0},{6,7},{7,6},{8,9},{9,8},{14,15},{15,14},{16,17},{17,16... | collective-permute-start | bytes 6291464 | tf_op jit(solution)/shard_map/ppermute | solution.py:218
  29.5 62.5 %collective-permute-start.2 = (f32[2120,128]{1,0:T(8,128)}, f32[2120,128]{1,0:T(8,128)S(1)}, u32[]{:S(2)}, u32[]{:S(2)}) collective-permute-start(f32[2120,128]{1,0:T(8,128)} %select_maximum_fusion), channel_id=1, source_target_pairs={{0,0},{2,4},{4,2},{6,6},{1,1},{3,5},{5,3},{7,7},{8,8},{10,12},{12,... | collective-permute-start | bytes 3256328 | tf_op jit(solution)/shard_map/ppermute | solution.py:209
  57.5 35.8 %collective-permute-start.11 = (f32[24,4,32,128]{3,2,1,0:T(8,128)}, f32[24,4,32,128]{3,2,1,0:T(8,128)}, u32[]{:S(2)}, u32[]{:S(2)}) collective-permute-start(f32[24,4,32,128]{3,2,1,0:T(8,128)} %collective-permute-done.7.refs_3_), channel_id=1, source_target_pairs={{0,1},{1,0},{6,7},{7,6},{8,9},{9,8},{14,15},{15,14},{16,17},{17,16... | collective-permute-start | bytes 4718600 | tf_op jit(solution)/shard_map/ppermute | solution.py:218
  59.3 32.7 %collective-permute-start.4 = (f32[8,4,32,128]{3,2,1,0:T(8,128)}, f32[8,4,32,128]{3,2,1,0:T(8,128)}, u32[]{:S(2)}, u32[]{:S(2)}) collective-permute-start(f32[8,4,32,128]{3,2,1,0:T(8,128)} %pad_maximum_fusion.4), channel_id=1, source_target_pairs={{2,0},{4,6},{3,1},{5,7},{10,8},{12,14},{11,9},{13,15},{18,16},{20,... | collective-permute-start | bytes 1572872 | tf_op jit(solution)/shard_map/ppermute | solution.py:212
  72.6 24.1 %collective-permute-start.5 = (f32[32,4,32,128]{3,2,1,0:T(8,128)S(1)}, f32[32,4,32,128]{3,2,1,0:T(8,128)}, u32[]{:S(2)}, u32[]{:S(2)}) collective-permute-start(f32[32,4,32,128]{3,2,1,0:T(8,128)S(1)} %pad_maximum_fusion.refs_1_), channel_id=1, source_target_pairs={{0,4},{6,2},{1,5},{7,3},{8,12},{14,10},{9,13},{15,11},{16,20},{22,... | collective-permute-start | bytes 6291464 | tf_op jit(solution)/shard_map/ppermute | solution.py:215
  73.9 29.2 %collective-permute-start.6 = (f32[32,4,32,128]{3,2,1,0:T(8,128)}, f32[32,4,32,128]{3,2,1,0:T(8,128)}, u32[]{:S(2)}, u32[]{:S(2)}) collective-permute-start(f32[32,4,32,128]{3,2,1,0:T(8,128)} %collective-permute-done.3.refs_2_), channel_id=1, source_target_pairs={{0,4},{6,2},{1,5},{7,3},{8,12},{14,10},{9,13},{15,11},{16,20},{22,... | collective-permute-start | bytes 6291464 | tf_op jit(solution)/shard_map/ppermute | solution.py:215
  92.0 11.1 %collective-permute-start.8 = (f32[24,4,32,128]{3,2,1,0:T(8,128)}, f32[24,4,32,128]{3,2,1,0:T(8,128)}, u32[]{:S(2)}, u32[]{:S(2)}) collective-permute-start(f32[24,4,32,128]{3,2,1,0:T(8,128)} %collective-permute-done.7.refs_3_), channel_id=1, source_target_pairs={{0,4},{6,2},{1,5},{7,3},{8,12},{14,10},{9,13},{15,11},{16,20},{22,... | collective-permute-start | bytes 4718600 | tf_op jit(solution)/shard_map/ppermute | solution.py:215
  93.3 16.0 %collective-permute-start.12 = (f32[24,4,32,128]{3,2,1,0:T(8,128)}, f32[24,4,32,128]{3,2,1,0:T(8,128)}, u32[]{:S(2)}, u32[]{:S(2)}) collective-permute-start(f32[24,4,32,128]{3,2,1,0:T(8,128)} %collective-permute-done.11.refs_4_), channel_id=1, source_target_pairs={{0,4},{6,2},{1,5},{7,3},{8,12},{14,10},{9,13},{15,11},{16,20},{22,... | collective-permute-start | bytes 4718600 | tf_op jit(solution)/shard_map/ppermute | solution.py:215
  95.3 26.8 %collective-permute-start.10 = (f32[8,4,32,128]{3,2,1,0:T(8,128)}, f32[8,4,32,128]{3,2,1,0:T(8,128)}, u32[]{:S(2)}, u32[]{:S(2)}) collective-permute-start(f32[8,4,32,128]{3,2,1,0:T(8,128)} %collective-permute-done.4.refs_3_), channel_id=1, source_target_pairs={{0,4},{6,2},{1,5},{7,3},{8,12},{14,10},{9,13},{15,11},{16,20},{22,... | collective-permute-start | bytes 1572872 | tf_op jit(solution)/shard_map/ppermute | solution.py:215
  103.1 17.8 %collective-permute-start.9 = (f32[8,4,32,128]{3,2,1,0:T(8,128)}, f32[8,4,32,128]{3,2,1,0:T(8,128)}, u32[]{:S(2)}, u32[]{:S(2)}) collective-permute-start(f32[8,4,32,128]{3,2,1,0:T(8,128)} %collective-permute-done.4.refs_3_), channel_id=1, source_target_pairs={{0,1},{1,0},{6,7},{7,6},{8,9},{9,8},{14,15},{15,14},{16,17},{17,16... | collective-permute-start | bytes 1572872 | tf_op jit(solution)/shard_map/ppermute | solution.py:218
  120.8 11.7 %copy-start.2 = (bf16[24,384,128]{2,1,0:T(8,128)(2,1)}, bf16[24,384,128]{2,1,0:T(8,128)(2,1)S(1)}, u32[]{:S(2)}) copy-start(bf16[24,384,128]{2,1,0:T(8,128)(2,1)S(1)} %get-tuple-element.62.high) | copy-start | bytes 7077892
  120.8 11.7 %copy-start.4 = (bf16[24,384,128]{2,1,0:T(8,128)(2,1)}, bf16[24,384,128]{2,1,0:T(8,128)(2,1)S(1)}, u32[]{:S(2)}) copy-start(bf16[24,384,128]{2,1,0:T(8,128)(2,1)S(1)} %get-tuple-element.63.low) | copy-start | bytes 7077892
  120.8 11.7 %copy-start.6 = (f32[24,64,128]{2,1,0:T(8,128)}, f32[24,64,128]{2,1,0:T(8,128)S(1)}, u32[]{:S(2)}) copy-start(f32[24,64,128]{2,1,0:T(8,128)S(1)} %get-tuple-element.64.scaled) | copy-start | bytes 2359300
  120.9 5.8 %collective-permute-start.13 = (f32[8,4,32,128]{3,2,1,0:T(8,128)}, f32[8,4,32,128]{3,2,1,0:T(8,128)S(1)}, u32[]{:S(2)}, u32[]{:S(2)}) collective-permute-start(f32[8,4,32,128]{3,2,1,0:T(8,128)} %collective-permute-done.9.refs_4_), channel_id=1, source_target_pairs={{0,4},{6,2},{1,5},{7,3},{8,12},{14,10},{9,13},{15,11},{16,20},{22,... | collective-permute-start | bytes 1572872 | tf_op jit(solution)/shard_map/ppermute | solution.py:215
  132.5 0.9 copy-start.8
  133.4 0.9 copy-start.10
  134.3 0.7 copy-start.12
  135.0 9.6 %all-to-all-start = ((f32[8,5,8,128]{3,2,1,0:T(8,128)}), f32[8,5,8,128]{3,2,1,0:T(8,128)S(1)}, u32[]{:S(2)}, u32[]{:S(2)}) async-start(f32[8,5,8,128]{3,2,1,0:T(8,128)} %get-tuple-element.54), calls=%async_computation | async-start | bytes 327680 | tf_op jit(solution)/shard_map/all_to_all | solution.py:308
  138.5 1.6 copy-start.1
  144.6 12.4 %copy-start.9 = (bf16[8,384,128]{2,1,0:T(8,128)(2,1)S(1)}, bf16[8,384,128]{2,1,0:T(8,128)(2,1)}, u32[]{:S(2)}) copy-start(bf16[8,384,128]{2,1,0:T(8,128)(2,1)} %copy-done.8) | copy-start | bytes 2359300
  144.6 12.4 %copy-start.11 = (bf16[8,384,128]{2,1,0:T(8,128)(2,1)S(1)}, bf16[8,384,128]{2,1,0:T(8,128)(2,1)}, u32[]{:S(2)}) copy-start(bf16[8,384,128]{2,1,0:T(8,128)(2,1)} %copy-done.10) | copy-start | bytes 2359300
  144.6 12.4 %copy-start.13 = (f32[8,64,128]{2,1,0:T(8,128)S(1)}, f32[8,64,128]{2,1,0:T(8,128)}, u32[]{:S(2)}) copy-start(f32[8,64,128]{2,1,0:T(8,128)} %copy-done.12) | copy-start | bytes 786436
  157.0 2.2 %copy-start.3 = (bf16[24,384,128]{2,1,0:T(8,128)(2,1)S(1)}, bf16[24,384,128]{2,1,0:T(8,128)(2,1)}, u32[]{:S(2)}) copy-start(bf16[24,384,128]{2,1,0:T(8,128)(2,1)} %copy-done.2) | copy-start | bytes 7077892
  157.0 2.4 %copy-start.5 = (bf16[24,384,128]{2,1,0:T(8,128)(2,1)S(1)}, bf16[24,384,128]{2,1,0:T(8,128)(2,1)}, u32[]{:S(2)}) copy-start(bf16[24,384,128]{2,1,0:T(8,128)(2,1)} %copy-done.4) | copy-start | bytes 7077892
  157.1 2.5 %copy-start.7 = (f32[24,64,128]{2,1,0:T(8,128)S(1)}, f32[24,64,128]{2,1,0:T(8,128)}, u32[]{:S(2)}) copy-start(f32[24,64,128]{2,1,0:T(8,128)} %copy-done.6) | copy-start | bytes 2359300
  163.8 18.3 %collective-permute-start.14 = (f32[8,64,128]{2,1,0:T(8,128)S(1)}, f32[8,64,128]{2,1,0:T(8,128)S(1)}, u32[]{:S(2)}, u32[]{:S(2)}) collective-permute-start(f32[8,64,128]{2,1,0:T(8,128)S(1)} %get-tuple-element.61), channel_id=1, source_target_pairs={{0,0},{2,4},{4,2},{6,6},{1,1},{3,5},{5,3},{7,7},{8,8},{10,12},{12,... | collective-permute-start | bytes 786440 | tf_op jit(solution)/shard_map/ppermute | solution.py:209
  169.4 18.7 %collective-permute-start.16 = (f32[17,64,128]{2,1,0:T(8,128)S(1)}, f32[17,64,128]{2,1,0:T(8,128)S(1)}, u32[]{:S(2)}, u32[]{:S(2)}) collective-permute-start(f32[17,64,128]{2,1,0:T(8,128)S(1)} %pad_maximum_fusion.3), channel_id=1, source_target_pairs={{0,0},{2,4},{4,2},{6,6},{1,1},{3,5},{5,3},{7,7},{8,8},{10,12},{12,... | collective-permute-start | bytes 1671176 | tf_op jit(solution)/shard_map/ppermute | solution.py:209
  182.2 11.6 %collective-permute-start.15 = (f32[8,64,128]{2,1,0:T(8,128)S(1)}, f32[8,64,128]{2,1,0:T(8,128)S(1)}, u32[]{:S(2)}, u32[]{:S(2)}) collective-permute-start(f32[8,64,128]{2,1,0:T(8,128)S(1)} %get-tuple-element.69), channel_id=1, source_target_pairs={{0,0},{2,4},{4,2},{6,6},{1,1},{3,5},{5,3},{7,7},{8,8},{10,12},{12,... | collective-permute-start | bytes 786440 | tf_op jit(solution)/shard_map/ppermute | solution.py:209
Sparse Core Ops, SparseCore 0:
  92.1 34.6 all-gather.2

commit v5 on v4

--- a/solution.py
+++ b/solution.py
@@ -226,9 +226,6 @@
 
     chosen = jnp.take(top_blocks[:, 0], jnp.asarray(padded(above, most))[2 * xy + core], axis=0)
     top = jnp.concatenate([chosen, top_dinv], axis=0)
-    top = jnp.stack([top, other(top, "zh")])
-    top = jnp.concatenate([top, other(top, "zl")])
-
     names = jnp.zeros((8, wide), f32).at[:3, :leafs].set(leaf_struct.T.astype(f32))
     sides = jnp.concatenate([rhs_leaf.reshape(-1, wide), rhs_top.reshape(-1, wide), names], axis=0)
     def joined(at):
@@ -236,7 +233,6 @@
 
     own = joined(slice(None))
     parts = [joined(slice(at, end)) for at, end in zip(starts, starts[1:])]
-    own, parts, sides = after(top, (own, parts, sides))
 
     near = keepers(own)
     sides = swap(sides)
@@ -244,6 +240,9 @@
     across = [keepers(far[0])]
     early = [to_trader(value) for value in (own, near, far[0])]
     across += [keepers(after(early, value)) for value in far[1:]]
+    top = after(early[:2], top)
+    top = jnp.stack([top, other(top, "zh")])
+    top = jnp.concatenate([top, other(top, "zl")])
     top = lax.all_gather(after((far[-1], sides), top), ("xy", "core"), axis=0, tiled=False)
 
     names = sides[(leafs + 1) * columns :][:3, :leafs].T.astype(jnp.int32).reshape(-1)
@@ -339,7 +338,7 @@
         )(meta, *factors[held], state)
     late = swap(found[-1])
     middle = swap(jnp.concatenate(found[1:-1] + [own_top], axis=0))
-    first = swap(after(late, found[0]))
+    first = swap(found[0])
     leaf_solution = jnp.concatenate([first, middle[:-1], late], axis=0)
     return (leaf_solution, middle[-1:])
 

time: 203 us -> 207 us (1.020)
  starting transfers between devices: 53.3 us -> 95.7 us
  waiting for transfers between devices: 74.2 us -> 38.9 us
  local copies, waits for them, and re-layouts: 8.64 us -> 6.41 us
    ppermute x2, waiting for transfers between devices: 40 us -> 0.01 us  [to_keeper(): return lax.ppermute(value, ('core', 'zh'), [(1, 0), (2, 3)])]
    ppermute x2, starting transfers between devices: 18 us -> 46.2 us  [to_keeper(): return lax.ppermute(value, ('core', 'zh'), [(1, 0), (2, 3)])]
    ppermute x2, starting transfers between devices: 4.57 us -> 18.4 us  [other(): return lax.ppermute(value, axes, [(i, last - i) for i in range(last + 1)])]
    ppermute x2, waiting for transfers between devices: 0.36 us -> 9.56 us  [other(): return lax.ppermute(value, axes, [(i, last - i) for i in range(last + 1)])]
    ppermute x4, waiting for transfers between devices: 16.6 us -> 13 us  [swap(): return lax.ppermute(value, ('core', 'zh'), [(0, 0), (1, 2), (2, 1), (3, 3)])]
    ppermute x6, waiting for transfers between devices: 15.4 us -> 12.1 us  [to_trader(): return lax.ppermute(value, ('core', 'zh'), [(0, 2), (3, 1)])]
    all_to_all x1, waiting for transfers between devices: 1.82 us -> 4.3 us  [local(): lax.all_to_all(results[4], ('xy', 'zh'), split_axis=0, concat_axis=0, til...]
    unnamed x34 -> x38, local copies, waits for them, and re-layouts: 4.5 us -> 4.16 us
  transfers between devices with their start and end apart: 19 -> 19, of which waited for: 10 -> 8; matrix products, arithmetic and copies ran while one was open for 4% -> 4% of each run, Pallas kernels for 12% -> 13%
where the time goes in v5:
time: 207 us; the launch traced here: 206 us
  starting transfers between devices  95.7 us (46%)
  waiting for transfers between devices  38.9 us (19%)
  Pallas kernels  32.3 us (16%)
  between operations  14.5 us (7%)
  blocking collectives  9.76 us (5%)
  other arithmetic  8.41 us (4%)
  local copies, waits for them, and re-layouts  6.41 us (3%)
    ppermute x2, starting transfers between devices, to_keeper(): return lax.ppermute(value, ('core', 'zh'), [(1, 0), (2, 3)])  46.2 us
    ppermute x2, starting transfers between devices, other(): return lax.ppermute(value, axes, [(i, last - i) for i in range(last + 1)])  18.4 us
    pallas_call x2, Pallas kernels, local(): pl.pallas_call(functools.partial(forward_kernel, base, leafs, k == 0, las...  17.3 us
    ppermute x4, waiting for transfers between devices, swap(): return lax.ppermute(value, ('core', 'zh'), [(0, 0), (1, 2), (2, 1), (3, 3)])  13 us
    ppermute x4, starting transfers between devices, swap(): return lax.ppermute(value, ('core', 'zh'), [(0, 0), (1, 2), (2, 1), (3, 3)])  12.5 us
    ppermute x6, waiting for transfers between devices, to_trader(): return lax.ppermute(value, ('core', 'zh'), [(0, 2), (3, 1)])  12.1 us
    all_to_all x1, blocking collectives, local(): lax.all_to_all(outgoing, ('xy', 'zh'), split_axis=0, concat_axis=0, tiled...  9.76 us
    pallas_call x4, Pallas kernels, local(): pl.pallas_call(functools.partial(backward_kernel, k * turn, k == TURNS -...  9.62 us
  transfers between devices with their start and end apart: 19, of which 8 were waited for; matrix products, arithmetic and copies ran while one was open for 4% of the time, Pallas kernels for 13%

profile of v5, /device:TPU:1, one launch (start us, length us, event | category | flops | bytes accessed | tf_op | source)
XLA Modules:
  0.0 206.0 jit_solution(13317615729956944761)
XLA Ops:
  7.2 1.8 pad_maximum_fusion.refs_1_
  9.0 2.2 %collective-permute-start.1 = (f32[32,4,32,128]{3,2,1,0:T(8,128)S(1)}, f32[32,4,32,128]{3,2,1,0:T(8,128)}, u32[]{:S(2)}, u32[]{:S(2)}) collective-permute-start(f32[32,4,32,128]{3,2,1,0:T(8,128)S(1)} %pad_maximum_fusion.refs_1_), channel_id=1, source_target_pairs={{0,1},{1,0},{6,7},{7,6},{8,9},{9,8},{14,15},{15,14},{16,17},{17,16... | collective-permute-start | bytes 6291464 | tf_op jit(solution)/shard_map/ppermute | solution.py:218
  11.3 1.3 pad_maximum_fusion.1
  12.6 7.4 %collective-permute-start.2 = (f32[24,4,32,128]{3,2,1,0:T(8,128)}, f32[24,4,32,128]{3,2,1,0:T(8,128)}, u32[]{:S(2)}, u32[]{:S(2)}) collective-permute-start(f32[24,4,32,128]{3,2,1,0:T(8,128)} %pad_maximum_fusion.1), channel_id=1, source_target_pairs={{2,0},{4,6},{3,1},{5,7},{10,8},{12,14},{11,9},{13,15},{18,16},{20,... | collective-permute-start | bytes 4718600 | tf_op jit(solution)/shard_map/ppermute | solution.py:212
  20.0 1.3 collective-permute-start.4
  21.3 1.3 collective-permute-start.5
  22.6 1.1 select_maximum_fusion
  23.7 3.2 %collective-permute-start = (f32[2120,128]{1,0:T(8,128)}, f32[2120,128]{1,0:T(8,128)S(1)}, u32[]{:S(2)}, u32[]{:S(2)}) collective-permute-start(f32[2120,128]{1,0:T(8,128)} %select_maximum_fusion), channel_id=1, source_target_pairs={{0,0},{2,4},{4,2},{6,6},{1,1},{3,5},{5,3},{7,7},{8,8},{10,12},{12,... | collective-permute-start | bytes 3256328 | tf_op jit(solution)/shard_map/ppermute | solution.py:209
  26.9 0.8 pad_maximum_fusion.4
  27.8 38.9 %collective-permute-start.7 = (f32[8,4,32,128]{3,2,1,0:T(8,128)}, f32[8,4,32,128]{3,2,1,0:T(8,128)}, u32[]{:S(2)}, u32[]{:S(2)}) collective-permute-start(f32[8,4,32,128]{3,2,1,0:T(8,128)} %pad_maximum_fusion.4), channel_id=1, source_target_pairs={{2,0},{4,6},{3,1},{5,7},{10,8},{12,14},{11,9},{13,15},{18,16},{20,... | collective-permute-start | bytes 1572872 | tf_op jit(solution)/shard_map/ppermute | solution.py:212
  66.7 1.8 collective-permute-start.3
  68.5 0.7 fusion.1
  69.7 0.7 compare_and_fusion
  70.5 1.1 collective-permute-start.12
  71.6 5.3 %collective-permute-done.12 = f32[4,32,128]{2,1,0:T(8,128)S(1)} collective-permute-done((f32[4,32,128]{2,1,0:T(8,128)S(1)}, f32[4,32,128]{2,1,0:T(8,128)S(1)}, u32[]{:S(2)}, u32[]{:S(2)}) %collective-permute-start.12) | collective-permute-done | bytes 65568 | tf_op jit(solution)/shard_map/ppermute | solution.py:222
  77.0 17.3 %collective-permute-start.13 = (f32[2,4,32,128]{3,2,1,0:T(8,128)S(1)}, f32[2,4,32,128]{3,2,1,0:T(8,128)S(1)}, u32[]{:S(2)}, u32[]{:S(2)}) collective-permute-start(f32[2,4,32,128]{3,2,1,0:T(8,128)S(1)} %pad_maximum_fusion.6), channel_id=1, source_target_pairs={{0,1},{1,0},{2,3},{3,2},{4,5},{5,4},{6,7},{7,6},{8,9},{9,8},{10,11... | collective-permute-start | bytes 393224 | tf_op jit(solution)/shard_map/ppermute | solution.py:222
  94.2 4.2 %collective-permute-done.13 = f32[2,4,32,128]{3,2,1,0:T(8,128)S(1)} collective-permute-done((f32[2,4,32,128]{3,2,1,0:T(8,128)S(1)}, f32[2,4,32,128]{3,2,1,0:T(8,128)S(1)}, u32[]{:S(2)}, u32[]{:S(2)}) %collective-permute-start.13) | collective-permute-done | bytes 131104 | tf_op jit(solution)/shard_map/ppermute | solution.py:222
  98.5 0.7 pad_maximum_fusion.5
  99.2 1.3 collective-permute-start.6
  100.5 1.3 collective-permute-start.8
  101.8 0.7 dynamic-slice_bitcast_fusion
  102.5 1.3 collective-permute-start.10
  103.8 6.9 %collective-permute-done.6.refs_7_ = f32[24,4,32,128]{3,2,1,0:T(8,128)} collective-permute-done((f32[24,4,32,128]{3,2,1,0:T(8,128)}, f32[24,4,32,128]{3,2,1,0:T(8,128)}, u32[]{:S(2)}, u32[]{:S(2)}) %collective-permute-start.6) | collective-permute-done | bytes 1572896 | tf_op jit(solution)/shard_map/ppermute | solution.py:215
  110.8 1.5 collective-permute-start.9
  112.5 0.7 collective-permute-done.8.refs_8_
  113.2 11.5 %leaf_forward.2 = (f32[40,64,128]{2,1,0:T(8,128)S(1)}, bf16[24,384,128]{2,1,0:T(8,128)(2,1)S(1)}, bf16[24,384,128]{2,1,0:T(8,128)(2,1)S(1)}, f32[24,64,128]{2,1,0:T(8,128)S(1)}) custom-call(s32[105]{0:T(128)S(1)} %concatenate.31.refs_0_.meta, f32[32,4,32,128]{3,2,1,0:T(8,128)S(1)} %pad_maximum_fusion.refs_1_, ...), custom_call_target="tpu_custom_call" | custom-call | flops 4000000000 | bytes 8388608 | tf_op jit(solution)/shard_map/leaf_forward/pallas_call | solution.py:274
  124.7 1.3 collective-permute-start.11
  126.1 4.4 %collective-permute-done.11.refs_8_ = f32[8,4,32,128]{3,2,1,0:T(8,128)S(1)} collective-permute-done((f32[8,4,32,128]{3,2,1,0:T(8,128)}, f32[8,4,32,128]{3,2,1,0:T(8,128)S(1)}, u32[]{:S(2)}, u32[]{:S(2)}) %collective-permute-start.11) | collective-permute-done | bytes 524320 | tf_op jit(solution)/shard_map/ppermute | solution.py:215
  130.5 5.8 %leaf_forward.3 = (f32[40,64,128]{2,1,0:T(8,128)}, bf16[8,384,128]{2,1,0:T(8,128)(2,1)S(1)}, bf16[8,384,128]{2,1,0:T(8,128)(2,1)S(1)}, f32[8,64,128]{2,1,0:T(8,128)S(1)}, f32[8,5,8,128]{3,2,1,0:T(8,128)}) custom-call(s32[105]{0:T(128)S(1)} %concatenate.31.refs_0_.meta, f32[32,4,32,128]{3,2,1,0:T(8,128)S(1)} %pad_maximum_fusion.refs_1_, ...), custom_call_target="tpu_custom_call" | custom-call | flops 4000000000 | bytes 8388608 | tf_op jit(solution)/shard_map/leaf_forward/pallas_call | solution.py:274
  136.3 0.9 copy-done.8
  137.2 0.9 copy-done.10
  138.1 0.7 copy-done.12
  138.8 5.4 %all-to-all-start = ((f32[8,5,8,128]{3,2,1,0:T(8,128)}), f32[8,5,8,128]{3,2,1,0:T(8,128)S(1)}, u32[]{:S(2)}, u32[]{:S(2)}) async-start(f32[8,5,8,128]{3,2,1,0:T(8,128)} %get-tuple-element.49), calls=%async_computation | async-start | bytes 327680 | tf_op jit(solution)/shard_map/all_to_all | solution.py:307
  144.3 1.6 copy-done.1
  145.9 2.7 %top_prepare.1 = (bf16[8,384,128]{2,1,0:T(8,128)(2,1)S(1)}, bf16[8,384,128]{2,1,0:T(8,128)(2,1)S(1)}, bf16[8,128,128]{2,1,0:T(8,128)(2,1)S(1)}, bf16[8,128,128]{2,1,0:T(8,128)(2,1)S(1)}) custom-call(s32[4]{0:T(128)S(1)} %pad_add_fusion.places, f32[8,4,4,32,128]{4,3,2,1,0:T(8,128)S(1)} %bitcast.31), custom_call_target="tpu_custom_call" | custom-call | tf_op jit(solution)/shard_map/top_prepare/pallas_call | solution.py:295
  148.6 4.3 %all-to-all-done.incoming = f32[8,5,8,128]{3,2,1,0:T(8,128)S(1)} async-done(((f32[8,5,8,128]{3,2,1,0:T(8,128)}), f32[8,5,8,128]{3,2,1,0:T(8,128)S(1)}, u32[]{:S(2)}, u32[]{:S(2)}) %all-to-all-start) | async-done | bytes 163872 | tf_op jit(solution)/shard_map/all_to_all | solution.py:307
  152.9 2.7 %top_solve.1 = f32[8,5,8,128]{3,2,1,0:T(8,128)S(1)} custom-call(f32[8,5,8,128]{3,2,1,0:T(8,128)S(1)} %all-to-all-done.incoming, bf16[8,384,128]{2,1,0:T(8,128)(2,1)S(1)} %get-tuple-element.53.high, bf16[8,384,128]{2,1,0:T(8,128)(2,1)S(1)} %get-tuple-element.54.low, bf16[8,128,128]{2,1,0:T(8,128)(2,1)S(1)} %get-tuple-element.55.inverse_high, ...), custom_call_target="tpu_custom_call" | custom-call | tf_op jit(solution)/shard_map/top_solve/pallas_call | solution.py:308
  155.6 9.8 %all_to_all.10.state = f32[8,5,8,128]{3,2,1,0:T(8,128)S(1)} all-to-all(f32[8,5,8,128]{3,2,1,0:T(8,128)S(1)} %top_solve.1), channel_id=1, replica_groups=mesh['xy'=4,'core'=2,'zh'=2,'zl'=2] {'xy','zh'}, dimensions={0} | all-to-all | bytes 327680 | tf_op jit(solution)/shard_map/all_to_all | solution.py:316
  165.4 2.1 %leaf_backward.4 = (f32[8,64,128]{2,1,0:T(8,128)S(1)}, f32[40,64,128]{2,1,0:T(8,128)S(1)}) custom-call(s32[105]{0:T(128)S(1)} %concatenate.31.refs_0_.meta, bf16[8,384,128]{2,1,0:T(8,128)(2,1)S(1)} %copy-done.9, bf16[8,384,128]{2,1,0:T(8,128)(2,1)S(1)} %copy-done.11, f32[8,64,128]{2,1,0:T(8,128)S(1)} %copy-done.13, f32[8,5,8,128]{3,2,1,0:T(8,128)S(1)} %all_to_all.10.state), custom_call_target="tpu_custom_call" | custom-call | flops 4000000000 | bytes 8388608 | tf_op jit(solution)/shard_map/leaf_backward/pallas_call | solution.py:329
  167.6 2.8 %collective-permute-start.16 = (f32[8,64,128]{2,1,0:T(8,128)S(1)}, f32[8,64,128]{2,1,0:T(8,128)S(1)}, u32[]{:S(2)}, u32[]{:S(2)}) collective-permute-start(f32[8,64,128]{2,1,0:T(8,128)S(1)} %get-tuple-element.63), channel_id=1, source_target_pairs={{0,0},{2,4},{4,2},{6,6},{1,1},{3,5},{5,3},{7,7},{8,8},{10,12},{12,... | collective-permute-start | bytes 786440 | tf_op jit(solution)/shard_map/ppermute | solution.py:209
  170.4 2.1 %leaf_backward.5 = (f32[8,64,128]{2,1,0:T(8,128)S(1)}, f32[40,64,128]{2,1,0:T(8,128)S(1)}) custom-call(s32[105]{0:T(128)S(1)} %concatenate.31.refs_0_.meta, bf16[24,384,128]{2,1,0:T(8,128)(2,1)S(1)} %copy-done.3, bf16[24,384,128]{2,1,0:T(8,128)(2,1)S(1)} %copy-done.5, f32[24,64,128]{2,1,0:T(8,128)S(1)} %copy-done.7, f32[40,64,128]{2,1,0:T(8,128)S(1)} %get-tuple-element.57.state), custom_call_target="tpu_custom_call" | custom-call | flops 4000000000 | bytes 8388608 | tf_op jit(solution)/shard_map/leaf_backward/pallas_call | solution.py:329
  172.5 2.1 %leaf_backward.6 = (f32[8,64,128]{2,1,0:T(8,128)S(1)}, f32[40,64,128]{2,1,0:T(8,128)S(1)}) custom-call(s32[105]{0:T(128)S(1)} %concatenate.31.refs_0_.meta, bf16[24,384,128]{2,1,0:T(8,128)(2,1)S(1)} %copy-done.3, bf16[24,384,128]{2,1,0:T(8,128)(2,1)S(1)} %copy-done.5, f32[24,64,128]{2,1,0:T(8,128)S(1)} %copy-done.7, f32[40,64,128]{2,1,0:T(8,128)S(1)} %get-tuple-element.58.state), custom_call_target="tpu_custom_call" | custom-call | flops 4000000000 | bytes 8388608 | tf_op jit(solution)/shard_map/leaf_backward/pallas_call | solution.py:329
  174.8 3.8 %collective-permute-start.15 = (f32[17,64,128]{2,1,0:T(8,128)S(1)}, f32[17,64,128]{2,1,0:T(8,128)S(1)}, u32[]{:S(2)}, u32[]{:S(2)}) collective-permute-start(f32[17,64,128]{2,1,0:T(8,128)S(1)} %pad_maximum_fusion.3), channel_id=1, source_target_pairs={{0,0},{2,4},{4,2},{6,6},{1,1},{3,5},{5,3},{7,7},{8,8},{10,12},{12,... | collective-permute-start | bytes 1671176 | tf_op jit(solution)/shard_map/ppermute | solution.py:209
  178.6 3.2 %leaf_backward.7 = (f32[8,64,128]{2,1,0:T(8,128)S(1)}, f32[40,64,128]{2,1,0:T(8,128)}) custom-call(s32[105]{0:T(128)S(1)} %concatenate.31.refs_0_.meta, bf16[24,384,128]{2,1,0:T(8,128)(2,1)S(1)} %copy-done.3, bf16[24,384,128]{2,1,0:T(8,128)(2,1)S(1)} %copy-done.5, f32[24,64,128]{2,1,0:T(8,128)S(1)} %copy-done.7, f32[40,64,128]{2,1,0:T(8,128)S(1)} %get-tuple-element.59.state), custom_call_target="tpu_custom_call" | custom-call | flops 4000000000 | bytes 8388608 | tf_op jit(solution)/shard_map/leaf_backward/pallas_call | solution.py:329
  181.8 2.6 %collective-permute-start.14 = (f32[8,64,128]{2,1,0:T(8,128)S(1)}, f32[8,64,128]{2,1,0:T(8,128)S(1)}, u32[]{:S(2)}, u32[]{:S(2)}) collective-permute-start(f32[8,64,128]{2,1,0:T(8,128)S(1)} %get-tuple-element.60), channel_id=1, source_target_pairs={{0,0},{2,4},{4,2},{6,6},{1,1},{3,5},{5,3},{7,7},{8,8},{10,12},{12,... | collective-permute-start | bytes 786440 | tf_op jit(solution)/shard_map/ppermute | solution.py:209
  184.5 10.8 %collective-permute-done.15 = f32[17,64,128]{2,1,0:T(8,128)S(1)} collective-permute-done((f32[17,64,128]{2,1,0:T(8,128)S(1)}, f32[17,64,128]{2,1,0:T(8,128)S(1)}, u32[]{:S(2)}, u32[]{:S(2)}) %collective-permute-start.15) | collective-permute-done | bytes 557088 | tf_op jit(solution)/shard_map/ppermute | solution.py:209
  195.9 2.1 %collective-permute-done.14 = f32[8,64,128]{2,1,0:T(8,128)S(1)} collective-permute-done((f32[8,64,128]{2,1,0:T(8,128)S(1)}, f32[8,64,128]{2,1,0:T(8,128)S(1)}, u32[]{:S(2)}, u32[]{:S(2)}) %collective-permute-start.14) | collective-permute-done | bytes 262176 | tf_op jit(solution)/shard_map/ppermute | solution.py:209
  198.1 1.1 pad_maximum_fusion.2
  (68 shorter events, 1.9 us)
Async XLA Ops:
  7.2 62.0 %copy-start = (f32[8,1,32,128]{3,2,1,0:T(8,128)S(1)}, f32[8,1,32,128]{3,2,1,0:T(8,128)}, u32[]{:S(2)}) copy-start(f32[8,1,32,128]{3,2,1,0:T(8,128)} %param.16) | copy-start | bytes 393220
  7.2 137.1 %all-gather.3.cloned.1.call-start = ((), (), s32[]{:S(2)}) async-start(), calls=%async_computation.2 | async-start | bytes 2359296 | tf_op jit(solution)/shard_map/all_gather | solution.py:246
  9.0 2.2 %copy-start.14 = (f32[32,32,128]{2,1,0:T(8,128)S(1)}, f32[32,32,128]{2,1,0:T(8,128)}, u32[]{:S(2)}) copy-start(f32[32,32,128]{2,1,0:T(8,128)} %param.14) | copy-start | bytes 1572868
  9.0 2.2 %slice-start = ((f32[32,3,32,128]{3,2,1,0:T(8,128)}), f32[24,3,32,128]{3,2,1,0:T(8,128)S(1)}, s32[]{:S(2)}) async-start(f32[32,3,32,128]{3,2,1,0:T(8,128)} %param.13), calls=%async_computation.3 | async-start | bytes 2359296 | tf_op jit(solution)/shard_map/slice | solution.py:232
  9.0 12.2 %collective-permute-start.1 = (f32[32,4,32,128]{3,2,1,0:T(8,128)S(1)}, f32[32,4,32,128]{3,2,1,0:T(8,128)}, u32[]{:S(2)}, u32[]{:S(2)}) collective-permute-start(f32[32,4,32,128]{3,2,1,0:T(8,128)S(1)} %pad_maximum_fusion.refs_1_), channel_id=1, source_target_pairs={{0,1},{1,0},{6,7},{7,6},{8,9},{9,8},{14,15},{15,14},{16,17},{17,16... | collective-permute-start | bytes 6291464 | tf_op jit(solution)/shard_map/ppermute | solution.py:218
  11.3 11.3 %copy-start.18 = (s32[32,3]{0,1:T(4,128)S(1)}, s32[32,3]{0,1:T(4,128)}, u32[]{:S(2)}) copy-start(s32[32,3]{0,1:T(4,128)} %param.15) | copy-start | bytes 1156
  11.3 11.3 %copy-start.15 = (f32[32,64,128]{2,1,0:T(8,128)S(1)}, f32[32,64,128]{2,1,0:T(8,128)}, u32[]{:S(2)}) copy-start(f32[32,64,128]{2,1,0:T(8,128)} %param.11) | copy-start | bytes 3145732
  11.3 11.3 %copy-start.16 = (f32[1,64,128]{2,1,0:T(8,128)S(1)}, f32[1,64,128]{2,1,0:T(8,128)}, u32[]{:S(2)}) copy-start(f32[1,64,128]{2,1,0:T(8,128)} %param.12) | copy-start | bytes 98308
  12.6 54.1 %collective-permute-start.2 = (f32[24,4,32,128]{3,2,1,0:T(8,128)}, f32[24,4,32,128]{3,2,1,0:T(8,128)}, u32[]{:S(2)}, u32[]{:S(2)}) collective-permute-start(f32[24,4,32,128]{3,2,1,0:T(8,128)} %pad_maximum_fusion.1), channel_id=1, source_target_pairs={{2,0},{4,6},{3,1},{5,7},{10,8},{12,14},{11,9},{13,15},{18,16},{20,... | collective-permute-start | bytes 4718600 | tf_op jit(solution)/shard_map/ppermute | solution.py:212
  20.0 50.5 %collective-permute-start.4 = (f32[32,4,32,128]{3,2,1,0:T(8,128)S(1)}, f32[32,4,32,128]{3,2,1,0:T(8,128)}, u32[]{:S(2)}, u32[]{:S(2)}) collective-permute-start(f32[32,4,32,128]{3,2,1,0:T(8,128)S(1)} %pad_maximum_fusion.refs_1_), channel_id=1, source_target_pairs={{0,4},{6,2},{1,5},{7,3},{8,12},{14,10},{9,13},{15,11},{16,20},{22,... | collective-permute-start | bytes 6291464 | tf_op jit(solution)/shard_map/ppermute | solution.py:215
  21.3 49.3 %collective-permute-start.5 = (f32[32,4,32,128]{3,2,1,0:T(8,128)}, f32[32,4,32,128]{3,2,1,0:T(8,128)}, u32[]{:S(2)}, u32[]{:S(2)}) collective-permute-start(f32[32,4,32,128]{3,2,1,0:T(8,128)} %collective-permute-done.1.refs_2_), channel_id=1, source_target_pairs={{0,4},{6,2},{1,5},{7,3},{8,12},{14,10},{9,13},{15,11},{16,20},{22,... | collective-permute-start | bytes 6291464 | tf_op jit(solution)/shard_map/ppermute | solution.py:215
  22.6 4.3 %slice-start.1 = ((f32[32,3,32,128]{3,2,1,0:T(8,128)}), f32[8,3,32,128]{3,2,1,0:T(8,128)S(1)}, s32[]{:S(2)}) async-start(f32[32,3,32,128]{3,2,1,0:T(8,128)} %param.13), calls=%async_computation.4 | async-start | bytes 786432 | tf_op jit(solution)/shard_map/slice | solution.py:232
  23.7 46.8 %copy-start.17 = (f32[1,32,128]{2,1,0:T(8,128)S(1)}, f32[1,32,128]{2,1,0:T(8,128)}, u32[]{:S(2)}) copy-start(f32[1,32,128]{2,1,0:T(8,128)} %param.17) | copy-start | bytes 49156
  23.7 75.5 %collective-permute-start = (f32[2120,128]{1,0:T(8,128)}, f32[2120,128]{1,0:T(8,128)S(1)}, u32[]{:S(2)}, u32[]{:S(2)}) collective-permute-start(f32[2120,128]{1,0:T(8,128)} %select_maximum_fusion), channel_id=1, source_target_pairs={{0,0},{2,4},{4,2},{6,6},{1,1},{3,5},{5,3},{7,7},{8,8},{10,12},{12,... | collective-permute-start | bytes 3256328 | tf_op jit(solution)/shard_map/ppermute | solution.py:209
  27.8 71.4 %collective-permute-start.7 = (f32[8,4,32,128]{3,2,1,0:T(8,128)}, f32[8,4,32,128]{3,2,1,0:T(8,128)}, u32[]{:S(2)}, u32[]{:S(2)}) collective-permute-start(f32[8,4,32,128]{3,2,1,0:T(8,128)} %pad_maximum_fusion.4), channel_id=1, source_target_pairs={{2,0},{4,6},{3,1},{5,7},{10,8},{12,14},{11,9},{13,15},{18,16},{20,... | collective-permute-start | bytes 1572872 | tf_op jit(solution)/shard_map/ppermute | solution.py:212
  66.7 33.9 %collective-permute-start.3 = (f32[24,4,32,128]{3,2,1,0:T(8,128)}, f32[24,4,32,128]{3,2,1,0:T(8,128)}, u32[]{:S(2)}, u32[]{:S(2)}) collective-permute-start(f32[24,4,32,128]{3,2,1,0:T(8,128)} %collective-permute-done.2.refs_3_), channel_id=1, source_target_pairs={{0,1},{1,0},{6,7},{7,6},{8,9},{9,8},{14,15},{15,14},{16,17},{17,16... | collective-permute-start | bytes 4718600 | tf_op jit(solution)/shard_map/ppermute | solution.py:218
  70.5 6.4 %collective-permute-start.12 = (f32[4,32,128]{2,1,0:T(8,128)S(1)}, f32[4,32,128]{2,1,0:T(8,128)S(1)}, u32[]{:S(2)}, u32[]{:S(2)}) collective-permute-start(f32[4,32,128]{2,1,0:T(8,128)S(1)} %pad_maximum_fusion.7), channel_id=1, source_target_pairs={{0,2},{2,0},{1,3},{3,1},{4,6},{6,4},{5,7},{7,5},{8,10},{10,8},{9,1... | collective-permute-start | bytes 196616 | tf_op jit(solution)/shard_map/ppermute | solution.py:222
  77.0 21.5 %collective-permute-start.13 = (f32[2,4,32,128]{3,2,1,0:T(8,128)S(1)}, f32[2,4,32,128]{3,2,1,0:T(8,128)S(1)}, u32[]{:S(2)}, u32[]{:S(2)}) collective-permute-start(f32[2,4,32,128]{3,2,1,0:T(8,128)S(1)} %pad_maximum_fusion.6), channel_id=1, source_target_pairs={{0,1},{1,0},{2,3},{3,2},{4,5},{5,4},{6,7},{7,6},{8,9},{9,8},{10,11... | collective-permute-start | bytes 393224 | tf_op jit(solution)/shard_map/ppermute | solution.py:222
  99.2 11.6 %collective-permute-start.6 = (f32[24,4,32,128]{3,2,1,0:T(8,128)}, f32[24,4,32,128]{3,2,1,0:T(8,128)}, u32[]{:S(2)}, u32[]{:S(2)}) collective-permute-start(f32[24,4,32,128]{3,2,1,0:T(8,128)} %collective-permute-done.2.refs_3_), channel_id=1, source_target_pairs={{0,4},{6,2},{1,5},{7,3},{8,12},{14,10},{9,13},{15,11},{16,20},{22,... | collective-permute-start | bytes 4718600 | tf_op jit(solution)/shard_map/ppermute | solution.py:215
  100.5 12.7 %collective-permute-start.8 = (f32[24,4,32,128]{3,2,1,0:T(8,128)}, f32[24,4,32,128]{3,2,1,0:T(8,128)}, u32[]{:S(2)}, u32[]{:S(2)}) collective-permute-start(f32[24,4,32,128]{3,2,1,0:T(8,128)} %collective-permute-done.3.refs_4_), channel_id=1, source_target_pairs={{0,4},{6,2},{1,5},{7,3},{8,12},{14,10},{9,13},{15,11},{16,20},{22,... | collective-permute-start | bytes 4718600 | tf_op jit(solution)/shard_map/ppermute | solution.py:215
  102.5 23.5 %collective-permute-start.10 = (f32[8,4,32,128]{3,2,1,0:T(8,128)}, f32[8,4,32,128]{3,2,1,0:T(8,128)}, u32[]{:S(2)}, u32[]{:S(2)}) collective-permute-start(f32[8,4,32,128]{3,2,1,0:T(8,128)} %collective-permute-done.7.refs_3_), channel_id=1, source_target_pairs={{0,4},{6,2},{1,5},{7,3},{8,12},{14,10},{9,13},{15,11},{16,20},{22,... | collective-permute-start | bytes 1572872 | tf_op jit(solution)/shard_map/ppermute | solution.py:215
  110.8 14.0 %collective-permute-start.9 = (f32[8,4,32,128]{3,2,1,0:T(8,128)}, f32[8,4,32,128]{3,2,1,0:T(8,128)}, u32[]{:S(2)}, u32[]{:S(2)}) collective-permute-start(f32[8,4,32,128]{3,2,1,0:T(8,128)} %collective-permute-done.7.refs_3_), channel_id=1, source_target_pairs={{0,1},{1,0},{6,7},{7,6},{8,9},{9,8},{14,15},{15,14},{16,17},{17,16... | collective-permute-start | bytes 1572872 | tf_op jit(solution)/shard_map/ppermute | solution.py:218
  124.7 11.6 %copy-start.2 = (bf16[24,384,128]{2,1,0:T(8,128)(2,1)}, bf16[24,384,128]{2,1,0:T(8,128)(2,1)S(1)}, u32[]{:S(2)}) copy-start(bf16[24,384,128]{2,1,0:T(8,128)(2,1)S(1)} %get-tuple-element.40.high) | copy-start | bytes 7077892
  124.7 11.6 %copy-start.4 = (bf16[24,384,128]{2,1,0:T(8,128)(2,1)}, bf16[24,384,128]{2,1,0:T(8,128)(2,1)S(1)}, u32[]{:S(2)}) copy-start(bf16[24,384,128]{2,1,0:T(8,128)(2,1)S(1)} %get-tuple-element.41.low) | copy-start | bytes 7077892
  124.7 11.6 %copy-start.6 = (f32[24,64,128]{2,1,0:T(8,128)}, f32[24,64,128]{2,1,0:T(8,128)S(1)}, u32[]{:S(2)}) copy-start(f32[24,64,128]{2,1,0:T(8,128)S(1)} %get-tuple-element.42.scaled) | copy-start | bytes 2359300
  124.7 5.7 %collective-permute-start.11 = (f32[8,4,32,128]{3,2,1,0:T(8,128)}, f32[8,4,32,128]{3,2,1,0:T(8,128)S(1)}, u32[]{:S(2)}, u32[]{:S(2)}) collective-permute-start(f32[8,4,32,128]{3,2,1,0:T(8,128)} %collective-permute-done.9.refs_4_), channel_id=1, source_target_pairs={{0,4},{6,2},{1,5},{7,3},{8,12},{14,10},{9,13},{15,11},{16,20},{22,... | collective-permute-start | bytes 1572872 | tf_op jit(solution)/shard_map/ppermute | solution.py:215
  136.3 0.9 copy-start.8
  137.2 0.9 copy-start.10
  138.1 0.7 copy-start.12
  138.8 14.1 %all-to-all-start = ((f32[8,5,8,128]{3,2,1,0:T(8,128)}), f32[8,5,8,128]{3,2,1,0:T(8,128)S(1)}, u32[]{:S(2)}, u32[]{:S(2)}) async-start(f32[8,5,8,128]{3,2,1,0:T(8,128)} %get-tuple-element.49), calls=%async_computation | async-start | bytes 327680 | tf_op jit(solution)/shard_map/all_to_all | solution.py:307
  144.3 1.6 copy-start.1
  152.9 12.5 %copy-start.9 = (bf16[8,384,128]{2,1,0:T(8,128)(2,1)S(1)}, bf16[8,384,128]{2,1,0:T(8,128)(2,1)}, u32[]{:S(2)}) copy-start(bf16[8,384,128]{2,1,0:T(8,128)(2,1)} %copy-done.8) | copy-start | bytes 2359300
  152.9 12.5 %copy-start.11 = (bf16[8,384,128]{2,1,0:T(8,128)(2,1)S(1)}, bf16[8,384,128]{2,1,0:T(8,128)(2,1)}, u32[]{:S(2)}) copy-start(bf16[8,384,128]{2,1,0:T(8,128)(2,1)} %copy-done.10) | copy-start | bytes 2359300
  152.9 12.5 %copy-start.13 = (f32[8,64,128]{2,1,0:T(8,128)S(1)}, f32[8,64,128]{2,1,0:T(8,128)}, u32[]{:S(2)}) copy-start(f32[8,64,128]{2,1,0:T(8,128)} %copy-done.12) | copy-start | bytes 786436
  165.4 5.0 %copy-start.3 = (bf16[24,384,128]{2,1,0:T(8,128)(2,1)S(1)}, bf16[24,384,128]{2,1,0:T(8,128)(2,1)}, u32[]{:S(2)}) copy-start(bf16[24,384,128]{2,1,0:T(8,128)(2,1)} %copy-done.2) | copy-start | bytes 7077892
  165.4 5.0 %copy-start.5 = (bf16[24,384,128]{2,1,0:T(8,128)(2,1)S(1)}, bf16[24,384,128]{2,1,0:T(8,128)(2,1)}, u32[]{:S(2)}) copy-start(bf16[24,384,128]{2,1,0:T(8,128)(2,1)} %copy-done.4) | copy-start | bytes 7077892
  165.4 5.0 %copy-start.7 = (f32[24,64,128]{2,1,0:T(8,128)S(1)}, f32[24,64,128]{2,1,0:T(8,128)}, u32[]{:S(2)}) copy-start(f32[24,64,128]{2,1,0:T(8,128)} %copy-done.6) | copy-start | bytes 2359300
  167.6 28.4 %collective-permute-start.16 = (f32[8,64,128]{2,1,0:T(8,128)S(1)}, f32[8,64,128]{2,1,0:T(8,128)S(1)}, u32[]{:S(2)}, u32[]{:S(2)}) collective-permute-start(f32[8,64,128]{2,1,0:T(8,128)S(1)} %get-tuple-element.63), channel_id=1, source_target_pairs={{0,0},{2,4},{4,2},{6,6},{1,1},{3,5},{5,3},{7,7},{8,8},{10,12},{12,... | collective-permute-start | bytes 786440 | tf_op jit(solution)/shard_map/ppermute | solution.py:209
  174.8 20.5 %collective-permute-start.15 = (f32[17,64,128]{2,1,0:T(8,128)S(1)}, f32[17,64,128]{2,1,0:T(8,128)S(1)}, u32[]{:S(2)}, u32[]{:S(2)}) collective-permute-start(f32[17,64,128]{2,1,0:T(8,128)S(1)} %pad_maximum_fusion.3), channel_id=1, source_target_pairs={{0,0},{2,4},{4,2},{6,6},{1,1},{3,5},{5,3},{7,7},{8,8},{10,12},{12,... | collective-permute-start | bytes 1671176 | tf_op jit(solution)/shard_map/ppermute | solution.py:209
  181.8 16.3 %collective-permute-start.14 = (f32[8,64,128]{2,1,0:T(8,128)S(1)}, f32[8,64,128]{2,1,0:T(8,128)S(1)}, u32[]{:S(2)}, u32[]{:S(2)}) collective-permute-start(f32[8,64,128]{2,1,0:T(8,128)S(1)} %get-tuple-element.60), channel_id=1, source_target_pairs={{0,0},{2,4},{4,2},{6,6},{1,1},{3,5},{5,3},{7,7},{8,8},{10,12},{12,... | collective-permute-start | bytes 786440 | tf_op jit(solution)/shard_map/ppermute | solution.py:209
Sparse Core Ops, SparseCore 0:
  99.3 34.5 all-gather.2

commit v6 on v4

--- a/solution.py
+++ b/solution.py
@@ -262,9 +262,10 @@
         chunk = jax.ShapeDtypeStruct((steps, columns, wide), f32)
         shapes = [vectors, merged, merged, chunk]
         if k == 0:
-            passed = (early[2], to_trader(after(far[-1], across[k])))
+            last_far = to_trader(far[-1])
+            passed = (early[2], to_trader(after(last_far, across[k])))
         else:
-            passed = (to_trader(far[k]), to_trader(after(state, across[k])))
+            passed = (last_far, to_trader(after(state, across[k])))
         specs = [SMEM] + [pl.BlockSpec(memory_space=pl.ANY)] * 8 + [
             pl.BlockSpec((steps * columns, wide), functools.partial(lambda k, i: (k, 0), base // steps)),
             pl.BlockSpec((columns, wide), lambda i: (leafs, 0)),
@@ -339,7 +340,7 @@
         )(meta, *factors[held], state)
     late = swap(found[-1])
     middle = swap(jnp.concatenate(found[1:-1] + [own_top], axis=0))
-    first = swap(after(late, found[0]))
+    first = swap(found[0])
     leaf_solution = jnp.concatenate([first, middle[:-1], late], axis=0)
     return (leaf_solution, middle[-1:])
 

time: 203 us -> 202 us (level)
    ppermute x4, waiting for transfers between devices: 16.6 us -> 13.9 us  [swap(): return lax.ppermute(value, ('core', 'zh'), [(0, 0), (1, 2), (2, 1), (3, 3)])]
    all_to_all x1, waiting for transfers between devices: 1.82 us -> 4.15 us  [local(): lax.all_to_all(results[4], ('xy', 'zh'), split_axis=0, concat_axis=0, til...]
    unnamed x34 -> x38, local copies, waits for them, and re-layouts: 4.5 us -> 5.29 us
  transfers between devices with their start and end apart: 19 -> 19, of which waited for: 10 -> 11; matrix products, arithmetic and copies ran while one was open for 4% -> 4% of each run, Pallas kernels for 12% -> 12%
where the time goes in v6:
time: 202 us; the launch traced here: 201 us
  waiting for transfers between devices  72.3 us (36%)
  starting transfers between devices  54.6 us (27%)
  Pallas kernels  32.3 us (16%)
  between operations  14.4 us (7%)
  local copies, waits for them, and re-layouts  9.44 us (5%)
  other arithmetic  9.08 us (4%)
  blocking collectives  8.6 us (4%)
    ppermute x2, waiting for transfers between devices, to_keeper(): return lax.ppermute(value, ('core', 'zh'), [(1, 0), (2, 3)])  40 us
    ppermute x2, starting transfers between devices, to_keeper(): return lax.ppermute(value, ('core', 'zh'), [(1, 0), (2, 3)])  18 us
    pallas_call x2, Pallas kernels, local(): pl.pallas_call(functools.partial(forward_kernel, base, leafs, k == 0, las...  17.2 us
    ppermute x4, starting transfers between devices, swap(): return lax.ppermute(value, ('core', 'zh'), [(0, 0), (1, 2), (2, 1), (3, 3)])  15.5 us
    ppermute x4, waiting for transfers between devices, swap(): return lax.ppermute(value, ('core', 'zh'), [(0, 0), (1, 2), (2, 1), (3, 3)])  13.9 us
    ppermute x6, waiting for transfers between devices, to_trader(): return lax.ppermute(value, ('core', 'zh'), [(0, 2), (3, 1)])  13.9 us
    pallas_call x4, Pallas kernels, local(): pl.pallas_call(functools.partial(backward_kernel, k * turn, k == TURNS -...  9.63 us
    all_to_all x1, blocking collectives, local(): lax.all_to_all(outgoing, ('xy', 'zh'), split_axis=0, concat_axis=0, tiled...  8.6 us
  transfers between devices with their start and end apart: 19, of which 11 were waited for; matrix products, arithmetic and copies ran while one was open for 4% of the time, Pallas kernels for 12%

profile of v6, /device:TPU:1, one launch (start us, length us, event | category | flops | bytes accessed | tf_op | source)
XLA Modules:
  0.0 200.7 jit_solution(7531734772261892450)
XLA Ops:
  7.2 0.8 fusion.1
  9.4 0.7 fusion.2
  10.1 3.2 %collective-permute-start = (f32[4,32,128]{2,1,0:T(8,128)S(1)}, f32[4,32,128]{2,1,0:T(8,128)S(1)}, u32[]{:S(2)}, u32[]{:S(2)}) collective-permute-start(f32[4,32,128]{2,1,0:T(8,128)S(1)} %get-tuple-element.71), channel_id=1, source_target_pairs={{0,2},{2,0},{1,3},{3,1},{4,6},{6,4},{5,7},{7,5},{8,10},{10,8},{9,1... | collective-permute-start | bytes 196616 | tf_op jit(solution)/shard_map/ppermute | solution.py:222
  13.3 1.0 slice_bitcast_fusion
  14.4 0.9 slice_bitcast_fusion.1
  16.0 1.8 select_maximum_fusion
  18.1 1.4 collective-permute-start.1
  19.4 1.3 pad_maximum_fusion.1
  20.7 0.8 pad_maximum_fusion.4
  22.7 4.7 %collective-permute-start.4 = (f32[24,4,32,128]{3,2,1,0:T(8,128)}, f32[24,4,32,128]{3,2,1,0:T(8,128)}, u32[]{:S(2)}, u32[]{:S(2)}) collective-permute-start(f32[24,4,32,128]{3,2,1,0:T(8,128)} %pad_maximum_fusion.1), channel_id=1, source_target_pairs={{2,0},{4,6},{3,1},{5,7},{10,8},{12,14},{11,9},{13,15},{18,16},{20,... | collective-permute-start | bytes 4718600 | tf_op jit(solution)/shard_map/ppermute | solution.py:212
  27.4 2.1 %collective-permute-start.3 = (f32[32,4,32,128]{3,2,1,0:T(8,128)S(1)}, f32[32,4,32,128]{3,2,1,0:T(8,128)}, u32[]{:S(2)}, u32[]{:S(2)}) collective-permute-start(f32[32,4,32,128]{3,2,1,0:T(8,128)S(1)} %pad_maximum_fusion.refs_1_), channel_id=1, source_target_pairs={{0,1},{1,0},{6,7},{7,6},{8,9},{9,8},{14,15},{15,14},{16,17},{17,16... | collective-permute-start | bytes 6291464 | tf_op jit(solution)/shard_map/ppermute | solution.py:218
  29.5 4.9 %collective-permute-start.2 = (f32[2120,128]{1,0:T(8,128)}, f32[2120,128]{1,0:T(8,128)S(1)}, u32[]{:S(2)}, u32[]{:S(2)}) collective-permute-start(f32[2120,128]{1,0:T(8,128)} %select_maximum_fusion), channel_id=1, source_target_pairs={{0,0},{2,4},{4,2},{6,6},{1,1},{3,5},{5,3},{7,7},{8,8},{10,12},{12,... | collective-permute-start | bytes 3256328 | tf_op jit(solution)/shard_map/ppermute | solution.py:209
  34.4 23.1 %collective-permute-done.4.refs_3_ = f32[24,4,32,128]{3,2,1,0:T(8,128)} collective-permute-done((f32[24,4,32,128]{3,2,1,0:T(8,128)}, f32[24,4,32,128]{3,2,1,0:T(8,128)}, u32[]{:S(2)}, u32[]{:S(2)}) %collective-permute-start.4) | collective-permute-done | bytes 1572896 | tf_op jit(solution)/shard_map/ppermute | solution.py:212
  57.5 1.8 collective-permute-start.5
  59.3 13.3 %collective-permute-start.9 = (f32[8,4,32,128]{3,2,1,0:T(8,128)}, f32[8,4,32,128]{3,2,1,0:T(8,128)}, u32[]{:S(2)}, u32[]{:S(2)}) collective-permute-start(f32[8,4,32,128]{3,2,1,0:T(8,128)} %pad_maximum_fusion.4), channel_id=1, source_target_pairs={{2,0},{4,6},{3,1},{5,7},{10,8},{12,14},{11,9},{13,15},{18,16},{20,... | collective-permute-start | bytes 1572872 | tf_op jit(solution)/shard_map/ppermute | solution.py:212
  72.5 1.3 collective-permute-start.6
  73.8 1.3 collective-permute-start.7
  75.1 16.8 %collective-permute-done.9.refs_3_ = f32[8,4,32,128]{3,2,1,0:T(8,128)} collective-permute-done((f32[8,4,32,128]{3,2,1,0:T(8,128)}, f32[8,4,32,128]{3,2,1,0:T(8,128)}, u32[]{:S(2)}, u32[]{:S(2)}) %collective-permute-start.9) | collective-permute-done | bytes 524320 | tf_op jit(solution)/shard_map/ppermute | solution.py:212
  92.0 1.3 collective-permute-start.10
  93.3 1.3 collective-permute-start.8
  94.6 6.9 %collective-permute-done.10.refs_7_ = f32[8,4,32,128]{3,2,1,0:T(8,128)S(1)} collective-permute-done((f32[8,4,32,128]{3,2,1,0:T(8,128)}, f32[8,4,32,128]{3,2,1,0:T(8,128)S(1)}, u32[]{:S(2)}, u32[]{:S(2)}) %collective-permute-start.10) | collective-permute-done | bytes 524320 | tf_op jit(solution)/shard_map/ppermute | solution.py:215
  101.5 0.8 copy-done.8
  102.3 1.3 collective-permute-start.11
  104.4 1.5 collective-permute-start.12
  106.2 3.2 %collective-permute-done.11.refs_8_ = f32[24,4,32,128]{3,2,1,0:T(8,128)} collective-permute-done((f32[24,4,32,128]{3,2,1,0:T(8,128)}, f32[24,4,32,128]{3,2,1,0:T(8,128)}, u32[]{:S(2)}, u32[]{:S(2)}) %collective-permute-start.11) | collective-permute-done | bytes 1572896 | tf_op jit(solution)/shard_map/ppermute | solution.py:215
  109.4 11.4 %leaf_forward.2 = (f32[40,64,128]{2,1,0:T(8,128)S(1)}, bf16[24,384,128]{2,1,0:T(8,128)(2,1)S(1)}, bf16[24,384,128]{2,1,0:T(8,128)(2,1)S(1)}, f32[24,64,128]{2,1,0:T(8,128)S(1)}) custom-call(s32[105]{0:T(128)S(1)} %concatenate.36.refs_0_.meta, f32[32,4,32,128]{3,2,1,0:T(8,128)S(1)} %pad_maximum_fusion.refs_1_, ...), custom_call_target="tpu_custom_call" | custom-call | flops 4000000000 | bytes 8388608 | tf_op jit(solution)/shard_map/leaf_forward/pallas_call | solution.py:276
  120.9 1.3 collective-permute-start.13
  122.2 3.7 %collective-permute-done.13.refs_8_ = f32[8,4,32,128]{3,2,1,0:T(8,128)S(1)} collective-permute-done((f32[8,4,32,128]{3,2,1,0:T(8,128)}, f32[8,4,32,128]{3,2,1,0:T(8,128)S(1)}, u32[]{:S(2)}, u32[]{:S(2)}) %collective-permute-start.13) | collective-permute-done | bytes 524320 | tf_op jit(solution)/shard_map/ppermute | solution.py:215
  125.8 5.8 %leaf_forward.3 = (f32[40,64,128]{2,1,0:T(8,128)}, bf16[8,384,128]{2,1,0:T(8,128)(2,1)S(1)}, bf16[8,384,128]{2,1,0:T(8,128)(2,1)S(1)}, f32[8,64,128]{2,1,0:T(8,128)S(1)}, f32[8,5,8,128]{3,2,1,0:T(8,128)}) custom-call(s32[105]{0:T(128)S(1)} %concatenate.36.refs_0_.meta, f32[32,4,32,128]{3,2,1,0:T(8,128)S(1)} %pad_maximum_fusion.refs_1_, ...), custom_call_target="tpu_custom_call" | custom-call | flops 4000000000 | bytes 8388608 | tf_op jit(solution)/shard_map/leaf_forward/pallas_call | solution.py:276
  131.6 0.9 copy-done.10
  132.5 0.9 copy-done.12
  134.1 3.4 %all-to-all-start = ((f32[8,5,8,128]{3,2,1,0:T(8,128)}), f32[8,5,8,128]{3,2,1,0:T(8,128)S(1)}, u32[]{:S(2)}, u32[]{:S(2)}) async-start(f32[8,5,8,128]{3,2,1,0:T(8,128)} %get-tuple-element.56), calls=%async_computation | async-start | bytes 327680 | tf_op jit(solution)/shard_map/all_to_all | solution.py:309
  137.6 1.6 copy-done.1
  139.2 2.7 %top_prepare.1 = (bf16[8,384,128]{2,1,0:T(8,128)(2,1)S(1)}, bf16[8,384,128]{2,1,0:T(8,128)(2,1)S(1)}, bf16[8,128,128]{2,1,0:T(8,128)(2,1)S(1)}, bf16[8,128,128]{2,1,0:T(8,128)(2,1)S(1)}) custom-call(s32[4]{0:T(128)S(1)} %pad_add_fusion.places, f32[8,4,4,32,128]{4,3,2,1,0:T(8,128)S(1)} %bitcast.32), custom_call_target="tpu_custom_call" | custom-call | tf_op jit(solution)/shard_map/top_prepare/pallas_call | solution.py:297
  141.9 4.1 %all-to-all-done.incoming = f32[8,5,8,128]{3,2,1,0:T(8,128)S(1)} async-done(((f32[8,5,8,128]{3,2,1,0:T(8,128)}), f32[8,5,8,128]{3,2,1,0:T(8,128)S(1)}, u32[]{:S(2)}, u32[]{:S(2)}) %all-to-all-start) | async-done | bytes 163872 | tf_op jit(solution)/shard_map/all_to_all | solution.py:309
  146.1 2.7 %top_solve.1 = f32[8,5,8,128]{3,2,1,0:T(8,128)S(1)} custom-call(f32[8,5,8,128]{3,2,1,0:T(8,128)S(1)} %all-to-all-done.incoming, bf16[8,384,128]{2,1,0:T(8,128)(2,1)S(1)} %get-tuple-element.59.high, bf16[8,384,128]{2,1,0:T(8,128)(2,1)S(1)} %get-tuple-element.60.low, bf16[8,128,128]{2,1,0:T(8,128)(2,1)S(1)} %get-tuple-element.61.inverse_high, ...), custom_call_target="tpu_custom_call" | custom-call | tf_op jit(solution)/shard_map/top_solve/pallas_call | solution.py:310
  148.8 8.6 %all_to_all.10.state = f32[8,5,8,128]{3,2,1,0:T(8,128)S(1)} all-to-all(f32[8,5,8,128]{3,2,1,0:T(8,128)S(1)} %top_solve.1), channel_id=1, replica_groups=mesh['xy'=4,'core'=2,'zh'=2,'zl'=2] {'xy','zh'}, dimensions={0} | all-to-all | bytes 327680 | tf_op jit(solution)/shard_map/all_to_all | solution.py:318
  157.4 2.1 %leaf_backward.4 = (f32[8,64,128]{2,1,0:T(8,128)S(1)}, f32[40,64,128]{2,1,0:T(8,128)S(1)}) custom-call(s32[105]{0:T(128)S(1)} %concatenate.36.refs_0_.meta, bf16[8,384,128]{2,1,0:T(8,128)(2,1)S(1)} %copy-done.11, bf16[8,384,128]{2,1,0:T(8,128)(2,1)S(1)} %copy-done.13, f32[8,64,128]{2,1,0:T(8,128)S(1)} %copy-done.15, f32[8,5,8,128]{3,2,1,0:T(8,128)S(1)} %all_to_all.10.state), custom_call_target="tpu_custom_call" | custom-call | flops 4000000000 | bytes 8388608 | tf_op jit(solution)/shard_map/leaf_backward/pallas_call | solution.py:331
  160.0 2.1 %leaf_backward.5 = (f32[8,64,128]{2,1,0:T(8,128)S(1)}, f32[40,64,128]{2,1,0:T(8,128)S(1)}) custom-call(s32[105]{0:T(128)S(1)} %concatenate.36.refs_0_.meta, bf16[24,384,128]{2,1,0:T(8,128)(2,1)S(1)} %copy-done.3, bf16[24,384,128]{2,1,0:T(8,128)(2,1)S(1)} %copy-done.5, f32[24,64,128]{2,1,0:T(8,128)S(1)} %copy-done.7, f32[40,64,128]{2,1,0:T(8,128)S(1)} %get-tuple-element.63.state), custom_call_target="tpu_custom_call" | custom-call | flops 4000000000 | bytes 8388608 | tf_op jit(solution)/shard_map/leaf_backward/pallas_call | solution.py:331
  162.1 2.1 %leaf_backward.6 = (f32[8,64,128]{2,1,0:T(8,128)S(1)}, f32[40,64,128]{2,1,0:T(8,128)S(1)}) custom-call(s32[105]{0:T(128)S(1)} %concatenate.36.refs_0_.meta, bf16[24,384,128]{2,1,0:T(8,128)(2,1)S(1)} %copy-done.3, bf16[24,384,128]{2,1,0:T(8,128)(2,1)S(1)} %copy-done.5, f32[24,64,128]{2,1,0:T(8,128)S(1)} %copy-done.7, f32[40,64,128]{2,1,0:T(8,128)S(1)} %get-tuple-element.64.state), custom_call_target="tpu_custom_call" | custom-call | flops 4000000000 | bytes 8388608 | tf_op jit(solution)/shard_map/leaf_backward/pallas_call | solution.py:331
  164.3 4.2 %collective-permute-start.15 = (f32[17,64,128]{2,1,0:T(8,128)S(1)}, f32[17,64,128]{2,1,0:T(8,128)S(1)}, u32[]{:S(2)}, u32[]{:S(2)}) collective-permute-start(f32[17,64,128]{2,1,0:T(8,128)S(1)} %pad_maximum_fusion.3), channel_id=1, source_target_pairs={{0,0},{2,4},{4,2},{6,6},{1,1},{3,5},{5,3},{7,7},{8,8},{10,12},{12,... | collective-permute-start | bytes 1671176 | tf_op jit(solution)/shard_map/ppermute | solution.py:209
  168.5 3.2 %leaf_backward.7 = (f32[8,64,128]{2,1,0:T(8,128)S(1)}, f32[40,64,128]{2,1,0:T(8,128)}) custom-call(s32[105]{0:T(128)S(1)} %concatenate.36.refs_0_.meta, bf16[24,384,128]{2,1,0:T(8,128)(2,1)S(1)} %copy-done.3, bf16[24,384,128]{2,1,0:T(8,128)(2,1)S(1)} %copy-done.5, f32[24,64,128]{2,1,0:T(8,128)S(1)} %copy-done.7, f32[40,64,128]{2,1,0:T(8,128)S(1)} %get-tuple-element.65.state), custom_call_target="tpu_custom_call" | custom-call | flops 4000000000 | bytes 8388608 | tf_op jit(solution)/shard_map/leaf_backward/pallas_call | solution.py:331
  171.7 2.2 %collective-permute-start.14 = (f32[8,64,128]{2,1,0:T(8,128)S(1)}, f32[8,64,128]{2,1,0:T(8,128)S(1)}, u32[]{:S(2)}, u32[]{:S(2)}) collective-permute-start(f32[8,64,128]{2,1,0:T(8,128)S(1)} %get-tuple-element.66), channel_id=1, source_target_pairs={{0,0},{2,4},{4,2},{6,6},{1,1},{3,5},{5,3},{7,7},{8,8},{10,12},{12,... | collective-permute-start | bytes 786440 | tf_op jit(solution)/shard_map/ppermute | solution.py:209
  174.0 4.2 %collective-permute-start.16 = (f32[8,64,128]{2,1,0:T(8,128)S(1)}, f32[8,64,128]{2,1,0:T(8,128)S(1)}, u32[]{:S(2)}, u32[]{:S(2)}) collective-permute-start(f32[8,64,128]{2,1,0:T(8,128)S(1)} %get-tuple-element.69), channel_id=1, source_target_pairs={{0,0},{2,4},{4,2},{6,6},{1,1},{3,5},{5,3},{7,7},{8,8},{10,12},{12,... | collective-permute-start | bytes 786440 | tf_op jit(solution)/shard_map/ppermute | solution.py:209
  178.2 9.0 %collective-permute-done.15 = f32[17,64,128]{2,1,0:T(8,128)S(1)} collective-permute-done((f32[17,64,128]{2,1,0:T(8,128)S(1)}, f32[17,64,128]{2,1,0:T(8,128)S(1)}, u32[]{:S(2)}, u32[]{:S(2)}) %collective-permute-start.15) | collective-permute-done | bytes 557088 | tf_op jit(solution)/shard_map/ppermute | solution.py:209
  187.8 2.1 %collective-permute-done.14 = f32[8,64,128]{2,1,0:T(8,128)S(1)} collective-permute-done((f32[8,64,128]{2,1,0:T(8,128)S(1)}, f32[8,64,128]{2,1,0:T(8,128)S(1)}, u32[]{:S(2)}, u32[]{:S(2)}) %collective-permute-start.14) | collective-permute-done | bytes 262176 | tf_op jit(solution)/shard_map/ppermute | solution.py:209
  190.0 2.8 %collective-permute-done.16 = f32[8,64,128]{2,1,0:T(8,128)S(1)} collective-permute-done((f32[8,64,128]{2,1,0:T(8,128)S(1)}, f32[8,64,128]{2,1,0:T(8,128)S(1)}, u32[]{:S(2)}, u32[]{:S(2)}) %collective-permute-start.16) | collective-permute-done | bytes 262176 | tf_op jit(solution)/shard_map/ppermute | solution.py:209
  192.8 1.1 pad_maximum_fusion.2
  (68 shorter events, 6.5 us)
Async XLA Ops:
  7.2 1.6 copy-start
  7.2 8.8 %copy-start.18 = (f32[32,64,128]{2,1,0:T(8,128)S(1)}, f32[32,64,128]{2,1,0:T(8,128)}, u32[]{:S(2)}) copy-start(f32[32,64,128]{2,1,0:T(8,128)} %param.11) | copy-start | bytes 3145732
  7.2 130.4 %all-gather.3.cloned.1.call-start = ((), (), s32[]{:S(2)}) async-start(), calls=%async_computation.2 | async-start | bytes 2359296 | tf_op jit(solution)/shard_map/all_gather | solution.py:247
  10.1 7.7 %copy-start.16 = (f32[32,3,32,128]{3,2,1,0:T(8,128)S(1)}, f32[32,3,32,128]{3,2,1,0:T(8,128)}, u32[]{:S(2)}) copy-start(f32[32,3,32,128]{3,2,1,0:T(8,128)} %param.13) | copy-start | bytes 4718596
  10.1 7.7 %copy-start.17 = (f32[32,32,128]{2,1,0:T(8,128)S(1)}, f32[32,32,128]{2,1,0:T(8,128)}, u32[]{:S(2)}) copy-start(f32[32,32,128]{2,1,0:T(8,128)} %param.14) | copy-start | bytes 1572868
  10.1 7.9 %collective-permute-start = (f32[4,32,128]{2,1,0:T(8,128)S(1)}, f32[4,32,128]{2,1,0:T(8,128)S(1)}, u32[]{:S(2)}, u32[]{:S(2)}) collective-permute-start(f32[4,32,128]{2,1,0:T(8,128)S(1)} %get-tuple-element.71), channel_id=1, source_target_pairs={{0,2},{2,0},{1,3},{3,1},{4,6},{6,4},{5,7},{7,5},{8,10},{10,8},{9,1... | collective-permute-start | bytes 196616 | tf_op jit(solution)/shard_map/ppermute | solution.py:222
  18.0 1.4 slice-start
  18.1 2.7 %slice-start.1 = ((f32[32,3,32,128]{3,2,1,0:T(8,128)}), f32[8,3,32,128]{3,2,1,0:T(8,128)S(1)}, s32[]{:S(2)}) async-start(f32[32,3,32,128]{3,2,1,0:T(8,128)} %param.13), calls=%async_computation.4 | async-start | bytes 786432 | tf_op jit(solution)/shard_map/slice | solution.py:235
  18.1 3.9 %collective-permute-start.1 = (f32[2,4,32,128]{3,2,1,0:T(8,128)S(1)}, f32[2,4,32,128]{3,2,1,0:T(8,128)S(1)}, u32[]{:S(2)}, u32[]{:S(2)}) collective-permute-start(f32[2,4,32,128]{3,2,1,0:T(8,128)S(1)} %pad_maximum_fusion.6), channel_id=1, source_target_pairs={{0,1},{1,0},{2,3},{3,2},{4,5},{5,4},{6,7},{7,6},{8,9},{9,8},{10,11... | collective-permute-start | bytes 393224 | tf_op jit(solution)/shard_map/ppermute | solution.py:222
  22.7 34.8 %collective-permute-start.4 = (f32[24,4,32,128]{3,2,1,0:T(8,128)}, f32[24,4,32,128]{3,2,1,0:T(8,128)}, u32[]{:S(2)}, u32[]{:S(2)}) collective-permute-start(f32[24,4,32,128]{3,2,1,0:T(8,128)} %pad_maximum_fusion.1), channel_id=1, source_target_pairs={{2,0},{4,6},{3,1},{5,7},{10,8},{12,14},{11,9},{13,15},{18,16},{20,... | collective-permute-start | bytes 4718600 | tf_op jit(solution)/shard_map/ppermute | solution.py:212
  27.4 46.4 %collective-permute-start.3 = (f32[32,4,32,128]{3,2,1,0:T(8,128)S(1)}, f32[32,4,32,128]{3,2,1,0:T(8,128)}, u32[]{:S(2)}, u32[]{:S(2)}) collective-permute-start(f32[32,4,32,128]{3,2,1,0:T(8,128)S(1)} %pad_maximum_fusion.refs_1_), channel_id=1, source_target_pairs={{0,1},{1,0},{6,7},{7,6},{8,9},{9,8},{14,15},{15,14},{16,17},{17,16... | collective-permute-start | bytes 6291464 | tf_op jit(solution)/shard_map/ppermute | solution.py:218
  29.5 62.5 %collective-permute-start.2 = (f32[2120,128]{1,0:T(8,128)}, f32[2120,128]{1,0:T(8,128)S(1)}, u32[]{:S(2)}, u32[]{:S(2)}) collective-permute-start(f32[2120,128]{1,0:T(8,128)} %select_maximum_fusion), channel_id=1, source_target_pairs={{0,0},{2,4},{4,2},{6,6},{1,1},{3,5},{5,3},{7,7},{8,8},{10,12},{12,... | collective-permute-start | bytes 3256328 | tf_op jit(solution)/shard_map/ppermute | solution.py:209
  57.5 44.8 %collective-permute-start.5 = (f32[24,4,32,128]{3,2,1,0:T(8,128)}, f32[24,4,32,128]{3,2,1,0:T(8,128)}, u32[]{:S(2)}, u32[]{:S(2)}) collective-permute-start(f32[24,4,32,128]{3,2,1,0:T(8,128)} %collective-permute-done.4.refs_3_), channel_id=1, source_target_pairs={{0,1},{1,0},{6,7},{7,6},{8,9},{9,8},{14,15},{15,14},{16,17},{17,16... | collective-permute-start | bytes 4718600 | tf_op jit(solution)/shard_map/ppermute | solution.py:218
  59.3 32.7 %collective-permute-start.9 = (f32[8,4,32,128]{3,2,1,0:T(8,128)}, f32[8,4,32,128]{3,2,1,0:T(8,128)}, u32[]{:S(2)}, u32[]{:S(2)}) collective-permute-start(f32[8,4,32,128]{3,2,1,0:T(8,128)} %pad_maximum_fusion.4), channel_id=1, source_target_pairs={{2,0},{4,6},{3,1},{5,7},{10,8},{12,14},{11,9},{13,15},{18,16},{20,... | collective-permute-start | bytes 1572872 | tf_op jit(solution)/shard_map/ppermute | solution.py:212
  72.5 31.8 %collective-permute-start.6 = (f32[32,4,32,128]{3,2,1,0:T(8,128)S(1)}, f32[32,4,32,128]{3,2,1,0:T(8,128)}, u32[]{:S(2)}, u32[]{:S(2)}) collective-permute-start(f32[32,4,32,128]{3,2,1,0:T(8,128)S(1)} %pad_maximum_fusion.refs_1_), channel_id=1, source_target_pairs={{0,4},{6,2},{1,5},{7,3},{8,12},{14,10},{9,13},{15,11},{16,20},{22,... | collective-permute-start | bytes 6291464 | tf_op jit(solution)/shard_map/ppermute | solution.py:215
  73.8 30.6 %collective-permute-start.7 = (f32[32,4,32,128]{3,2,1,0:T(8,128)}, f32[32,4,32,128]{3,2,1,0:T(8,128)}, u32[]{:S(2)}, u32[]{:S(2)}) collective-permute-start(f32[32,4,32,128]{3,2,1,0:T(8,128)} %collective-permute-done.3.refs_2_), channel_id=1, source_target_pairs={{0,4},{6,2},{1,5},{7,3},{8,12},{14,10},{9,13},{15,11},{16,20},{22,... | collective-permute-start | bytes 6291464 | tf_op jit(solution)/shard_map/ppermute | solution.py:215
  92.0 9.5 %collective-permute-start.10 = (f32[8,4,32,128]{3,2,1,0:T(8,128)}, f32[8,4,32,128]{3,2,1,0:T(8,128)S(1)}, u32[]{:S(2)}, u32[]{:S(2)}) collective-permute-start(f32[8,4,32,128]{3,2,1,0:T(8,128)} %collective-permute-done.9.refs_3_), channel_id=1, source_target_pairs={{0,4},{6,2},{1,5},{7,3},{8,12},{14,10},{9,13},{15,11},{16,20},{22,... | collective-permute-start | bytes 1572872 | tf_op jit(solution)/shard_map/ppermute | solution.py:215
  93.3 11.1 %collective-permute-start.8 = (f32[24,4,32,128]{3,2,1,0:T(8,128)}, f32[24,4,32,128]{3,2,1,0:T(8,128)}, u32[]{:S(2)}, u32[]{:S(2)}) collective-permute-start(f32[24,4,32,128]{3,2,1,0:T(8,128)} %collective-permute-done.4.refs_3_), channel_id=1, source_target_pairs={{0,4},{6,2},{1,5},{7,3},{8,12},{14,10},{9,13},{15,11},{16,20},{22,... | collective-permute-start | bytes 4718600 | tf_op jit(solution)/shard_map/ppermute | solution.py:215
  101.5 0.8 copy-start.8
  102.3 7.1 %collective-permute-start.11 = (f32[24,4,32,128]{3,2,1,0:T(8,128)}, f32[24,4,32,128]{3,2,1,0:T(8,128)}, u32[]{:S(2)}, u32[]{:S(2)}) collective-permute-start(f32[24,4,32,128]{3,2,1,0:T(8,128)} %collective-permute-done.5.refs_4_), channel_id=1, source_target_pairs={{0,4},{6,2},{1,5},{7,3},{8,12},{14,10},{9,13},{15,11},{16,20},{22,... | collective-permute-start | bytes 4718600 | tf_op jit(solution)/shard_map/ppermute | solution.py:215
  104.4 16.4 %collective-permute-start.12 = (f32[8,4,32,128]{3,2,1,0:T(8,128)}, f32[8,4,32,128]{3,2,1,0:T(8,128)}, u32[]{:S(2)}, u32[]{:S(2)}) collective-permute-start(f32[8,4,32,128]{3,2,1,0:T(8,128)} %collective-permute-done.9.refs_3_), channel_id=1, source_target_pairs={{0,1},{1,0},{6,7},{7,6},{8,9},{9,8},{14,15},{15,14},{16,17},{17,16... | collective-permute-start | bytes 1572872 | tf_op jit(solution)/shard_map/ppermute | solution.py:218
  106.2 19.6 %copy-start.9 = (f32[8,4,32,128]{3,2,1,0:T(8,128)S(1)}, f32[8,4,32,128]{3,2,1,0:T(8,128)}, u32[]{:S(2)}) copy-start(f32[8,4,32,128]{3,2,1,0:T(8,128)} %copy-done.8) | copy-start | bytes 1572868
  120.8 10.8 %copy-start.2 = (bf16[24,384,128]{2,1,0:T(8,128)(2,1)}, bf16[24,384,128]{2,1,0:T(8,128)(2,1)S(1)}, u32[]{:S(2)}) copy-start(bf16[24,384,128]{2,1,0:T(8,128)(2,1)S(1)} %get-tuple-element.47.high) | copy-start | bytes 7077892
  120.8 10.8 %copy-start.4 = (bf16[24,384,128]{2,1,0:T(8,128)(2,1)}, bf16[24,384,128]{2,1,0:T(8,128)(2,1)S(1)}, u32[]{:S(2)}) copy-start(bf16[24,384,128]{2,1,0:T(8,128)(2,1)S(1)} %get-tuple-element.48.low) | copy-start | bytes 7077892
  120.9 10.8 %copy-start.6 = (f32[24,64,128]{2,1,0:T(8,128)}, f32[24,64,128]{2,1,0:T(8,128)S(1)}, u32[]{:S(2)}) copy-start(f32[24,64,128]{2,1,0:T(8,128)S(1)} %get-tuple-element.49.scaled) | copy-start | bytes 2359300
  120.9 5.0 %collective-permute-start.13 = (f32[8,4,32,128]{3,2,1,0:T(8,128)}, f32[8,4,32,128]{3,2,1,0:T(8,128)S(1)}, u32[]{:S(2)}, u32[]{:S(2)}) collective-permute-start(f32[8,4,32,128]{3,2,1,0:T(8,128)} %collective-permute-done.12.refs_4_), channel_id=1, source_target_pairs={{0,4},{6,2},{1,5},{7,3},{8,12},{14,10},{9,13},{15,11},{16,20},{22,... | collective-permute-start | bytes 1572872 | tf_op jit(solution)/shard_map/ppermute | solution.py:215
  131.6 0.9 copy-start.10
  132.5 0.9 copy-start.12
  133.4 0.7 copy-start.14
  134.1 12.0 %all-to-all-start = ((f32[8,5,8,128]{3,2,1,0:T(8,128)}), f32[8,5,8,128]{3,2,1,0:T(8,128)S(1)}, u32[]{:S(2)}, u32[]{:S(2)}) async-start(f32[8,5,8,128]{3,2,1,0:T(8,128)} %get-tuple-element.56), calls=%async_computation | async-start | bytes 327680 | tf_op jit(solution)/shard_map/all_to_all | solution.py:309
  137.6 1.6 copy-start.1
  146.1 11.3 %copy-start.11 = (bf16[8,384,128]{2,1,0:T(8,128)(2,1)S(1)}, bf16[8,384,128]{2,1,0:T(8,128)(2,1)}, u32[]{:S(2)}) copy-start(bf16[8,384,128]{2,1,0:T(8,128)(2,1)} %copy-done.10) | copy-start | bytes 2359300
  146.1 11.3 %copy-start.13 = (bf16[8,384,128]{2,1,0:T(8,128)(2,1)S(1)}, bf16[8,384,128]{2,1,0:T(8,128)(2,1)}, u32[]{:S(2)}) copy-start(bf16[8,384,128]{2,1,0:T(8,128)(2,1)} %copy-done.12) | copy-start | bytes 2359300
  146.1 11.3 %copy-start.15 = (f32[8,64,128]{2,1,0:T(8,128)S(1)}, f32[8,64,128]{2,1,0:T(8,128)}, u32[]{:S(2)}) copy-start(f32[8,64,128]{2,1,0:T(8,128)} %copy-done.14) | copy-start | bytes 786436
  157.4 2.2 %copy-start.3 = (bf16[24,384,128]{2,1,0:T(8,128)(2,1)S(1)}, bf16[24,384,128]{2,1,0:T(8,128)(2,1)}, u32[]{:S(2)}) copy-start(bf16[24,384,128]{2,1,0:T(8,128)(2,1)} %copy-done.2) | copy-start | bytes 7077892
  157.4 2.4 %copy-start.5 = (bf16[24,384,128]{2,1,0:T(8,128)(2,1)S(1)}, bf16[24,384,128]{2,1,0:T(8,128)(2,1)}, u32[]{:S(2)}) copy-start(bf16[24,384,128]{2,1,0:T(8,128)(2,1)} %copy-done.4) | copy-start | bytes 7077892
  157.4 2.5 %copy-start.7 = (f32[24,64,128]{2,1,0:T(8,128)S(1)}, f32[24,64,128]{2,1,0:T(8,128)}, u32[]{:S(2)}) copy-start(f32[24,64,128]{2,1,0:T(8,128)} %copy-done.6) | copy-start | bytes 2359300
  164.3 22.9 %collective-permute-start.15 = (f32[17,64,128]{2,1,0:T(8,128)S(1)}, f32[17,64,128]{2,1,0:T(8,128)S(1)}, u32[]{:S(2)}, u32[]{:S(2)}) collective-permute-start(f32[17,64,128]{2,1,0:T(8,128)S(1)} %pad_maximum_fusion.3), channel_id=1, source_target_pairs={{0,0},{2,4},{4,2},{6,6},{1,1},{3,5},{5,3},{7,7},{8,8},{10,12},{12,... | collective-permute-start | bytes 1671176 | tf_op jit(solution)/shard_map/ppermute | solution.py:209
  171.7 18.2 %collective-permute-start.14 = (f32[8,64,128]{2,1,0:T(8,128)S(1)}, f32[8,64,128]{2,1,0:T(8,128)S(1)}, u32[]{:S(2)}, u32[]{:S(2)}) collective-permute-start(f32[8,64,128]{2,1,0:T(8,128)S(1)} %get-tuple-element.66), channel_id=1, source_target_pairs={{0,0},{2,4},{4,2},{6,6},{1,1},{3,5},{5,3},{7,7},{8,8},{10,12},{12,... | collective-permute-start | bytes 786440 | tf_op jit(solution)/shard_map/ppermute | solution.py:209
  174.0 18.8 %collective-permute-start.16 = (f32[8,64,128]{2,1,0:T(8,128)S(1)}, f32[8,64,128]{2,1,0:T(8,128)S(1)}, u32[]{:S(2)}, u32[]{:S(2)}) collective-permute-start(f32[8,64,128]{2,1,0:T(8,128)S(1)} %get-tuple-element.69), channel_id=1, source_target_pairs={{0,0},{2,4},{4,2},{6,6},{1,1},{3,5},{5,3},{7,7},{8,8},{10,12},{12,... | collective-permute-start | bytes 786440 | tf_op jit(solution)/shard_map/ppermute | solution.py:209
Sparse Core Ops, SparseCore 0:
  92.1 34.5 all-gather.2

commit v7 on v6

--- a/solution.py
+++ b/solution.py
@@ -9,7 +9,7 @@
 from jax.sharding import Mesh
 from jax.sharding import PartitionSpec as P
 
-CHUNKS = (3, 1)
+CHUNKS = (2, 2)
 TURNS = 4
 GROUP = 4
 f32 = jnp.float32
@@ -338,11 +338,11 @@
             cost_estimate=cost,
             name="leaf_backward",
         )(meta, *factors[held], state)
-    late = swap(found[-1])
-    middle = swap(jnp.concatenate(found[1:-1] + [own_top], axis=0))
+    late = swap(jnp.concatenate([own_top, found[-1]], axis=0))
+    middle = swap(jnp.concatenate(found[1:-1], axis=0))
     first = swap(found[0])
-    leaf_solution = jnp.concatenate([first, middle[:-1], late], axis=0)
-    return (leaf_solution, middle[-1:])
+    leaf_solution = jnp.concatenate([first, middle, late[1:]], axis=0)
+    return (leaf_solution, late[:1])
 
 
 def solution(mesh):

time: 202 us -> 216 us (1.069)
  waiting for transfers between devices: 72.3 us -> 95.3 us
  starting transfers between devices: 54.6 us -> 42.9 us
  local copies, waits for them, and re-layouts: 9.44 us -> 13.3 us
    ppermute x4, waiting for transfers between devices: 13.9 us -> 40.1 us  [swap(): return lax.ppermute(value, ('core', 'zh'), [(0, 0), (1, 2), (2, 1), (3, 3)])]
    ppermute x2, starting transfers between devices: 18 us -> 8.49 us  [to_keeper(): return lax.ppermute(value, ('core', 'zh'), [(1, 0), (2, 3)])]
    ppermute x2, waiting for transfers between devices: 40 us -> 32.2 us  [to_keeper(): return lax.ppermute(value, ('core', 'zh'), [(1, 0), (2, 3)])]
    unnamed x38, local copies, waits for them, and re-layouts: 5.29 us -> 9.61 us
    ppermute x6, waiting for transfers between devices: 13.9 us -> 17.8 us  [to_trader(): return lax.ppermute(value, ('core', 'zh'), [(0, 2), (3, 1)])]
    ppermute x4, starting transfers between devices: 15.5 us -> 13.4 us  [swap(): return lax.ppermute(value, ('core', 'zh'), [(0, 0), (1, 2), (2, 1), (3, 3)])]
  transfers between devices with their start and end apart: 19 -> 19, of which waited for: 11 -> 10; matrix products, arithmetic and copies ran while one was open for 4% -> 3% of each run, Pallas kernels for 12% -> 11%
where the time goes in v7:
time: 216 us; the launch traced here: 215 us
  waiting for transfers between devices  95.3 us (44%)
  starting transfers between devices  42.9 us (20%)
  Pallas kernels  32.5 us (15%)
  between operations  14.4 us (7%)
  local copies, waits for them, and re-layouts  13.3 us (6%)
  blocking collectives  10 us (5%)
  other arithmetic  6.94 us (3%)
    ppermute x4, waiting for transfers between devices, swap(): return lax.ppermute(value, ('core', 'zh'), [(0, 0), (1, 2), (2, 1), (3, 3)])  40.1 us
    ppermute x2, waiting for transfers between devices, to_keeper(): return lax.ppermute(value, ('core', 'zh'), [(1, 0), (2, 3)])  32.2 us
    ppermute x6, waiting for transfers between devices, to_trader(): return lax.ppermute(value, ('core', 'zh'), [(0, 2), (3, 1)])  17.8 us
    pallas_call x2, Pallas kernels, local(): pl.pallas_call(functools.partial(forward_kernel, base, leafs, k == 0, las...  17.5 us
    ppermute x4, starting transfers between devices, swap(): return lax.ppermute(value, ('core', 'zh'), [(0, 0), (1, 2), (2, 1), (3, 3)])  13.4 us
    all_to_all x1, blocking collectives, local(): lax.all_to_all(outgoing, ('xy', 'zh'), split_axis=0, concat_axis=0, tiled...  10 us
    pallas_call x4, Pallas kernels, local(): pl.pallas_call(functools.partial(backward_kernel, k * turn, k == TURNS -...  9.65 us
    unnamed x38, local copies, waits for them, and re-layouts  9.61 us
  transfers between devices with their start and end apart: 19, of which 10 were waited for; matrix products, arithmetic and copies ran while one was open for 3% of the time, Pallas kernels for 11%

profile of v7, /device:TPU:1, one launch (start us, length us, event | category | flops | bytes accessed | tf_op | source)
XLA Modules:
  0.0 215.4 jit_solution(17332615582740782739)
XLA Ops:
  10.1 3.2 %collective-permute-start = (f32[4,32,128]{2,1,0:T(8,128)S(1)}, f32[4,32,128]{2,1,0:T(8,128)S(1)}, u32[]{:S(2)}, u32[]{:S(2)}) collective-permute-start(f32[4,32,128]{2,1,0:T(8,128)S(1)} %get-tuple-element.75), channel_id=1, source_target_pairs={{0,2},{2,0},{1,3},{3,1},{4,6},{6,4},{5,7},{7,5},{8,10},{10,8},{9,1... | collective-permute-start | bytes 196616 | tf_op jit(solution)/shard_map/ppermute | solution.py:222
  13.3 1.5 fusion.3
  14.9 1.1 copy-done.16
  16.0 1.1 select_maximum_fusion
  17.3 1.4 collective-permute-start.1
  18.7 1.5 pad_maximum_fusion.1
  20.2 1.0 collective-permute-done.1
  21.9 2.0 collective-permute-start.3
  23.9 6.2 %collective-permute-start.9 = (f32[16,4,32,128]{3,2,1,0:T(8,128)}, f32[16,4,32,128]{3,2,1,0:T(8,128)}, u32[]{:S(2)}, u32[]{:S(2)}) collective-permute-start(f32[16,4,32,128]{3,2,1,0:T(8,128)} %get-tuple-element.45), channel_id=1, source_target_pairs={{2,0},{4,6},{3,1},{5,7},{10,8},{12,14},{11,9},{13,15},{18,16},{20,... | collective-permute-start | bytes 3145736 | tf_op jit(solution)/shard_map/ppermute | solution.py:212
  30.2 2.2 %collective-permute-start.4 = (f32[16,4,32,128]{3,2,1,0:T(8,128)}, f32[16,4,32,128]{3,2,1,0:T(8,128)}, u32[]{:S(2)}, u32[]{:S(2)}) collective-permute-start(f32[16,4,32,128]{3,2,1,0:T(8,128)} %get-tuple-element.44), channel_id=1, source_target_pairs={{2,0},{4,6},{3,1},{5,7},{10,8},{12,14},{11,9},{13,15},{18,16},{20,... | collective-permute-start | bytes 3145736 | tf_op jit(solution)/shard_map/ppermute | solution.py:212
  32.4 4.7 %collective-permute-start.2 = (f32[2120,128]{1,0:T(8,128)}, f32[2120,128]{1,0:T(8,128)S(1)}, u32[]{:S(2)}, u32[]{:S(2)}) collective-permute-start(f32[2120,128]{1,0:T(8,128)} %select_maximum_fusion), channel_id=1, source_target_pairs={{0,0},{2,4},{4,2},{6,6},{1,1},{3,5},{5,3},{7,7},{8,8},{10,12},{12,... | collective-permute-start | bytes 3256328 | tf_op jit(solution)/shard_map/ppermute | solution.py:209
  37.1 1.3 collective-permute-start.6
  38.4 1.3 collective-permute-start.7
  39.7 12.8 %collective-permute-done.9.refs_3_ = f32[16,4,32,128]{3,2,1,0:T(8,128)} collective-permute-done((f32[16,4,32,128]{3,2,1,0:T(8,128)}, f32[16,4,32,128]{3,2,1,0:T(8,128)}, u32[]{:S(2)}, u32[]{:S(2)}) %collective-permute-start.9) | collective-permute-done | bytes 1048608 | tf_op jit(solution)/shard_map/ppermute | solution.py:212
  52.5 1.3 collective-permute-start.10
  53.8 19.4 %collective-permute-done.4.refs_3_ = f32[16,4,32,128]{3,2,1,0:T(8,128)} collective-permute-done((f32[16,4,32,128]{3,2,1,0:T(8,128)}, f32[16,4,32,128]{3,2,1,0:T(8,128)}, u32[]{:S(2)}, u32[]{:S(2)}) %collective-permute-start.4) | collective-permute-done | bytes 1048608 | tf_op jit(solution)/shard_map/ppermute | solution.py:212
  73.2 1.6 collective-permute-start.5
  74.8 26.8 %collective-permute-done.2.refs_9_.refs_10_ = f32[2120,128]{1,0:T(8,128)S(1)} collective-permute-done((f32[2120,128]{1,0:T(8,128)}, f32[2120,128]{1,0:T(8,128)S(1)}, u32[]{:S(2)}, u32[]{:S(2)}) %collective-permute-start.2) | collective-permute-done | bytes 1085472 | tf_op jit(solution)/shard_map/ppermute | solution.py:209
  101.7 1.3 collective-permute-start.8
  103.0 1.3 collective-permute-start.11
  104.3 2.3 %collective-permute-done.8.refs_7_ = f32[16,4,32,128]{3,2,1,0:T(8,128)} collective-permute-done((f32[16,4,32,128]{3,2,1,0:T(8,128)}, f32[16,4,32,128]{3,2,1,0:T(8,128)}, u32[]{:S(2)}, u32[]{:S(2)}) %collective-permute-start.8) | collective-permute-done | bytes 1048608 | tf_op jit(solution)/shard_map/ppermute | solution.py:215
  106.6 1.6 collective-permute-start.12
  109.2 8.2 %collective-permute-done.11.refs_8_ = f32[16,4,32,128]{3,2,1,0:T(8,128)} collective-permute-done((f32[16,4,32,128]{3,2,1,0:T(8,128)}, f32[16,4,32,128]{3,2,1,0:T(8,128)}, u32[]{:S(2)}, u32[]{:S(2)}) %collective-permute-start.11) | collective-permute-done | bytes 1048608 | tf_op jit(solution)/shard_map/ppermute | solution.py:215
  117.4 8.3 %leaf_forward.2 = (f32[40,64,128]{2,1,0:T(8,128)S(1)}, bf16[16,384,128]{2,1,0:T(8,128)(2,1)S(1)}, bf16[16,384,128]{2,1,0:T(8,128)(2,1)S(1)}, f32[16,64,128]{2,1,0:T(8,128)S(1)}) custom-call(s32[105]{0:T(128)S(1)} %concatenate.39.refs_0_.meta, f32[32,4,32,128]{3,2,1,0:T(8,128)S(1)} %pad_maximum_fusion.refs_1_, ...), custom_call_target="tpu_custom_call" | custom-call | flops 4000000000 | bytes 8388608 | tf_op jit(solution)/shard_map/leaf_forward/pallas_call | solution.py:276
  125.7 1.1 copy-done.8
  126.8 1.1 copy-done.10
  127.9 1.3 collective-permute-start.13
  129.2 7.3 %collective-permute-done.13.refs_8_ = f32[16,4,32,128]{3,2,1,0:T(8,128)S(1)} collective-permute-done((f32[16,4,32,128]{3,2,1,0:T(8,128)}, f32[16,4,32,128]{3,2,1,0:T(8,128)S(1)}, u32[]{:S(2)}, u32[]{:S(2)}) %collective-permute-start.13) | collective-permute-done | bytes 1048608 | tf_op jit(solution)/shard_map/ppermute | solution.py:215
  136.6 9.2 %leaf_forward.3 = (f32[40,64,128]{2,1,0:T(8,128)}, bf16[16,384,128]{2,1,0:T(8,128)(2,1)S(1)}, bf16[16,384,128]{2,1,0:T(8,128)(2,1)S(1)}, f32[16,64,128]{2,1,0:T(8,128)S(1)}, f32[8,5,8,128]{3,2,1,0:T(8,128)}) custom-call(s32[105]{0:T(128)S(1)} %concatenate.39.refs_0_.meta, f32[32,4,32,128]{3,2,1,0:T(8,128)S(1)} %pad_maximum_fusion.refs_1_, ...), custom_call_target="tpu_custom_call" | custom-call | flops 4000000000 | bytes 8388608 | tf_op jit(solution)/shard_map/leaf_forward/pallas_call | solution.py:276
  145.8 1.1 copy-done.2
  146.9 1.2 copy-done.4
  148.9 3.4 %all-to-all-start = ((f32[8,5,8,128]{3,2,1,0:T(8,128)}), f32[8,5,8,128]{3,2,1,0:T(8,128)S(1)}, u32[]{:S(2)}, u32[]{:S(2)}) async-start(f32[8,5,8,128]{3,2,1,0:T(8,128)} %get-tuple-element.56), calls=%async_computation | async-start | bytes 327680 | tf_op jit(solution)/shard_map/all_to_all | solution.py:309
  152.4 1.6 copy-done.1
  154.0 2.7 %top_prepare.1 = (bf16[8,384,128]{2,1,0:T(8,128)(2,1)S(1)}, bf16[8,384,128]{2,1,0:T(8,128)(2,1)S(1)}, bf16[8,128,128]{2,1,0:T(8,128)(2,1)S(1)}, bf16[8,128,128]{2,1,0:T(8,128)(2,1)S(1)}) custom-call(s32[4]{0:T(128)S(1)} %pad_add_fusion.places, f32[8,4,4,32,128]{4,3,2,1,0:T(8,128)S(1)} %bitcast.32), custom_call_target="tpu_custom_call" | custom-call | tf_op jit(solution)/shard_map/top_prepare/pallas_call | solution.py:297
  156.7 4.1 %all-to-all-done.incoming = f32[8,5,8,128]{3,2,1,0:T(8,128)S(1)} async-done(((f32[8,5,8,128]{3,2,1,0:T(8,128)}), f32[8,5,8,128]{3,2,1,0:T(8,128)S(1)}, u32[]{:S(2)}, u32[]{:S(2)}) %all-to-all-start) | async-done | bytes 163872 | tf_op jit(solution)/shard_map/all_to_all | solution.py:309
  160.8 2.7 %top_solve.1 = f32[8,5,8,128]{3,2,1,0:T(8,128)S(1)} custom-call(f32[8,5,8,128]{3,2,1,0:T(8,128)S(1)} %all-to-all-done.incoming, bf16[8,384,128]{2,1,0:T(8,128)(2,1)S(1)} %get-tuple-element.59.high, bf16[8,384,128]{2,1,0:T(8,128)(2,1)S(1)} %get-tuple-element.60.low, bf16[8,128,128]{2,1,0:T(8,128)(2,1)S(1)} %get-tuple-element.61.inverse_high, ...), custom_call_target="tpu_custom_call" | custom-call | tf_op jit(solution)/shard_map/top_solve/pallas_call | solution.py:310
  163.6 10.0 %all_to_all.10.state = f32[8,5,8,128]{3,2,1,0:T(8,128)S(1)} all-to-all(f32[8,5,8,128]{3,2,1,0:T(8,128)S(1)} %top_solve.1), channel_id=1, replica_groups=mesh['xy'=4,'core'=2,'zh'=2,'zl'=2] {'xy','zh'}, dimensions={0} | all-to-all | bytes 327680 | tf_op jit(solution)/shard_map/all_to_all | solution.py:318
  173.6 1.4 copy-done.5
  175.0 2.1 leaf_backward.4
  177.2 2.1 leaf_backward.5
  179.4 2.1 leaf_backward.6
  181.5 2.3 %collective-permute-start.15 = (f32[16,64,128]{2,1,0:T(8,128)S(1)}, f32[16,64,128]{2,1,0:T(8,128)S(1)}, u32[]{:S(2)}, u32[]{:S(2)}) collective-permute-start(f32[16,64,128]{2,1,0:T(8,128)S(1)} %pad_maximum_fusion.4), channel_id=1, source_target_pairs={{0,0},{2,4},{4,2},{6,6},{1,1},{3,5},{5,3},{7,7},{8,8},{10,12},{12,... | collective-permute-start | bytes 1572872 | tf_op jit(solution)/shard_map/ppermute | solution.py:209
  183.9 4.2 %collective-permute-start.16 = (f32[9,64,128]{2,1,0:T(8,128)S(1)}, f32[9,64,128]{2,1,0:T(8,128)S(1)}, u32[]{:S(2)}, u32[]{:S(2)}) collective-permute-start(f32[9,64,128]{2,1,0:T(8,128)S(1)} %pad_maximum_fusion.5), channel_id=1, source_target_pairs={{0,0},{2,4},{4,2},{6,6},{1,1},{3,5},{5,3},{7,7},{8,8},{10,12},{12,... | collective-permute-start | bytes 884744 | tf_op jit(solution)/shard_map/ppermute | solution.py:209
  188.1 3.2 %leaf_backward.7 = (f32[8,64,128]{2,1,0:T(8,128)S(1)}, f32[40,64,128]{2,1,0:T(8,128)}) custom-call(s32[105]{0:T(128)S(1)} %concatenate.39.refs_0_.meta, bf16[16,384,128]{2,1,0:T(8,128)(2,1)S(1)} %copy-done.9, bf16[16,384,128]{2,1,0:T(8,128)(2,1)S(1)} %copy-done.11, f32[16,64,128]{2,1,0:T(8,128)S(1)} %copy-done.13, f32[40,64,128]{2,1,0:T(8,128)S(1)} %get-tuple-element.65.state), custom_call_target="tpu_custom_call" | custom-call | flops 4000000000 | bytes 8388608 | tf_op jit(solution)/shard_map/leaf_backward/pallas_call | solution.py:331
  191.3 2.2 %collective-permute-start.14 = (f32[8,64,128]{2,1,0:T(8,128)S(1)}, f32[8,64,128]{2,1,0:T(8,128)S(1)}, u32[]{:S(2)}, u32[]{:S(2)}) collective-permute-start(f32[8,64,128]{2,1,0:T(8,128)S(1)} %get-tuple-element.66), channel_id=1, source_target_pairs={{0,0},{2,4},{4,2},{6,6},{1,1},{3,5},{5,3},{7,7},{8,8},{10,12},{12,... | collective-permute-start | bytes 786440 | tf_op jit(solution)/shard_map/ppermute | solution.py:209
  193.6 11.1 %collective-permute-done.16 = f32[9,64,128]{2,1,0:T(8,128)S(1)} collective-permute-done((f32[9,64,128]{2,1,0:T(8,128)S(1)}, f32[9,64,128]{2,1,0:T(8,128)S(1)}, u32[]{:S(2)}, u32[]{:S(2)}) %collective-permute-start.16) | collective-permute-done | bytes 294944 | tf_op jit(solution)/shard_map/ppermute | solution.py:209
  205.3 2.2 %collective-permute-done.14 = f32[8,64,128]{2,1,0:T(8,128)S(1)} collective-permute-done((f32[8,64,128]{2,1,0:T(8,128)S(1)}, f32[8,64,128]{2,1,0:T(8,128)S(1)}, u32[]{:S(2)}, u32[]{:S(2)}) %collective-permute-start.14) | collective-permute-done | bytes 262176 | tf_op jit(solution)/shard_map/ppermute | solution.py:209
  207.5 1.0 pad_maximum_fusion.3
  (64 shorter events, 6.5 us)
Async XLA Ops:
  7.2 1.5 copy-start
  7.2 145.2 %all-gather.3.cloned.1.call-start = ((), (), s32[]{:S(2)}) async-start(), calls=%async_computation.2 | async-start | bytes 2359296 | tf_op jit(solution)/shard_map/all_gather | solution.py:247
  10.0 4.7 %copy-start.15 = (f32[32,32,128]{2,1,0:T(8,128)S(1)}, f32[32,32,128]{2,1,0:T(8,128)}, u32[]{:S(2)}) copy-start(f32[32,32,128]{2,1,0:T(8,128)} %param.14) | copy-start | bytes 1572868
  10.0 4.8 %copy-start.18 = (s32[32,3]{0,1:T(4,128)S(1)}, s32[32,3]{0,1:T(4,128)}, u32[]{:S(2)}) copy-start(s32[32,3]{0,1:T(4,128)} %param.15) | copy-start | bytes 1156
  10.0 4.8 %copy-start.17 = (f32[1,64,128]{2,1,0:T(8,128)S(1)}, f32[1,64,128]{2,1,0:T(8,128)}, u32[]{:S(2)}) copy-start(f32[1,64,128]{2,1,0:T(8,128)} %param.12) | copy-start | bytes 98308
  10.1 7.2 %collective-permute-start = (f32[4,32,128]{2,1,0:T(8,128)S(1)}, f32[4,32,128]{2,1,0:T(8,128)S(1)}, u32[]{:S(2)}, u32[]{:S(2)}) collective-permute-start(f32[4,32,128]{2,1,0:T(8,128)S(1)} %get-tuple-element.75), channel_id=1, source_target_pairs={{0,2},{2,0},{1,3},{3,1},{4,6},{6,4},{5,7},{7,5},{8,10},{10,8},{9,1... | collective-permute-start | bytes 196616 | tf_op jit(solution)/shard_map/ppermute | solution.py:222
  14.8 1.2 copy-start.16
  14.8 2.2 %copy-start.14 = (f32[32,3,32,128]{3,2,1,0:T(8,128)S(1)}, f32[32,3,32,128]{3,2,1,0:T(8,128)}, u32[]{:S(2)}) copy-start(f32[32,3,32,128]{3,2,1,0:T(8,128)} %param.13) | copy-start | bytes 4718596
  17.3 3.9 %collective-permute-start.1 = (f32[2,4,32,128]{3,2,1,0:T(8,128)S(1)}, f32[2,4,32,128]{3,2,1,0:T(8,128)S(1)}, u32[]{:S(2)}, u32[]{:S(2)}) collective-permute-start(f32[2,4,32,128]{3,2,1,0:T(8,128)S(1)} %pad_maximum_fusion.7), channel_id=1, source_target_pairs={{0,1},{1,0},{2,3},{3,2},{4,5},{5,4},{6,7},{7,6},{8,9},{9,8},{10,11... | collective-permute-start | bytes 393224 | tf_op jit(solution)/shard_map/ppermute | solution.py:222
  21.9 16.5 %collective-permute-start.3 = (f32[32,4,32,128]{3,2,1,0:T(8,128)S(1)}, f32[32,4,32,128]{3,2,1,0:T(8,128)}, u32[]{:S(2)}, u32[]{:S(2)}) collective-permute-start(f32[32,4,32,128]{3,2,1,0:T(8,128)S(1)} %pad_maximum_fusion.refs_1_), channel_id=1, source_target_pairs={{0,1},{1,0},{6,7},{7,6},{8,9},{9,8},{14,15},{15,14},{16,17},{17,16... | collective-permute-start | bytes 6291464 | tf_op jit(solution)/shard_map/ppermute | solution.py:218
  23.9 28.6 %collective-permute-start.9 = (f32[16,4,32,128]{3,2,1,0:T(8,128)}, f32[16,4,32,128]{3,2,1,0:T(8,128)}, u32[]{:S(2)}, u32[]{:S(2)}) collective-permute-start(f32[16,4,32,128]{3,2,1,0:T(8,128)} %get-tuple-element.45), channel_id=1, source_target_pairs={{2,0},{4,6},{3,1},{5,7},{10,8},{12,14},{11,9},{13,15},{18,16},{20,... | collective-permute-start | bytes 3145736 | tf_op jit(solution)/shard_map/ppermute | solution.py:212
  30.2 43.1 %collective-permute-start.4 = (f32[16,4,32,128]{3,2,1,0:T(8,128)}, f32[16,4,32,128]{3,2,1,0:T(8,128)}, u32[]{:S(2)}, u32[]{:S(2)}) collective-permute-start(f32[16,4,32,128]{3,2,1,0:T(8,128)} %get-tuple-element.44), channel_id=1, source_target_pairs={{2,0},{4,6},{3,1},{5,7},{10,8},{12,14},{11,9},{13,15},{18,16},{20,... | collective-permute-start | bytes 3145736 | tf_op jit(solution)/shard_map/ppermute | solution.py:212
  32.4 69.3 %collective-permute-start.2 = (f32[2120,128]{1,0:T(8,128)}, f32[2120,128]{1,0:T(8,128)S(1)}, u32[]{:S(2)}, u32[]{:S(2)}) collective-permute-start(f32[2120,128]{1,0:T(8,128)} %select_maximum_fusion), channel_id=1, source_target_pairs={{0,0},{2,4},{4,2},{6,6},{1,1},{3,5},{5,3},{7,7},{8,8},{10,12},{12,... | collective-permute-start | bytes 3256328 | tf_op jit(solution)/shard_map/ppermute | solution.py:209
  37.1 69.5 %collective-permute-start.6 = (f32[32,4,32,128]{3,2,1,0:T(8,128)S(1)}, f32[32,4,32,128]{3,2,1,0:T(8,128)}, u32[]{:S(2)}, u32[]{:S(2)}) collective-permute-start(f32[32,4,32,128]{3,2,1,0:T(8,128)S(1)} %pad_maximum_fusion.refs_1_), channel_id=1, source_target_pairs={{0,4},{6,2},{1,5},{7,3},{8,12},{14,10},{9,13},{15,11},{16,20},{22,... | collective-permute-start | bytes 6291464 | tf_op jit(solution)/shard_map/ppermute | solution.py:215
  38.4 68.2 %collective-permute-start.7 = (f32[32,4,32,128]{3,2,1,0:T(8,128)}, f32[32,4,32,128]{3,2,1,0:T(8,128)}, u32[]{:S(2)}, u32[]{:S(2)}) collective-permute-start(f32[32,4,32,128]{3,2,1,0:T(8,128)} %collective-permute-done.3.refs_2_), channel_id=1, source_target_pairs={{0,4},{6,2},{1,5},{7,3},{8,12},{14,10},{9,13},{15,11},{16,20},{22,... | collective-permute-start | bytes 6291464 | tf_op jit(solution)/shard_map/ppermute | solution.py:215
  52.5 50.5 %collective-permute-start.10 = (f32[16,4,32,128]{3,2,1,0:T(8,128)}, f32[16,4,32,128]{3,2,1,0:T(8,128)}, u32[]{:S(2)}, u32[]{:S(2)}) collective-permute-start(f32[16,4,32,128]{3,2,1,0:T(8,128)} %collective-permute-done.9.refs_3_), channel_id=1, source_target_pairs={{0,4},{6,2},{1,5},{7,3},{8,12},{14,10},{9,13},{15,11},{16,20},{22,... | collective-permute-start | bytes 3145736 | tf_op jit(solution)/shard_map/ppermute | solution.py:215
  73.2 29.8 %collective-permute-start.5 = (f32[16,4,32,128]{3,2,1,0:T(8,128)}, f32[16,4,32,128]{3,2,1,0:T(8,128)}, u32[]{:S(2)}, u32[]{:S(2)}) collective-permute-start(f32[16,4,32,128]{3,2,1,0:T(8,128)} %collective-permute-done.4.refs_3_), channel_id=1, source_target_pairs={{0,1},{1,0},{6,7},{7,6},{8,9},{9,8},{14,15},{15,14},{16,17},{17,16... | collective-permute-start | bytes 3145736 | tf_op jit(solution)/shard_map/ppermute | solution.py:218
  101.7 4.9 %collective-permute-start.8 = (f32[16,4,32,128]{3,2,1,0:T(8,128)}, f32[16,4,32,128]{3,2,1,0:T(8,128)}, u32[]{:S(2)}, u32[]{:S(2)}) collective-permute-start(f32[16,4,32,128]{3,2,1,0:T(8,128)} %collective-permute-done.4.refs_3_), channel_id=1, source_target_pairs={{0,4},{6,2},{1,5},{7,3},{8,12},{14,10},{9,13},{15,11},{16,20},{22,... | collective-permute-start | bytes 3145736 | tf_op jit(solution)/shard_map/ppermute | solution.py:215
  103.0 14.4 %collective-permute-start.11 = (f32[16,4,32,128]{3,2,1,0:T(8,128)}, f32[16,4,32,128]{3,2,1,0:T(8,128)}, u32[]{:S(2)}, u32[]{:S(2)}) collective-permute-start(f32[16,4,32,128]{3,2,1,0:T(8,128)} %collective-permute-done.5.refs_4_), channel_id=1, source_target_pairs={{0,4},{6,2},{1,5},{7,3},{8,12},{14,10},{9,13},{15,11},{16,20},{22,... | collective-permute-start | bytes 3145736 | tf_op jit(solution)/shard_map/ppermute | solution.py:215
  106.6 21.4 %collective-permute-start.12 = (f32[16,4,32,128]{3,2,1,0:T(8,128)}, f32[16,4,32,128]{3,2,1,0:T(8,128)}, u32[]{:S(2)}, u32[]{:S(2)}) collective-permute-start(f32[16,4,32,128]{3,2,1,0:T(8,128)} %collective-permute-done.9.refs_3_), channel_id=1, source_target_pairs={{0,1},{1,0},{6,7},{7,6},{8,9},{9,8},{14,15},{15,14},{16,17},{17,16... | collective-permute-start | bytes 3145736 | tf_op jit(solution)/shard_map/ppermute | solution.py:218
  125.7 1.1 copy-start.8
  126.8 1.1 copy-start.10
  127.9 17.8 %copy-start.12 = (f32[16,64,128]{2,1,0:T(8,128)}, f32[16,64,128]{2,1,0:T(8,128)S(1)}, u32[]{:S(2)}) copy-start(f32[16,64,128]{2,1,0:T(8,128)S(1)} %get-tuple-element.49.scaled) | copy-start | bytes 1572868
  127.9 8.6 %collective-permute-start.13 = (f32[16,4,32,128]{3,2,1,0:T(8,128)}, f32[16,4,32,128]{3,2,1,0:T(8,128)S(1)}, u32[]{:S(2)}, u32[]{:S(2)}) collective-permute-start(f32[16,4,32,128]{3,2,1,0:T(8,128)} %collective-permute-done.12.refs_4_), channel_id=1, source_target_pairs={{0,4},{6,2},{1,5},{7,3},{8,12},{14,10},{9,13},{15,11},{16,20},{22,... | collective-permute-start | bytes 3145736 | tf_op jit(solution)/shard_map/ppermute | solution.py:215
  145.8 1.2 copy-start.2
  146.9 1.2 copy-start.4
  148.1 0.8 copy-start.6
  148.9 11.9 %all-to-all-start = ((f32[8,5,8,128]{3,2,1,0:T(8,128)}), f32[8,5,8,128]{3,2,1,0:T(8,128)S(1)}, u32[]{:S(2)}, u32[]{:S(2)}) async-start(f32[8,5,8,128]{3,2,1,0:T(8,128)} %get-tuple-element.56), calls=%async_computation | async-start | bytes 327680 | tf_op jit(solution)/shard_map/all_to_all | solution.py:309
  152.4 1.6 copy-start.1
  160.8 12.8 %copy-start.3 = (bf16[16,384,128]{2,1,0:T(8,128)(2,1)S(1)}, bf16[16,384,128]{2,1,0:T(8,128)(2,1)}, u32[]{:S(2)}) copy-start(bf16[16,384,128]{2,1,0:T(8,128)(2,1)} %copy-done.2) | copy-start | bytes 4718596
  160.8 12.8 %copy-start.7 = (f32[16,64,128]{2,1,0:T(8,128)S(1)}, f32[16,64,128]{2,1,0:T(8,128)}, u32[]{:S(2)}) copy-start(f32[16,64,128]{2,1,0:T(8,128)} %copy-done.6) | copy-start | bytes 1572868
  173.6 1.4 copy-start.5
  177.1 2.2 %copy-start.9 = (bf16[16,384,128]{2,1,0:T(8,128)(2,1)S(1)}, bf16[16,384,128]{2,1,0:T(8,128)(2,1)}, u32[]{:S(2)}) copy-start(bf16[16,384,128]{2,1,0:T(8,128)(2,1)} %copy-done.8) | copy-start | bytes 4718596
  177.2 2.2 %copy-start.11 = (bf16[16,384,128]{2,1,0:T(8,128)(2,1)S(1)}, bf16[16,384,128]{2,1,0:T(8,128)(2,1)}, u32[]{:S(2)}) copy-start(bf16[16,384,128]{2,1,0:T(8,128)(2,1)} %copy-done.10) | copy-start | bytes 4718596
  177.2 2.2 %copy-start.13 = (f32[16,64,128]{2,1,0:T(8,128)S(1)}, f32[16,64,128]{2,1,0:T(8,128)}, u32[]{:S(2)}) copy-start(f32[16,64,128]{2,1,0:T(8,128)} %copy-done.12) | copy-start | bytes 1572868
  181.5 25.9 %collective-permute-start.15 = (f32[16,64,128]{2,1,0:T(8,128)S(1)}, f32[16,64,128]{2,1,0:T(8,128)S(1)}, u32[]{:S(2)}, u32[]{:S(2)}) collective-permute-start(f32[16,64,128]{2,1,0:T(8,128)S(1)} %pad_maximum_fusion.4), channel_id=1, source_target_pairs={{0,0},{2,4},{4,2},{6,6},{1,1},{3,5},{5,3},{7,7},{8,8},{10,12},{12,... | collective-permute-start | bytes 1572872 | tf_op jit(solution)/shard_map/ppermute | solution.py:209
  183.9 20.8 %collective-permute-start.16 = (f32[9,64,128]{2,1,0:T(8,128)S(1)}, f32[9,64,128]{2,1,0:T(8,128)S(1)}, u32[]{:S(2)}, u32[]{:S(2)}) collective-permute-start(f32[9,64,128]{2,1,0:T(8,128)S(1)} %pad_maximum_fusion.5), channel_id=1, source_target_pairs={{0,0},{2,4},{4,2},{6,6},{1,1},{3,5},{5,3},{7,7},{8,8},{10,12},{12,... | collective-permute-start | bytes 884744 | tf_op jit(solution)/shard_map/ppermute | solution.py:209
  191.3 16.2 %collective-permute-start.14 = (f32[8,64,128]{2,1,0:T(8,128)S(1)}, f32[8,64,128]{2,1,0:T(8,128)S(1)}, u32[]{:S(2)}, u32[]{:S(2)}) collective-permute-start(f32[8,64,128]{2,1,0:T(8,128)S(1)} %get-tuple-element.66), channel_id=1, source_target_pairs={{0,0},{2,4},{4,2},{6,6},{1,1},{3,5},{5,3},{7,7},{8,8},{10,12},{12,... | collective-permute-start | bytes 786440 | tf_op jit(solution)/shard_map/ppermute | solution.py:209
Sparse Core Ops, SparseCore 0:
  103.1 28.0 all-gather.2

commit v8 on v7

--- a/solution.py
+++ b/solution.py
@@ -9,13 +9,14 @@
 from jax.sharding import Mesh
 from jax.sharding import PartitionSpec as P
 
-CHUNKS = (2, 2)
+CHUNKS = (3, 1)
 TURNS = 4
 GROUP = 4
 f32 = jnp.float32
 bf16 = jnp.bfloat16
 SMEM = pl.BlockSpec(memory_space=pltpu.SMEM)
 VMEM = pl.BlockSpec(memory_space=pltpu.VMEM)
+HBM = pl.BlockSpec(memory_space=pltpu.HBM)
 
 
 def params():
@@ -60,10 +61,10 @@
     refs = refs[11:]
     if not first:
         acc_in, refs = refs[0], refs[1:]
-    acc, high, low, scaled, refs = refs[0], refs[1], refs[2], refs[3], refs[4:]
+    acc, high_out, low_out, scaled, refs = refs[0], refs[1], refs[2], refs[3], refs[4:]
     if last:
         payload, refs = refs[0], refs[1:]
-    full, arrived = refs
+    full, high, low, arrived, stored = refs
     steps, columns, rows = scaled.shape[0], scaled.shape[1], kept[0].shape[2]
     wide = full.shape[2]
 
@@ -80,6 +81,13 @@
                 )
             )
         return made
+
+    def stores(group):
+        at = pl.ds(group * GROUP, GROUP)
+        return [
+            pltpu.make_async_copy(high.at[at], high_out.at[at], stored.at[group, 0]),
+            pltpu.make_async_copy(low.at[at], low_out.at[at], stored.at[group, 1]),
+        ]
 
     def start(pieces):
         for group in range(steps // GROUP):
@@ -102,6 +110,8 @@
             merged = split(product(blocks, split(full[s, 3]), False))
             high[s] = merged[0]
             low[s] = merged[1]
+        for store in stores(group):
+            store.start()
         for s in members:
             at = s * columns
             source = split(rhs[at : at + columns] - acc[base + s])
@@ -120,6 +130,9 @@
             for p in range(peers):
                 at = (p % groups) * part
                 payload[p, i] = node[at : at + part]
+    for group in range(steps // GROUP):
+        for store in stores(group):
+            store.wait()
 
 
 def backward_kernel(base, first, width, meta, high, low, scaled, state, out, z):
@@ -277,11 +290,14 @@
             functools.partial(forward_kernel, base, leafs, k == 0, last, width),
             grid=(1,),
             in_specs=specs + [VMEM] * (k > 0),
-            out_specs=[VMEM] * len(shapes),
+            out_specs=[VMEM, HBM, HBM, VMEM] + [VMEM] * last,
             out_shape=shapes,
             scratch_shapes=[
                 pltpu.VMEM((steps, 4, wide, wide), f32),
+                pltpu.VMEM((steps, 3 * wide, wide), bf16),
+                pltpu.VMEM((steps, 3 * wide, wide), bf16),
                 pltpu.SemaphoreType.DMA((steps // GROUP, 4)),
+                pltpu.SemaphoreType.DMA((steps // GROUP, 2)),
             ],
             compiler_params=params(),
             cost_estimate=cost,

time: 216 us -> 206 us (0.954)
  waiting for transfers between devices: 95.3 us -> 72.3 us
  starting transfers between devices: 42.9 us -> 54.6 us
  Pallas kernels: 32.5 us -> 37 us
  local copies, waits for them, and re-layouts: 13.3 us -> 9.42 us
    ppermute x4, waiting for transfers between devices: 40.1 us -> 13.9 us  [swap(): return lax.ppermute(value, ('core', 'zh'), [(0, 0), (1, 2), (2, 1), (3, 3)])]
    ppermute x2, starting transfers between devices: 8.49 us -> 18 us  [to_keeper(): return lax.ppermute(value, ('core', 'zh'), [(1, 0), (2, 3)])]
    ppermute x2, waiting for transfers between devices: 32.2 us -> 40 us  [to_keeper(): return lax.ppermute(value, ('core', 'zh'), [(1, 0), (2, 3)])]
    pallas_call x2, Pallas kernels: 17.5 us -> 22 us  [local(): pl.pallas_call(functools.partial(forward_kernel, base, leafs, k == 0, las...]
    unnamed x38, local copies, waits for them, and re-layouts: 9.61 us -> 5.29 us
    ppermute x6, waiting for transfers between devices: 17.8 us -> 13.9 us  [to_trader(): return lax.ppermute(value, ('core', 'zh'), [(0, 2), (3, 1)])]
    ppermute x4, starting transfers between devices: 13.4 us -> 15.5 us  [swap(): return lax.ppermute(value, ('core', 'zh'), [(0, 0), (1, 2), (2, 1), (3, 3)])]
  transfers between devices with their start and end apart: 19 -> 19, of which waited for: 10 -> 10; matrix products, arithmetic and copies ran while one was open for 3% -> 4% of each run, Pallas kernels for 11% -> 14%
where the time goes in v8:
time: 206 us; the launch traced here: 205 us
  waiting for transfers between devices  72.3 us (35%)
  starting transfers between devices  54.6 us (27%)
  Pallas kernels  37 us (18%)
  between operations  14.4 us (7%)
  local copies, waits for them, and re-layouts  9.42 us (5%)
  other arithmetic  9.1 us (4%)
  blocking collectives  8.6 us (4%)
    ppermute x2, waiting for transfers between devices, to_keeper(): return lax.ppermute(value, ('core', 'zh'), [(1, 0), (2, 3)])  40 us
    pallas_call x2, Pallas kernels, local(): pl.pallas_call(functools.partial(forward_kernel, base, leafs, k == 0, las...  22 us
    ppermute x2, starting transfers between devices, to_keeper(): return lax.ppermute(value, ('core', 'zh'), [(1, 0), (2, 3)])  18 us
    ppermute x4, starting transfers between devices, swap(): return lax.ppermute(value, ('core', 'zh'), [(0, 0), (1, 2), (2, 1), (3, 3)])  15.5 us
    ppermute x4, waiting for transfers between devices, swap(): return lax.ppermute(value, ('core', 'zh'), [(0, 0), (1, 2), (2, 1), (3, 3)])  13.9 us
    ppermute x6, waiting for transfers between devices, to_trader(): return lax.ppermute(value, ('core', 'zh'), [(0, 2), (3, 1)])  13.9 us
    pallas_call x4, Pallas kernels, local(): pl.pallas_call(functools.partial(backward_kernel, k * turn, k == TURNS -...  9.63 us
    all_to_all x1, blocking collectives, local(): lax.all_to_all(outgoing, ('xy', 'zh'), split_axis=0, concat_axis=0, tiled...  8.6 us
  transfers between devices with their start and end apart: 19, of which 10 were waited for; matrix products, arithmetic and copies ran while one was open for 4% of the time, Pallas kernels for 14%

profile of v8, /device:TPU:1, one launch (start us, length us, event | category | flops | bytes accessed | tf_op | source)
XLA Modules:
  0.0 205.5 jit_solution(10847784791699812221)
XLA Ops:
  7.2 0.8 fusion.1
  9.4 0.7 fusion.2
  10.1 3.2 %collective-permute-start = (f32[4,32,128]{2,1,0:T(8,128)S(1)}, f32[4,32,128]{2,1,0:T(8,128)S(1)}, u32[]{:S(2)}, u32[]{:S(2)}) collective-permute-start(f32[4,32,128]{2,1,0:T(8,128)S(1)} %get-tuple-element.71), channel_id=1, source_target_pairs={{0,2},{2,0},{1,3},{3,1},{4,6},{6,4},{5,7},{7,5},{8,10},{10,8},{9,1... | collective-permute-start | bytes 196616 | tf_op jit(solution)/shard_map/ppermute | solution.py:235
  13.3 1.0 slice_bitcast_fusion
  14.4 0.9 slice_bitcast_fusion.1
  16.0 1.8 select_maximum_fusion
  18.1 1.4 collective-permute-start.1
  19.4 1.3 pad_maximum_fusion.1
  20.7 0.8 pad_maximum_fusion.3
  22.0 0.7 pad_maximum_fusion.6
  22.7 4.7 %collective-permute-start.4 = (f32[24,4,32,128]{3,2,1,0:T(8,128)}, f32[24,4,32,128]{3,2,1,0:T(8,128)}, u32[]{:S(2)}, u32[]{:S(2)}) collective-permute-start(f32[24,4,32,128]{3,2,1,0:T(8,128)} %pad_maximum_fusion.1), channel_id=1, source_target_pairs={{2,0},{4,6},{3,1},{5,7},{10,8},{12,14},{11,9},{13,15},{18,16},{20,... | collective-permute-start | bytes 4718600 | tf_op jit(solution)/shard_map/ppermute | solution.py:225
  27.4 2.1 %collective-permute-start.3 = (f32[32,4,32,128]{3,2,1,0:T(8,128)S(1)}, f32[32,4,32,128]{3,2,1,0:T(8,128)}, u32[]{:S(2)}, u32[]{:S(2)}) collective-permute-start(f32[32,4,32,128]{3,2,1,0:T(8,128)S(1)} %pad_maximum_fusion.refs_1_), channel_id=1, source_target_pairs={{0,1},{1,0},{6,7},{7,6},{8,9},{9,8},{14,15},{15,14},{16,17},{17,16... | collective-permute-start | bytes 6291464 | tf_op jit(solution)/shard_map/ppermute | solution.py:231
  29.5 4.9 %collective-permute-start.2 = (f32[2120,128]{1,0:T(8,128)}, f32[2120,128]{1,0:T(8,128)S(1)}, u32[]{:S(2)}, u32[]{:S(2)}) collective-permute-start(f32[2120,128]{1,0:T(8,128)} %select_maximum_fusion), channel_id=1, source_target_pairs={{0,0},{2,4},{4,2},{6,6},{1,1},{3,5},{5,3},{7,7},{8,8},{10,12},{12,... | collective-permute-start | bytes 3256328 | tf_op jit(solution)/shard_map/ppermute | solution.py:222
  34.4 23.1 %collective-permute-done.4.refs_3_ = f32[24,4,32,128]{3,2,1,0:T(8,128)} collective-permute-done((f32[24,4,32,128]{3,2,1,0:T(8,128)}, f32[24,4,32,128]{3,2,1,0:T(8,128)}, u32[]{:S(2)}, u32[]{:S(2)}) %collective-permute-start.4) | collective-permute-done | bytes 1572896 | tf_op jit(solution)/shard_map/ppermute | solution.py:225
  57.5 1.8 collective-permute-start.5
  59.3 13.3 %collective-permute-start.9 = (f32[8,4,32,128]{3,2,1,0:T(8,128)}, f32[8,4,32,128]{3,2,1,0:T(8,128)}, u32[]{:S(2)}, u32[]{:S(2)}) collective-permute-start(f32[8,4,32,128]{3,2,1,0:T(8,128)} %pad_maximum_fusion.3), channel_id=1, source_target_pairs={{2,0},{4,6},{3,1},{5,7},{10,8},{12,14},{11,9},{13,15},{18,16},{20,... | collective-permute-start | bytes 1572872 | tf_op jit(solution)/shard_map/ppermute | solution.py:225
  72.5 1.3 collective-permute-start.6
  73.8 1.3 collective-permute-start.7
  75.1 16.8 %collective-permute-done.9.refs_3_ = f32[8,4,32,128]{3,2,1,0:T(8,128)} collective-permute-done((f32[8,4,32,128]{3,2,1,0:T(8,128)}, f32[8,4,32,128]{3,2,1,0:T(8,128)}, u32[]{:S(2)}, u32[]{:S(2)}) %collective-permute-start.9) | collective-permute-done | bytes 524320 | tf_op jit(solution)/shard_map/ppermute | solution.py:225
  92.0 1.3 collective-permute-start.10
  93.3 1.3 collective-permute-start.8
  94.6 6.9 %collective-permute-done.10.refs_7_ = f32[8,4,32,128]{3,2,1,0:T(8,128)S(1)} collective-permute-done((f32[8,4,32,128]{3,2,1,0:T(8,128)}, f32[8,4,32,128]{3,2,1,0:T(8,128)S(1)}, u32[]{:S(2)}, u32[]{:S(2)}) %collective-permute-start.10) | collective-permute-done | bytes 524320 | tf_op jit(solution)/shard_map/ppermute | solution.py:228
  101.5 0.8 copy-done.8
  102.3 1.3 collective-permute-start.11
  104.4 1.5 collective-permute-start.12
  106.2 3.2 %collective-permute-done.11.refs_8_ = f32[24,4,32,128]{3,2,1,0:T(8,128)} collective-permute-done((f32[24,4,32,128]{3,2,1,0:T(8,128)}, f32[24,4,32,128]{3,2,1,0:T(8,128)}, u32[]{:S(2)}, u32[]{:S(2)}) %collective-permute-start.11) | collective-permute-done | bytes 1572896 | tf_op jit(solution)/shard_map/ppermute | solution.py:228
  109.4 14.9 %leaf_forward.2 = (f32[40,64,128]{2,1,0:T(8,128)S(1)}, bf16[24,384,128]{2,1,0:T(8,128)(2,1)S(1)}, bf16[24,384,128]{2,1,0:T(8,128)(2,1)S(1)}, f32[24,64,128]{2,1,0:T(8,128)S(1)}) custom-call(s32[105]{0:T(128)S(1)} %concatenate.39.refs_0_.meta, f32[32,4,32,128]{3,2,1,0:T(8,128)S(1)} %pad_maximum_fusion.refs_1_, ...), custom_call_target="tpu_custom_call" | custom-call | flops 4000000000 | bytes 8388608 | tf_op jit(solution)/shard_map/leaf_forward/pallas_call | solution.py:289
  124.3 1.3 collective-permute-start.13
  125.6 3.7 %collective-permute-done.13.refs_8_ = f32[8,4,32,128]{3,2,1,0:T(8,128)S(1)} collective-permute-done((f32[8,4,32,128]{3,2,1,0:T(8,128)}, f32[8,4,32,128]{3,2,1,0:T(8,128)S(1)}, u32[]{:S(2)}, u32[]{:S(2)}) %collective-permute-start.13) | collective-permute-done | bytes 524320 | tf_op jit(solution)/shard_map/ppermute | solution.py:228
  129.3 7.1 %leaf_forward.3 = (f32[40,64,128]{2,1,0:T(8,128)}, bf16[8,384,128]{2,1,0:T(8,128)(2,1)S(1)}, bf16[8,384,128]{2,1,0:T(8,128)(2,1)S(1)}, f32[8,64,128]{2,1,0:T(8,128)S(1)}, f32[8,5,8,128]{3,2,1,0:T(8,128)}) custom-call(s32[105]{0:T(128)S(1)} %concatenate.39.refs_0_.meta, f32[32,4,32,128]{3,2,1,0:T(8,128)S(1)} %pad_maximum_fusion.refs_1_, ...), custom_call_target="tpu_custom_call" | custom-call | flops 4000000000 | bytes 8388608 | tf_op jit(solution)/shard_map/leaf_forward/pallas_call | solution.py:289
  136.4 0.9 copy-done.10
  137.3 0.9 copy-done.12
  138.9 3.4 %all-to-all-start = ((f32[8,5,8,128]{3,2,1,0:T(8,128)}), f32[8,5,8,128]{3,2,1,0:T(8,128)S(1)}, u32[]{:S(2)}, u32[]{:S(2)}) async-start(f32[8,5,8,128]{3,2,1,0:T(8,128)} %get-tuple-element.56), calls=%async_computation | async-start | bytes 327680 | tf_op jit(solution)/shard_map/all_to_all | solution.py:325
  142.4 1.6 copy-done.1
  144.0 2.7 %top_prepare.1 = (bf16[8,384,128]{2,1,0:T(8,128)(2,1)S(1)}, bf16[8,384,128]{2,1,0:T(8,128)(2,1)S(1)}, bf16[8,128,128]{2,1,0:T(8,128)(2,1)S(1)}, bf16[8,128,128]{2,1,0:T(8,128)(2,1)S(1)}) custom-call(s32[4]{0:T(128)S(1)} %pad_add_fusion.places, f32[8,4,4,32,128]{4,3,2,1,0:T(8,128)S(1)} %bitcast.32), custom_call_target="tpu_custom_call" | custom-call | tf_op jit(solution)/shard_map/top_prepare/pallas_call | solution.py:313
  146.7 4.1 %all-to-all-done.incoming = f32[8,5,8,128]{3,2,1,0:T(8,128)S(1)} async-done(((f32[8,5,8,128]{3,2,1,0:T(8,128)}), f32[8,5,8,128]{3,2,1,0:T(8,128)S(1)}, u32[]{:S(2)}, u32[]{:S(2)}) %all-to-all-start) | async-done | bytes 163872 | tf_op jit(solution)/shard_map/all_to_all | solution.py:325
  150.9 2.7 %top_solve.1 = f32[8,5,8,128]{3,2,1,0:T(8,128)S(1)} custom-call(f32[8,5,8,128]{3,2,1,0:T(8,128)S(1)} %all-to-all-done.incoming, bf16[8,384,128]{2,1,0:T(8,128)(2,1)S(1)} %get-tuple-element.59.high, bf16[8,384,128]{2,1,0:T(8,128)(2,1)S(1)} %get-tuple-element.60.low, bf16[8,128,128]{2,1,0:T(8,128)(2,1)S(1)} %get-tuple-element.61.inverse_high, ...), custom_call_target="tpu_custom_call" | custom-call | tf_op jit(solution)/shard_map/top_solve/pallas_call | solution.py:326
  153.6 8.6 %all_to_all.10.state = f32[8,5,8,128]{3,2,1,0:T(8,128)S(1)} all-to-all(f32[8,5,8,128]{3,2,1,0:T(8,128)S(1)} %top_solve.1), channel_id=1, replica_groups=mesh['xy'=4,'core'=2,'zh'=2,'zl'=2] {'xy','zh'}, dimensions={0} | all-to-all | bytes 327680 | tf_op jit(solution)/shard_map/all_to_all | solution.py:334
  162.2 2.1 %leaf_backward.4 = (f32[8,64,128]{2,1,0:T(8,128)S(1)}, f32[40,64,128]{2,1,0:T(8,128)S(1)}) custom-call(s32[105]{0:T(128)S(1)} %concatenate.39.refs_0_.meta, bf16[8,384,128]{2,1,0:T(8,128)(2,1)S(1)} %copy-done.11, bf16[8,384,128]{2,1,0:T(8,128)(2,1)S(1)} %copy-done.13, f32[8,64,128]{2,1,0:T(8,128)S(1)} %copy-done.15, f32[8,5,8,128]{3,2,1,0:T(8,128)S(1)} %all_to_all.10.state), custom_call_target="tpu_custom_call" | custom-call | flops 4000000000 | bytes 8388608 | tf_op jit(solution)/shard_map/leaf_backward/pallas_call | solution.py:347
  164.7 2.1 %leaf_backward.5 = (f32[8,64,128]{2,1,0:T(8,128)S(1)}, f32[40,64,128]{2,1,0:T(8,128)S(1)}) custom-call(s32[105]{0:T(128)S(1)} %concatenate.39.refs_0_.meta, bf16[24,384,128]{2,1,0:T(8,128)(2,1)S(1)} %copy-done.3, bf16[24,384,128]{2,1,0:T(8,128)(2,1)S(1)} %copy-done.5, f32[24,64,128]{2,1,0:T(8,128)S(1)} %copy-done.7, f32[40,64,128]{2,1,0:T(8,128)S(1)} %get-tuple-element.63.state), custom_call_target="tpu_custom_call" | custom-call | flops 4000000000 | bytes 8388608 | tf_op jit(solution)/shard_map/leaf_backward/pallas_call | solution.py:347
  166.8 2.1 %leaf_backward.6 = (f32[8,64,128]{2,1,0:T(8,128)S(1)}, f32[40,64,128]{2,1,0:T(8,128)S(1)}) custom-call(s32[105]{0:T(128)S(1)} %concatenate.39.refs_0_.meta, bf16[24,384,128]{2,1,0:T(8,128)(2,1)S(1)} %copy-done.3, bf16[24,384,128]{2,1,0:T(8,128)(2,1)S(1)} %copy-done.5, f32[24,64,128]{2,1,0:T(8,128)S(1)} %copy-done.7, f32[40,64,128]{2,1,0:T(8,128)S(1)} %get-tuple-element.64.state), custom_call_target="tpu_custom_call" | custom-call | flops 4000000000 | bytes 8388608 | tf_op jit(solution)/shard_map/leaf_backward/pallas_call | solution.py:347
  169.0 4.2 %collective-permute-start.15 = (f32[16,64,128]{2,1,0:T(8,128)S(1)}, f32[16,64,128]{2,1,0:T(8,128)S(1)}, u32[]{:S(2)}, u32[]{:S(2)}) collective-permute-start(f32[16,64,128]{2,1,0:T(8,128)S(1)} %pad_maximum_fusion.4), channel_id=1, source_target_pairs={{0,0},{2,4},{4,2},{6,6},{1,1},{3,5},{5,3},{7,7},{8,8},{10,12},{12,... | collective-permute-start | bytes 1572872 | tf_op jit(solution)/shard_map/ppermute | solution.py:222
  173.3 2.2 %collective-permute-start.16 = (f32[9,64,128]{2,1,0:T(8,128)S(1)}, f32[9,64,128]{2,1,0:T(8,128)S(1)}, u32[]{:S(2)}, u32[]{:S(2)}) collective-permute-start(f32[9,64,128]{2,1,0:T(8,128)S(1)} %pad_maximum_fusion.5), channel_id=1, source_target_pairs={{0,0},{2,4},{4,2},{6,6},{1,1},{3,5},{5,3},{7,7},{8,8},{10,12},{12,... | collective-permute-start | bytes 884744 | tf_op jit(solution)/shard_map/ppermute | solution.py:222
  175.6 3.2 %leaf_backward.7 = (f32[8,64,128]{2,1,0:T(8,128)S(1)}, f32[40,64,128]{2,1,0:T(8,128)}) custom-call(s32[105]{0:T(128)S(1)} %concatenate.39.refs_0_.meta, bf16[24,384,128]{2,1,0:T(8,128)(2,1)S(1)} %copy-done.3, bf16[24,384,128]{2,1,0:T(8,128)(2,1)S(1)} %copy-done.5, f32[24,64,128]{2,1,0:T(8,128)S(1)} %copy-done.7, f32[40,64,128]{2,1,0:T(8,128)S(1)} %get-tuple-element.65.state), custom_call_target="tpu_custom_call" | custom-call | flops 4000000000 | bytes 8388608 | tf_op jit(solution)/shard_map/leaf_backward/pallas_call | solution.py:347
  178.8 4.2 %collective-permute-start.14 = (f32[8,64,128]{2,1,0:T(8,128)S(1)}, f32[8,64,128]{2,1,0:T(8,128)S(1)}, u32[]{:S(2)}, u32[]{:S(2)}) collective-permute-start(f32[8,64,128]{2,1,0:T(8,128)S(1)} %get-tuple-element.66), channel_id=1, source_target_pairs={{0,0},{2,4},{4,2},{6,6},{1,1},{3,5},{5,3},{7,7},{8,8},{10,12},{12,... | collective-permute-start | bytes 786440 | tf_op jit(solution)/shard_map/ppermute | solution.py:222
  183.0 11.7 %collective-permute-done.16 = f32[9,64,128]{2,1,0:T(8,128)S(1)} collective-permute-done((f32[9,64,128]{2,1,0:T(8,128)S(1)}, f32[9,64,128]{2,1,0:T(8,128)S(1)}, u32[]{:S(2)}, u32[]{:S(2)}) %collective-permute-start.16) | collective-permute-done | bytes 294944 | tf_op jit(solution)/shard_map/ppermute | solution.py:222
  195.4 2.2 %collective-permute-done.14 = f32[8,64,128]{2,1,0:T(8,128)S(1)} collective-permute-done((f32[8,64,128]{2,1,0:T(8,128)S(1)}, f32[8,64,128]{2,1,0:T(8,128)S(1)}, u32[]{:S(2)}, u32[]{:S(2)}) %collective-permute-start.14) | collective-permute-done | bytes 262176 | tf_op jit(solution)/shard_map/ppermute | solution.py:222
  197.6 1.1 pad_maximum_fusion.2
  (69 shorter events, 5.8 us)
Async XLA Ops:
  7.2 1.6 copy-start
  7.2 8.8 %copy-start.18 = (f32[32,64,128]{2,1,0:T(8,128)S(1)}, f32[32,64,128]{2,1,0:T(8,128)}, u32[]{:S(2)}) copy-start(f32[32,64,128]{2,1,0:T(8,128)} %param.11) | copy-start | bytes 3145732
  7.2 135.2 %all-gather.3.cloned.1.call-start = ((), (), s32[]{:S(2)}) async-start(), calls=%async_computation.2 | async-start | bytes 2359296 | tf_op jit(solution)/shard_map/all_gather | solution.py:260
  10.1 7.7 %copy-start.16 = (f32[32,3,32,128]{3,2,1,0:T(8,128)S(1)}, f32[32,3,32,128]{3,2,1,0:T(8,128)}, u32[]{:S(2)}) copy-start(f32[32,3,32,128]{3,2,1,0:T(8,128)} %param.13) | copy-start | bytes 4718596
  10.1 7.7 %copy-start.17 = (f32[32,32,128]{2,1,0:T(8,128)S(1)}, f32[32,32,128]{2,1,0:T(8,128)}, u32[]{:S(2)}) copy-start(f32[32,32,128]{2,1,0:T(8,128)} %param.14) | copy-start | bytes 1572868
  10.1 7.9 %collective-permute-start = (f32[4,32,128]{2,1,0:T(8,128)S(1)}, f32[4,32,128]{2,1,0:T(8,128)S(1)}, u32[]{:S(2)}, u32[]{:S(2)}) collective-permute-start(f32[4,32,128]{2,1,0:T(8,128)S(1)} %get-tuple-element.71), channel_id=1, source_target_pairs={{0,2},{2,0},{1,3},{3,1},{4,6},{6,4},{5,7},{7,5},{8,10},{10,8},{9,1... | collective-permute-start | bytes 196616 | tf_op jit(solution)/shard_map/ppermute | solution.py:235
  18.0 1.4 slice-start
  18.1 2.7 %slice-start.1 = ((f32[32,3,32,128]{3,2,1,0:T(8,128)}), f32[8,3,32,128]{3,2,1,0:T(8,128)S(1)}, s32[]{:S(2)}) async-start(f32[32,3,32,128]{3,2,1,0:T(8,128)} %param.13), calls=%async_computation.4 | async-start | bytes 786432 | tf_op jit(solution)/shard_map/slice | solution.py:248
  18.1 3.9 %collective-permute-start.1 = (f32[2,4,32,128]{3,2,1,0:T(8,128)S(1)}, f32[2,4,32,128]{3,2,1,0:T(8,128)S(1)}, u32[]{:S(2)}, u32[]{:S(2)}) collective-permute-start(f32[2,4,32,128]{3,2,1,0:T(8,128)S(1)} %pad_maximum_fusion.7), channel_id=1, source_target_pairs={{0,1},{1,0},{2,3},{3,2},{4,5},{5,4},{6,7},{7,6},{8,9},{9,8},{10,11... | collective-permute-start | bytes 393224 | tf_op jit(solution)/shard_map/ppermute | solution.py:235
  22.7 34.8 %collective-permute-start.4 = (f32[24,4,32,128]{3,2,1,0:T(8,128)}, f32[24,4,32,128]{3,2,1,0:T(8,128)}, u32[]{:S(2)}, u32[]{:S(2)}) collective-permute-start(f32[24,4,32,128]{3,2,1,0:T(8,128)} %pad_maximum_fusion.1), channel_id=1, source_target_pairs={{2,0},{4,6},{3,1},{5,7},{10,8},{12,14},{11,9},{13,15},{18,16},{20,... | collective-permute-start | bytes 4718600 | tf_op jit(solution)/shard_map/ppermute | solution.py:225
  27.4 46.4 %collective-permute-start.3 = (f32[32,4,32,128]{3,2,1,0:T(8,128)S(1)}, f32[32,4,32,128]{3,2,1,0:T(8,128)}, u32[]{:S(2)}, u32[]{:S(2)}) collective-permute-start(f32[32,4,32,128]{3,2,1,0:T(8,128)S(1)} %pad_maximum_fusion.refs_1_), channel_id=1, source_target_pairs={{0,1},{1,0},{6,7},{7,6},{8,9},{9,8},{14,15},{15,14},{16,17},{17,16... | collective-permute-start | bytes 6291464 | tf_op jit(solution)/shard_map/ppermute | solution.py:231
  29.5 62.5 %collective-permute-start.2 = (f32[2120,128]{1,0:T(8,128)}, f32[2120,128]{1,0:T(8,128)S(1)}, u32[]{:S(2)}, u32[]{:S(2)}) collective-permute-start(f32[2120,128]{1,0:T(8,128)} %select_maximum_fusion), channel_id=1, source_target_pairs={{0,0},{2,4},{4,2},{6,6},{1,1},{3,5},{5,3},{7,7},{8,8},{10,12},{12,... | collective-permute-start | bytes 3256328 | tf_op jit(solution)/shard_map/ppermute | solution.py:222
  57.5 44.8 %collective-permute-start.5 = (f32[24,4,32,128]{3,2,1,0:T(8,128)}, f32[24,4,32,128]{3,2,1,0:T(8,128)}, u32[]{:S(2)}, u32[]{:S(2)}) collective-permute-start(f32[24,4,32,128]{3,2,1,0:T(8,128)} %collective-permute-done.4.refs_3_), channel_id=1, source_target_pairs={{0,1},{1,0},{6,7},{7,6},{8,9},{9,8},{14,15},{15,14},{16,17},{17,16... | collective-permute-start | bytes 4718600 | tf_op jit(solution)/shard_map/ppermute | solution.py:231
  59.3 32.7 %collective-permute-start.9 = (f32[8,4,32,128]{3,2,1,0:T(8,128)}, f32[8,4,32,128]{3,2,1,0:T(8,128)}, u32[]{:S(2)}, u32[]{:S(2)}) collective-permute-start(f32[8,4,32,128]{3,2,1,0:T(8,128)} %pad_maximum_fusion.3), channel_id=1, source_target_pairs={{2,0},{4,6},{3,1},{5,7},{10,8},{12,14},{11,9},{13,15},{18,16},{20,... | collective-permute-start | bytes 1572872 | tf_op jit(solution)/shard_map/ppermute | solution.py:225
  72.5 31.8 %collective-permute-start.6 = (f32[32,4,32,128]{3,2,1,0:T(8,128)S(1)}, f32[32,4,32,128]{3,2,1,0:T(8,128)}, u32[]{:S(2)}, u32[]{:S(2)}) collective-permute-start(f32[32,4,32,128]{3,2,1,0:T(8,128)S(1)} %pad_maximum_fusion.refs_1_), channel_id=1, source_target_pairs={{0,4},{6,2},{1,5},{7,3},{8,12},{14,10},{9,13},{15,11},{16,20},{22,... | collective-permute-start | bytes 6291464 | tf_op jit(solution)/shard_map/ppermute | solution.py:228
  73.8 30.6 %collective-permute-start.7 = (f32[32,4,32,128]{3,2,1,0:T(8,128)}, f32[32,4,32,128]{3,2,1,0:T(8,128)}, u32[]{:S(2)}, u32[]{:S(2)}) collective-permute-start(f32[32,4,32,128]{3,2,1,0:T(8,128)} %collective-permute-done.3.refs_2_), channel_id=1, source_target_pairs={{0,4},{6,2},{1,5},{7,3},{8,12},{14,10},{9,13},{15,11},{16,20},{22,... | collective-permute-start | bytes 6291464 | tf_op jit(solution)/shard_map/ppermute | solution.py:228
  92.0 9.5 %collective-permute-start.10 = (f32[8,4,32,128]{3,2,1,0:T(8,128)}, f32[8,4,32,128]{3,2,1,0:T(8,128)S(1)}, u32[]{:S(2)}, u32[]{:S(2)}) collective-permute-start(f32[8,4,32,128]{3,2,1,0:T(8,128)} %collective-permute-done.9.refs_3_), channel_id=1, source_target_pairs={{0,4},{6,2},{1,5},{7,3},{8,12},{14,10},{9,13},{15,11},{16,20},{22,... | collective-permute-start | bytes 1572872 | tf_op jit(solution)/shard_map/ppermute | solution.py:228
  93.3 11.1 %collective-permute-start.8 = (f32[24,4,32,128]{3,2,1,0:T(8,128)}, f32[24,4,32,128]{3,2,1,0:T(8,128)}, u32[]{:S(2)}, u32[]{:S(2)}) collective-permute-start(f32[24,4,32,128]{3,2,1,0:T(8,128)} %collective-permute-done.4.refs_3_), channel_id=1, source_target_pairs={{0,4},{6,2},{1,5},{7,3},{8,12},{14,10},{9,13},{15,11},{16,20},{22,... | collective-permute-start | bytes 4718600 | tf_op jit(solution)/shard_map/ppermute | solution.py:228
  101.5 0.8 copy-start.8
  102.3 7.1 %collective-permute-start.11 = (f32[24,4,32,128]{3,2,1,0:T(8,128)}, f32[24,4,32,128]{3,2,1,0:T(8,128)}, u32[]{:S(2)}, u32[]{:S(2)}) collective-permute-start(f32[24,4,32,128]{3,2,1,0:T(8,128)} %collective-permute-done.5.refs_4_), channel_id=1, source_target_pairs={{0,4},{6,2},{1,5},{7,3},{8,12},{14,10},{9,13},{15,11},{16,20},{22,... | collective-permute-start | bytes 4718600 | tf_op jit(solution)/shard_map/ppermute | solution.py:228
  104.4 19.9 %collective-permute-start.12 = (f32[8,4,32,128]{3,2,1,0:T(8,128)}, f32[8,4,32,128]{3,2,1,0:T(8,128)}, u32[]{:S(2)}, u32[]{:S(2)}) collective-permute-start(f32[8,4,32,128]{3,2,1,0:T(8,128)} %collective-permute-done.9.refs_3_), channel_id=1, source_target_pairs={{0,1},{1,0},{6,7},{7,6},{8,9},{9,8},{14,15},{15,14},{16,17},{17,16... | collective-permute-start | bytes 1572872 | tf_op jit(solution)/shard_map/ppermute | solution.py:231
  106.2 23.1 %copy-start.9 = (f32[8,4,32,128]{3,2,1,0:T(8,128)S(1)}, f32[8,4,32,128]{3,2,1,0:T(8,128)}, u32[]{:S(2)}) copy-start(f32[8,4,32,128]{3,2,1,0:T(8,128)} %copy-done.8) | copy-start | bytes 1572868
  124.3 12.1 %copy-start.2 = (bf16[24,384,128]{2,1,0:T(8,128)(2,1)}, bf16[24,384,128]{2,1,0:T(8,128)(2,1)S(1)}, u32[]{:S(2)}) copy-start(bf16[24,384,128]{2,1,0:T(8,128)(2,1)S(1)} %get-tuple-element.47.high) | copy-start | bytes 7077892
  124.3 12.1 %copy-start.4 = (bf16[24,384,128]{2,1,0:T(8,128)(2,1)}, bf16[24,384,128]{2,1,0:T(8,128)(2,1)S(1)}, u32[]{:S(2)}) copy-start(bf16[24,384,128]{2,1,0:T(8,128)(2,1)S(1)} %get-tuple-element.48.low) | copy-start | bytes 7077892
  124.3 12.1 %copy-start.6 = (f32[24,64,128]{2,1,0:T(8,128)}, f32[24,64,128]{2,1,0:T(8,128)S(1)}, u32[]{:S(2)}) copy-start(f32[24,64,128]{2,1,0:T(8,128)S(1)} %get-tuple-element.49.scaled) | copy-start | bytes 2359300
  124.3 5.0 %collective-permute-start.13 = (f32[8,4,32,128]{3,2,1,0:T(8,128)}, f32[8,4,32,128]{3,2,1,0:T(8,128)S(1)}, u32[]{:S(2)}, u32[]{:S(2)}) collective-permute-start(f32[8,4,32,128]{3,2,1,0:T(8,128)} %collective-permute-done.12.refs_4_), channel_id=1, source_target_pairs={{0,4},{6,2},{1,5},{7,3},{8,12},{14,10},{9,13},{15,11},{16,20},{22,... | collective-permute-start | bytes 1572872 | tf_op jit(solution)/shard_map/ppermute | solution.py:228
  136.4 0.9 copy-start.10
  137.3 0.9 copy-start.12
  138.2 0.7 copy-start.14
  138.9 12.0 %all-to-all-start = ((f32[8,5,8,128]{3,2,1,0:T(8,128)}), f32[8,5,8,128]{3,2,1,0:T(8,128)S(1)}, u32[]{:S(2)}, u32[]{:S(2)}) async-start(f32[8,5,8,128]{3,2,1,0:T(8,128)} %get-tuple-element.56), calls=%async_computation | async-start | bytes 327680 | tf_op jit(solution)/shard_map/all_to_all | solution.py:325
  142.4 1.6 copy-start.1
  150.8 11.3 %copy-start.11 = (bf16[8,384,128]{2,1,0:T(8,128)(2,1)S(1)}, bf16[8,384,128]{2,1,0:T(8,128)(2,1)}, u32[]{:S(2)}) copy-start(bf16[8,384,128]{2,1,0:T(8,128)(2,1)} %copy-done.10) | copy-start | bytes 2359300
  150.8 11.3 %copy-start.13 = (bf16[8,384,128]{2,1,0:T(8,128)(2,1)S(1)}, bf16[8,384,128]{2,1,0:T(8,128)(2,1)}, u32[]{:S(2)}) copy-start(bf16[8,384,128]{2,1,0:T(8,128)(2,1)} %copy-done.12) | copy-start | bytes 2359300
  150.8 11.3 %copy-start.15 = (f32[8,64,128]{2,1,0:T(8,128)S(1)}, f32[8,64,128]{2,1,0:T(8,128)}, u32[]{:S(2)}) copy-start(f32[8,64,128]{2,1,0:T(8,128)} %copy-done.14) | copy-start | bytes 786436
  162.2 2.2 %copy-start.3 = (bf16[24,384,128]{2,1,0:T(8,128)(2,1)S(1)}, bf16[24,384,128]{2,1,0:T(8,128)(2,1)}, u32[]{:S(2)}) copy-start(bf16[24,384,128]{2,1,0:T(8,128)(2,1)} %copy-done.2) | copy-start | bytes 7077892
  162.2 2.4 %copy-start.5 = (bf16[24,384,128]{2,1,0:T(8,128)(2,1)S(1)}, bf16[24,384,128]{2,1,0:T(8,128)(2,1)}, u32[]{:S(2)}) copy-start(bf16[24,384,128]{2,1,0:T(8,128)(2,1)} %copy-done.4) | copy-start | bytes 7077892
  162.2 2.5 %copy-start.7 = (f32[24,64,128]{2,1,0:T(8,128)S(1)}, f32[24,64,128]{2,1,0:T(8,128)}, u32[]{:S(2)}) copy-start(f32[24,64,128]{2,1,0:T(8,128)} %copy-done.6) | copy-start | bytes 2359300
  169.0 28.5 %collective-permute-start.15 = (f32[16,64,128]{2,1,0:T(8,128)S(1)}, f32[16,64,128]{2,1,0:T(8,128)S(1)}, u32[]{:S(2)}, u32[]{:S(2)}) collective-permute-start(f32[16,64,128]{2,1,0:T(8,128)S(1)} %pad_maximum_fusion.4), channel_id=1, source_target_pairs={{0,0},{2,4},{4,2},{6,6},{1,1},{3,5},{5,3},{7,7},{8,8},{10,12},{12,... | collective-permute-start | bytes 1572872 | tf_op jit(solution)/shard_map/ppermute | solution.py:222
  173.3 21.4 %collective-permute-start.16 = (f32[9,64,128]{2,1,0:T(8,128)S(1)}, f32[9,64,128]{2,1,0:T(8,128)S(1)}, u32[]{:S(2)}, u32[]{:S(2)}) collective-permute-start(f32[9,64,128]{2,1,0:T(8,128)S(1)} %pad_maximum_fusion.5), channel_id=1, source_target_pairs={{0,0},{2,4},{4,2},{6,6},{1,1},{3,5},{5,3},{7,7},{8,8},{10,12},{12,... | collective-permute-start | bytes 884744 | tf_op jit(solution)/shard_map/ppermute | solution.py:222
  178.8 18.8 %collective-permute-start.14 = (f32[8,64,128]{2,1,0:T(8,128)S(1)}, f32[8,64,128]{2,1,0:T(8,128)S(1)}, u32[]{:S(2)}, u32[]{:S(2)}) collective-permute-start(f32[8,64,128]{2,1,0:T(8,128)S(1)} %get-tuple-element.66), channel_id=1, source_target_pairs={{0,0},{2,4},{4,2},{6,6},{1,1},{3,5},{5,3},{7,7},{8,8},{10,12},{12,... | collective-permute-start | bytes 786440 | tf_op jit(solution)/shard_map/ppermute | solution.py:222
Sparse Core Ops, SparseCore 0:
  92.1 34.6 all-gather.2

commit v9 on v6

--- a/solution.py
+++ b/solution.py
@@ -339,7 +339,7 @@
             name="leaf_backward",
         )(meta, *factors[held], state)
     late = swap(found[-1])
-    middle = swap(jnp.concatenate(found[1:-1] + [own_top], axis=0))
+    middle = swap(after(late, jnp.concatenate(found[1:-1] + [own_top], axis=0)))
     first = swap(found[0])
     leaf_solution = jnp.concatenate([first, middle[:-1], late], axis=0)
     return (leaf_solution, middle[-1:])

time: 202 us -> 207 us (1.025)
  waiting for transfers between devices: 72.3 us -> 78 us
    ppermute x4, waiting for transfers between devices: 13.9 us -> 19.6 us  [swap(): return lax.ppermute(value, ('core', 'zh'), [(0, 0), (1, 2), (2, 1), (3, 3)])]
  transfers between devices with their start and end apart: 19 -> 19, of which waited for: 11 -> 11; matrix products, arithmetic and copies ran while one was open for 4% -> 4% of each run, Pallas kernels for 12% -> 11%
where the time goes in v9:
time: 207 us; the launch traced here: 206 us
  waiting for transfers between devices  78 us (38%)
  starting transfers between devices  54.6 us (26%)
  Pallas kernels  32.3 us (16%)
  between operations  14.4 us (7%)
  local copies, waits for them, and re-layouts  9.43 us (5%)
  other arithmetic  9.06 us (4%)
  blocking collectives  8.6 us (4%)
    ppermute x2, waiting for transfers between devices, to_keeper(): return lax.ppermute(value, ('core', 'zh'), [(1, 0), (2, 3)])  40 us
    ppermute x4, waiting for transfers between devices, swap(): return lax.ppermute(value, ('core', 'zh'), [(0, 0), (1, 2), (2, 1), (3, 3)])  19.6 us
    ppermute x2, starting transfers between devices, to_keeper(): return lax.ppermute(value, ('core', 'zh'), [(1, 0), (2, 3)])  18 us
    pallas_call x2, Pallas kernels, local(): pl.pallas_call(functools.partial(forward_kernel, base, leafs, k == 0, las...  17.2 us
    ppermute x4, starting transfers between devices, swap(): return lax.ppermute(value, ('core', 'zh'), [(0, 0), (1, 2), (2, 1), (3, 3)])  15.5 us
    ppermute x6, waiting for transfers between devices, to_trader(): return lax.ppermute(value, ('core', 'zh'), [(0, 2), (3, 1)])  13.9 us
    pallas_call x4, Pallas kernels, local(): pl.pallas_call(functools.partial(backward_kernel, k * turn, k == TURNS -...  9.64 us
    all_to_all x1, blocking collectives, local(): lax.all_to_all(outgoing, ('xy', 'zh'), split_axis=0, concat_axis=0, tiled...  8.6 us
  transfers between devices with their start and end apart: 19, of which 11 were waited for; matrix products, arithmetic and copies ran while one was open for 4% of the time, Pallas kernels for 11%

profile of v9, /device:TPU:1, one launch (start us, length us, event | category | flops | bytes accessed | tf_op | source)
XLA Modules:
  0.0 206.4 jit_solution(8260211161383685541)
XLA Ops:
  7.2 0.8 fusion.1
  9.4 0.7 fusion.2
  10.1 3.2 %collective-permute-start = (f32[4,32,128]{2,1,0:T(8,128)S(1)}, f32[4,32,128]{2,1,0:T(8,128)S(1)}, u32[]{:S(2)}, u32[]{:S(2)}) collective-permute-start(f32[4,32,128]{2,1,0:T(8,128)S(1)} %get-tuple-element.73), channel_id=1, source_target_pairs={{0,2},{2,0},{1,3},{3,1},{4,6},{6,4},{5,7},{7,5},{8,10},{10,8},{9,1... | collective-permute-start | bytes 196616 | tf_op jit(solution)/shard_map/ppermute | solution.py:222
  13.3 1.0 slice_bitcast_fusion
  14.4 0.9 slice_bitcast_fusion.1
  16.0 1.8 select_maximum_fusion
  18.1 1.4 collective-permute-start.1
  19.4 1.3 pad_maximum_fusion.1
  20.7 0.8 pad_maximum_fusion.4
  22.7 4.7 %collective-permute-start.4 = (f32[24,4,32,128]{3,2,1,0:T(8,128)}, f32[24,4,32,128]{3,2,1,0:T(8,128)}, u32[]{:S(2)}, u32[]{:S(2)}) collective-permute-start(f32[24,4,32,128]{3,2,1,0:T(8,128)} %pad_maximum_fusion.1), channel_id=1, source_target_pairs={{2,0},{4,6},{3,1},{5,7},{10,8},{12,14},{11,9},{13,15},{18,16},{20,... | collective-permute-start | bytes 4718600 | tf_op jit(solution)/shard_map/ppermute | solution.py:212
  27.4 2.1 %collective-permute-start.3 = (f32[32,4,32,128]{3,2,1,0:T(8,128)S(1)}, f32[32,4,32,128]{3,2,1,0:T(8,128)}, u32[]{:S(2)}, u32[]{:S(2)}) collective-permute-start(f32[32,4,32,128]{3,2,1,0:T(8,128)S(1)} %pad_maximum_fusion.refs_1_), channel_id=1, source_target_pairs={{0,1},{1,0},{6,7},{7,6},{8,9},{9,8},{14,15},{15,14},{16,17},{17,16... | collective-permute-start | bytes 6291464 | tf_op jit(solution)/shard_map/ppermute | solution.py:218
  29.5 4.9 %collective-permute-start.2 = (f32[2120,128]{1,0:T(8,128)}, f32[2120,128]{1,0:T(8,128)S(1)}, u32[]{:S(2)}, u32[]{:S(2)}) collective-permute-start(f32[2120,128]{1,0:T(8,128)} %select_maximum_fusion), channel_id=1, source_target_pairs={{0,0},{2,4},{4,2},{6,6},{1,1},{3,5},{5,3},{7,7},{8,8},{10,12},{12,... | collective-permute-start | bytes 3256328 | tf_op jit(solution)/shard_map/ppermute | solution.py:209
  34.4 23.1 %collective-permute-done.4.refs_3_ = f32[24,4,32,128]{3,2,1,0:T(8,128)} collective-permute-done((f32[24,4,32,128]{3,2,1,0:T(8,128)}, f32[24,4,32,128]{3,2,1,0:T(8,128)}, u32[]{:S(2)}, u32[]{:S(2)}) %collective-permute-start.4) | collective-permute-done | bytes 1572896 | tf_op jit(solution)/shard_map/ppermute | solution.py:212
  57.5 1.8 collective-permute-start.5
  59.3 13.3 %collective-permute-start.9 = (f32[8,4,32,128]{3,2,1,0:T(8,128)}, f32[8,4,32,128]{3,2,1,0:T(8,128)}, u32[]{:S(2)}, u32[]{:S(2)}) collective-permute-start(f32[8,4,32,128]{3,2,1,0:T(8,128)} %pad_maximum_fusion.4), channel_id=1, source_target_pairs={{2,0},{4,6},{3,1},{5,7},{10,8},{12,14},{11,9},{13,15},{18,16},{20,... | collective-permute-start | bytes 1572872 | tf_op jit(solution)/shard_map/ppermute | solution.py:212
  72.5 1.3 collective-permute-start.6
  73.8 1.3 collective-permute-start.7
  75.1 16.8 %collective-permute-done.9.refs_3_ = f32[8,4,32,128]{3,2,1,0:T(8,128)} collective-permute-done((f32[8,4,32,128]{3,2,1,0:T(8,128)}, f32[8,4,32,128]{3,2,1,0:T(8,128)}, u32[]{:S(2)}, u32[]{:S(2)}) %collective-permute-start.9) | collective-permute-done | bytes 524320 | tf_op jit(solution)/shard_map/ppermute | solution.py:212
  92.0 1.3 collective-permute-start.10
  93.3 1.3 collective-permute-start.8
  94.6 6.9 %collective-permute-done.10.refs_7_ = f32[8,4,32,128]{3,2,1,0:T(8,128)S(1)} collective-permute-done((f32[8,4,32,128]{3,2,1,0:T(8,128)}, f32[8,4,32,128]{3,2,1,0:T(8,128)S(1)}, u32[]{:S(2)}, u32[]{:S(2)}) %collective-permute-start.10) | collective-permute-done | bytes 524320 | tf_op jit(solution)/shard_map/ppermute | solution.py:215
  101.5 0.8 copy-done.8
  102.3 1.3 collective-permute-start.11
  104.4 1.5 collective-permute-start.12
  106.2 3.2 %collective-permute-done.11.refs_8_ = f32[24,4,32,128]{3,2,1,0:T(8,128)} collective-permute-done((f32[24,4,32,128]{3,2,1,0:T(8,128)}, f32[24,4,32,128]{3,2,1,0:T(8,128)}, u32[]{:S(2)}, u32[]{:S(2)}) %collective-permute-start.11) | collective-permute-done | bytes 1572896 | tf_op jit(solution)/shard_map/ppermute | solution.py:215
  109.4 11.4 %leaf_forward.2 = (f32[40,64,128]{2,1,0:T(8,128)S(1)}, bf16[24,384,128]{2,1,0:T(8,128)(2,1)S(1)}, bf16[24,384,128]{2,1,0:T(8,128)(2,1)S(1)}, f32[24,64,128]{2,1,0:T(8,128)S(1)}) custom-call(s32[105]{0:T(128)S(1)} %concatenate.36.refs_0_.meta, f32[32,4,32,128]{3,2,1,0:T(8,128)S(1)} %pad_maximum_fusion.refs_1_, ...), custom_call_target="tpu_custom_call" | custom-call | flops 4000000000 | bytes 8388608 | tf_op jit(solution)/shard_map/leaf_forward/pallas_call | solution.py:276
  120.9 1.3 collective-permute-start.13
  122.2 3.7 %collective-permute-done.13.refs_8_ = f32[8,4,32,128]{3,2,1,0:T(8,128)S(1)} collective-permute-done((f32[8,4,32,128]{3,2,1,0:T(8,128)}, f32[8,4,32,128]{3,2,1,0:T(8,128)S(1)}, u32[]{:S(2)}, u32[]{:S(2)}) %collective-permute-start.13) | collective-permute-done | bytes 524320 | tf_op jit(solution)/shard_map/ppermute | solution.py:215
  125.8 5.8 %leaf_forward.3 = (f32[40,64,128]{2,1,0:T(8,128)}, bf16[8,384,128]{2,1,0:T(8,128)(2,1)S(1)}, bf16[8,384,128]{2,1,0:T(8,128)(2,1)S(1)}, f32[8,64,128]{2,1,0:T(8,128)S(1)}, f32[8,5,8,128]{3,2,1,0:T(8,128)}) custom-call(s32[105]{0:T(128)S(1)} %concatenate.36.refs_0_.meta, f32[32,4,32,128]{3,2,1,0:T(8,128)S(1)} %pad_maximum_fusion.refs_1_, ...), custom_call_target="tpu_custom_call" | custom-call | flops 4000000000 | bytes 8388608 | tf_op jit(solution)/shard_map/leaf_forward/pallas_call | solution.py:276
  131.6 0.9 copy-done.10
  132.5 0.9 copy-done.12
  134.1 3.4 %all-to-all-start = ((f32[8,5,8,128]{3,2,1,0:T(8,128)}), f32[8,5,8,128]{3,2,1,0:T(8,128)S(1)}, u32[]{:S(2)}, u32[]{:S(2)}) async-start(f32[8,5,8,128]{3,2,1,0:T(8,128)} %get-tuple-element.57), calls=%async_computation | async-start | bytes 327680 | tf_op jit(solution)/shard_map/all_to_all | solution.py:309
  137.6 1.6 copy-done.1
  139.2 2.7 %top_prepare.1 = (bf16[8,384,128]{2,1,0:T(8,128)(2,1)S(1)}, bf16[8,384,128]{2,1,0:T(8,128)(2,1)S(1)}, bf16[8,128,128]{2,1,0:T(8,128)(2,1)S(1)}, bf16[8,128,128]{2,1,0:T(8,128)(2,1)S(1)}) custom-call(s32[4]{0:T(128)S(1)} %pad_add_fusion.places, f32[8,4,4,32,128]{4,3,2,1,0:T(8,128)S(1)} %bitcast.32), custom_call_target="tpu_custom_call" | custom-call | tf_op jit(solution)/shard_map/top_prepare/pallas_call | solution.py:297
  141.9 4.1 %all-to-all-done.incoming = f32[8,5,8,128]{3,2,1,0:T(8,128)S(1)} async-done(((f32[8,5,8,128]{3,2,1,0:T(8,128)}), f32[8,5,8,128]{3,2,1,0:T(8,128)S(1)}, u32[]{:S(2)}, u32[]{:S(2)}) %all-to-all-start) | async-done | bytes 163872 | tf_op jit(solution)/shard_map/all_to_all | solution.py:309
  146.1 2.7 %top_solve.1 = f32[8,5,8,128]{3,2,1,0:T(8,128)S(1)} custom-call(f32[8,5,8,128]{3,2,1,0:T(8,128)S(1)} %all-to-all-done.incoming, bf16[8,384,128]{2,1,0:T(8,128)(2,1)S(1)} %get-tuple-element.60.high, bf16[8,384,128]{2,1,0:T(8,128)(2,1)S(1)} %get-tuple-element.61.low, bf16[8,128,128]{2,1,0:T(8,128)(2,1)S(1)} %get-tuple-element.62.inverse_high, ...), custom_call_target="tpu_custom_call" | custom-call | tf_op jit(solution)/shard_map/top_solve/pallas_call | solution.py:310
  148.8 8.6 %all_to_all.10.state = f32[8,5,8,128]{3,2,1,0:T(8,128)S(1)} all-to-all(f32[8,5,8,128]{3,2,1,0:T(8,128)S(1)} %top_solve.1), channel_id=1, replica_groups=mesh['xy'=4,'core'=2,'zh'=2,'zl'=2] {'xy','zh'}, dimensions={0} | all-to-all | bytes 327680 | tf_op jit(solution)/shard_map/all_to_all | solution.py:318
  157.4 2.1 %leaf_backward.4 = (f32[8,64,128]{2,1,0:T(8,128)S(1)}, f32[40,64,128]{2,1,0:T(8,128)S(1)}) custom-call(s32[105]{0:T(128)S(1)} %concatenate.36.refs_0_.meta, bf16[8,384,128]{2,1,0:T(8,128)(2,1)S(1)} %copy-done.11, bf16[8,384,128]{2,1,0:T(8,128)(2,1)S(1)} %copy-done.13, f32[8,64,128]{2,1,0:T(8,128)S(1)} %copy-done.15, f32[8,5,8,128]{3,2,1,0:T(8,128)S(1)} %all_to_all.10.state), custom_call_target="tpu_custom_call" | custom-call | flops 4000000000 | bytes 8388608 | tf_op jit(solution)/shard_map/leaf_backward/pallas_call | solution.py:331
  160.0 2.1 %leaf_backward.5 = (f32[8,64,128]{2,1,0:T(8,128)S(1)}, f32[40,64,128]{2,1,0:T(8,128)S(1)}) custom-call(s32[105]{0:T(128)S(1)} %concatenate.36.refs_0_.meta, bf16[24,384,128]{2,1,0:T(8,128)(2,1)S(1)} %copy-done.3, bf16[24,384,128]{2,1,0:T(8,128)(2,1)S(1)} %copy-done.5, f32[24,64,128]{2,1,0:T(8,128)S(1)} %copy-done.7, f32[40,64,128]{2,1,0:T(8,128)S(1)} %get-tuple-element.64.state), custom_call_target="tpu_custom_call" | custom-call | flops 4000000000 | bytes 8388608 | tf_op jit(solution)/shard_map/leaf_backward/pallas_call | solution.py:331
  162.1 2.1 %leaf_backward.6 = (f32[8,64,128]{2,1,0:T(8,128)S(1)}, f32[40,64,128]{2,1,0:T(8,128)S(1)}) custom-call(s32[105]{0:T(128)S(1)} %concatenate.36.refs_0_.meta, bf16[24,384,128]{2,1,0:T(8,128)(2,1)S(1)} %copy-done.3, bf16[24,384,128]{2,1,0:T(8,128)(2,1)S(1)} %copy-done.5, f32[24,64,128]{2,1,0:T(8,128)S(1)} %copy-done.7, f32[40,64,128]{2,1,0:T(8,128)S(1)} %get-tuple-element.65.state), custom_call_target="tpu_custom_call" | custom-call | flops 4000000000 | bytes 8388608 | tf_op jit(solution)/shard_map/leaf_backward/pallas_call | solution.py:331
  164.2 4.2 %collective-permute-start.15 = (f32[8,64,128]{2,1,0:T(8,128)S(1)}, f32[8,64,128]{2,1,0:T(8,128)S(1)}, u32[]{:S(2)}, u32[]{:S(2)}) collective-permute-start(f32[8,64,128]{2,1,0:T(8,128)S(1)} %get-tuple-element.68), channel_id=1, source_target_pairs={{0,0},{2,4},{4,2},{6,6},{1,1},{3,5},{5,3},{7,7},{8,8},{10,12},{12,... | collective-permute-start | bytes 786440 | tf_op jit(solution)/shard_map/ppermute | solution.py:209
  168.5 6.7 %collective-permute-done.15 = f32[8,64,128]{2,1,0:T(8,128)S(1)} collective-permute-done((f32[8,64,128]{2,1,0:T(8,128)S(1)}, f32[8,64,128]{2,1,0:T(8,128)S(1)}, u32[]{:S(2)}, u32[]{:S(2)}) %collective-permute-start.15) | collective-permute-done | bytes 262176 | tf_op jit(solution)/shard_map/ppermute | solution.py:209
  175.2 1.9 collective-permute-start.16
  177.1 3.2 %leaf_backward.7 = (f32[8,64,128]{2,1,0:T(8,128)S(1)}, f32[40,64,128]{2,1,0:T(8,128)}) custom-call(s32[105]{0:T(128)S(1)} %concatenate.36.refs_0_.meta, bf16[24,384,128]{2,1,0:T(8,128)(2,1)S(1)} %copy-done.3, bf16[24,384,128]{2,1,0:T(8,128)(2,1)S(1)} %copy-done.5, f32[24,64,128]{2,1,0:T(8,128)S(1)} %copy-done.7, f32[40,64,128]{2,1,0:T(8,128)S(1)} %get-tuple-element.66.state), custom_call_target="tpu_custom_call" | custom-call | flops 4000000000 | bytes 8388608 | tf_op jit(solution)/shard_map/leaf_backward/pallas_call | solution.py:331
  180.4 4.5 %collective-permute-start.14 = (f32[8,64,128]{2,1,0:T(8,128)S(1)}, f32[8,64,128]{2,1,0:T(8,128)S(1)}, u32[]{:S(2)}, u32[]{:S(2)}) collective-permute-start(f32[8,64,128]{2,1,0:T(8,128)S(1)} %get-tuple-element.67), channel_id=1, source_target_pairs={{0,0},{2,4},{4,2},{6,6},{1,1},{3,5},{5,3},{7,7},{8,8},{10,12},{12,... | collective-permute-start | bytes 786440 | tf_op jit(solution)/shard_map/ppermute | solution.py:209
  184.9 10.8 %collective-permute-done.16 = f32[17,64,128]{2,1,0:T(8,128)S(1)} collective-permute-done((f32[17,64,128]{2,1,0:T(8,128)S(1)}, f32[17,64,128]{2,1,0:T(8,128)S(1)}, u32[]{:S(2)}, u32[]{:S(2)}) %collective-permute-start.16) | collective-permute-done | bytes 557088 | tf_op jit(solution)/shard_map/ppermute | solution.py:209
  196.3 2.2 %collective-permute-done.14 = f32[8,64,128]{2,1,0:T(8,128)S(1)} collective-permute-done((f32[8,64,128]{2,1,0:T(8,128)S(1)}, f32[8,64,128]{2,1,0:T(8,128)S(1)}, u32[]{:S(2)}, u32[]{:S(2)}) %collective-permute-start.14) | collective-permute-done | bytes 262176 | tf_op jit(solution)/shard_map/ppermute | solution.py:209
  198.5 1.1 pad_maximum_fusion.2
  (68 shorter events, 6.4 us)
Async XLA Ops:
  7.2 1.6 copy-start
  7.2 8.8 %copy-start.18 = (f32[32,64,128]{2,1,0:T(8,128)S(1)}, f32[32,64,128]{2,1,0:T(8,128)}, u32[]{:S(2)}) copy-start(f32[32,64,128]{2,1,0:T(8,128)} %param.11) | copy-start | bytes 3145732
  7.2 130.4 %all-gather.3.cloned.1.call-start = ((), (), s32[]{:S(2)}) async-start(), calls=%async_computation.2 | async-start | bytes 2359296 | tf_op jit(solution)/shard_map/all_gather | solution.py:247
  10.1 7.7 %copy-start.16 = (f32[32,3,32,128]{3,2,1,0:T(8,128)S(1)}, f32[32,3,32,128]{3,2,1,0:T(8,128)}, u32[]{:S(2)}) copy-start(f32[32,3,32,128]{3,2,1,0:T(8,128)} %param.13) | copy-start | bytes 4718596
  10.1 7.7 %copy-start.17 = (f32[32,32,128]{2,1,0:T(8,128)S(1)}, f32[32,32,128]{2,1,0:T(8,128)}, u32[]{:S(2)}) copy-start(f32[32,32,128]{2,1,0:T(8,128)} %param.14) | copy-start | bytes 1572868
  10.1 7.9 %collective-permute-start = (f32[4,32,128]{2,1,0:T(8,128)S(1)}, f32[4,32,128]{2,1,0:T(8,128)S(1)}, u32[]{:S(2)}, u32[]{:S(2)}) collective-permute-start(f32[4,32,128]{2,1,0:T(8,128)S(1)} %get-tuple-element.73), channel_id=1, source_target_pairs={{0,2},{2,0},{1,3},{3,1},{4,6},{6,4},{5,7},{7,5},{8,10},{10,8},{9,1... | collective-permute-start | bytes 196616 | tf_op jit(solution)/shard_map/ppermute | solution.py:222
  18.0 1.4 slice-start
  18.1 2.7 %slice-start.1 = ((f32[32,3,32,128]{3,2,1,0:T(8,128)}), f32[8,3,32,128]{3,2,1,0:T(8,128)S(1)}, s32[]{:S(2)}) async-start(f32[32,3,32,128]{3,2,1,0:T(8,128)} %param.13), calls=%async_computation.4 | async-start | bytes 786432 | tf_op jit(solution)/shard_map/slice | solution.py:235
  18.1 3.9 %collective-permute-start.1 = (f32[2,4,32,128]{3,2,1,0:T(8,128)S(1)}, f32[2,4,32,128]{3,2,1,0:T(8,128)S(1)}, u32[]{:S(2)}, u32[]{:S(2)}) collective-permute-start(f32[2,4,32,128]{3,2,1,0:T(8,128)S(1)} %pad_maximum_fusion.6), channel_id=1, source_target_pairs={{0,1},{1,0},{2,3},{3,2},{4,5},{5,4},{6,7},{7,6},{8,9},{9,8},{10,11... | collective-permute-start | bytes 393224 | tf_op jit(solution)/shard_map/ppermute | solution.py:222
  22.7 34.8 %collective-permute-start.4 = (f32[24,4,32,128]{3,2,1,0:T(8,128)}, f32[24,4,32,128]{3,2,1,0:T(8,128)}, u32[]{:S(2)}, u32[]{:S(2)}) collective-permute-start(f32[24,4,32,128]{3,2,1,0:T(8,128)} %pad_maximum_fusion.1), channel_id=1, source_target_pairs={{2,0},{4,6},{3,1},{5,7},{10,8},{12,14},{11,9},{13,15},{18,16},{20,... | collective-permute-start | bytes 4718600 | tf_op jit(solution)/shard_map/ppermute | solution.py:212
  27.4 46.4 %collective-permute-start.3 = (f32[32,4,32,128]{3,2,1,0:T(8,128)S(1)}, f32[32,4,32,128]{3,2,1,0:T(8,128)}, u32[]{:S(2)}, u32[]{:S(2)}) collective-permute-start(f32[32,4,32,128]{3,2,1,0:T(8,128)S(1)} %pad_maximum_fusion.refs_1_), channel_id=1, source_target_pairs={{0,1},{1,0},{6,7},{7,6},{8,9},{9,8},{14,15},{15,14},{16,17},{17,16... | collective-permute-start | bytes 6291464 | tf_op jit(solution)/shard_map/ppermute | solution.py:218
  29.5 62.5 %collective-permute-start.2 = (f32[2120,128]{1,0:T(8,128)}, f32[2120,128]{1,0:T(8,128)S(1)}, u32[]{:S(2)}, u32[]{:S(2)}) collective-permute-start(f32[2120,128]{1,0:T(8,128)} %select_maximum_fusion), channel_id=1, source_target_pairs={{0,0},{2,4},{4,2},{6,6},{1,1},{3,5},{5,3},{7,7},{8,8},{10,12},{12,... | collective-permute-start | bytes 3256328 | tf_op jit(solution)/shard_map/ppermute | solution.py:209
  57.5 44.8 %collective-permute-start.5 = (f32[24,4,32,128]{3,2,1,0:T(8,128)}, f32[24,4,32,128]{3,2,1,0:T(8,128)}, u32[]{:S(2)}, u32[]{:S(2)}) collective-permute-start(f32[24,4,32,128]{3,2,1,0:T(8,128)} %collective-permute-done.4.refs_3_), channel_id=1, source_target_pairs={{0,1},{1,0},{6,7},{7,6},{8,9},{9,8},{14,15},{15,14},{16,17},{17,16... | collective-permute-start | bytes 4718600 | tf_op jit(solution)/shard_map/ppermute | solution.py:218
  59.3 32.7 %collective-permute-start.9 = (f32[8,4,32,128]{3,2,1,0:T(8,128)}, f32[8,4,32,128]{3,2,1,0:T(8,128)}, u32[]{:S(2)}, u32[]{:S(2)}) collective-permute-start(f32[8,4,32,128]{3,2,1,0:T(8,128)} %pad_maximum_fusion.4), channel_id=1, source_target_pairs={{2,0},{4,6},{3,1},{5,7},{10,8},{12,14},{11,9},{13,15},{18,16},{20,... | collective-permute-start | bytes 1572872 | tf_op jit(solution)/shard_map/ppermute | solution.py:212
  72.5 31.8 %collective-permute-start.6 = (f32[32,4,32,128]{3,2,1,0:T(8,128)S(1)}, f32[32,4,32,128]{3,2,1,0:T(8,128)}, u32[]{:S(2)}, u32[]{:S(2)}) collective-permute-start(f32[32,4,32,128]{3,2,1,0:T(8,128)S(1)} %pad_maximum_fusion.refs_1_), channel_id=1, source_target_pairs={{0,4},{6,2},{1,5},{7,3},{8,12},{14,10},{9,13},{15,11},{16,20},{22,... | collective-permute-start | bytes 6291464 | tf_op jit(solution)/shard_map/ppermute | solution.py:215
  73.8 30.6 %collective-permute-start.7 = (f32[32,4,32,128]{3,2,1,0:T(8,128)}, f32[32,4,32,128]{3,2,1,0:T(8,128)}, u32[]{:S(2)}, u32[]{:S(2)}) collective-permute-start(f32[32,4,32,128]{3,2,1,0:T(8,128)} %collective-permute-done.3.refs_2_), channel_id=1, source_target_pairs={{0,4},{6,2},{1,5},{7,3},{8,12},{14,10},{9,13},{15,11},{16,20},{22,... | collective-permute-start | bytes 6291464 | tf_op jit(solution)/shard_map/ppermute | solution.py:215
  92.0 9.5 %collective-permute-start.10 = (f32[8,4,32,128]{3,2,1,0:T(8,128)}, f32[8,4,32,128]{3,2,1,0:T(8,128)S(1)}, u32[]{:S(2)}, u32[]{:S(2)}) collective-permute-start(f32[8,4,32,128]{3,2,1,0:T(8,128)} %collective-permute-done.9.refs_3_), channel_id=1, source_target_pairs={{0,4},{6,2},{1,5},{7,3},{8,12},{14,10},{9,13},{15,11},{16,20},{22,... | collective-permute-start | bytes 1572872 | tf_op jit(solution)/shard_map/ppermute | solution.py:215
  93.3 11.1 %collective-permute-start.8 = (f32[24,4,32,128]{3,2,1,0:T(8,128)}, f32[24,4,32,128]{3,2,1,0:T(8,128)}, u32[]{:S(2)}, u32[]{:S(2)}) collective-permute-start(f32[24,4,32,128]{3,2,1,0:T(8,128)} %collective-permute-done.4.refs_3_), channel_id=1, source_target_pairs={{0,4},{6,2},{1,5},{7,3},{8,12},{14,10},{9,13},{15,11},{16,20},{22,... | collective-permute-start | bytes 4718600 | tf_op jit(solution)/shard_map/ppermute | solution.py:215
  101.5 0.8 copy-start.8
  102.3 7.1 %collective-permute-start.11 = (f32[24,4,32,128]{3,2,1,0:T(8,128)}, f32[24,4,32,128]{3,2,1,0:T(8,128)}, u32[]{:S(2)}, u32[]{:S(2)}) collective-permute-start(f32[24,4,32,128]{3,2,1,0:T(8,128)} %collective-permute-done.5.refs_4_), channel_id=1, source_target_pairs={{0,4},{6,2},{1,5},{7,3},{8,12},{14,10},{9,13},{15,11},{16,20},{22,... | collective-permute-start | bytes 4718600 | tf_op jit(solution)/shard_map/ppermute | solution.py:215
  104.4 16.4 %collective-permute-start.12 = (f32[8,4,32,128]{3,2,1,0:T(8,128)}, f32[8,4,32,128]{3,2,1,0:T(8,128)}, u32[]{:S(2)}, u32[]{:S(2)}) collective-permute-start(f32[8,4,32,128]{3,2,1,0:T(8,128)} %collective-permute-done.9.refs_3_), channel_id=1, source_target_pairs={{0,1},{1,0},{6,7},{7,6},{8,9},{9,8},{14,15},{15,14},{16,17},{17,16... | collective-permute-start | bytes 1572872 | tf_op jit(solution)/shard_map/ppermute | solution.py:218
  106.2 19.6 %copy-start.9 = (f32[8,4,32,128]{3,2,1,0:T(8,128)S(1)}, f32[8,4,32,128]{3,2,1,0:T(8,128)}, u32[]{:S(2)}) copy-start(f32[8,4,32,128]{3,2,1,0:T(8,128)} %copy-done.8) | copy-start | bytes 1572868
  120.8 10.8 %copy-start.2 = (bf16[24,384,128]{2,1,0:T(8,128)(2,1)}, bf16[24,384,128]{2,1,0:T(8,128)(2,1)S(1)}, u32[]{:S(2)}) copy-start(bf16[24,384,128]{2,1,0:T(8,128)(2,1)S(1)} %get-tuple-element.48.high) | copy-start | bytes 7077892
  120.8 10.8 %copy-start.4 = (bf16[24,384,128]{2,1,0:T(8,128)(2,1)}, bf16[24,384,128]{2,1,0:T(8,128)(2,1)S(1)}, u32[]{:S(2)}) copy-start(bf16[24,384,128]{2,1,0:T(8,128)(2,1)S(1)} %get-tuple-element.49.low) | copy-start | bytes 7077892
  120.9 10.8 %copy-start.6 = (f32[24,64,128]{2,1,0:T(8,128)}, f32[24,64,128]{2,1,0:T(8,128)S(1)}, u32[]{:S(2)}) copy-start(f32[24,64,128]{2,1,0:T(8,128)S(1)} %get-tuple-element.50.scaled) | copy-start | bytes 2359300
  120.9 5.0 %collective-permute-start.13 = (f32[8,4,32,128]{3,2,1,0:T(8,128)}, f32[8,4,32,128]{3,2,1,0:T(8,128)S(1)}, u32[]{:S(2)}, u32[]{:S(2)}) collective-permute-start(f32[8,4,32,128]{3,2,1,0:T(8,128)} %collective-permute-done.12.refs_4_), channel_id=1, source_target_pairs={{0,4},{6,2},{1,5},{7,3},{8,12},{14,10},{9,13},{15,11},{16,20},{22,... | collective-permute-start | bytes 1572872 | tf_op jit(solution)/shard_map/ppermute | solution.py:215
  131.6 0.9 copy-start.10
  132.5 0.9 copy-start.12
  133.4 0.7 copy-start.14
  134.1 12.0 %all-to-all-start = ((f32[8,5,8,128]{3,2,1,0:T(8,128)}), f32[8,5,8,128]{3,2,1,0:T(8,128)S(1)}, u32[]{:S(2)}, u32[]{:S(2)}) async-start(f32[8,5,8,128]{3,2,1,0:T(8,128)} %get-tuple-element.57), calls=%async_computation | async-start | bytes 327680 | tf_op jit(solution)/shard_map/all_to_all | solution.py:309
  137.6 1.6 copy-start.1
  146.1 11.3 %copy-start.11 = (bf16[8,384,128]{2,1,0:T(8,128)(2,1)S(1)}, bf16[8,384,128]{2,1,0:T(8,128)(2,1)}, u32[]{:S(2)}) copy-start(bf16[8,384,128]{2,1,0:T(8,128)(2,1)} %copy-done.10) | copy-start | bytes 2359300
  146.1 11.3 %copy-start.13 = (bf16[8,384,128]{2,1,0:T(8,128)(2,1)S(1)}, bf16[8,384,128]{2,1,0:T(8,128)(2,1)}, u32[]{:S(2)}) copy-start(bf16[8,384,128]{2,1,0:T(8,128)(2,1)} %copy-done.12) | copy-start | bytes 2359300
  146.1 11.3 %copy-start.15 = (f32[8,64,128]{2,1,0:T(8,128)S(1)}, f32[8,64,128]{2,1,0:T(8,128)}, u32[]{:S(2)}) copy-start(f32[8,64,128]{2,1,0:T(8,128)} %copy-done.14) | copy-start | bytes 786436
  157.4 2.2 %copy-start.3 = (bf16[24,384,128]{2,1,0:T(8,128)(2,1)S(1)}, bf16[24,384,128]{2,1,0:T(8,128)(2,1)}, u32[]{:S(2)}) copy-start(bf16[24,384,128]{2,1,0:T(8,128)(2,1)} %copy-done.2) | copy-start | bytes 7077892
  157.4 2.4 %copy-start.5 = (bf16[24,384,128]{2,1,0:T(8,128)(2,1)S(1)}, bf16[24,384,128]{2,1,0:T(8,128)(2,1)}, u32[]{:S(2)}) copy-start(bf16[24,384,128]{2,1,0:T(8,128)(2,1)} %copy-done.4) | copy-start | bytes 7077892
  157.4 2.5 %copy-start.7 = (f32[24,64,128]{2,1,0:T(8,128)S(1)}, f32[24,64,128]{2,1,0:T(8,128)}, u32[]{:S(2)}) copy-start(f32[24,64,128]{2,1,0:T(8,128)} %copy-done.6) | copy-start | bytes 2359300
  164.2 11.0 %collective-permute-start.15 = (f32[8,64,128]{2,1,0:T(8,128)S(1)}, f32[8,64,128]{2,1,0:T(8,128)S(1)}, u32[]{:S(2)}, u32[]{:S(2)}) collective-permute-start(f32[8,64,128]{2,1,0:T(8,128)S(1)} %get-tuple-element.68), channel_id=1, source_target_pairs={{0,0},{2,4},{4,2},{6,6},{1,1},{3,5},{5,3},{7,7},{8,8},{10,12},{12,... | collective-permute-start | bytes 786440 | tf_op jit(solution)/shard_map/ppermute | solution.py:209
  175.2 20.5 %collective-permute-start.16 = (f32[17,64,128]{2,1,0:T(8,128)S(1)}, f32[17,64,128]{2,1,0:T(8,128)S(1)}, u32[]{:S(2)}, u32[]{:S(2)}) collective-permute-start(f32[17,64,128]{2,1,0:T(8,128)S(1)} %pad_maximum_fusion.3), channel_id=1, source_target_pairs={{0,0},{2,4},{4,2},{6,6},{1,1},{3,5},{5,3},{7,7},{8,8},{10,12},{12,... | collective-permute-start | bytes 1671176 | tf_op jit(solution)/shard_map/ppermute | solution.py:209
  180.4 18.1 %collective-permute-start.14 = (f32[8,64,128]{2,1,0:T(8,128)S(1)}, f32[8,64,128]{2,1,0:T(8,128)S(1)}, u32[]{:S(2)}, u32[]{:S(2)}) collective-permute-start(f32[8,64,128]{2,1,0:T(8,128)S(1)} %get-tuple-element.67), channel_id=1, source_target_pairs={{0,0},{2,4},{4,2},{6,6},{1,1},{3,5},{5,3},{7,7},{8,8},{10,12},{12,... | collective-permute-start | bytes 786440 | tf_op jit(solution)/shard_map/ppermute | solution.py:209
Sparse Core Ops, SparseCore 0:
  92.1 34.5 all-gather.2

commit v10 on v6

--- a/solution.py
+++ b/solution.py
@@ -226,8 +226,7 @@
 
     chosen = jnp.take(top_blocks[:, 0], jnp.asarray(padded(above, most))[2 * xy + core], axis=0)
     top = jnp.concatenate([chosen, top_dinv], axis=0)
-    top = jnp.stack([top, other(top, "zh")])
-    top = jnp.concatenate([top, other(top, "zl")])
+    top = jnp.stack([top, other(top, "zh"), other(top, "zl"), other(top, "zh", "zl")])
 
     names = jnp.zeros((8, wide), f32).at[:3, :leafs].set(leaf_struct.T.astype(f32))
     sides = jnp.concatenate([rhs_leaf.reshape(-1, wide), rhs_top.reshape(-1, wide), names], axis=0)

time: 202 us -> 199 us (0.985)
  starting transfers between devices: 54.6 us -> 51.2 us
    ppermute x2, waiting for transfers between devices: 40 us -> 47.8 us  [to_keeper(): return lax.ppermute(value, ('core', 'zh'), [(1, 0), (2, 3)])]
    ppermute x2, starting transfers between devices: 18 us -> 13.8 us  [to_keeper(): return lax.ppermute(value, ('core', 'zh'), [(1, 0), (2, 3)])]
    ppermute x6, waiting for transfers between devices: 13.9 us -> 10.2 us  [to_trader(): return lax.ppermute(value, ('core', 'zh'), [(0, 2), (3, 1)])]
    all_to_all x1, waiting for transfers between devices: 4.15 us -> 1.82 us  [local(): lax.all_to_all(results[4], ('xy', 'zh'), split_axis=0, concat_axis=0, til...]
    unnamed x38 -> x42, local copies, waits for them, and re-layouts: 5.29 us -> 6.03 us
    ppermute x2 -> x3, starting transfers between devices: 4.57 us -> 4.5 us  [other(): return lax.ppermute(value, axes, [(i, last - i) for i in range(last + 1)])]
  transfers between devices with their start and end apart: 19 -> 20, of which waited for: 11 -> 11; matrix products, arithmetic and copies ran while one was open for 4% -> 3% of each run, Pallas kernels for 12% -> 12%
where the time goes in v10:
time: 199 us; the launch traced here: 198 us
  waiting for transfers between devices  74 us (37%)
  starting transfers between devices  51.2 us (26%)
  Pallas kernels  32.3 us (16%)
  between operations  14.4 us (7%)
  blocking collectives  9.66 us (5%)
  local copies, waits for them, and re-layouts  8.88 us (4%)
  other arithmetic  7.53 us (4%)
    ppermute x2, waiting for transfers between devices, to_keeper(): return lax.ppermute(value, ('core', 'zh'), [(1, 0), (2, 3)])  47.8 us
    pallas_call x2, Pallas kernels, local(): pl.pallas_call(functools.partial(forward_kernel, base, leafs, k == 0, las...  17.2 us
    ppermute x4, starting transfers between devices, swap(): return lax.ppermute(value, ('core', 'zh'), [(0, 0), (1, 2), (2, 1), (3, 3)])  16.3 us
    ppermute x4, waiting for transfers between devices, swap(): return lax.ppermute(value, ('core', 'zh'), [(0, 0), (1, 2), (2, 1), (3, 3)])  14 us
    ppermute x2, starting transfers between devices, to_keeper(): return lax.ppermute(value, ('core', 'zh'), [(1, 0), (2, 3)])  13.8 us
    ppermute x6, waiting for transfers between devices, to_trader(): return lax.ppermute(value, ('core', 'zh'), [(0, 2), (3, 1)])  10.2 us
    all_to_all x1, blocking collectives, local(): lax.all_to_all(outgoing, ('xy', 'zh'), split_axis=0, concat_axis=0, tiled...  9.66 us
    pallas_call x4, Pallas kernels, local(): pl.pallas_call(functools.partial(backward_kernel, k * turn, k == TURNS -...  9.65 us
  transfers between devices with their start and end apart: 20, of which 11 were waited for; matrix products, arithmetic and copies ran while one was open for 3% of the time, Pallas kernels for 12%

profile of v10, /device:TPU:1, one launch (start us, length us, event | category | flops | bytes accessed | tf_op | source)
XLA Modules:
  0.0 198.0 jit_solution(10614406519843679855)
XLA Ops:
  7.2 0.7 fusion.1
  9.3 0.7 fusion.2
  10.0 3.2 %collective-permute-start = (f32[4,32,128]{2,1,0:T(8,128)S(1)}, f32[4,32,128]{2,1,0:T(8,128)S(1)}, u32[]{:S(2)}, u32[]{:S(2)}) collective-permute-start(f32[4,32,128]{2,1,0:T(8,128)S(1)} %get-tuple-element.71), channel_id=1, source_target_pairs={{0,2},{2,0},{1,3},{3,1},{4,6},{6,4},{5,7},{7,5},{8,10},{10,8},{9,1... | collective-permute-start | bytes 196616 | tf_op jit(solution)/shard_map/ppermute | solution.py:222
  13.2 1.3 collective-permute-start.1
  15.9 1.3 pad_maximum_fusion.1
  17.5 1.1 select_maximum_fusion
  18.5 0.8 pad_maximum_fusion.4
  19.6 0.7 pad_maximum_fusion.5
  20.3 5.5 %collective-permute-start.5 = (f32[24,4,32,128]{3,2,1,0:T(8,128)}, f32[24,4,32,128]{3,2,1,0:T(8,128)}, u32[]{:S(2)}, u32[]{:S(2)}) collective-permute-start(f32[24,4,32,128]{3,2,1,0:T(8,128)} %pad_maximum_fusion.1), channel_id=1, source_target_pairs={{2,0},{4,6},{3,1},{5,7},{10,8},{12,14},{11,9},{13,15},{18,16},{20,... | collective-permute-start | bytes 4718600 | tf_op jit(solution)/shard_map/ppermute | solution.py:212
  25.8 2.1 %collective-permute-start.4 = (f32[32,4,32,128]{3,2,1,0:T(8,128)S(1)}, f32[32,4,32,128]{3,2,1,0:T(8,128)}, u32[]{:S(2)}, u32[]{:S(2)}) collective-permute-start(f32[32,4,32,128]{3,2,1,0:T(8,128)S(1)} %pad_maximum_fusion.refs_1_), channel_id=1, source_target_pairs={{0,1},{1,0},{6,7},{7,6},{8,9},{9,8},{14,15},{15,14},{16,17},{17,16... | collective-permute-start | bytes 6291464 | tf_op jit(solution)/shard_map/ppermute | solution.py:218
  27.9 4.2 %collective-permute-start.3 = (f32[2120,128]{1,0:T(8,128)}, f32[2120,128]{1,0:T(8,128)S(1)}, u32[]{:S(2)}, u32[]{:S(2)}) collective-permute-start(f32[2120,128]{1,0:T(8,128)} %select_maximum_fusion), channel_id=1, source_target_pairs={{0,0},{2,4},{4,2},{6,6},{1,1},{3,5},{5,3},{7,7},{8,8},{10,12},{12,... | collective-permute-start | bytes 3256328 | tf_op jit(solution)/shard_map/ppermute | solution.py:209
  32.1 26.0 %collective-permute-done.5.refs_3_ = f32[24,4,32,128]{3,2,1,0:T(8,128)} collective-permute-done((f32[24,4,32,128]{3,2,1,0:T(8,128)}, f32[24,4,32,128]{3,2,1,0:T(8,128)}, u32[]{:S(2)}, u32[]{:S(2)}) %collective-permute-start.5) | collective-permute-done | bytes 1572896 | tf_op jit(solution)/shard_map/ppermute | solution.py:212
  58.1 1.8 collective-permute-start.6
  59.9 8.3 %collective-permute-start.10 = (f32[8,4,32,128]{3,2,1,0:T(8,128)}, f32[8,4,32,128]{3,2,1,0:T(8,128)}, u32[]{:S(2)}, u32[]{:S(2)}) collective-permute-start(f32[8,4,32,128]{3,2,1,0:T(8,128)} %pad_maximum_fusion.4), channel_id=1, source_target_pairs={{2,0},{4,6},{3,1},{5,7},{10,8},{12,14},{11,9},{13,15},{18,16},{20,... | collective-permute-start | bytes 1572872 | tf_op jit(solution)/shard_map/ppermute | solution.py:212
  68.2 1.3 collective-permute-start.7
  69.5 1.3 collective-permute-start.8
  70.8 21.8 %collective-permute-done.10.refs_3_ = f32[8,4,32,128]{3,2,1,0:T(8,128)} collective-permute-done((f32[8,4,32,128]{3,2,1,0:T(8,128)}, f32[8,4,32,128]{3,2,1,0:T(8,128)}, u32[]{:S(2)}, u32[]{:S(2)}) %collective-permute-start.10) | collective-permute-done | bytes 524320 | tf_op jit(solution)/shard_map/ppermute | solution.py:212
  92.7 1.3 collective-permute-start.11
  94.0 1.3 collective-permute-start.9
  95.3 4.5 %collective-permute-done.11.refs_7_ = f32[8,4,32,128]{3,2,1,0:T(8,128)S(1)} collective-permute-done((f32[8,4,32,128]{3,2,1,0:T(8,128)}, f32[8,4,32,128]{3,2,1,0:T(8,128)S(1)}, u32[]{:S(2)}, u32[]{:S(2)}) %collective-permute-start.11) | collective-permute-done | bytes 524320 | tf_op jit(solution)/shard_map/ppermute | solution.py:215
  99.8 0.8 copy-done.8
  100.6 1.3 collective-permute-start.12
  101.9 0.7 dynamic-slice_bitcast_fusion
  102.7 1.4 collective-permute-start.13
  104.5 2.8 %collective-permute-done.12.refs_8_ = f32[24,4,32,128]{3,2,1,0:T(8,128)} collective-permute-done((f32[24,4,32,128]{3,2,1,0:T(8,128)}, f32[24,4,32,128]{3,2,1,0:T(8,128)}, u32[]{:S(2)}, u32[]{:S(2)}) %collective-permute-start.12) | collective-permute-done | bytes 1572896 | tf_op jit(solution)/shard_map/ppermute | solution.py:215
  107.3 11.4 %leaf_forward.2 = (f32[40,64,128]{2,1,0:T(8,128)S(1)}, bf16[24,384,128]{2,1,0:T(8,128)(2,1)S(1)}, bf16[24,384,128]{2,1,0:T(8,128)(2,1)S(1)}, f32[24,64,128]{2,1,0:T(8,128)S(1)}) custom-call(s32[105]{0:T(128)S(1)} %concatenate.31.refs_0_.meta, f32[32,4,32,128]{3,2,1,0:T(8,128)S(1)} %pad_maximum_fusion.refs_1_, ...), custom_call_target="tpu_custom_call" | custom-call | flops 4000000000 | bytes 8388608 | tf_op jit(solution)/shard_map/leaf_forward/pallas_call | solution.py:275
  118.8 1.3 collective-permute-start.14
  120.0 2.7 %collective-permute-done.14.refs_8_ = f32[8,4,32,128]{3,2,1,0:T(8,128)S(1)} collective-permute-done((f32[8,4,32,128]{3,2,1,0:T(8,128)}, f32[8,4,32,128]{3,2,1,0:T(8,128)S(1)}, u32[]{:S(2)}, u32[]{:S(2)}) %collective-permute-start.14) | collective-permute-done | bytes 524320 | tf_op jit(solution)/shard_map/ppermute | solution.py:215
  122.8 5.8 %leaf_forward.3 = (f32[40,64,128]{2,1,0:T(8,128)}, bf16[8,384,128]{2,1,0:T(8,128)(2,1)S(1)}, bf16[8,384,128]{2,1,0:T(8,128)(2,1)S(1)}, f32[8,64,128]{2,1,0:T(8,128)S(1)}, f32[8,5,8,128]{3,2,1,0:T(8,128)}) custom-call(s32[105]{0:T(128)S(1)} %concatenate.31.refs_0_.meta, f32[32,4,32,128]{3,2,1,0:T(8,128)S(1)} %pad_maximum_fusion.refs_1_, ...), custom_call_target="tpu_custom_call" | custom-call | flops 4000000000 | bytes 8388608 | tf_op jit(solution)/shard_map/leaf_forward/pallas_call | solution.py:275
  128.6 0.9 copy-done.10
  129.5 0.9 copy-done.12
  131.1 3.6 %all-to-all-start = ((f32[8,5,8,128]{3,2,1,0:T(8,128)}), f32[8,5,8,128]{3,2,1,0:T(8,128)S(1)}, u32[]{:S(2)}, u32[]{:S(2)}) async-start(f32[8,5,8,128]{3,2,1,0:T(8,128)} %get-tuple-element.56), calls=%async_computation | async-start | bytes 327680 | tf_op jit(solution)/shard_map/all_to_all | solution.py:308
  134.7 1.6 copy-done.1
  136.3 2.7 %top_prepare.1 = (bf16[8,384,128]{2,1,0:T(8,128)(2,1)S(1)}, bf16[8,384,128]{2,1,0:T(8,128)(2,1)S(1)}, bf16[8,128,128]{2,1,0:T(8,128)(2,1)S(1)}, bf16[8,128,128]{2,1,0:T(8,128)(2,1)S(1)}) custom-call(s32[4]{0:T(128)S(1)} %pad_add_fusion.places, f32[8,4,4,32,128]{4,3,2,1,0:T(8,128)S(1)} %bitcast.34), custom_call_target="tpu_custom_call" | custom-call | tf_op jit(solution)/shard_map/top_prepare/pallas_call | solution.py:296
  139.0 1.8 all-to-all-done.incoming
  140.9 2.7 %top_solve.1 = f32[8,5,8,128]{3,2,1,0:T(8,128)S(1)} custom-call(f32[8,5,8,128]{3,2,1,0:T(8,128)S(1)} %all-to-all-done.incoming, bf16[8,384,128]{2,1,0:T(8,128)(2,1)S(1)} %get-tuple-element.59.high, bf16[8,384,128]{2,1,0:T(8,128)(2,1)S(1)} %get-tuple-element.60.low, bf16[8,128,128]{2,1,0:T(8,128)(2,1)S(1)} %get-tuple-element.61.inverse_high, ...), custom_call_target="tpu_custom_call" | custom-call | tf_op jit(solution)/shard_map/top_solve/pallas_call | solution.py:309
  143.6 9.7 %all_to_all.10.state = f32[8,5,8,128]{3,2,1,0:T(8,128)S(1)} all-to-all(f32[8,5,8,128]{3,2,1,0:T(8,128)S(1)} %top_solve.1), channel_id=1, replica_groups=mesh['xy'=4,'core'=2,'zh'=2,'zl'=2] {'xy','zh'}, dimensions={0} | all-to-all | bytes 327680 | tf_op jit(solution)/shard_map/all_to_all | solution.py:317
  153.3 2.1 %leaf_backward.4 = (f32[8,64,128]{2,1,0:T(8,128)S(1)}, f32[40,64,128]{2,1,0:T(8,128)S(1)}) custom-call(s32[105]{0:T(128)S(1)} %concatenate.31.refs_0_.meta, bf16[8,384,128]{2,1,0:T(8,128)(2,1)S(1)} %copy-done.11, bf16[8,384,128]{2,1,0:T(8,128)(2,1)S(1)} %copy-done.13, f32[8,64,128]{2,1,0:T(8,128)S(1)} %copy-done.15, f32[8,5,8,128]{3,2,1,0:T(8,128)S(1)} %all_to_all.10.state), custom_call_target="tpu_custom_call" | custom-call | flops 4000000000 | bytes 8388608 | tf_op jit(solution)/shard_map/leaf_backward/pallas_call | solution.py:330
  155.8 2.1 %leaf_backward.5 = (f32[8,64,128]{2,1,0:T(8,128)S(1)}, f32[40,64,128]{2,1,0:T(8,128)S(1)}) custom-call(s32[105]{0:T(128)S(1)} %concatenate.31.refs_0_.meta, bf16[24,384,128]{2,1,0:T(8,128)(2,1)S(1)} %copy-done.3, bf16[24,384,128]{2,1,0:T(8,128)(2,1)S(1)} %copy-done.5, f32[24,64,128]{2,1,0:T(8,128)S(1)} %copy-done.7, f32[40,64,128]{2,1,0:T(8,128)S(1)} %get-tuple-element.63.state), custom_call_target="tpu_custom_call" | custom-call | flops 4000000000 | bytes 8388608 | tf_op jit(solution)/shard_map/leaf_backward/pallas_call | solution.py:330
  157.9 2.1 %leaf_backward.6 = (f32[8,64,128]{2,1,0:T(8,128)S(1)}, f32[40,64,128]{2,1,0:T(8,128)S(1)}) custom-call(s32[105]{0:T(128)S(1)} %concatenate.31.refs_0_.meta, bf16[24,384,128]{2,1,0:T(8,128)(2,1)S(1)} %copy-done.3, bf16[24,384,128]{2,1,0:T(8,128)(2,1)S(1)} %copy-done.5, f32[24,64,128]{2,1,0:T(8,128)S(1)} %copy-done.7, f32[40,64,128]{2,1,0:T(8,128)S(1)} %get-tuple-element.64.state), custom_call_target="tpu_custom_call" | custom-call | flops 4000000000 | bytes 8388608 | tf_op jit(solution)/shard_map/leaf_backward/pallas_call | solution.py:330
  160.1 5.6 %collective-permute-start.16 = (f32[17,64,128]{2,1,0:T(8,128)S(1)}, f32[17,64,128]{2,1,0:T(8,128)S(1)}, u32[]{:S(2)}, u32[]{:S(2)}) collective-permute-start(f32[17,64,128]{2,1,0:T(8,128)S(1)} %pad_maximum_fusion.3), channel_id=1, source_target_pairs={{0,0},{2,4},{4,2},{6,6},{1,1},{3,5},{5,3},{7,7},{8,8},{10,12},{12,... | collective-permute-start | bytes 1671176 | tf_op jit(solution)/shard_map/ppermute | solution.py:209
  165.7 3.3 %leaf_backward.7 = (f32[8,64,128]{2,1,0:T(8,128)S(1)}, f32[40,64,128]{2,1,0:T(8,128)}) custom-call(s32[105]{0:T(128)S(1)} %concatenate.31.refs_0_.meta, bf16[24,384,128]{2,1,0:T(8,128)(2,1)S(1)} %copy-done.3, bf16[24,384,128]{2,1,0:T(8,128)(2,1)S(1)} %copy-done.5, f32[24,64,128]{2,1,0:T(8,128)S(1)} %copy-done.7, f32[40,64,128]{2,1,0:T(8,128)S(1)} %get-tuple-element.65.state), custom_call_target="tpu_custom_call" | custom-call | flops 4000000000 | bytes 8388608 | tf_op jit(solution)/shard_map/leaf_backward/pallas_call | solution.py:330
  169.0 1.9 collective-permute-start.15
  170.9 4.5 %collective-permute-start.17 = (f32[8,64,128]{2,1,0:T(8,128)S(1)}, f32[8,64,128]{2,1,0:T(8,128)S(1)}, u32[]{:S(2)}, u32[]{:S(2)}) collective-permute-start(f32[8,64,128]{2,1,0:T(8,128)S(1)} %get-tuple-element.69), channel_id=1, source_target_pairs={{0,0},{2,4},{4,2},{6,6},{1,1},{3,5},{5,3},{7,7},{8,8},{10,12},{12,... | collective-permute-start | bytes 786440 | tf_op jit(solution)/shard_map/ppermute | solution.py:209
  175.4 9.1 %collective-permute-done.16 = f32[17,64,128]{2,1,0:T(8,128)S(1)} collective-permute-done((f32[17,64,128]{2,1,0:T(8,128)S(1)}, f32[17,64,128]{2,1,0:T(8,128)S(1)}, u32[]{:S(2)}, u32[]{:S(2)}) %collective-permute-start.16) | collective-permute-done | bytes 557088 | tf_op jit(solution)/shard_map/ppermute | solution.py:209
  185.2 2.1 %collective-permute-done.15 = f32[8,64,128]{2,1,0:T(8,128)S(1)} collective-permute-done((f32[8,64,128]{2,1,0:T(8,128)S(1)}, f32[8,64,128]{2,1,0:T(8,128)S(1)}, u32[]{:S(2)}, u32[]{:S(2)}) %collective-permute-start.15) | collective-permute-done | bytes 262176 | tf_op jit(solution)/shard_map/ppermute | solution.py:209
  187.3 2.8 %collective-permute-done.17 = f32[8,64,128]{2,1,0:T(8,128)S(1)} collective-permute-done((f32[8,64,128]{2,1,0:T(8,128)S(1)}, f32[8,64,128]{2,1,0:T(8,128)S(1)}, u32[]{:S(2)}, u32[]{:S(2)}) %collective-permute-start.17) | collective-permute-done | bytes 262176 | tf_op jit(solution)/shard_map/ppermute | solution.py:209
  190.1 1.1 pad_maximum_fusion.2
  (73 shorter events, 5.5 us)
Async XLA Ops:
  7.2 1.5 copy-start
  7.2 127.6 %all-gather.3.cloned.1.call-start = ((), (), s32[]{:S(2)}) async-start(), calls=%async_computation.2 | async-start | bytes 2359296 | tf_op jit(solution)/shard_map/all_gather | solution.py:246
  10.0 4.5 %copy-start.17 = (f32[32,32,128]{2,1,0:T(8,128)S(1)}, f32[32,32,128]{2,1,0:T(8,128)}, u32[]{:S(2)}) copy-start(f32[32,32,128]{2,1,0:T(8,128)} %param.14) | copy-start | bytes 1572868
  10.0 4.6 %copy-start.16 = (f32[32,3,32,128]{3,2,1,0:T(8,128)S(1)}, f32[32,3,32,128]{3,2,1,0:T(8,128)}, u32[]{:S(2)}) copy-start(f32[32,3,32,128]{3,2,1,0:T(8,128)} %param.13) | copy-start | bytes 4718596
  10.0 9.3 %collective-permute-start = (f32[4,32,128]{2,1,0:T(8,128)S(1)}, f32[4,32,128]{2,1,0:T(8,128)S(1)}, u32[]{:S(2)}, u32[]{:S(2)}) collective-permute-start(f32[4,32,128]{2,1,0:T(8,128)S(1)} %get-tuple-element.71), channel_id=1, source_target_pairs={{0,2},{2,0},{1,3},{3,1},{4,6},{6,4},{5,7},{7,5},{8,10},{10,8},{9,1... | collective-permute-start | bytes 196616 | tf_op jit(solution)/shard_map/ppermute | solution.py:222
  13.2 6.1 %collective-permute-start.1 = (f32[4,32,128]{2,1,0:T(8,128)S(1)}, f32[4,32,128]{2,1,0:T(8,128)S(1)}, u32[]{:S(2)}, u32[]{:S(2)}) collective-permute-start(f32[4,32,128]{2,1,0:T(8,128)S(1)} %get-tuple-element.71), channel_id=1, source_target_pairs={{0,1},{1,0},{2,3},{3,2},{4,5},{5,4},{6,7},{7,6},{8,9},{9,8},{10,11... | collective-permute-start | bytes 196616 | tf_op jit(solution)/shard_map/ppermute | solution.py:222
  14.5 5.0 %collective-permute-start.2 = (f32[4,32,128]{2,1,0:T(8,128)S(1)}, f32[4,32,128]{2,1,0:T(8,128)S(1)}, u32[]{:S(2)}, u32[]{:S(2)}) collective-permute-start(f32[4,32,128]{2,1,0:T(8,128)S(1)} %get-tuple-element.71), channel_id=1, source_target_pairs={{0,3},{1,2},{2,1},{3,0},{4,7},{5,6},{6,5},{7,4},{8,11},{9,10},{10,... | collective-permute-start | bytes 196616 | tf_op jit(solution)/shard_map/ppermute | solution.py:222
  14.6 0.7 copy-start.20
  14.6 1.3 slice-start
  15.9 1.6 copy-start.18
  15.9 1.6 copy-start.19
  17.2 1.3 slice-start.1
  20.3 37.8 %collective-permute-start.5 = (f32[24,4,32,128]{3,2,1,0:T(8,128)}, f32[24,4,32,128]{3,2,1,0:T(8,128)}, u32[]{:S(2)}, u32[]{:S(2)}) collective-permute-start(f32[24,4,32,128]{3,2,1,0:T(8,128)} %pad_maximum_fusion.1), channel_id=1, source_target_pairs={{2,0},{4,6},{3,1},{5,7},{10,8},{12,14},{11,9},{13,15},{18,16},{20,... | collective-permute-start | bytes 4718600 | tf_op jit(solution)/shard_map/ppermute | solution.py:212
  25.8 43.7 %collective-permute-start.4 = (f32[32,4,32,128]{3,2,1,0:T(8,128)S(1)}, f32[32,4,32,128]{3,2,1,0:T(8,128)}, u32[]{:S(2)}, u32[]{:S(2)}) collective-permute-start(f32[32,4,32,128]{3,2,1,0:T(8,128)S(1)} %pad_maximum_fusion.refs_1_), channel_id=1, source_target_pairs={{0,1},{1,0},{6,7},{7,6},{8,9},{9,8},{14,15},{15,14},{16,17},{17,16... | collective-permute-start | bytes 6291464 | tf_op jit(solution)/shard_map/ppermute | solution.py:218
  27.9 64.8 %collective-permute-start.3 = (f32[2120,128]{1,0:T(8,128)}, f32[2120,128]{1,0:T(8,128)S(1)}, u32[]{:S(2)}, u32[]{:S(2)}) collective-permute-start(f32[2120,128]{1,0:T(8,128)} %select_maximum_fusion), channel_id=1, source_target_pairs={{0,0},{2,4},{4,2},{6,6},{1,1},{3,5},{5,3},{7,7},{8,8},{10,12},{12,... | collective-permute-start | bytes 3256328 | tf_op jit(solution)/shard_map/ppermute | solution.py:209
  58.1 42.4 %collective-permute-start.6 = (f32[24,4,32,128]{3,2,1,0:T(8,128)}, f32[24,4,32,128]{3,2,1,0:T(8,128)}, u32[]{:S(2)}, u32[]{:S(2)}) collective-permute-start(f32[24,4,32,128]{3,2,1,0:T(8,128)} %collective-permute-done.5.refs_3_), channel_id=1, source_target_pairs={{0,1},{1,0},{6,7},{7,6},{8,9},{9,8},{14,15},{15,14},{16,17},{17,16... | collective-permute-start | bytes 4718600 | tf_op jit(solution)/shard_map/ppermute | solution.py:218
  59.9 32.7 %collective-permute-start.10 = (f32[8,4,32,128]{3,2,1,0:T(8,128)}, f32[8,4,32,128]{3,2,1,0:T(8,128)}, u32[]{:S(2)}, u32[]{:S(2)}) collective-permute-start(f32[8,4,32,128]{3,2,1,0:T(8,128)} %pad_maximum_fusion.4), channel_id=1, source_target_pairs={{2,0},{4,6},{3,1},{5,7},{10,8},{12,14},{11,9},{13,15},{18,16},{20,... | collective-permute-start | bytes 1572872 | tf_op jit(solution)/shard_map/ppermute | solution.py:212
  68.2 34.4 %collective-permute-start.7 = (f32[32,4,32,128]{3,2,1,0:T(8,128)S(1)}, f32[32,4,32,128]{3,2,1,0:T(8,128)}, u32[]{:S(2)}, u32[]{:S(2)}) collective-permute-start(f32[32,4,32,128]{3,2,1,0:T(8,128)S(1)} %pad_maximum_fusion.refs_1_), channel_id=1, source_target_pairs={{0,4},{6,2},{1,5},{7,3},{8,12},{14,10},{9,13},{15,11},{16,20},{22,... | collective-permute-start | bytes 6291464 | tf_op jit(solution)/shard_map/ppermute | solution.py:215
  69.5 33.2 %collective-permute-start.8 = (f32[32,4,32,128]{3,2,1,0:T(8,128)}, f32[32,4,32,128]{3,2,1,0:T(8,128)}, u32[]{:S(2)}, u32[]{:S(2)}) collective-permute-start(f32[32,4,32,128]{3,2,1,0:T(8,128)} %collective-permute-done.4.refs_2_), channel_id=1, source_target_pairs={{0,4},{6,2},{1,5},{7,3},{8,12},{14,10},{9,13},{15,11},{16,20},{22,... | collective-permute-start | bytes 6291464 | tf_op jit(solution)/shard_map/ppermute | solution.py:215
  92.7 7.1 %collective-permute-start.11 = (f32[8,4,32,128]{3,2,1,0:T(8,128)}, f32[8,4,32,128]{3,2,1,0:T(8,128)S(1)}, u32[]{:S(2)}, u32[]{:S(2)}) collective-permute-start(f32[8,4,32,128]{3,2,1,0:T(8,128)} %collective-permute-done.10.refs_3_), channel_id=1, source_target_pairs={{0,4},{6,2},{1,5},{7,3},{8,12},{14,10},{9,13},{15,11},{16,20},{22,... | collective-permute-start | bytes 1572872 | tf_op jit(solution)/shard_map/ppermute | solution.py:215
  94.0 8.8 %collective-permute-start.9 = (f32[24,4,32,128]{3,2,1,0:T(8,128)}, f32[24,4,32,128]{3,2,1,0:T(8,128)}, u32[]{:S(2)}, u32[]{:S(2)}) collective-permute-start(f32[24,4,32,128]{3,2,1,0:T(8,128)} %collective-permute-done.5.refs_3_), channel_id=1, source_target_pairs={{0,4},{6,2},{1,5},{7,3},{8,12},{14,10},{9,13},{15,11},{16,20},{22,... | collective-permute-start | bytes 4718600 | tf_op jit(solution)/shard_map/ppermute | solution.py:215
  99.8 0.8 copy-start.8
  100.6 6.7 %collective-permute-start.12 = (f32[24,4,32,128]{3,2,1,0:T(8,128)}, f32[24,4,32,128]{3,2,1,0:T(8,128)}, u32[]{:S(2)}, u32[]{:S(2)}) collective-permute-start(f32[24,4,32,128]{3,2,1,0:T(8,128)} %collective-permute-done.6.refs_4_), channel_id=1, source_target_pairs={{0,4},{6,2},{1,5},{7,3},{8,12},{14,10},{9,13},{15,11},{16,20},{22,... | collective-permute-start | bytes 4718600 | tf_op jit(solution)/shard_map/ppermute | solution.py:215
  102.7 16.0 %collective-permute-start.13 = (f32[8,4,32,128]{3,2,1,0:T(8,128)}, f32[8,4,32,128]{3,2,1,0:T(8,128)}, u32[]{:S(2)}, u32[]{:S(2)}) collective-permute-start(f32[8,4,32,128]{3,2,1,0:T(8,128)} %collective-permute-done.10.refs_3_), channel_id=1, source_target_pairs={{0,1},{1,0},{6,7},{7,6},{8,9},{9,8},{14,15},{15,14},{16,17},{17,16... | collective-permute-start | bytes 1572872 | tf_op jit(solution)/shard_map/ppermute | solution.py:218
  104.5 18.3 %copy-start.9 = (f32[8,4,32,128]{3,2,1,0:T(8,128)S(1)}, f32[8,4,32,128]{3,2,1,0:T(8,128)}, u32[]{:S(2)}) copy-start(f32[8,4,32,128]{3,2,1,0:T(8,128)} %copy-done.8) | copy-start | bytes 1572868
  118.7 9.8 %copy-start.2 = (bf16[24,384,128]{2,1,0:T(8,128)(2,1)}, bf16[24,384,128]{2,1,0:T(8,128)(2,1)S(1)}, u32[]{:S(2)}) copy-start(bf16[24,384,128]{2,1,0:T(8,128)(2,1)S(1)} %get-tuple-element.47.high) | copy-start | bytes 7077892
  118.7 9.8 %copy-start.4 = (bf16[24,384,128]{2,1,0:T(8,128)(2,1)}, bf16[24,384,128]{2,1,0:T(8,128)(2,1)S(1)}, u32[]{:S(2)}) copy-start(bf16[24,384,128]{2,1,0:T(8,128)(2,1)S(1)} %get-tuple-element.48.low) | copy-start | bytes 7077892
  118.7 9.8 %copy-start.6 = (f32[24,64,128]{2,1,0:T(8,128)}, f32[24,64,128]{2,1,0:T(8,128)S(1)}, u32[]{:S(2)}) copy-start(f32[24,64,128]{2,1,0:T(8,128)S(1)} %get-tuple-element.49.scaled) | copy-start | bytes 2359300
  118.8 4.0 %collective-permute-start.14 = (f32[8,4,32,128]{3,2,1,0:T(8,128)}, f32[8,4,32,128]{3,2,1,0:T(8,128)S(1)}, u32[]{:S(2)}, u32[]{:S(2)}) collective-permute-start(f32[8,4,32,128]{3,2,1,0:T(8,128)} %collective-permute-done.13.refs_4_), channel_id=1, source_target_pairs={{0,4},{6,2},{1,5},{7,3},{8,12},{14,10},{9,13},{15,11},{16,20},{22,... | collective-permute-start | bytes 1572872 | tf_op jit(solution)/shard_map/ppermute | solution.py:215
  128.6 0.9 copy-start.10
  129.5 0.9 copy-start.12
  130.4 0.7 copy-start.14
  131.1 9.8 %all-to-all-start = ((f32[8,5,8,128]{3,2,1,0:T(8,128)}), f32[8,5,8,128]{3,2,1,0:T(8,128)S(1)}, u32[]{:S(2)}, u32[]{:S(2)}) async-start(f32[8,5,8,128]{3,2,1,0:T(8,128)} %get-tuple-element.56), calls=%async_computation | async-start | bytes 327680 | tf_op jit(solution)/shard_map/all_to_all | solution.py:308
  134.7 1.6 copy-start.1
  140.9 12.4 %copy-start.11 = (bf16[8,384,128]{2,1,0:T(8,128)(2,1)S(1)}, bf16[8,384,128]{2,1,0:T(8,128)(2,1)}, u32[]{:S(2)}) copy-start(bf16[8,384,128]{2,1,0:T(8,128)(2,1)} %copy-done.10) | copy-start | bytes 2359300
  140.9 12.4 %copy-start.13 = (bf16[8,384,128]{2,1,0:T(8,128)(2,1)S(1)}, bf16[8,384,128]{2,1,0:T(8,128)(2,1)}, u32[]{:S(2)}) copy-start(bf16[8,384,128]{2,1,0:T(8,128)(2,1)} %copy-done.12) | copy-start | bytes 2359300
  140.9 12.4 %copy-start.15 = (f32[8,64,128]{2,1,0:T(8,128)S(1)}, f32[8,64,128]{2,1,0:T(8,128)}, u32[]{:S(2)}) copy-start(f32[8,64,128]{2,1,0:T(8,128)} %copy-done.14) | copy-start | bytes 786436
  153.2 2.2 %copy-start.3 = (bf16[24,384,128]{2,1,0:T(8,128)(2,1)S(1)}, bf16[24,384,128]{2,1,0:T(8,128)(2,1)}, u32[]{:S(2)}) copy-start(bf16[24,384,128]{2,1,0:T(8,128)(2,1)} %copy-done.2) | copy-start | bytes 7077892
  153.3 2.4 %copy-start.5 = (bf16[24,384,128]{2,1,0:T(8,128)(2,1)S(1)}, bf16[24,384,128]{2,1,0:T(8,128)(2,1)}, u32[]{:S(2)}) copy-start(bf16[24,384,128]{2,1,0:T(8,128)(2,1)} %copy-done.4) | copy-start | bytes 7077892
  153.3 2.5 %copy-start.7 = (f32[24,64,128]{2,1,0:T(8,128)S(1)}, f32[24,64,128]{2,1,0:T(8,128)}, u32[]{:S(2)}) copy-start(f32[24,64,128]{2,1,0:T(8,128)} %copy-done.6) | copy-start | bytes 2359300
  160.1 24.4 %collective-permute-start.16 = (f32[17,64,128]{2,1,0:T(8,128)S(1)}, f32[17,64,128]{2,1,0:T(8,128)S(1)}, u32[]{:S(2)}, u32[]{:S(2)}) collective-permute-start(f32[17,64,128]{2,1,0:T(8,128)S(1)} %pad_maximum_fusion.3), channel_id=1, source_target_pairs={{0,0},{2,4},{4,2},{6,6},{1,1},{3,5},{5,3},{7,7},{8,8},{10,12},{12,... | collective-permute-start | bytes 1671176 | tf_op jit(solution)/shard_map/ppermute | solution.py:209
  169.0 18.3 %collective-permute-start.15 = (f32[8,64,128]{2,1,0:T(8,128)S(1)}, f32[8,64,128]{2,1,0:T(8,128)S(1)}, u32[]{:S(2)}, u32[]{:S(2)}) collective-permute-start(f32[8,64,128]{2,1,0:T(8,128)S(1)} %get-tuple-element.66), channel_id=1, source_target_pairs={{0,0},{2,4},{4,2},{6,6},{1,1},{3,5},{5,3},{7,7},{8,8},{10,12},{12,... | collective-permute-start | bytes 786440 | tf_op jit(solution)/shard_map/ppermute | solution.py:209
  170.9 19.2 %collective-permute-start.17 = (f32[8,64,128]{2,1,0:T(8,128)S(1)}, f32[8,64,128]{2,1,0:T(8,128)S(1)}, u32[]{:S(2)}, u32[]{:S(2)}) collective-permute-start(f32[8,64,128]{2,1,0:T(8,128)S(1)} %get-tuple-element.69), channel_id=1, source_target_pairs={{0,0},{2,4},{4,2},{6,6},{1,1},{3,5},{5,3},{7,7},{8,8},{10,12},{12,... | collective-permute-start | bytes 786440 | tf_op jit(solution)/shard_map/ppermute | solution.py:209
Sparse Core Ops, SparseCore 0:
  92.8 30.2 all-gather.2

commit v11 on v10

--- a/solution.py
+++ b/solution.py
@@ -242,7 +242,7 @@
     far = [to_keeper(part) for part in parts]
     across = [keepers(far[0])]
     early = [to_trader(value) for value in (own, near, far[0])]
-    across += [keepers(after(early, value)) for value in far[1:]]
+    across += [keepers(after(early[:2], value)) for value in far[1:]]
     top = lax.all_gather(after((far[-1], sides), top), ("xy", "core"), axis=0, tiled=False)
 
     names = sides[(leafs + 1) * columns :][:3, :leafs].T.astype(jnp.int32).reshape(-1)

time: 199 us -> 199 us (level)
  transfers between devices with their start and end apart: 20 -> 20, of which waited for: 11 -> 10; matrix products, arithmetic and copies ran while one was open for 3% -> 3% of each run, Pallas kernels for 12% -> 12%
where the time goes in v11:
time: 199 us; the launch traced here: 198 us
  waiting for transfers between devices  74 us (37%)
  starting transfers between devices  51.3 us (26%)
  Pallas kernels  32.3 us (16%)
  between operations  14.4 us (7%)
  blocking collectives  9.66 us (5%)
  local copies, waits for them, and re-layouts  8.88 us (4%)
  other arithmetic  7.53 us (4%)
    ppermute x2, waiting for transfers between devices, to_keeper(): return lax.ppermute(value, ('core', 'zh'), [(1, 0), (2, 3)])  47.8 us
    pallas_call x2, Pallas kernels, local(): pl.pallas_call(functools.partial(forward_kernel, base, leafs, k == 0, las...  17.2 us
    ppermute x4, starting transfers between devices, swap(): return lax.ppermute(value, ('core', 'zh'), [(0, 0), (1, 2), (2, 1), (3, 3)])  16.3 us
    ppermute x4, waiting for transfers between devices, swap(): return lax.ppermute(value, ('core', 'zh'), [(0, 0), (1, 2), (2, 1), (3, 3)])  14 us
    ppermute x2, starting transfers between devices, to_keeper(): return lax.ppermute(value, ('core', 'zh'), [(1, 0), (2, 3)])  13.8 us
    ppermute x6, waiting for transfers between devices, to_trader(): return lax.ppermute(value, ('core', 'zh'), [(0, 2), (3, 1)])  10.1 us
    all_to_all x1, blocking collectives, local(): lax.all_to_all(outgoing, ('xy', 'zh'), split_axis=0, concat_axis=0, tiled...  9.66 us
    pallas_call x4, Pallas kernels, local(): pl.pallas_call(functools.partial(backward_kernel, k * turn, k == TURNS -...  9.65 us
  transfers between devices with their start and end apart: 20, of which 10 were waited for; matrix products, arithmetic and copies ran while one was open for 3% of the time, Pallas kernels for 12%

profile of v11, /device:TPU:1, one launch (start us, length us, event | category | flops | bytes accessed | tf_op | source)
XLA Modules:
  0.0 198.0 jit_solution(13869656211920191930)
XLA Ops:
  7.2 0.7 fusion.1
  9.3 0.7 fusion.2
  10.0 3.2 %collective-permute-start = (f32[4,32,128]{2,1,0:T(8,128)S(1)}, f32[4,32,128]{2,1,0:T(8,128)S(1)}, u32[]{:S(2)}, u32[]{:S(2)}) collective-permute-start(f32[4,32,128]{2,1,0:T(8,128)S(1)} %get-tuple-element.71), channel_id=1, source_target_pairs={{0,2},{2,0},{1,3},{3,1},{4,6},{6,4},{5,7},{7,5},{8,10},{10,8},{9,1... | collective-permute-start | bytes 196616 | tf_op jit(solution)/shard_map/ppermute | solution.py:222
  13.2 1.3 collective-permute-start.1
  15.9 1.3 pad_maximum_fusion.1
  17.5 1.1 select_maximum_fusion
  18.5 0.8 pad_maximum_fusion.4
  19.6 0.7 pad_maximum_fusion.5
  20.3 5.5 %collective-permute-start.5 = (f32[24,4,32,128]{3,2,1,0:T(8,128)}, f32[24,4,32,128]{3,2,1,0:T(8,128)}, u32[]{:S(2)}, u32[]{:S(2)}) collective-permute-start(f32[24,4,32,128]{3,2,1,0:T(8,128)} %pad_maximum_fusion.1), channel_id=1, source_target_pairs={{2,0},{4,6},{3,1},{5,7},{10,8},{12,14},{11,9},{13,15},{18,16},{20,... | collective-permute-start | bytes 4718600 | tf_op jit(solution)/shard_map/ppermute | solution.py:212
  25.8 2.1 %collective-permute-start.4 = (f32[32,4,32,128]{3,2,1,0:T(8,128)S(1)}, f32[32,4,32,128]{3,2,1,0:T(8,128)}, u32[]{:S(2)}, u32[]{:S(2)}) collective-permute-start(f32[32,4,32,128]{3,2,1,0:T(8,128)S(1)} %pad_maximum_fusion.refs_1_), channel_id=1, source_target_pairs={{0,1},{1,0},{6,7},{7,6},{8,9},{9,8},{14,15},{15,14},{16,17},{17,16... | collective-permute-start | bytes 6291464 | tf_op jit(solution)/shard_map/ppermute | solution.py:218
  27.9 4.2 %collective-permute-start.3 = (f32[2120,128]{1,0:T(8,128)}, f32[2120,128]{1,0:T(8,128)S(1)}, u32[]{:S(2)}, u32[]{:S(2)}) collective-permute-start(f32[2120,128]{1,0:T(8,128)} %select_maximum_fusion), channel_id=1, source_target_pairs={{0,0},{2,4},{4,2},{6,6},{1,1},{3,5},{5,3},{7,7},{8,8},{10,12},{12,... | collective-permute-start | bytes 3256328 | tf_op jit(solution)/shard_map/ppermute | solution.py:209
  32.1 26.0 %collective-permute-done.5.refs_3_ = f32[24,4,32,128]{3,2,1,0:T(8,128)} collective-permute-done((f32[24,4,32,128]{3,2,1,0:T(8,128)}, f32[24,4,32,128]{3,2,1,0:T(8,128)}, u32[]{:S(2)}, u32[]{:S(2)}) %collective-permute-start.5) | collective-permute-done | bytes 1572896 | tf_op jit(solution)/shard_map/ppermute | solution.py:212
  58.1 1.8 collective-permute-start.6
  59.9 8.3 %collective-permute-start.10 = (f32[8,4,32,128]{3,2,1,0:T(8,128)}, f32[8,4,32,128]{3,2,1,0:T(8,128)}, u32[]{:S(2)}, u32[]{:S(2)}) collective-permute-start(f32[8,4,32,128]{3,2,1,0:T(8,128)} %pad_maximum_fusion.4), channel_id=1, source_target_pairs={{2,0},{4,6},{3,1},{5,7},{10,8},{12,14},{11,9},{13,15},{18,16},{20,... | collective-permute-start | bytes 1572872 | tf_op jit(solution)/shard_map/ppermute | solution.py:212
  68.2 1.3 collective-permute-start.7
  69.5 1.3 collective-permute-start.8
  70.8 21.8 %collective-permute-done.10.refs_3_ = f32[8,4,32,128]{3,2,1,0:T(8,128)} collective-permute-done((f32[8,4,32,128]{3,2,1,0:T(8,128)}, f32[8,4,32,128]{3,2,1,0:T(8,128)}, u32[]{:S(2)}, u32[]{:S(2)}) %collective-permute-start.10) | collective-permute-done | bytes 524320 | tf_op jit(solution)/shard_map/ppermute | solution.py:212
  92.7 1.3 collective-permute-start.11
  94.0 1.3 collective-permute-start.9
  95.3 4.5 %collective-permute-done.11.refs_7_ = f32[8,4,32,128]{3,2,1,0:T(8,128)S(1)} collective-permute-done((f32[8,4,32,128]{3,2,1,0:T(8,128)}, f32[8,4,32,128]{3,2,1,0:T(8,128)S(1)}, u32[]{:S(2)}, u32[]{:S(2)}) %collective-permute-start.11) | collective-permute-done | bytes 524320 | tf_op jit(solution)/shard_map/ppermute | solution.py:215
  99.8 0.8 copy-done.8
  100.6 1.3 collective-permute-start.12
  101.9 0.7 dynamic-slice_bitcast_fusion
  102.6 1.5 collective-permute-start.13
  104.3 2.9 %collective-permute-done.12.refs_8_ = f32[24,4,32,128]{3,2,1,0:T(8,128)} collective-permute-done((f32[24,4,32,128]{3,2,1,0:T(8,128)}, f32[24,4,32,128]{3,2,1,0:T(8,128)}, u32[]{:S(2)}, u32[]{:S(2)}) %collective-permute-start.12) | collective-permute-done | bytes 1572896 | tf_op jit(solution)/shard_map/ppermute | solution.py:215
  107.3 11.4 %leaf_forward.2 = (f32[40,64,128]{2,1,0:T(8,128)S(1)}, bf16[24,384,128]{2,1,0:T(8,128)(2,1)S(1)}, bf16[24,384,128]{2,1,0:T(8,128)(2,1)S(1)}, f32[24,64,128]{2,1,0:T(8,128)S(1)}) custom-call(s32[105]{0:T(128)S(1)} %concatenate.31.refs_0_.meta, f32[32,4,32,128]{3,2,1,0:T(8,128)S(1)} %pad_maximum_fusion.refs_1_, ...), custom_call_target="tpu_custom_call" | custom-call | flops 4000000000 | bytes 8388608 | tf_op jit(solution)/shard_map/leaf_forward/pallas_call | solution.py:275
  118.8 1.3 collective-permute-start.14
  120.0 2.7 %collective-permute-done.14.refs_8_ = f32[8,4,32,128]{3,2,1,0:T(8,128)S(1)} collective-permute-done((f32[8,4,32,128]{3,2,1,0:T(8,128)}, f32[8,4,32,128]{3,2,1,0:T(8,128)S(1)}, u32[]{:S(2)}, u32[]{:S(2)}) %collective-permute-start.14) | collective-permute-done | bytes 524320 | tf_op jit(solution)/shard_map/ppermute | solution.py:215
  122.8 5.8 %leaf_forward.3 = (f32[40,64,128]{2,1,0:T(8,128)}, bf16[8,384,128]{2,1,0:T(8,128)(2,1)S(1)}, bf16[8,384,128]{2,1,0:T(8,128)(2,1)S(1)}, f32[8,64,128]{2,1,0:T(8,128)S(1)}, f32[8,5,8,128]{3,2,1,0:T(8,128)}) custom-call(s32[105]{0:T(128)S(1)} %concatenate.31.refs_0_.meta, f32[32,4,32,128]{3,2,1,0:T(8,128)S(1)} %pad_maximum_fusion.refs_1_, ...), custom_call_target="tpu_custom_call" | custom-call | flops 4000000000 | bytes 8388608 | tf_op jit(solution)/shard_map/leaf_forward/pallas_call | solution.py:275
  128.6 0.9 copy-done.10
  129.5 0.9 copy-done.12
  131.1 3.6 %all-to-all-start = ((f32[8,5,8,128]{3,2,1,0:T(8,128)}), f32[8,5,8,128]{3,2,1,0:T(8,128)S(1)}, u32[]{:S(2)}, u32[]{:S(2)}) async-start(f32[8,5,8,128]{3,2,1,0:T(8,128)} %get-tuple-element.56), calls=%async_computation | async-start | bytes 327680 | tf_op jit(solution)/shard_map/all_to_all | solution.py:308
  134.7 1.6 copy-done.1
  136.3 2.7 %top_prepare.1 = (bf16[8,384,128]{2,1,0:T(8,128)(2,1)S(1)}, bf16[8,384,128]{2,1,0:T(8,128)(2,1)S(1)}, bf16[8,128,128]{2,1,0:T(8,128)(2,1)S(1)}, bf16[8,128,128]{2,1,0:T(8,128)(2,1)S(1)}) custom-call(s32[4]{0:T(128)S(1)} %pad_add_fusion.places, f32[8,4,4,32,128]{4,3,2,1,0:T(8,128)S(1)} %bitcast.34), custom_call_target="tpu_custom_call" | custom-call | tf_op jit(solution)/shard_map/top_prepare/pallas_call | solution.py:296
  139.0 1.8 all-to-all-done.incoming
  140.9 2.7 %top_solve.1 = f32[8,5,8,128]{3,2,1,0:T(8,128)S(1)} custom-call(f32[8,5,8,128]{3,2,1,0:T(8,128)S(1)} %all-to-all-done.incoming, bf16[8,384,128]{2,1,0:T(8,128)(2,1)S(1)} %get-tuple-element.59.high, bf16[8,384,128]{2,1,0:T(8,128)(2,1)S(1)} %get-tuple-element.60.low, bf16[8,128,128]{2,1,0:T(8,128)(2,1)S(1)} %get-tuple-element.61.inverse_high, ...), custom_call_target="tpu_custom_call" | custom-call | tf_op jit(solution)/shard_map/top_solve/pallas_call | solution.py:309
  143.6 9.7 %all_to_all.10.state = f32[8,5,8,128]{3,2,1,0:T(8,128)S(1)} all-to-all(f32[8,5,8,128]{3,2,1,0:T(8,128)S(1)} %top_solve.1), channel_id=1, replica_groups=mesh['xy'=4,'core'=2,'zh'=2,'zl'=2] {'xy','zh'}, dimensions={0} | all-to-all | bytes 327680 | tf_op jit(solution)/shard_map/all_to_all | solution.py:317
  153.3 2.1 %leaf_backward.4 = (f32[8,64,128]{2,1,0:T(8,128)S(1)}, f32[40,64,128]{2,1,0:T(8,128)S(1)}) custom-call(s32[105]{0:T(128)S(1)} %concatenate.31.refs_0_.meta, bf16[8,384,128]{2,1,0:T(8,128)(2,1)S(1)} %copy-done.11, bf16[8,384,128]{2,1,0:T(8,128)(2,1)S(1)} %copy-done.13, f32[8,64,128]{2,1,0:T(8,128)S(1)} %copy-done.15, f32[8,5,8,128]{3,2,1,0:T(8,128)S(1)} %all_to_all.10.state), custom_call_target="tpu_custom_call" | custom-call | flops 4000000000 | bytes 8388608 | tf_op jit(solution)/shard_map/leaf_backward/pallas_call | solution.py:330
  155.8 2.1 %leaf_backward.5 = (f32[8,64,128]{2,1,0:T(8,128)S(1)}, f32[40,64,128]{2,1,0:T(8,128)S(1)}) custom-call(s32[105]{0:T(128)S(1)} %concatenate.31.refs_0_.meta, bf16[24,384,128]{2,1,0:T(8,128)(2,1)S(1)} %copy-done.3, bf16[24,384,128]{2,1,0:T(8,128)(2,1)S(1)} %copy-done.5, f32[24,64,128]{2,1,0:T(8,128)S(1)} %copy-done.7, f32[40,64,128]{2,1,0:T(8,128)S(1)} %get-tuple-element.63.state), custom_call_target="tpu_custom_call" | custom-call | flops 4000000000 | bytes 8388608 | tf_op jit(solution)/shard_map/leaf_backward/pallas_call | solution.py:330
  157.9 2.1 %leaf_backward.6 = (f32[8,64,128]{2,1,0:T(8,128)S(1)}, f32[40,64,128]{2,1,0:T(8,128)S(1)}) custom-call(s32[105]{0:T(128)S(1)} %concatenate.31.refs_0_.meta, bf16[24,384,128]{2,1,0:T(8,128)(2,1)S(1)} %copy-done.3, bf16[24,384,128]{2,1,0:T(8,128)(2,1)S(1)} %copy-done.5, f32[24,64,128]{2,1,0:T(8,128)S(1)} %copy-done.7, f32[40,64,128]{2,1,0:T(8,128)S(1)} %get-tuple-element.64.state), custom_call_target="tpu_custom_call" | custom-call | flops 4000000000 | bytes 8388608 | tf_op jit(solution)/shard_map/leaf_backward/pallas_call | solution.py:330
  160.1 5.6 %collective-permute-start.16 = (f32[17,64,128]{2,1,0:T(8,128)S(1)}, f32[17,64,128]{2,1,0:T(8,128)S(1)}, u32[]{:S(2)}, u32[]{:S(2)}) collective-permute-start(f32[17,64,128]{2,1,0:T(8,128)S(1)} %pad_maximum_fusion.3), channel_id=1, source_target_pairs={{0,0},{2,4},{4,2},{6,6},{1,1},{3,5},{5,3},{7,7},{8,8},{10,12},{12,... | collective-permute-start | bytes 1671176 | tf_op jit(solution)/shard_map/ppermute | solution.py:209
  165.7 3.3 %leaf_backward.7 = (f32[8,64,128]{2,1,0:T(8,128)S(1)}, f32[40,64,128]{2,1,0:T(8,128)}) custom-call(s32[105]{0:T(128)S(1)} %concatenate.31.refs_0_.meta, bf16[24,384,128]{2,1,0:T(8,128)(2,1)S(1)} %copy-done.3, bf16[24,384,128]{2,1,0:T(8,128)(2,1)S(1)} %copy-done.5, f32[24,64,128]{2,1,0:T(8,128)S(1)} %copy-done.7, f32[40,64,128]{2,1,0:T(8,128)S(1)} %get-tuple-element.65.state), custom_call_target="tpu_custom_call" | custom-call | flops 4000000000 | bytes 8388608 | tf_op jit(solution)/shard_map/leaf_backward/pallas_call | solution.py:330
  169.0 1.9 collective-permute-start.15
  170.9 4.5 %collective-permute-start.17 = (f32[8,64,128]{2,1,0:T(8,128)S(1)}, f32[8,64,128]{2,1,0:T(8,128)S(1)}, u32[]{:S(2)}, u32[]{:S(2)}) collective-permute-start(f32[8,64,128]{2,1,0:T(8,128)S(1)} %get-tuple-element.69), channel_id=1, source_target_pairs={{0,0},{2,4},{4,2},{6,6},{1,1},{3,5},{5,3},{7,7},{8,8},{10,12},{12,... | collective-permute-start | bytes 786440 | tf_op jit(solution)/shard_map/ppermute | solution.py:209
  175.4 9.1 %collective-permute-done.16 = f32[17,64,128]{2,1,0:T(8,128)S(1)} collective-permute-done((f32[17,64,128]{2,1,0:T(8,128)S(1)}, f32[17,64,128]{2,1,0:T(8,128)S(1)}, u32[]{:S(2)}, u32[]{:S(2)}) %collective-permute-start.16) | collective-permute-done | bytes 557088 | tf_op jit(solution)/shard_map/ppermute | solution.py:209
  185.2 2.1 %collective-permute-done.15 = f32[8,64,128]{2,1,0:T(8,128)S(1)} collective-permute-done((f32[8,64,128]{2,1,0:T(8,128)S(1)}, f32[8,64,128]{2,1,0:T(8,128)S(1)}, u32[]{:S(2)}, u32[]{:S(2)}) %collective-permute-start.15) | collective-permute-done | bytes 262176 | tf_op jit(solution)/shard_map/ppermute | solution.py:209
  187.3 2.8 %collective-permute-done.17 = f32[8,64,128]{2,1,0:T(8,128)S(1)} collective-permute-done((f32[8,64,128]{2,1,0:T(8,128)S(1)}, f32[8,64,128]{2,1,0:T(8,128)S(1)}, u32[]{:S(2)}, u32[]{:S(2)}) %collective-permute-start.17) | collective-permute-done | bytes 262176 | tf_op jit(solution)/shard_map/ppermute | solution.py:209
  190.1 1.1 pad_maximum_fusion.2
  (73 shorter events, 5.4 us)
Async XLA Ops:
  7.2 1.5 copy-start
  7.2 127.6 %all-gather.3.cloned.1.call-start = ((), (), s32[]{:S(2)}) async-start(), calls=%async_computation.2 | async-start | bytes 2359296 | tf_op jit(solution)/shard_map/all_gather | solution.py:246
  10.0 4.5 %copy-start.17 = (f32[32,32,128]{2,1,0:T(8,128)S(1)}, f32[32,32,128]{2,1,0:T(8,128)}, u32[]{:S(2)}) copy-start(f32[32,32,128]{2,1,0:T(8,128)} %param.14) | copy-start | bytes 1572868
  10.0 4.6 %copy-start.16 = (f32[32,3,32,128]{3,2,1,0:T(8,128)S(1)}, f32[32,3,32,128]{3,2,1,0:T(8,128)}, u32[]{:S(2)}) copy-start(f32[32,3,32,128]{3,2,1,0:T(8,128)} %param.13) | copy-start | bytes 4718596
  10.0 9.3 %collective-permute-start = (f32[4,32,128]{2,1,0:T(8,128)S(1)}, f32[4,32,128]{2,1,0:T(8,128)S(1)}, u32[]{:S(2)}, u32[]{:S(2)}) collective-permute-start(f32[4,32,128]{2,1,0:T(8,128)S(1)} %get-tuple-element.71), channel_id=1, source_target_pairs={{0,2},{2,0},{1,3},{3,1},{4,6},{6,4},{5,7},{7,5},{8,10},{10,8},{9,1... | collective-permute-start | bytes 196616 | tf_op jit(solution)/shard_map/ppermute | solution.py:222
  13.2 6.1 %collective-permute-start.1 = (f32[4,32,128]{2,1,0:T(8,128)S(1)}, f32[4,32,128]{2,1,0:T(8,128)S(1)}, u32[]{:S(2)}, u32[]{:S(2)}) collective-permute-start(f32[4,32,128]{2,1,0:T(8,128)S(1)} %get-tuple-element.71), channel_id=1, source_target_pairs={{0,1},{1,0},{2,3},{3,2},{4,5},{5,4},{6,7},{7,6},{8,9},{9,8},{10,11... | collective-permute-start | bytes 196616 | tf_op jit(solution)/shard_map/ppermute | solution.py:222
  14.5 5.0 %collective-permute-start.2 = (f32[4,32,128]{2,1,0:T(8,128)S(1)}, f32[4,32,128]{2,1,0:T(8,128)S(1)}, u32[]{:S(2)}, u32[]{:S(2)}) collective-permute-start(f32[4,32,128]{2,1,0:T(8,128)S(1)} %get-tuple-element.71), channel_id=1, source_target_pairs={{0,3},{1,2},{2,1},{3,0},{4,7},{5,6},{6,5},{7,4},{8,11},{9,10},{10,... | collective-permute-start | bytes 196616 | tf_op jit(solution)/shard_map/ppermute | solution.py:222
  14.6 0.7 copy-start.20
  14.6 1.3 slice-start
  15.9 1.6 copy-start.18
  15.9 1.6 copy-start.19
  17.2 1.3 slice-start.1
  20.3 37.8 %collective-permute-start.5 = (f32[24,4,32,128]{3,2,1,0:T(8,128)}, f32[24,4,32,128]{3,2,1,0:T(8,128)}, u32[]{:S(2)}, u32[]{:S(2)}) collective-permute-start(f32[24,4,32,128]{3,2,1,0:T(8,128)} %pad_maximum_fusion.1), channel_id=1, source_target_pairs={{2,0},{4,6},{3,1},{5,7},{10,8},{12,14},{11,9},{13,15},{18,16},{20,... | collective-permute-start | bytes 4718600 | tf_op jit(solution)/shard_map/ppermute | solution.py:212
  25.8 43.7 %collective-permute-start.4 = (f32[32,4,32,128]{3,2,1,0:T(8,128)S(1)}, f32[32,4,32,128]{3,2,1,0:T(8,128)}, u32[]{:S(2)}, u32[]{:S(2)}) collective-permute-start(f32[32,4,32,128]{3,2,1,0:T(8,128)S(1)} %pad_maximum_fusion.refs_1_), channel_id=1, source_target_pairs={{0,1},{1,0},{6,7},{7,6},{8,9},{9,8},{14,15},{15,14},{16,17},{17,16... | collective-permute-start | bytes 6291464 | tf_op jit(solution)/shard_map/ppermute | solution.py:218
  27.9 64.8 %collective-permute-start.3 = (f32[2120,128]{1,0:T(8,128)}, f32[2120,128]{1,0:T(8,128)S(1)}, u32[]{:S(2)}, u32[]{:S(2)}) collective-permute-start(f32[2120,128]{1,0:T(8,128)} %select_maximum_fusion), channel_id=1, source_target_pairs={{0,0},{2,4},{4,2},{6,6},{1,1},{3,5},{5,3},{7,7},{8,8},{10,12},{12,... | collective-permute-start | bytes 3256328 | tf_op jit(solution)/shard_map/ppermute | solution.py:209
  58.1 42.4 %collective-permute-start.6 = (f32[24,4,32,128]{3,2,1,0:T(8,128)}, f32[24,4,32,128]{3,2,1,0:T(8,128)}, u32[]{:S(2)}, u32[]{:S(2)}) collective-permute-start(f32[24,4,32,128]{3,2,1,0:T(8,128)} %collective-permute-done.5.refs_3_), channel_id=1, source_target_pairs={{0,1},{1,0},{6,7},{7,6},{8,9},{9,8},{14,15},{15,14},{16,17},{17,16... | collective-permute-start | bytes 4718600 | tf_op jit(solution)/shard_map/ppermute | solution.py:218
  59.9 32.7 %collective-permute-start.10 = (f32[8,4,32,128]{3,2,1,0:T(8,128)}, f32[8,4,32,128]{3,2,1,0:T(8,128)}, u32[]{:S(2)}, u32[]{:S(2)}) collective-permute-start(f32[8,4,32,128]{3,2,1,0:T(8,128)} %pad_maximum_fusion.4), channel_id=1, source_target_pairs={{2,0},{4,6},{3,1},{5,7},{10,8},{12,14},{11,9},{13,15},{18,16},{20,... | collective-permute-start | bytes 1572872 | tf_op jit(solution)/shard_map/ppermute | solution.py:212
  68.2 34.4 %collective-permute-start.7 = (f32[32,4,32,128]{3,2,1,0:T(8,128)S(1)}, f32[32,4,32,128]{3,2,1,0:T(8,128)}, u32[]{:S(2)}, u32[]{:S(2)}) collective-permute-start(f32[32,4,32,128]{3,2,1,0:T(8,128)S(1)} %pad_maximum_fusion.refs_1_), channel_id=1, source_target_pairs={{0,4},{6,2},{1,5},{7,3},{8,12},{14,10},{9,13},{15,11},{16,20},{22,... | collective-permute-start | bytes 6291464 | tf_op jit(solution)/shard_map/ppermute | solution.py:215
  69.5 33.1 %collective-permute-start.8 = (f32[32,4,32,128]{3,2,1,0:T(8,128)}, f32[32,4,32,128]{3,2,1,0:T(8,128)}, u32[]{:S(2)}, u32[]{:S(2)}) collective-permute-start(f32[32,4,32,128]{3,2,1,0:T(8,128)} %collective-permute-done.4.refs_2_), channel_id=1, source_target_pairs={{0,4},{6,2},{1,5},{7,3},{8,12},{14,10},{9,13},{15,11},{16,20},{22,... | collective-permute-start | bytes 6291464 | tf_op jit(solution)/shard_map/ppermute | solution.py:215
  92.7 7.1 %collective-permute-start.11 = (f32[8,4,32,128]{3,2,1,0:T(8,128)}, f32[8,4,32,128]{3,2,1,0:T(8,128)S(1)}, u32[]{:S(2)}, u32[]{:S(2)}) collective-permute-start(f32[8,4,32,128]{3,2,1,0:T(8,128)} %collective-permute-done.10.refs_3_), channel_id=1, source_target_pairs={{0,4},{6,2},{1,5},{7,3},{8,12},{14,10},{9,13},{15,11},{16,20},{22,... | collective-permute-start | bytes 1572872 | tf_op jit(solution)/shard_map/ppermute | solution.py:215
  94.0 10.4 %collective-permute-start.9 = (f32[24,4,32,128]{3,2,1,0:T(8,128)}, f32[24,4,32,128]{3,2,1,0:T(8,128)}, u32[]{:S(2)}, u32[]{:S(2)}) collective-permute-start(f32[24,4,32,128]{3,2,1,0:T(8,128)} %collective-permute-done.5.refs_3_), channel_id=1, source_target_pairs={{0,4},{6,2},{1,5},{7,3},{8,12},{14,10},{9,13},{15,11},{16,20},{22,... | collective-permute-start | bytes 4718600 | tf_op jit(solution)/shard_map/ppermute | solution.py:215
  99.8 0.8 copy-start.8
  100.6 6.7 %collective-permute-start.12 = (f32[24,4,32,128]{3,2,1,0:T(8,128)}, f32[24,4,32,128]{3,2,1,0:T(8,128)}, u32[]{:S(2)}, u32[]{:S(2)}) collective-permute-start(f32[24,4,32,128]{3,2,1,0:T(8,128)} %collective-permute-done.6.refs_4_), channel_id=1, source_target_pairs={{0,4},{6,2},{1,5},{7,3},{8,12},{14,10},{9,13},{15,11},{16,20},{22,... | collective-permute-start | bytes 4718600 | tf_op jit(solution)/shard_map/ppermute | solution.py:215
  102.6 16.1 %collective-permute-start.13 = (f32[8,4,32,128]{3,2,1,0:T(8,128)}, f32[8,4,32,128]{3,2,1,0:T(8,128)}, u32[]{:S(2)}, u32[]{:S(2)}) collective-permute-start(f32[8,4,32,128]{3,2,1,0:T(8,128)} %collective-permute-done.10.refs_3_), channel_id=1, source_target_pairs={{0,1},{1,0},{6,7},{7,6},{8,9},{9,8},{14,15},{15,14},{16,17},{17,16... | collective-permute-start | bytes 1572872 | tf_op jit(solution)/shard_map/ppermute | solution.py:218
  104.3 18.4 %copy-start.9 = (f32[8,4,32,128]{3,2,1,0:T(8,128)S(1)}, f32[8,4,32,128]{3,2,1,0:T(8,128)}, u32[]{:S(2)}) copy-start(f32[8,4,32,128]{3,2,1,0:T(8,128)} %copy-done.8) | copy-start | bytes 1572868
  118.7 9.8 %copy-start.2 = (bf16[24,384,128]{2,1,0:T(8,128)(2,1)}, bf16[24,384,128]{2,1,0:T(8,128)(2,1)S(1)}, u32[]{:S(2)}) copy-start(bf16[24,384,128]{2,1,0:T(8,128)(2,1)S(1)} %get-tuple-element.47.high) | copy-start | bytes 7077892
  118.7 9.8 %copy-start.4 = (bf16[24,384,128]{2,1,0:T(8,128)(2,1)}, bf16[24,384,128]{2,1,0:T(8,128)(2,1)S(1)}, u32[]{:S(2)}) copy-start(bf16[24,384,128]{2,1,0:T(8,128)(2,1)S(1)} %get-tuple-element.48.low) | copy-start | bytes 7077892
  118.7 9.8 %copy-start.6 = (f32[24,64,128]{2,1,0:T(8,128)}, f32[24,64,128]{2,1,0:T(8,128)S(1)}, u32[]{:S(2)}) copy-start(f32[24,64,128]{2,1,0:T(8,128)S(1)} %get-tuple-element.49.scaled) | copy-start | bytes 2359300
  118.8 4.0 %collective-permute-start.14 = (f32[8,4,32,128]{3,2,1,0:T(8,128)}, f32[8,4,32,128]{3,2,1,0:T(8,128)S(1)}, u32[]{:S(2)}, u32[]{:S(2)}) collective-permute-start(f32[8,4,32,128]{3,2,1,0:T(8,128)} %collective-permute-done.13.refs_4_), channel_id=1, source_target_pairs={{0,4},{6,2},{1,5},{7,3},{8,12},{14,10},{9,13},{15,11},{16,20},{22,... | collective-permute-start | bytes 1572872 | tf_op jit(solution)/shard_map/ppermute | solution.py:215
  128.6 0.9 copy-start.10
  129.5 0.9 copy-start.12
  130.4 0.7 copy-start.14
  131.1 9.8 %all-to-all-start = ((f32[8,5,8,128]{3,2,1,0:T(8,128)}), f32[8,5,8,128]{3,2,1,0:T(8,128)S(1)}, u32[]{:S(2)}, u32[]{:S(2)}) async-start(f32[8,5,8,128]{3,2,1,0:T(8,128)} %get-tuple-element.56), calls=%async_computation | async-start | bytes 327680 | tf_op jit(solution)/shard_map/all_to_all | solution.py:308
  134.7 1.6 copy-start.1
  140.9 12.4 %copy-start.11 = (bf16[8,384,128]{2,1,0:T(8,128)(2,1)S(1)}, bf16[8,384,128]{2,1,0:T(8,128)(2,1)}, u32[]{:S(2)}) copy-start(bf16[8,384,128]{2,1,0:T(8,128)(2,1)} %copy-done.10) | copy-start | bytes 2359300
  140.9 12.4 %copy-start.13 = (bf16[8,384,128]{2,1,0:T(8,128)(2,1)S(1)}, bf16[8,384,128]{2,1,0:T(8,128)(2,1)}, u32[]{:S(2)}) copy-start(bf16[8,384,128]{2,1,0:T(8,128)(2,1)} %copy-done.12) | copy-start | bytes 2359300
  140.9 12.4 %copy-start.15 = (f32[8,64,128]{2,1,0:T(8,128)S(1)}, f32[8,64,128]{2,1,0:T(8,128)}, u32[]{:S(2)}) copy-start(f32[8,64,128]{2,1,0:T(8,128)} %copy-done.14) | copy-start | bytes 786436
  153.2 2.2 %copy-start.3 = (bf16[24,384,128]{2,1,0:T(8,128)(2,1)S(1)}, bf16[24,384,128]{2,1,0:T(8,128)(2,1)}, u32[]{:S(2)}) copy-start(bf16[24,384,128]{2,1,0:T(8,128)(2,1)} %copy-done.2) | copy-start | bytes 7077892
  153.3 2.4 %copy-start.5 = (bf16[24,384,128]{2,1,0:T(8,128)(2,1)S(1)}, bf16[24,384,128]{2,1,0:T(8,128)(2,1)}, u32[]{:S(2)}) copy-start(bf16[24,384,128]{2,1,0:T(8,128)(2,1)} %copy-done.4) | copy-start | bytes 7077892
  153.3 2.5 %copy-start.7 = (f32[24,64,128]{2,1,0:T(8,128)S(1)}, f32[24,64,128]{2,1,0:T(8,128)}, u32[]{:S(2)}) copy-start(f32[24,64,128]{2,1,0:T(8,128)} %copy-done.6) | copy-start | bytes 2359300
  160.1 24.4 %collective-permute-start.16 = (f32[17,64,128]{2,1,0:T(8,128)S(1)}, f32[17,64,128]{2,1,0:T(8,128)S(1)}, u32[]{:S(2)}, u32[]{:S(2)}) collective-permute-start(f32[17,64,128]{2,1,0:T(8,128)S(1)} %pad_maximum_fusion.3), channel_id=1, source_target_pairs={{0,0},{2,4},{4,2},{6,6},{1,1},{3,5},{5,3},{7,7},{8,8},{10,12},{12,... | collective-permute-start | bytes 1671176 | tf_op jit(solution)/shard_map/ppermute | solution.py:209
  169.0 18.3 %collective-permute-start.15 = (f32[8,64,128]{2,1,0:T(8,128)S(1)}, f32[8,64,128]{2,1,0:T(8,128)S(1)}, u32[]{:S(2)}, u32[]{:S(2)}) collective-permute-start(f32[8,64,128]{2,1,0:T(8,128)S(1)} %get-tuple-element.66), channel_id=1, source_target_pairs={{0,0},{2,4},{4,2},{6,6},{1,1},{3,5},{5,3},{7,7},{8,8},{10,12},{12,... | collective-permute-start | bytes 786440 | tf_op jit(solution)/shard_map/ppermute | solution.py:209
  170.9 19.2 %collective-permute-start.17 = (f32[8,64,128]{2,1,0:T(8,128)S(1)}, f32[8,64,128]{2,1,0:T(8,128)S(1)}, u32[]{:S(2)}, u32[]{:S(2)}) collective-permute-start(f32[8,64,128]{2,1,0:T(8,128)S(1)} %get-tuple-element.69), channel_id=1, source_target_pairs={{0,0},{2,4},{4,2},{6,6},{1,1},{3,5},{5,3},{7,7},{8,8},{10,12},{12,... | collective-permute-start | bytes 786440 | tf_op jit(solution)/shard_map/ppermute | solution.py:209
Sparse Core Ops, SparseCore 0:
  92.8 30.2 all-gather.2

commit v12 on v11

--- a/solution.py
+++ b/solution.py
@@ -337,11 +337,10 @@
             cost_estimate=cost,
             name="leaf_backward",
         )(meta, *factors[held], state)
-    late = swap(found[-1])
-    middle = swap(jnp.concatenate(found[1:-1] + [own_top], axis=0))
+    most_of = swap(jnp.concatenate(found[1:] + [own_top], axis=0))
     first = swap(found[0])
-    leaf_solution = jnp.concatenate([first, middle[:-1], late], axis=0)
-    return (leaf_solution, middle[-1:])
+    leaf_solution = jnp.concatenate([first, most_of[:-1]], axis=0)
+    return (leaf_solution, most_of[-1:])
 
 
 def solution(mesh):

time: 199 us -> 199 us (level)
  starting transfers between devices: 51.3 us -> 46.7 us
  waiting for transfers between devices: 74 us -> 78.5 us
    ppermute x4 -> x3, starting transfers between devices: 16.3 us -> 11.7 us  [swap(): return lax.ppermute(value, ('core', 'zh'), [(0, 0), (1, 2), (2, 1), (3, 3)])]
    ppermute x4 -> x3, waiting for transfers between devices: 14 us -> 18.5 us  [swap(): return lax.ppermute(value, ('core', 'zh'), [(0, 0), (1, 2), (2, 1), (3, 3)])]
  transfers between devices with their start and end apart: 20 -> 19, of which waited for: 10 -> 9; matrix products, arithmetic and copies ran while one was open for 3% -> 3% of each run, Pallas kernels for 12% -> 12%
where the time goes in v12:
time: 199 us; the launch traced here: 198 us
  waiting for transfers between devices  78.5 us (39%)
  starting transfers between devices  46.7 us (23%)
  Pallas kernels  32.3 us (16%)
  between operations  14.4 us (7%)
  blocking collectives  9.66 us (5%)
  local copies, waits for them, and re-layouts  8.92 us (4%)
  other arithmetic  7.56 us (4%)
    ppermute x2, waiting for transfers between devices, to_keeper(): return lax.ppermute(value, ('core', 'zh'), [(1, 0), (2, 3)])  47.8 us
    ppermute x3, waiting for transfers between devices, swap(): return lax.ppermute(value, ('core', 'zh'), [(0, 0), (1, 2), (2, 1), (3, 3)])  18.5 us
    pallas_call x2, Pallas kernels, local(): pl.pallas_call(functools.partial(forward_kernel, base, leafs, k == 0, las...  17.2 us
    ppermute x2, starting transfers between devices, to_keeper(): return lax.ppermute(value, ('core', 'zh'), [(1, 0), (2, 3)])  13.8 us
    ppermute x3, starting transfers between devices, swap(): return lax.ppermute(value, ('core', 'zh'), [(0, 0), (1, 2), (2, 1), (3, 3)])  11.7 us
    ppermute x6, waiting for transfers between devices, to_trader(): return lax.ppermute(value, ('core', 'zh'), [(0, 2), (3, 1)])  10.1 us
    all_to_all x1, blocking collectives, local(): lax.all_to_all(outgoing, ('xy', 'zh'), split_axis=0, concat_axis=0, tiled...  9.66 us
    pallas_call x4, Pallas kernels, local(): pl.pallas_call(functools.partial(backward_kernel, k * turn, k == TURNS -...  9.66 us
  transfers between devices with their start and end apart: 19, of which 9 were waited for; matrix products, arithmetic and copies ran while one was open for 3% of the time, Pallas kernels for 12%

profile of v12, /device:TPU:1, one launch (start us, length us, event | category | flops | bytes accessed | tf_op | source)
XLA Modules:
  0.0 198.1 jit_solution(15457912848502989408)
XLA Ops:
  7.2 0.7 fusion.1
  7.9 0.7 compare_and_fusion
  9.3 0.7 fusion.2
  10.0 3.2 %collective-permute-start = (f32[4,32,128]{2,1,0:T(8,128)S(1)}, f32[4,32,128]{2,1,0:T(8,128)S(1)}, u32[]{:S(2)}, u32[]{:S(2)}) collective-permute-start(f32[4,32,128]{2,1,0:T(8,128)S(1)} %get-tuple-element.71), channel_id=1, source_target_pairs={{0,2},{2,0},{1,3},{3,1},{4,6},{6,4},{5,7},{7,5},{8,10},{10,8},{9,1... | collective-permute-start | bytes 196616 | tf_op jit(solution)/shard_map/ppermute | solution.py:222
  13.2 1.3 collective-permute-start.1
  15.9 1.3 pad_maximum_fusion.1
  17.5 1.1 select_maximum_fusion
  18.5 0.8 pad_maximum_fusion.4
  19.6 0.7 pad_maximum_fusion.5
  20.3 5.5 %collective-permute-start.5 = (f32[24,4,32,128]{3,2,1,0:T(8,128)}, f32[24,4,32,128]{3,2,1,0:T(8,128)}, u32[]{:S(2)}, u32[]{:S(2)}) collective-permute-start(f32[24,4,32,128]{3,2,1,0:T(8,128)} %pad_maximum_fusion.1), channel_id=1, source_target_pairs={{2,0},{4,6},{3,1},{5,7},{10,8},{12,14},{11,9},{13,15},{18,16},{20,... | collective-permute-start | bytes 4718600 | tf_op jit(solution)/shard_map/ppermute | solution.py:212
  25.8 2.1 %collective-permute-start.4 = (f32[32,4,32,128]{3,2,1,0:T(8,128)S(1)}, f32[32,4,32,128]{3,2,1,0:T(8,128)}, u32[]{:S(2)}, u32[]{:S(2)}) collective-permute-start(f32[32,4,32,128]{3,2,1,0:T(8,128)S(1)} %pad_maximum_fusion.refs_1_), channel_id=1, source_target_pairs={{0,1},{1,0},{6,7},{7,6},{8,9},{9,8},{14,15},{15,14},{16,17},{17,16... | collective-permute-start | bytes 6291464 | tf_op jit(solution)/shard_map/ppermute | solution.py:218
  27.9 4.2 %collective-permute-start.3 = (f32[2120,128]{1,0:T(8,128)}, f32[2120,128]{1,0:T(8,128)S(1)}, u32[]{:S(2)}, u32[]{:S(2)}) collective-permute-start(f32[2120,128]{1,0:T(8,128)} %select_maximum_fusion), channel_id=1, source_target_pairs={{0,0},{2,4},{4,2},{6,6},{1,1},{3,5},{5,3},{7,7},{8,8},{10,12},{12,... | collective-permute-start | bytes 3256328 | tf_op jit(solution)/shard_map/ppermute | solution.py:209
  32.1 26.0 %collective-permute-done.5.refs_3_ = f32[24,4,32,128]{3,2,1,0:T(8,128)} collective-permute-done((f32[24,4,32,128]{3,2,1,0:T(8,128)}, f32[24,4,32,128]{3,2,1,0:T(8,128)}, u32[]{:S(2)}, u32[]{:S(2)}) %collective-permute-start.5) | collective-permute-done | bytes 1572896 | tf_op jit(solution)/shard_map/ppermute | solution.py:212
  58.1 1.8 collective-permute-start.6
  59.9 8.3 %collective-permute-start.10 = (f32[8,4,32,128]{3,2,1,0:T(8,128)}, f32[8,4,32,128]{3,2,1,0:T(8,128)}, u32[]{:S(2)}, u32[]{:S(2)}) collective-permute-start(f32[8,4,32,128]{3,2,1,0:T(8,128)} %pad_maximum_fusion.4), channel_id=1, source_target_pairs={{2,0},{4,6},{3,1},{5,7},{10,8},{12,14},{11,9},{13,15},{18,16},{20,... | collective-permute-start | bytes 1572872 | tf_op jit(solution)/shard_map/ppermute | solution.py:212
  68.2 1.3 collective-permute-start.7
  69.5 1.3 collective-permute-start.8
  70.8 21.8 %collective-permute-done.10.refs_3_ = f32[8,4,32,128]{3,2,1,0:T(8,128)} collective-permute-done((f32[8,4,32,128]{3,2,1,0:T(8,128)}, f32[8,4,32,128]{3,2,1,0:T(8,128)}, u32[]{:S(2)}, u32[]{:S(2)}) %collective-permute-start.10) | collective-permute-done | bytes 524320 | tf_op jit(solution)/shard_map/ppermute | solution.py:212
  92.6 1.3 collective-permute-start.11
  93.9 1.3 collective-permute-start.9
  95.2 4.5 %collective-permute-done.11.refs_7_ = f32[8,4,32,128]{3,2,1,0:T(8,128)S(1)} collective-permute-done((f32[8,4,32,128]{3,2,1,0:T(8,128)}, f32[8,4,32,128]{3,2,1,0:T(8,128)S(1)}, u32[]{:S(2)}, u32[]{:S(2)}) %collective-permute-start.11) | collective-permute-done | bytes 524320 | tf_op jit(solution)/shard_map/ppermute | solution.py:215
  99.8 0.8 copy-done.8
  100.6 1.3 collective-permute-start.12
  101.9 0.7 dynamic-slice_bitcast_fusion
  102.6 1.5 collective-permute-start.13
  104.4 2.9 %collective-permute-done.12.refs_8_ = f32[24,4,32,128]{3,2,1,0:T(8,128)} collective-permute-done((f32[24,4,32,128]{3,2,1,0:T(8,128)}, f32[24,4,32,128]{3,2,1,0:T(8,128)}, u32[]{:S(2)}, u32[]{:S(2)}) %collective-permute-start.12) | collective-permute-done | bytes 1572896 | tf_op jit(solution)/shard_map/ppermute | solution.py:215
  107.2 11.4 %leaf_forward.2 = (f32[40,64,128]{2,1,0:T(8,128)S(1)}, bf16[24,384,128]{2,1,0:T(8,128)(2,1)S(1)}, bf16[24,384,128]{2,1,0:T(8,128)(2,1)S(1)}, f32[24,64,128]{2,1,0:T(8,128)S(1)}) custom-call(s32[105]{0:T(128)S(1)} %concatenate.31.refs_0_.meta, f32[32,4,32,128]{3,2,1,0:T(8,128)S(1)} %pad_maximum_fusion.refs_1_, ...), custom_call_target="tpu_custom_call" | custom-call | flops 4000000000 | bytes 8388608 | tf_op jit(solution)/shard_map/leaf_forward/pallas_call | solution.py:275
  118.7 1.3 collective-permute-start.14
  120.0 2.7 %collective-permute-done.14.refs_8_ = f32[8,4,32,128]{3,2,1,0:T(8,128)S(1)} collective-permute-done((f32[8,4,32,128]{3,2,1,0:T(8,128)}, f32[8,4,32,128]{3,2,1,0:T(8,128)S(1)}, u32[]{:S(2)}, u32[]{:S(2)}) %collective-permute-start.14) | collective-permute-done | bytes 524320 | tf_op jit(solution)/shard_map/ppermute | solution.py:215
  122.8 5.8 %leaf_forward.3 = (f32[40,64,128]{2,1,0:T(8,128)}, bf16[8,384,128]{2,1,0:T(8,128)(2,1)S(1)}, bf16[8,384,128]{2,1,0:T(8,128)(2,1)S(1)}, f32[8,64,128]{2,1,0:T(8,128)S(1)}, f32[8,5,8,128]{3,2,1,0:T(8,128)}) custom-call(s32[105]{0:T(128)S(1)} %concatenate.31.refs_0_.meta, f32[32,4,32,128]{3,2,1,0:T(8,128)S(1)} %pad_maximum_fusion.refs_1_, ...), custom_call_target="tpu_custom_call" | custom-call | flops 4000000000 | bytes 8388608 | tf_op jit(solution)/shard_map/leaf_forward/pallas_call | solution.py:275
  128.6 0.9 copy-done.10
  129.5 0.9 copy-done.12
  130.4 0.7 copy-done.14
  131.1 3.6 %all-to-all-start = ((f32[8,5,8,128]{3,2,1,0:T(8,128)}), f32[8,5,8,128]{3,2,1,0:T(8,128)S(1)}, u32[]{:S(2)}, u32[]{:S(2)}) async-start(f32[8,5,8,128]{3,2,1,0:T(8,128)} %get-tuple-element.56), calls=%async_computation | async-start | bytes 327680 | tf_op jit(solution)/shard_map/all_to_all | solution.py:308
  134.7 1.6 copy-done.1
  136.3 2.7 %top_prepare.1 = (bf16[8,384,128]{2,1,0:T(8,128)(2,1)S(1)}, bf16[8,384,128]{2,1,0:T(8,128)(2,1)S(1)}, bf16[8,128,128]{2,1,0:T(8,128)(2,1)S(1)}, bf16[8,128,128]{2,1,0:T(8,128)(2,1)S(1)}) custom-call(s32[4]{0:T(128)S(1)} %pad_add_fusion.places, f32[8,4,4,32,128]{4,3,2,1,0:T(8,128)S(1)} %bitcast.34), custom_call_target="tpu_custom_call" | custom-call | tf_op jit(solution)/shard_map/top_prepare/pallas_call | solution.py:296
  139.0 1.8 all-to-all-done.incoming
  140.9 2.7 %top_solve.1 = f32[8,5,8,128]{3,2,1,0:T(8,128)S(1)} custom-call(f32[8,5,8,128]{3,2,1,0:T(8,128)S(1)} %all-to-all-done.incoming, bf16[8,384,128]{2,1,0:T(8,128)(2,1)S(1)} %get-tuple-element.59.high, bf16[8,384,128]{2,1,0:T(8,128)(2,1)S(1)} %get-tuple-element.60.low, bf16[8,128,128]{2,1,0:T(8,128)(2,1)S(1)} %get-tuple-element.61.inverse_high, ...), custom_call_target="tpu_custom_call" | custom-call | tf_op jit(solution)/shard_map/top_solve/pallas_call | solution.py:309
  143.6 9.7 %all_to_all.10.state = f32[8,5,8,128]{3,2,1,0:T(8,128)S(1)} all-to-all(f32[8,5,8,128]{3,2,1,0:T(8,128)S(1)} %top_solve.1), channel_id=1, replica_groups=mesh['xy'=4,'core'=2,'zh'=2,'zl'=2] {'xy','zh'}, dimensions={0} | all-to-all | bytes 327680 | tf_op jit(solution)/shard_map/all_to_all | solution.py:317
  153.3 2.1 %leaf_backward.4 = (f32[8,64,128]{2,1,0:T(8,128)S(1)}, f32[40,64,128]{2,1,0:T(8,128)S(1)}) custom-call(s32[105]{0:T(128)S(1)} %concatenate.31.refs_0_.meta, bf16[8,384,128]{2,1,0:T(8,128)(2,1)S(1)} %copy-done.11, bf16[8,384,128]{2,1,0:T(8,128)(2,1)S(1)} %copy-done.13, f32[8,64,128]{2,1,0:T(8,128)S(1)} %copy-done.15, f32[8,5,8,128]{3,2,1,0:T(8,128)S(1)} %all_to_all.10.state), custom_call_target="tpu_custom_call" | custom-call | flops 4000000000 | bytes 8388608 | tf_op jit(solution)/shard_map/leaf_backward/pallas_call | solution.py:330
  155.8 2.1 %leaf_backward.5 = (f32[8,64,128]{2,1,0:T(8,128)S(1)}, f32[40,64,128]{2,1,0:T(8,128)S(1)}) custom-call(s32[105]{0:T(128)S(1)} %concatenate.31.refs_0_.meta, bf16[24,384,128]{2,1,0:T(8,128)(2,1)S(1)} %copy-done.3, bf16[24,384,128]{2,1,0:T(8,128)(2,1)S(1)} %copy-done.5, f32[24,64,128]{2,1,0:T(8,128)S(1)} %copy-done.7, f32[40,64,128]{2,1,0:T(8,128)S(1)} %get-tuple-element.63.state), custom_call_target="tpu_custom_call" | custom-call | flops 4000000000 | bytes 8388608 | tf_op jit(solution)/shard_map/leaf_backward/pallas_call | solution.py:330
  157.9 2.1 %leaf_backward.6 = (f32[8,64,128]{2,1,0:T(8,128)S(1)}, f32[40,64,128]{2,1,0:T(8,128)S(1)}) custom-call(s32[105]{0:T(128)S(1)} %concatenate.31.refs_0_.meta, bf16[24,384,128]{2,1,0:T(8,128)(2,1)S(1)} %copy-done.3, bf16[24,384,128]{2,1,0:T(8,128)(2,1)S(1)} %copy-done.5, f32[24,64,128]{2,1,0:T(8,128)S(1)} %copy-done.7, f32[40,64,128]{2,1,0:T(8,128)S(1)} %get-tuple-element.64.state), custom_call_target="tpu_custom_call" | custom-call | flops 4000000000 | bytes 8388608 | tf_op jit(solution)/shard_map/leaf_backward/pallas_call | solution.py:330
  160.2 5.6 %collective-permute-start.16 = (f32[25,64,128]{2,1,0:T(8,128)S(1)}, f32[25,64,128]{2,1,0:T(8,128)S(1)}, u32[]{:S(2)}, u32[]{:S(2)}) collective-permute-start(f32[25,64,128]{2,1,0:T(8,128)S(1)} %pad_maximum_fusion.3), channel_id=1, source_target_pairs={{0,0},{2,4},{4,2},{6,6},{1,1},{3,5},{5,3},{7,7},{8,8},{10,12},{12,... | collective-permute-start | bytes 2457608 | tf_op jit(solution)/shard_map/ppermute | solution.py:209
  165.7 3.3 %leaf_backward.7 = (f32[8,64,128]{2,1,0:T(8,128)S(1)}, f32[40,64,128]{2,1,0:T(8,128)}) custom-call(s32[105]{0:T(128)S(1)} %concatenate.31.refs_0_.meta, bf16[24,384,128]{2,1,0:T(8,128)(2,1)S(1)} %copy-done.3, bf16[24,384,128]{2,1,0:T(8,128)(2,1)S(1)} %copy-done.5, f32[24,64,128]{2,1,0:T(8,128)S(1)} %copy-done.7, f32[40,64,128]{2,1,0:T(8,128)S(1)} %get-tuple-element.65.state), custom_call_target="tpu_custom_call" | custom-call | flops 4000000000 | bytes 8388608 | tf_op jit(solution)/shard_map/leaf_backward/pallas_call | solution.py:330
  169.0 1.9 collective-permute-start.15
  170.9 16.4 %collective-permute-done.16 = f32[25,64,128]{2,1,0:T(8,128)S(1)} collective-permute-done((f32[25,64,128]{2,1,0:T(8,128)S(1)}, f32[25,64,128]{2,1,0:T(8,128)S(1)}, u32[]{:S(2)}, u32[]{:S(2)}) %collective-permute-start.16) | collective-permute-done | bytes 819232 | tf_op jit(solution)/shard_map/ppermute | solution.py:209
  188.0 2.1 %collective-permute-done.15 = f32[8,64,128]{2,1,0:T(8,128)S(1)} collective-permute-done((f32[8,64,128]{2,1,0:T(8,128)S(1)}, f32[8,64,128]{2,1,0:T(8,128)S(1)}, u32[]{:S(2)}, u32[]{:S(2)}) %collective-permute-start.15) | collective-permute-done | bytes 262176 | tf_op jit(solution)/shard_map/ppermute | solution.py:209
  190.1 1.1 pad_maximum_fusion.2
  (71 shorter events, 4.1 us)
Async XLA Ops:
  7.2 1.5 copy-start
  7.2 127.6 %all-gather.3.cloned.1.call-start = ((), (), s32[]{:S(2)}) async-start(), calls=%async_computation.2 | async-start | bytes 2359296 | tf_op jit(solution)/shard_map/all_gather | solution.py:246
  10.0 4.5 %copy-start.17 = (f32[32,32,128]{2,1,0:T(8,128)S(1)}, f32[32,32,128]{2,1,0:T(8,128)}, u32[]{:S(2)}) copy-start(f32[32,32,128]{2,1,0:T(8,128)} %param.14) | copy-start | bytes 1572868
  10.0 4.6 %copy-start.16 = (f32[32,3,32,128]{3,2,1,0:T(8,128)S(1)}, f32[32,3,32,128]{3,2,1,0:T(8,128)}, u32[]{:S(2)}) copy-start(f32[32,3,32,128]{3,2,1,0:T(8,128)} %param.13) | copy-start | bytes 4718596
  10.0 9.3 %collective-permute-start = (f32[4,32,128]{2,1,0:T(8,128)S(1)}, f32[4,32,128]{2,1,0:T(8,128)S(1)}, u32[]{:S(2)}, u32[]{:S(2)}) collective-permute-start(f32[4,32,128]{2,1,0:T(8,128)S(1)} %get-tuple-element.71), channel_id=1, source_target_pairs={{0,2},{2,0},{1,3},{3,1},{4,6},{6,4},{5,7},{7,5},{8,10},{10,8},{9,1... | collective-permute-start | bytes 196616 | tf_op jit(solution)/shard_map/ppermute | solution.py:222
  13.2 6.1 %collective-permute-start.1 = (f32[4,32,128]{2,1,0:T(8,128)S(1)}, f32[4,32,128]{2,1,0:T(8,128)S(1)}, u32[]{:S(2)}, u32[]{:S(2)}) collective-permute-start(f32[4,32,128]{2,1,0:T(8,128)S(1)} %get-tuple-element.71), channel_id=1, source_target_pairs={{0,1},{1,0},{2,3},{3,2},{4,5},{5,4},{6,7},{7,6},{8,9},{9,8},{10,11... | collective-permute-start | bytes 196616 | tf_op jit(solution)/shard_map/ppermute | solution.py:222
  14.5 5.0 %collective-permute-start.2 = (f32[4,32,128]{2,1,0:T(8,128)S(1)}, f32[4,32,128]{2,1,0:T(8,128)S(1)}, u32[]{:S(2)}, u32[]{:S(2)}) collective-permute-start(f32[4,32,128]{2,1,0:T(8,128)S(1)} %get-tuple-element.71), channel_id=1, source_target_pairs={{0,3},{1,2},{2,1},{3,0},{4,7},{5,6},{6,5},{7,4},{8,11},{9,10},{10,... | collective-permute-start | bytes 196616 | tf_op jit(solution)/shard_map/ppermute | solution.py:222
  14.6 0.7 copy-start.20
  14.6 1.3 slice-start
  15.9 1.6 copy-start.18
  15.9 1.6 copy-start.19
  17.2 1.3 slice-start.1
  20.3 37.8 %collective-permute-start.5 = (f32[24,4,32,128]{3,2,1,0:T(8,128)}, f32[24,4,32,128]{3,2,1,0:T(8,128)}, u32[]{:S(2)}, u32[]{:S(2)}) collective-permute-start(f32[24,4,32,128]{3,2,1,0:T(8,128)} %pad_maximum_fusion.1), channel_id=1, source_target_pairs={{2,0},{4,6},{3,1},{5,7},{10,8},{12,14},{11,9},{13,15},{18,16},{20,... | collective-permute-start | bytes 4718600 | tf_op jit(solution)/shard_map/ppermute | solution.py:212
  25.8 43.7 %collective-permute-start.4 = (f32[32,4,32,128]{3,2,1,0:T(8,128)S(1)}, f32[32,4,32,128]{3,2,1,0:T(8,128)}, u32[]{:S(2)}, u32[]{:S(2)}) collective-permute-start(f32[32,4,32,128]{3,2,1,0:T(8,128)S(1)} %pad_maximum_fusion.refs_1_), channel_id=1, source_target_pairs={{0,1},{1,0},{6,7},{7,6},{8,9},{9,8},{14,15},{15,14},{16,17},{17,16... | collective-permute-start | bytes 6291464 | tf_op jit(solution)/shard_map/ppermute | solution.py:218
  27.9 64.8 %collective-permute-start.3 = (f32[2120,128]{1,0:T(8,128)}, f32[2120,128]{1,0:T(8,128)S(1)}, u32[]{:S(2)}, u32[]{:S(2)}) collective-permute-start(f32[2120,128]{1,0:T(8,128)} %select_maximum_fusion), channel_id=1, source_target_pairs={{0,0},{2,4},{4,2},{6,6},{1,1},{3,5},{5,3},{7,7},{8,8},{10,12},{12,... | collective-permute-start | bytes 3256328 | tf_op jit(solution)/shard_map/ppermute | solution.py:209
  58.1 42.5 %collective-permute-start.6 = (f32[24,4,32,128]{3,2,1,0:T(8,128)}, f32[24,4,32,128]{3,2,1,0:T(8,128)}, u32[]{:S(2)}, u32[]{:S(2)}) collective-permute-start(f32[24,4,32,128]{3,2,1,0:T(8,128)} %collective-permute-done.5.refs_3_), channel_id=1, source_target_pairs={{0,1},{1,0},{6,7},{7,6},{8,9},{9,8},{14,15},{15,14},{16,17},{17,16... | collective-permute-start | bytes 4718600 | tf_op jit(solution)/shard_map/ppermute | solution.py:218
  59.9 32.7 %collective-permute-start.10 = (f32[8,4,32,128]{3,2,1,0:T(8,128)}, f32[8,4,32,128]{3,2,1,0:T(8,128)}, u32[]{:S(2)}, u32[]{:S(2)}) collective-permute-start(f32[8,4,32,128]{3,2,1,0:T(8,128)} %pad_maximum_fusion.4), channel_id=1, source_target_pairs={{2,0},{4,6},{3,1},{5,7},{10,8},{12,14},{11,9},{13,15},{18,16},{20,... | collective-permute-start | bytes 1572872 | tf_op jit(solution)/shard_map/ppermute | solution.py:212
  68.2 34.4 %collective-permute-start.7 = (f32[32,4,32,128]{3,2,1,0:T(8,128)S(1)}, f32[32,4,32,128]{3,2,1,0:T(8,128)}, u32[]{:S(2)}, u32[]{:S(2)}) collective-permute-start(f32[32,4,32,128]{3,2,1,0:T(8,128)S(1)} %pad_maximum_fusion.refs_1_), channel_id=1, source_target_pairs={{0,4},{6,2},{1,5},{7,3},{8,12},{14,10},{9,13},{15,11},{16,20},{22,... | collective-permute-start | bytes 6291464 | tf_op jit(solution)/shard_map/ppermute | solution.py:215
  69.5 33.1 %collective-permute-start.8 = (f32[32,4,32,128]{3,2,1,0:T(8,128)}, f32[32,4,32,128]{3,2,1,0:T(8,128)}, u32[]{:S(2)}, u32[]{:S(2)}) collective-permute-start(f32[32,4,32,128]{3,2,1,0:T(8,128)} %collective-permute-done.4.refs_2_), channel_id=1, source_target_pairs={{0,4},{6,2},{1,5},{7,3},{8,12},{14,10},{9,13},{15,11},{16,20},{22,... | collective-permute-start | bytes 6291464 | tf_op jit(solution)/shard_map/ppermute | solution.py:215
  92.6 7.1 %collective-permute-start.11 = (f32[8,4,32,128]{3,2,1,0:T(8,128)}, f32[8,4,32,128]{3,2,1,0:T(8,128)S(1)}, u32[]{:S(2)}, u32[]{:S(2)}) collective-permute-start(f32[8,4,32,128]{3,2,1,0:T(8,128)} %collective-permute-done.10.refs_3_), channel_id=1, source_target_pairs={{0,4},{6,2},{1,5},{7,3},{8,12},{14,10},{9,13},{15,11},{16,20},{22,... | collective-permute-start | bytes 1572872 | tf_op jit(solution)/shard_map/ppermute | solution.py:215
  93.9 10.4 %collective-permute-start.9 = (f32[24,4,32,128]{3,2,1,0:T(8,128)}, f32[24,4,32,128]{3,2,1,0:T(8,128)}, u32[]{:S(2)}, u32[]{:S(2)}) collective-permute-start(f32[24,4,32,128]{3,2,1,0:T(8,128)} %collective-permute-done.5.refs_3_), channel_id=1, source_target_pairs={{0,4},{6,2},{1,5},{7,3},{8,12},{14,10},{9,13},{15,11},{16,20},{22,... | collective-permute-start | bytes 4718600 | tf_op jit(solution)/shard_map/ppermute | solution.py:215
  99.8 0.8 copy-start.8
  100.6 6.7 %collective-permute-start.12 = (f32[24,4,32,128]{3,2,1,0:T(8,128)}, f32[24,4,32,128]{3,2,1,0:T(8,128)}, u32[]{:S(2)}, u32[]{:S(2)}) collective-permute-start(f32[24,4,32,128]{3,2,1,0:T(8,128)} %collective-permute-done.6.refs_4_), channel_id=1, source_target_pairs={{0,4},{6,2},{1,5},{7,3},{8,12},{14,10},{9,13},{15,11},{16,20},{22,... | collective-permute-start | bytes 4718600 | tf_op jit(solution)/shard_map/ppermute | solution.py:215
  102.6 16.1 %collective-permute-start.13 = (f32[8,4,32,128]{3,2,1,0:T(8,128)}, f32[8,4,32,128]{3,2,1,0:T(8,128)}, u32[]{:S(2)}, u32[]{:S(2)}) collective-permute-start(f32[8,4,32,128]{3,2,1,0:T(8,128)} %collective-permute-done.10.refs_3_), channel_id=1, source_target_pairs={{0,1},{1,0},{6,7},{7,6},{8,9},{9,8},{14,15},{15,14},{16,17},{17,16... | collective-permute-start | bytes 1572872 | tf_op jit(solution)/shard_map/ppermute | solution.py:218
  104.3 18.4 %copy-start.9 = (f32[8,4,32,128]{3,2,1,0:T(8,128)S(1)}, f32[8,4,32,128]{3,2,1,0:T(8,128)}, u32[]{:S(2)}) copy-start(f32[8,4,32,128]{3,2,1,0:T(8,128)} %copy-done.8) | copy-start | bytes 1572868
  118.7 9.8 %copy-start.2 = (bf16[24,384,128]{2,1,0:T(8,128)(2,1)}, bf16[24,384,128]{2,1,0:T(8,128)(2,1)S(1)}, u32[]{:S(2)}) copy-start(bf16[24,384,128]{2,1,0:T(8,128)(2,1)S(1)} %get-tuple-element.47.high) | copy-start | bytes 7077892
  118.7 9.8 %copy-start.4 = (bf16[24,384,128]{2,1,0:T(8,128)(2,1)}, bf16[24,384,128]{2,1,0:T(8,128)(2,1)S(1)}, u32[]{:S(2)}) copy-start(bf16[24,384,128]{2,1,0:T(8,128)(2,1)S(1)} %get-tuple-element.48.low) | copy-start | bytes 7077892
  118.7 9.8 %copy-start.6 = (f32[24,64,128]{2,1,0:T(8,128)}, f32[24,64,128]{2,1,0:T(8,128)S(1)}, u32[]{:S(2)}) copy-start(f32[24,64,128]{2,1,0:T(8,128)S(1)} %get-tuple-element.49.scaled) | copy-start | bytes 2359300
  118.7 4.0 %collective-permute-start.14 = (f32[8,4,32,128]{3,2,1,0:T(8,128)}, f32[8,4,32,128]{3,2,1,0:T(8,128)S(1)}, u32[]{:S(2)}, u32[]{:S(2)}) collective-permute-start(f32[8,4,32,128]{3,2,1,0:T(8,128)} %collective-permute-done.13.refs_4_), channel_id=1, source_target_pairs={{0,4},{6,2},{1,5},{7,3},{8,12},{14,10},{9,13},{15,11},{16,20},{22,... | collective-permute-start | bytes 1572872 | tf_op jit(solution)/shard_map/ppermute | solution.py:215
  128.6 0.9 copy-start.10
  129.4 0.9 copy-start.12
  130.4 0.7 copy-start.14
  131.1 9.8 %all-to-all-start = ((f32[8,5,8,128]{3,2,1,0:T(8,128)}), f32[8,5,8,128]{3,2,1,0:T(8,128)S(1)}, u32[]{:S(2)}, u32[]{:S(2)}) async-start(f32[8,5,8,128]{3,2,1,0:T(8,128)} %get-tuple-element.56), calls=%async_computation | async-start | bytes 327680 | tf_op jit(solution)/shard_map/all_to_all | solution.py:308
  134.7 1.6 copy-start.1
  140.9 12.4 %copy-start.11 = (bf16[8,384,128]{2,1,0:T(8,128)(2,1)S(1)}, bf16[8,384,128]{2,1,0:T(8,128)(2,1)}, u32[]{:S(2)}) copy-start(bf16[8,384,128]{2,1,0:T(8,128)(2,1)} %copy-done.10) | copy-start | bytes 2359300
  140.9 12.4 %copy-start.13 = (bf16[8,384,128]{2,1,0:T(8,128)(2,1)S(1)}, bf16[8,384,128]{2,1,0:T(8,128)(2,1)}, u32[]{:S(2)}) copy-start(bf16[8,384,128]{2,1,0:T(8,128)(2,1)} %copy-done.12) | copy-start | bytes 2359300
  140.9 12.4 %copy-start.15 = (f32[8,64,128]{2,1,0:T(8,128)S(1)}, f32[8,64,128]{2,1,0:T(8,128)}, u32[]{:S(2)}) copy-start(f32[8,64,128]{2,1,0:T(8,128)} %copy-done.14) | copy-start | bytes 786436
  153.2 2.2 %copy-start.3 = (bf16[24,384,128]{2,1,0:T(8,128)(2,1)S(1)}, bf16[24,384,128]{2,1,0:T(8,128)(2,1)}, u32[]{:S(2)}) copy-start(bf16[24,384,128]{2,1,0:T(8,128)(2,1)} %copy-done.2) | copy-start | bytes 7077892
  153.3 2.4 %copy-start.5 = (bf16[24,384,128]{2,1,0:T(8,128)(2,1)S(1)}, bf16[24,384,128]{2,1,0:T(8,128)(2,1)}, u32[]{:S(2)}) copy-start(bf16[24,384,128]{2,1,0:T(8,128)(2,1)} %copy-done.4) | copy-start | bytes 7077892
  153.3 2.5 %copy-start.7 = (f32[24,64,128]{2,1,0:T(8,128)S(1)}, f32[24,64,128]{2,1,0:T(8,128)}, u32[]{:S(2)}) copy-start(f32[24,64,128]{2,1,0:T(8,128)} %copy-done.6) | copy-start | bytes 2359300
  160.2 27.2 %collective-permute-start.16 = (f32[25,64,128]{2,1,0:T(8,128)S(1)}, f32[25,64,128]{2,1,0:T(8,128)S(1)}, u32[]{:S(2)}, u32[]{:S(2)}) collective-permute-start(f32[25,64,128]{2,1,0:T(8,128)S(1)} %pad_maximum_fusion.3), channel_id=1, source_target_pairs={{0,0},{2,4},{4,2},{6,6},{1,1},{3,5},{5,3},{7,7},{8,8},{10,12},{12,... | collective-permute-start | bytes 2457608 | tf_op jit(solution)/shard_map/ppermute | solution.py:209
  169.0 21.1 %collective-permute-start.15 = (f32[8,64,128]{2,1,0:T(8,128)S(1)}, f32[8,64,128]{2,1,0:T(8,128)S(1)}, u32[]{:S(2)}, u32[]{:S(2)}) collective-permute-start(f32[8,64,128]{2,1,0:T(8,128)S(1)} %get-tuple-element.66), channel_id=1, source_target_pairs={{0,0},{2,4},{4,2},{6,6},{1,1},{3,5},{5,3},{7,7},{8,8},{10,12},{12,... | collective-permute-start | bytes 786440 | tf_op jit(solution)/shard_map/ppermute | solution.py:209
Sparse Core Ops, SparseCore 0:
  92.8 30.2 all-gather.2
